TPU v7x, 32 devices: a whole 2x2x4 slice. The times are simulated.
32 devices in a mesh: groups: 2 (over y), gx: 4 (over z), gy: 2 (over x), gz: 2 (over core).
Axes of the slice: x: 2, y: 2, z: 4, core: 2. Of those that a mesh axis runs over, the one named last changes fastest.
Arguments:
- state: float32 [64, 128, 512], P(('groups', 'gx'), 'gy', 'gz'), parts along dimension 0, may hold values from -6 to 6
- conduct: float32 [32, 128, 512], P('gx', 'gy', 'gz'), may hold values from 0.3 to 3
- sink: float32 [64, 128, 512], P(('groups', 'gx'), 'gy', 'gz'), parts along dimension 0, may hold values from 0.3 to 3
- labels: int32 [64, 128, 512], P(('groups', 'gx'), 'gy', 'gz'), parts along dimension 0, may hold values from 0 to 3
- cotangent: float32 [64, 128, 512], P(('groups', 'gx'), 'gy', 'gz'), parts along dimension 0, may hold values from -6 to 6
Outputs:
- grad_state: float32 [64, 128, 512], P(('groups', 'gx'), 'gy', 'gz'), parts along dimension 0
- grad_sink: float32 [64, 128, 512], P(('groups', 'gx'), 'gy', 'gz'), parts along dimension 0
There are 2 independent parts, one for each index of `groups`. A program takes and returns all parts, laid end to end along the dimension named above; an argument that names none is the same for every part. Nothing has to cross between parts.
Inputs may be any that keep to these rules, and one draw needn't show every extreme that they name: `labels`: each cell's class as in the meaning.
All inputs are finite; a program needn't handle non-finite values.
Results may differ from a plain program's by a relative error of at most 0.00002.
Values sent between devices are 32-bit elements; how exact they have to be, the bound alone decides.
No kernel may reach another device: no remote copies, remote signals or barrier semaphores. Data moves between devices by JAX's collectives and lax.ppermute only.
A program may use at most 64 MiB of HBM per device.

v0:
```python
import jax
import jax.numpy as jnp
from jax import lax
from jax.sharding import PartitionSpec as P

velocity = 0.5
time_step = 0.06


def from_behind(block, axis, distance):
    devices = range(lax.axis_size(axis))
    route = [((i - distance) % len(devices), i) for i in devices]
    return lax.ppermute(block, axis, route)


def from_behind_2(value, axis, steps):
    count = lax.axis_size(axis)
    leading, last = (max(0, -steps), min(count, count - steps))
    return lax.ppermute(value, axis, [(source, source + steps) for source in range(leading, last)])


def extended(block, sides, width):
    for axis, dim in sides:
        count = lax.axis_size(axis)
        forward = [(i, i + 1) for i in range(count - 1)]
        forward.append((count - 1, 0))
        backward = [(target, source) for source, target in forward]
        low = lax.ppermute(
            lax.slice_in_dim(block, block.shape[dim] - width, None, axis=dim), axis, forward
        )
        high = lax.ppermute(lax.slice_in_dim(block, 0, width, axis=dim), axis, backward)
        block = jnp.concatenate([low, block, high], axis=dim)
    return block


def window(array, axis, offset):
    index = []
    for which in range(3):
        if which == axis:
            if offset == 0:
                index.append(slice(0, -2))
            elif offset == 1:
                index.append(slice(1, -1))
            else:
                index.append(slice(2, None))
        else:
            index.append(slice(1, -1))
    return array[tuple(index)]


def trimmed(array):
    return array[1:-1, 1:-1, 1:-1]


def diffuse(padded, conduct_pad):
    centre = window(padded, 0, 1)
    middle = window(conduct_pad, 0, 1)
    total = jnp.zeros_like(centre)
    for axis in range(3):
        for offset in (2, 0):
            total = total + 0.5 * (middle + window(conduct_pad, axis, offset)) * (
                window(padded, axis, offset) - centre
            )
    return total


def rates(padded, conduct_pad, fluid, capacity, sink_term):
    centre = window(padded, 0, 1)
    advect = -velocity * fluid * (centre - window(padded, 0, 0))
    source = -sink_term * jnp.tanh(centre)
    return (diffuse(padded, conduct_pad) + advect + source) / capacity


def domain_mask(shape, margin):
    inner_y = shape[1] - 2 * margin
    inner_z = shape[2] - 2 * margin
    place_y = lax.axis_index("gy") * inner_y - margin + jnp.arange(shape[1], dtype=jnp.int32)
    place_z = lax.axis_index("gz") * inner_z - margin + jnp.arange(shape[2], dtype=jnp.int32)
    keep_y = jnp.logical_and(place_y >= 0, place_y < inner_y * lax.axis_size("gy"))
    keep_z = jnp.logical_and(place_z >= 0, place_z < inner_z * lax.axis_size("gz"))
    return jnp.logical_and(keep_y[:, None], keep_z[None, :]).astype(jnp.float32)[None]


def return_x(rim, offset):
    return from_behind(rim, "gx", offset)


def return_y(rim, offset):
    return from_behind_2(rim, "gy", offset)


def return_z(rim, offset):
    return from_behind_2(rim, "gz", offset)


def on_device(state, conduct, sink, labels, cotangent):
    fluid = (labels <= 1).astype(jnp.float32)
    solid = (labels >= 2).astype(jnp.float32)
    interface = jnp.logical_or(labels == 1, labels == 2).astype(jnp.float32)
    capacity = 1.0 + solid
    sink_term = sink * interface
    pad_shape = (state.shape[0] + 2, state.shape[1] + 2, state.shape[2] + 2)
    mask_one = domain_mask(pad_shape, 1)
    stacked = jnp.stack([state, conduct, fluid])
    padded = extended(stacked, (("gx", 1), ("gy", 2), ("gz", 3)), 1)
    state_pad = padded[0] * mask_one
    conduct_pad = padded[1] * mask_one
    first = state + time_step * rates(state_pad, conduct_pad, fluid, capacity, sink_term)
    first_pad = extended(first, (("gx", 0), ("gy", 1), ("gz", 2)), 1) * mask_one
    second = 0.75 * state + 0.25 * (
        first + time_step * rates(first_pad, conduct_pad, fluid, capacity, sink_term)
    )

    def transpose_rate(field, adjoint):

        def local(padded_field):
            return rates(padded_field, conduct_pad, fluid, capacity, sink_term)

        unused, pull = jax.vjp(local, jnp.pad(field, 1))
        (back,) = pull(adjoint)
        inner = trimmed(back)
        inner = inner.at[-1].add(return_x(back[0, 1:-1, 1:-1], -1))
        inner = inner.at[0].add(return_x(back[-1, 1:-1, 1:-1], 1))
        inner = inner.at[:, -1].add(return_y(back[1:-1, 0, 1:-1], -1))
        inner = inner.at[:, 0].add(return_y(back[1:-1, -1, 1:-1], 1))
        inner = inner.at[:, :, -1].add(return_z(back[1:-1, 1:-1, 0], -1))
        inner = inner.at[:, :, 0].add(return_z(back[1:-1, 1:-1, -1], 1))
        return inner

    def sink_part(field, adjoint):
        return time_step * (-jnp.tanh(field) / capacity) * adjoint

    third_back = transpose_rate(second, cotangent)
    second_adj = 2.0 / 3.0 * (cotangent + time_step * third_back)
    grad_state = cotangent / 3.0
    grad_term = 2.0 / 3.0 * sink_part(second, cotangent)
    second_back = transpose_rate(first, second_adj)
    first_adj = 0.25 * (second_adj + time_step * second_back)
    grad_state = grad_state + 0.75 * second_adj
    grad_term = grad_term + 0.25 * sink_part(first, second_adj)
    first_back = transpose_rate(state, first_adj)
    grad_state = grad_state + first_adj + time_step * first_back
    grad_term = grad_term + sink_part(state, first_adj)
    return (grad_state, grad_term * interface)


def solution(mesh):
    in_specs = (
        P(("groups", "gx"), "gy", "gz"),
        P("gx", "gy", "gz"),
        P(("groups", "gx"), "gy", "gz"),
        P(("groups", "gx"), "gy", "gz"),
        P(("groups", "gx"), "gy", "gz"),
    )
    out_specs = (P(("groups", "gx"), "gy", "gz"), P(("groups", "gx"), "gy", "gz"))
    return jax.shard_map(
        on_device, mesh=mesh, in_specs=in_specs, out_specs=out_specs, check_vma=False
    )
```

profile of v0, /device:TPU:0, one launch (start us, length us, event | category | flops | bytes accessed | tf_op | source)
XLA Modules:
  0.0 155.4 jit_solution(108919687285015746)
XLA Ops:
  2.0 3.1 %collective-permute-start = (f32[3,1,64,256]{3,2,1,0:T(8,128)S(1)}, f32[3,1,64,256]{3,2,1,0:T(8,128)S(1)}, u32[]{:S(2)}, u32[]{:S(2)}) collective-permute-start(f32[3,1,64,256]{3,2,1,0:T(8,128)S(1)} %get-tuple-element.271), channel_id=1, source_target_pairs={{0,4},{4,8},{8,12},{12,0},{1,5},{5,9},{9,13},{13,1},{2,6},{6,10},{... | collective-permute-start | bytes 589832 | tf_op jit(solution)/shard_map/ppermute | solution.py:28
  5.1 2.1 %collective-permute-start.1 = (f32[3,1,64,256]{3,2,1,0:T(8,128)S(1)}, f32[3,1,64,256]{3,2,1,0:T(8,128)S(1)}, u32[]{:S(2)}, u32[]{:S(2)}) collective-permute-start(f32[3,1,64,256]{3,2,1,0:T(8,128)S(1)} %get-tuple-element.272), channel_id=1, source_target_pairs={{4,0},{8,4},{12,8},{0,12},{5,1},{9,5},{13,9},{1,13},{6,2},{10,6},{... | collective-permute-start | bytes 589832 | tf_op jit(solution)/shard_map/ppermute | solution.py:31
  7.2 5.7 %collective-permute-done = f32[3,1,64,256]{3,2,1,0:T(8,128)S(1)} collective-permute-done((f32[3,1,64,256]{3,2,1,0:T(8,128)S(1)}, f32[3,1,64,256]{3,2,1,0:T(8,128)S(1)}, u32[]{:S(2)}, u32[]{:S(2)}) %collective-permute-start) | collective-permute-done | bytes 196640 | tf_op jit(solution)/shard_map/ppermute | solution.py:28
  12.9 2.8 %collective-permute-done.1 = f32[3,1,64,256]{3,2,1,0:T(8,128)S(1)} collective-permute-done((f32[3,1,64,256]{3,2,1,0:T(8,128)S(1)}, f32[3,1,64,256]{3,2,1,0:T(8,128)S(1)}, u32[]{:S(2)}, u32[]{:S(2)}) %collective-permute-start.1) | collective-permute-done | bytes 196640 | tf_op jit(solution)/shard_map/ppermute | solution.py:31
  15.7 1.6 %collective-permute-start.2 = (f32[3,10,1,256]{3,2,1,0:T(1,128)S(1)}, f32[3,10,1,256]{3,2,1,0:T(1,128)S(1)}, u32[]{:S(2)}, u32[]{:S(2)}) collective-permute-start(f32[3,10,1,256]{3,2,1,0:T(1,128)S(1)} %get-tuple-element.268), channel_id=1, source_target_pairs={{0,2},{2,0},{1,3},{3,1},{4,6},{6,4},{5,7},{7,5},{8,10},{10,8},{9,1... | collective-permute-start | bytes 92168 | tf_op jit(solution)/shard_map/ppermute | solution.py:28
  17.8 1.9 %collective-permute-done.2 = f32[3,10,1,256]{3,2,1,0:T(1,128)S(1)} collective-permute-done((f32[3,10,1,256]{3,2,1,0:T(1,128)S(1)}, f32[3,10,1,256]{3,2,1,0:T(1,128)S(1)}, u32[]{:S(2)}, u32[]{:S(2)}) %collective-permute-start.2) | collective-permute-done | bytes 30752 | tf_op jit(solution)/shard_map/ppermute | solution.py:28
  19.7 1.5 collective-permute-done.3
  21.4 1.4 fusion.77
  22.8 1.6 %copy.176 = f32[3,10,66,1]{2,3,1,0:T(1,128)S(1)} copy(f32[3,10,66,1]{3,2,1,0:T(8,128)} %get-tuple-element.266) | data formatting | bytes 15840 | tf_op jit(solution)/shard_map/slice | solution.py:29
  26.8 1.5 copy.179
  28.3 5.0 %pad_maximum_fusion = f32[3,10,66,258]{3,2,1,0:T(8,128)S(1)} fusion(f32[3,10,66,1]{3,2,1,0:T(8,128)} %copy.179, f32[3,10,1,256]{3,2,1,0:T(1,128)S(1)} %collective-permute-done.3, f32[3,1,64,256]{3,2,1,0:T(8,128)S(1)} %collective-permute-done.1, f32[1,8,64,256]{3,2,1,0:T(8,128)S(1)} %get-tuple-element.262, f32[1,8,64,256]{3,2,1,0:T(8,128)S(1)} %bitcast.73, ...), kind=kLoop, calls=%fused_computation | loop fusion | flops 4086720 | bytes 4086720 | tf_op jit(solution)/shard_map/concatenate | solution.py:32
  37.8 2.7 %collective-permute-start.7 = (f32[1,64,256]{2,1,0:T(8,128)S(1)}, f32[1,64,256]{2,1,0:T(8,128)S(1)}, u32[]{:S(2)}, u32[]{:S(2)}) collective-permute-start(f32[1,64,256]{2,1,0:T(8,128)S(1)} %get-tuple-element.294), channel_id=1, source_target_pairs={{4,0},{8,4},{12,8},{0,12},{5,1},{9,5},{13,9},{1,13},{6,2},{10,6},{... | collective-permute-start | bytes 196616 | tf_op jit(solution)/shard_map/ppermute | solution.py:31
  40.5 2.9 %collective-permute-done.6 = f32[1,64,256]{2,1,0:T(8,128)S(1)} collective-permute-done((f32[1,64,256]{2,1,0:T(8,128)S(1)}, f32[1,64,256]{2,1,0:T(8,128)S(1)}, u32[]{:S(2)}, u32[]{:S(2)}) %collective-permute-start.6) | collective-permute-done | bytes 65568 | tf_op jit(solution)/shard_map/ppermute | solution.py:28
  44.1 1.5 collective-permute-start.9
  45.6 1.6 %collective-permute-done.8 = f32[10,1,256]{2,1,0:T(1,128)S(1)} collective-permute-done((f32[10,1,256]{2,1,0:T(1,128)S(1)}, f32[10,1,256]{2,1,0:T(1,128)S(1)}, u32[]{:S(2)}, u32[]{:S(2)}) %collective-permute-start.8) | collective-permute-done | bytes 10272 | tf_op jit(solution)/shard_map/ppermute | solution.py:28
  50.9 2.0 %multiply_add_fusion.4 = (f32[8,64,256]{2,1,0:T(8,128)S(1)}, f32[8,64,256]{2,1,0:T(8,128)}) fusion(pred[8,64,256]{2,1,0:T(8,128)(4,1)S(1)} %get-tuple-element.263, pred[8,64,256]{2,1,0:T(8,128)(4,1)S(1)} %get-tuple-element.261, f32[8,64,256]{2,1,0:T(8,128)S(1)} %copy-done.8, f32[8,64,256]{2,1,0:T(8,128)S(1)} %copy-done.1, ...), kind=kLoop, calls=%fused_computation.79 | loop fusion | flops 5373952 | bytes 10354688 | tf_op jit(solution)/shard_map/transpose(jvp())/add_any | solution.py:69
  52.9 2.1 %pad_add_fusion.2 = f32[10,66,258]{2,1,0:T(8,128)S(1)} fusion(f32[8,64,256]{2,1,0:T(8,128)S(1)} %get-tuple-element.258, f32[8,64,256]{2,1,0:T(8,128)S(1)} %get-tuple-element.295, f32[8,64,256]{2,1,0:T(8,128)S(1)} %get-tuple-element.244, f32[8,64,256]{2,1,0:T(8,128)S(1)} %get-tuple-element.250, f32[8,64,256]{2,1,0:T(8,128)S(1)} %get-tuple-element.249, ...), kind=kLoop, calls=%fused_computation.14 | loop fusion | flops 1362240 | bytes 5399712 | tf_op jit(solution)/shard_map/transpose(jvp())/add_any | solution.py:48
  56.8 2.6 %collective-permute-start.17 = (f32[8,64]{1,0:T(8,128)}, f32[8,64]{1,0:T(8,128)}, u32[]{:S(2)}, u32[]{:S(2)}) collective-permute-start(f32[8,64]{1,0:T(8,128)} %get-tuple-element.226), channel_id=1, source_target_pairs={{0,1},{2,3},{4,5},{6,7},{8,9},{10,11},{12,13},{14,15},{16,17},{18,... | collective-permute-start | bytes 6152 | tf_op jit(solution)/shard_map/ppermute | solution.py:19
  60.7 3.1 %collective-permute-start.12 = (f32[64,256]{1,0:T(8,128)}, f32[64,256]{1,0:T(8,128)}, u32[]{:S(2)}, u32[]{:S(2)}) collective-permute-start(f32[64,256]{1,0:T(8,128)} %get-tuple-element.284), channel_id=1, source_target_pairs={{4,0},{8,4},{12,8},{0,12},{5,1},{9,5},{13,9},{1,13},{6,2},{10,6},{... | collective-permute-start | bytes 196616 | tf_op jit(solution)/shard_map/ppermute | solution.py:13
  65.4 1.5 collective-permute-start.14
  66.8 4.5 %collective-permute-start.15 = (f32[8,256]{1,0:T(8,128)}, f32[8,256]{1,0:T(8,128)S(1)}, u32[]{:S(2)}, u32[]{:S(2)}) collective-permute-start(f32[8,256]{1,0:T(8,128)} %bitcast.64), channel_id=1, source_target_pairs={{0,2},{1,3},{4,6},{5,7},{8,10},{9,11},{12,14},{13,15},{16,18},{17,... | collective-permute-start | bytes 24584 | tf_op jit(solution)/shard_map/ppermute | solution.py:19
  72.0 1.5 copy.182
  73.5 1.5 copy.183
  76.1 2.3 %collective-permute-done.13 = f32[64,256]{1,0:T(8,128)} collective-permute-done((f32[64,256]{1,0:T(8,128)}, f32[64,256]{1,0:T(8,128)}, u32[]{:S(2)}, u32[]{:S(2)}) %collective-permute-start.13) | collective-permute-done | bytes 65568 | tf_op jit(solution)/shard_map/ppermute | solution.py:13
  80.7 1.8 %slice_add_fusion.11 = f32[8,64,1]{2,1,0:T(8,128)} fusion(f32[8,64,1]{2,1,0:T(8,128)} %copy.182, f32[8,64,256]{2,1,0:T(8,128)S(1)} %scatter-add.65), kind=kLoop, calls=%fused_computation.102 | loop fusion | flops 512 | bytes 6144 | tf_op jit(solution)/shard_map/add | solution.py:126
  82.5 1.8 %scatter-add.66 = f32[8,64,256]{2,1,0:T(8,128)S(1)} dynamic-update-slice(f32[8,64,256]{2,1,0:T(8,128)S(1)} %scatter-add.65, f32[8,64,1]{2,1,0:T(8,128)} %slice_add_fusion.11, s32[]{:T(128)} %constant.433.clone.1, s32[]{:T(128)} %constant.433.clone.1, s32[]{:T(128)} %constant.447.clone.1) | dynamic-update-slice | bytes 4100 | tf_op jit(solution)/shard_map/scatter-add | solution.py:126
  84.3 1.7 %slice_add_fusion.10 = f32[8,64,1]{2,1,0:T(8,128)} fusion(f32[8,64,1]{2,1,0:T(8,128)} %copy.183, f32[8,64,256]{2,1,0:T(8,128)S(1)} %scatter-add.66), kind=kLoop, calls=%fused_computation.100 | loop fusion | flops 512 | bytes 6144 | tf_op jit(solution)/shard_map/add | solution.py:127
  87.1 2.1 %negate_add_fusion.1 = (f32[8,64,256]{2,1,0:T(8,128)S(1)}, f32[8,64,256]{2,1,0:T(8,128)S(1)}, f32[8,64,256]{2,1,0:T(8,128)S(1)}, f32[8,64,256]{2,1,0:T(8,128)S(1...) fusion(f32[8,64,256]{2,1,0:T(8,128)} %copy-done.5, ...), kind=kLoop, calls=%fused_computation.77 | loop fusion | flops 3014656 | bytes 8519680 | tf_op jit(solution)/shard_map/transpose(jvp())/add_any | solution.py:62
  89.6 2.2 %pad_add_fusion.1 = f32[10,66,258]{2,1,0:T(8,128)S(1)} fusion(f32[8,64,256]{2,1,0:T(8,128)S(1)} %get-tuple-element.290, f32[8,64,256]{2,1,0:T(8,128)S(1)} %get-tuple-element.289, f32[8,64,256]{2,1,0:T(8,128)S(1)} %get-tuple-element.236, f32[8,64,256]{2,1,0:T(8,128)S(1)} %get-tuple-element.242, f32[8,64,256]{2,1,0:T(8,128)S(1)} %get-tuple-element.241, ...), kind=kLoop, calls=%fused_computation.13 | loop fusion | flops 1362240 | bytes 5399712 | tf_op jit(solution)/shard_map/transpose(jvp())/add_any | solution.py:48
  93.5 2.0 %collective-permute-start.23 = (f32[8,64]{1,0:T(8,128)}, f32[8,64]{1,0:T(8,128)}, u32[]{:S(2)}, u32[]{:S(2)}) collective-permute-start(f32[8,64]{1,0:T(8,128)} %get-tuple-element.224), channel_id=1, source_target_pairs={{0,1},{2,3},{4,5},{6,7},{8,9},{10,11},{12,13},{14,15},{16,17},{18,... | collective-permute-start | bytes 6152 | tf_op jit(solution)/shard_map/ppermute | solution.py:19
  96.7 2.1 %collective-permute-start.18 = (f32[64,256]{1,0:T(8,128)}, f32[64,256]{1,0:T(8,128)}, u32[]{:S(2)}, u32[]{:S(2)}) collective-permute-start(f32[64,256]{1,0:T(8,128)} %get-tuple-element.280), channel_id=1, source_target_pairs={{4,0},{8,4},{12,8},{0,12},{5,1},{9,5},{13,9},{1,13},{6,2},{10,6},{... | collective-permute-start | bytes 196616 | tf_op jit(solution)/shard_map/ppermute | solution.py:13
  102.4 4.5 %collective-permute-start.21 = (f32[8,256]{1,0:T(8,128)}, f32[8,256]{1,0:T(8,128)S(1)}, u32[]{:S(2)}, u32[]{:S(2)}) collective-permute-start(f32[8,256]{1,0:T(8,128)} %bitcast.62), channel_id=1, source_target_pairs={{0,2},{1,3},{4,6},{5,7},{8,10},{9,11},{12,14},{13,15},{16,18},{17,... | collective-permute-start | bytes 24584 | tf_op jit(solution)/shard_map/ppermute | solution.py:19
  107.6 1.5 copy.186
  109.1 1.5 copy.187
  110.6 1.6 %fusion.50 = f32[8,64,256]{2,1,0:T(8,128)} fusion(f32[8,64,256]{2,1,0:T(8,128)} %slice.718, f32[10,66,258]{2,1,0:T(8,128)} %copy-done.12, f32[64,256]{1,0:T(8,128)} %collective-permute-done.18), kind=kLoop, calls=%fused_computation.120 | loop fusion | flops 16384 | bytes 196608 | tf_op jit(solution)/shard_map/scatter-add | solution.py:122
  112.2 1.7 %collective-permute-done.19 = f32[64,256]{1,0:T(8,128)} collective-permute-done((f32[64,256]{1,0:T(8,128)}, f32[64,256]{1,0:T(8,128)}, u32[]{:S(2)}, u32[]{:S(2)}) %collective-permute-start.19) | collective-permute-done | bytes 65568 | tf_op jit(solution)/shard_map/ppermute | solution.py:13
  114.0 1.5 fusion.49
  116.9 1.5 scatter-add.74
  119.3 1.5 scatter-add.75
  120.8 1.9 %slice_add_fusion.9 = f32[8,64,1]{2,1,0:T(8,128)} fusion(f32[8,64,1]{2,1,0:T(8,128)} %copy.186, f32[8,64,256]{2,1,0:T(8,128)} %scatter-add.75), kind=kLoop, calls=%fused_computation.98 | loop fusion | flops 512 | bytes 6144 | tf_op jit(solution)/shard_map/add | solution.py:126
  122.7 2.5 %scatter-add.76 = f32[8,64,256]{2,1,0:T(8,128)} dynamic-update-slice(f32[8,64,256]{2,1,0:T(8,128)} %scatter-add.75, f32[8,64,1]{2,1,0:T(8,128)} %slice_add_fusion.9, s32[]{:T(128)} %constant.433.clone.1, s32[]{:T(128)} %constant.433.clone.1, s32[]{:T(128)} %constant.447.clone.1) | dynamic-update-slice | bytes 4100 | tf_op jit(solution)/shard_map/scatter-add | solution.py:126
  125.2 1.7 %slice_add_fusion.8 = f32[8,64,1]{2,1,0:T(8,128)} fusion(f32[8,64,1]{2,1,0:T(8,128)} %copy.187, f32[8,64,256]{2,1,0:T(8,128)} %scatter-add.76), kind=kLoop, calls=%fused_computation.96 | loop fusion | flops 512 | bytes 6144 | tf_op jit(solution)/shard_map/add | solution.py:127
  126.9 1.8 %scatter-add.79 = f32[8,64,256]{2,1,0:T(8,128)} dynamic-update-slice(f32[8,64,256]{2,1,0:T(8,128)} %scatter-add.76, f32[8,64,1]{2,1,0:T(8,128)} %slice_add_fusion.8, s32[]{:T(128)} %constant.433.clone.1, s32[]{:T(128)} %constant.433.clone.1, s32[]{:T(128)} %constant.433.clone.1) | dynamic-update-slice | bytes 4100 | tf_op jit(solution)/shard_map/scatter-add | solution.py:127
  128.7 3.6 %negate_add_fusion = (f32[8,64,256]{2,1,0:T(8,128)S(1)}, f32[8,64,256]{2,1,0:T(8,128)S(1)}, f32[8,64,256]{2,1,0:T(8,128)S(1)}, f32[8,64,256]{2,1,0:T(8,128)S(1)}...) fusion(f32[8,64,256]{2,1,0:T(8,128)} %copy-done.5, ...), kind=kLoop, calls=%fused_computation.74 | loop fusion | flops 5636096 | bytes 11272192 | tf_op jit(solution)/shard_map/transpose(jvp())/add_any | solution.py:62
  132.6 2.2 %pad_add_fusion = f32[10,66,258]{2,1,0:T(8,128)S(1)} fusion(f32[8,64,256]{2,1,0:T(8,128)S(1)} %get-tuple-element.288, f32[8,64,256]{2,1,0:T(8,128)S(1)} %get-tuple-element.287, f32[8,64,256]{2,1,0:T(8,128)S(1)} %get-tuple-element.228, f32[8,64,256]{2,1,0:T(8,128)S(1)} %get-tuple-element.234, f32[8,64,256]{2,1,0:T(8,128)S(1)} %get-tuple-element.233, ...), kind=kLoop, calls=%fused_computation.12 | loop fusion | flops 1362240 | bytes 5399712 | tf_op jit(solution)/shard_map/transpose(jvp())/add_any | solution.py:48
  137.9 2.7 %collective-permute-start.24 = (f32[64,256]{1,0:T(8,128)S(1)}, f32[64,256]{1,0:T(8,128)S(1)}, u32[]{:S(2)}, u32[]{:S(2)}) collective-permute-start(f32[64,256]{1,0:T(8,128)S(1)} %get-tuple-element.276), channel_id=1, source_target_pairs={{4,0},{8,4},{12,8},{0,12},{5,1},{9,5},{13,9},{1,13},{6,2},{10,6},{... | collective-permute-start | bytes 196616 | tf_op jit(solution)/shard_map/ppermute | solution.py:13
  142.2 4.5 %collective-permute-start.27 = (f32[8,256]{1,0:T(8,128)S(1)}, f32[8,256]{1,0:T(8,128)S(1)}, u32[]{:S(2)}, u32[]{:S(2)}) collective-permute-start(f32[8,256]{1,0:T(8,128)S(1)} %bitcast.80), channel_id=1, source_target_pairs={{0,2},{1,3},{4,6},{5,7},{8,10},{9,11},{12,14},{13,15},{16,18},{17,... | collective-permute-start | bytes 24584 | tf_op jit(solution)/shard_map/ppermute | solution.py:19
  148.2 4.7 %collective-permute-done.25 = f32[64,256]{1,0:T(8,128)S(1)} collective-permute-done((f32[64,256]{1,0:T(8,128)S(1)}, f32[64,256]{1,0:T(8,128)S(1)}, u32[]{:S(2)}, u32[]{:S(2)}) %collective-permute-start.25) | collective-permute-done | bytes 65568 | tf_op jit(solution)/shard_map/ppermute | solution.py:13
  (138 shorter events, 41.4 us)
Async XLA Ops:
  0.6 1.2 copy-start
  0.6 1.3 copy-start.7
  2.0 10.9 %collective-permute-start = (f32[3,1,64,256]{3,2,1,0:T(8,128)S(1)}, f32[3,1,64,256]{3,2,1,0:T(8,128)S(1)}, u32[]{:S(2)}, u32[]{:S(2)}) collective-permute-start(f32[3,1,64,256]{3,2,1,0:T(8,128)S(1)} %get-tuple-element.271), channel_id=1, source_target_pairs={{0,4},{4,8},{8,12},{12,0},{1,5},{5,9},{9,13},{13,1},{2,6},{6,10},{... | collective-permute-start | bytes 589832 | tf_op jit(solution)/shard_map/ppermute | solution.py:28
  5.1 10.6 %collective-permute-start.1 = (f32[3,1,64,256]{3,2,1,0:T(8,128)S(1)}, f32[3,1,64,256]{3,2,1,0:T(8,128)S(1)}, u32[]{:S(2)}, u32[]{:S(2)}) collective-permute-start(f32[3,1,64,256]{3,2,1,0:T(8,128)S(1)} %get-tuple-element.272), channel_id=1, source_target_pairs={{4,0},{8,4},{12,8},{0,12},{5,1},{9,5},{13,9},{1,13},{6,2},{10,6},{... | collective-permute-start | bytes 589832 | tf_op jit(solution)/shard_map/ppermute | solution.py:31
  15.7 4.0 %collective-permute-start.2 = (f32[3,10,1,256]{3,2,1,0:T(1,128)S(1)}, f32[3,10,1,256]{3,2,1,0:T(1,128)S(1)}, u32[]{:S(2)}, u32[]{:S(2)}) collective-permute-start(f32[3,10,1,256]{3,2,1,0:T(1,128)S(1)} %get-tuple-element.268), channel_id=1, source_target_pairs={{0,2},{2,0},{1,3},{3,1},{4,6},{6,4},{5,7},{7,5},{8,10},{10,8},{9,1... | collective-permute-start | bytes 92168 | tf_op jit(solution)/shard_map/ppermute | solution.py:28
  17.3 3.9 %collective-permute-start.3 = (f32[3,10,1,256]{3,2,1,0:T(1,128)S(1)}, f32[3,10,1,256]{3,2,1,0:T(1,128)S(1)}, u32[]{:S(2)}, u32[]{:S(2)}) collective-permute-start(f32[3,10,1,256]{3,2,1,0:T(1,128)S(1)} %get-tuple-element.269), channel_id=1, source_target_pairs={{2,0},{0,2},{3,1},{1,3},{6,4},{4,6},{7,5},{5,7},{10,8},{8,10},{11,... | collective-permute-start | bytes 92168 | tf_op jit(solution)/shard_map/ppermute | solution.py:31
  24.9 1.9 %collective-permute-start.5 = (f32[3,10,66,1]{2,3,1,0:T(1,128)S(1)}, f32[3,10,66,1]{2,3,1,0:T(1,128)S(1)}, u32[]{:S(2)}, u32[]{:S(2)}) collective-permute-start(f32[3,10,66,1]{2,3,1,0:T(1,128)S(1)} %copy.177), channel_id=1, source_target_pairs={{1,0},{0,1},{3,2},{2,3},{5,4},{4,5},{7,6},{6,7},{9,8},{8,9},{11,10... | collective-permute-start | bytes 23768 | tf_op jit(solution)/shard_map/ppermute | solution.py:31
  24.9 1.3 collective-permute-start.4
  25.5 7.7 %copy-start.15 = (f32[66,258]{1,0:T(8,128)}, f32[66,258]{1,0:T(8,128)S(1)}, u32[]{:S(2)}) copy-start(f32[66,258]{1,0:T(8,128)S(1)} %and_convert_fusion) | copy-start | bytes 204340
  33.3 1.0 copy-start.1
  33.3 1.2 copy-start.14
  34.5 1.0 copy-start.8
  35.5 15.4 %copy-start.2 = (f32[8,64,256]{2,1,0:T(8,128)}, f32[8,64,256]{2,1,0:T(8,128)S(1)}, u32[]{:S(2)}) copy-start(f32[8,64,256]{2,1,0:T(8,128)S(1)} %get-tuple-element.253) | copy-start | bytes 1572868
  35.5 15.4 %copy-start.3 = (f32[8,64,256]{2,1,0:T(8,128)}, f32[8,64,256]{2,1,0:T(8,128)S(1)}, u32[]{:S(2)}) copy-start(f32[8,64,256]{2,1,0:T(8,128)S(1)} %get-tuple-element.254) | copy-start | bytes 1572868
  35.5 15.4 %copy-start.4 = (f32[8,64,256]{2,1,0:T(8,128)}, f32[8,64,256]{2,1,0:T(8,128)S(1)}, u32[]{:S(2)}) copy-start(f32[8,64,256]{2,1,0:T(8,128)S(1)} %get-tuple-element.255) | copy-start | bytes 1572868
  35.5 15.4 %copy-start.5 = (f32[8,64,256]{2,1,0:T(8,128)}, f32[8,64,256]{2,1,0:T(8,128)S(1)}, u32[]{:S(2)}) copy-start(f32[8,64,256]{2,1,0:T(8,128)S(1)} %get-tuple-element.256) | copy-start | bytes 1572868
  36.6 6.8 %collective-permute-start.6 = (f32[1,64,256]{2,1,0:T(8,128)S(1)}, f32[1,64,256]{2,1,0:T(8,128)S(1)}, u32[]{:S(2)}, u32[]{:S(2)}) collective-permute-start(f32[1,64,256]{2,1,0:T(8,128)S(1)} %get-tuple-element.293), channel_id=1, source_target_pairs={{0,4},{4,8},{8,12},{12,0},{1,5},{5,9},{9,13},{13,1},{2,6},{6,10},{... | collective-permute-start | bytes 196616 | tf_op jit(solution)/shard_map/ppermute | solution.py:28
  37.8 5.7 %collective-permute-start.7 = (f32[1,64,256]{2,1,0:T(8,128)S(1)}, f32[1,64,256]{2,1,0:T(8,128)S(1)}, u32[]{:S(2)}, u32[]{:S(2)}) collective-permute-start(f32[1,64,256]{2,1,0:T(8,128)S(1)} %get-tuple-element.294), channel_id=1, source_target_pairs={{4,0},{8,4},{12,8},{0,12},{5,1},{9,5},{13,9},{1,13},{6,2},{10,6},{... | collective-permute-start | bytes 196616 | tf_op jit(solution)/shard_map/ppermute | solution.py:31
  43.5 3.7 %collective-permute-start.8 = (f32[10,1,256]{2,1,0:T(1,128)S(1)}, f32[10,1,256]{2,1,0:T(1,128)S(1)}, u32[]{:S(2)}, u32[]{:S(2)}) collective-permute-start(f32[10,1,256]{2,1,0:T(1,128)S(1)} %get-tuple-element.291), channel_id=1, source_target_pairs={{0,2},{2,0},{1,3},{3,1},{4,6},{6,4},{5,7},{7,5},{8,10},{10,8},{9,1... | collective-permute-start | bytes 30728 | tf_op jit(solution)/shard_map/ppermute | solution.py:28
  44.1 6.2 %copy-start.16 = (f32[66,258]{1,0:T(8,128)S(1)}, f32[66,258]{1,0:T(8,128)}, u32[]{:S(2)}) copy-start(f32[66,258]{1,0:T(8,128)} %copy-done.15) | copy-start | bytes 204340
  44.1 3.7 %collective-permute-start.9 = (f32[10,1,256]{2,1,0:T(1,128)S(1)}, f32[10,1,256]{2,1,0:T(1,128)S(1)}, u32[]{:S(2)}, u32[]{:S(2)}) collective-permute-start(f32[10,1,256]{2,1,0:T(1,128)S(1)} %get-tuple-element.292), channel_id=1, source_target_pairs={{2,0},{0,2},{3,1},{1,3},{6,4},{4,6},{7,5},{5,7},{10,8},{8,10},{11,... | collective-permute-start | bytes 30728 | tf_op jit(solution)/shard_map/ppermute | solution.py:31
  48.0 1.8 %collective-permute-start.10 = (f32[10,66,1]{2,1,0:T(8,128)S(1)}, f32[10,66,1]{2,1,0:T(8,128)S(1)}, u32[]{:S(2)}, u32[]{:S(2)}) collective-permute-start(f32[10,66,1]{2,1,0:T(8,128)S(1)} %get-tuple-element.285), channel_id=1, source_target_pairs={{0,1},{1,0},{2,3},{3,2},{4,5},{5,4},{6,7},{7,6},{8,9},{9,8},{10,11... | collective-permute-start | bytes 7928 | tf_op jit(solution)/shard_map/ppermute | solution.py:28
  48.1 2.2 %collective-permute-start.11 = (f32[10,66,1]{2,1,0:T(8,128)S(1)}, f32[10,66,1]{2,1,0:T(8,128)S(1)}, u32[]{:S(2)}, u32[]{:S(2)}) collective-permute-start(f32[10,66,1]{2,1,0:T(8,128)S(1)} %get-tuple-element.286), channel_id=1, source_target_pairs={{1,0},{0,1},{3,2},{2,3},{5,4},{4,5},{7,6},{6,7},{9,8},{8,9},{11,10... | collective-permute-start | bytes 7928 | tf_op jit(solution)/shard_map/ppermute | solution.py:31
  55.0 8.9 %copy-start.11 = (f32[10,66,258]{2,1,0:T(8,128)}, f32[10,66,258]{2,1,0:T(8,128)S(1)}, u32[]{:S(2)}) copy-start(f32[10,66,258]{2,1,0:T(8,128)S(1)} %pad_add_fusion.2) | copy-start | bytes 2043364
  56.8 16.7 %collective-permute-start.17 = (f32[8,64]{1,0:T(8,128)}, f32[8,64]{1,0:T(8,128)}, u32[]{:S(2)}, u32[]{:S(2)}) collective-permute-start(f32[8,64]{1,0:T(8,128)} %get-tuple-element.226), channel_id=1, source_target_pairs={{0,1},{2,3},{4,5},{6,7},{8,9},{10,11},{12,13},{14,15},{16,17},{18,... | collective-permute-start | bytes 6152 | tf_op jit(solution)/shard_map/ppermute | solution.py:19
  59.4 12.0 %collective-permute-start.16 = (f32[8,64]{1,0:T(8,128)S(1)}, f32[8,64]{1,0:T(8,128)S(1)}, u32[]{:S(2)}, u32[]{:S(2)}) collective-permute-start(f32[8,64]{1,0:T(8,128)S(1)} %get-tuple-element.227), channel_id=1, source_target_pairs={{1,0},{3,2},{5,4},{7,6},{9,8},{11,10},{13,12},{15,14},{17,16},{19,... | collective-permute-start | bytes 6152 | tf_op jit(solution)/shard_map/ppermute | solution.py:19
  60.7 14.4 %collective-permute-start.12 = (f32[64,256]{1,0:T(8,128)}, f32[64,256]{1,0:T(8,128)}, u32[]{:S(2)}, u32[]{:S(2)}) collective-permute-start(f32[64,256]{1,0:T(8,128)} %get-tuple-element.284), channel_id=1, source_target_pairs={{4,0},{8,4},{12,8},{0,12},{5,1},{9,5},{13,9},{1,13},{6,2},{10,6},{... | collective-permute-start | bytes 196616 | tf_op jit(solution)/shard_map/ppermute | solution.py:13
  65.4 13.9 %collective-permute-start.14 = (f32[8,256]{1,0:T(8,128)}, f32[8,256]{1,0:T(8,128)S(1)}, u32[]{:S(2)}, u32[]{:S(2)}) collective-permute-start(f32[8,256]{1,0:T(8,128)} %bitcast.65), channel_id=1, source_target_pairs={{2,0},{3,1},{6,4},{7,5},{10,8},{11,9},{14,12},{15,13},{18,16},{19,... | collective-permute-start | bytes 24584 | tf_op jit(solution)/shard_map/ppermute | solution.py:19
  66.8 13.8 %collective-permute-start.15 = (f32[8,256]{1,0:T(8,128)}, f32[8,256]{1,0:T(8,128)S(1)}, u32[]{:S(2)}, u32[]{:S(2)}) collective-permute-start(f32[8,256]{1,0:T(8,128)} %bitcast.64), channel_id=1, source_target_pairs={{0,2},{1,3},{4,6},{5,7},{8,10},{9,11},{12,14},{13,15},{16,18},{17,... | collective-permute-start | bytes 24584 | tf_op jit(solution)/shard_map/ppermute | solution.py:19
  72.0 6.4 %collective-permute-start.13 = (f32[64,256]{1,0:T(8,128)}, f32[64,256]{1,0:T(8,128)}, u32[]{:S(2)}, u32[]{:S(2)}) collective-permute-start(f32[64,256]{1,0:T(8,128)} %get-tuple-element.283), channel_id=1, source_target_pairs={{12,0},{0,4},{4,8},{8,12},{13,1},{1,5},{5,9},{9,13},{14,2},{2,6},{... | collective-permute-start | bytes 196616 | tf_op jit(solution)/shard_map/ppermute | solution.py:13
  87.1 2.2 %copy-start.9 = (f32[8,64,256]{2,1,0:T(8,128)S(1)}, f32[8,64,256]{2,1,0:T(8,128)}, u32[]{:S(2)}) copy-start(f32[8,64,256]{2,1,0:T(8,128)} %param.43) | copy-start | bytes 1572868
  91.7 7.2 %copy-start.12 = (f32[10,66,258]{2,1,0:T(8,128)}, f32[10,66,258]{2,1,0:T(8,128)S(1)}, u32[]{:S(2)}) copy-start(f32[10,66,258]{2,1,0:T(8,128)S(1)} %pad_add_fusion.1) | copy-start | bytes 2043364
  93.5 15.6 %collective-permute-start.23 = (f32[8,64]{1,0:T(8,128)}, f32[8,64]{1,0:T(8,128)}, u32[]{:S(2)}, u32[]{:S(2)}) collective-permute-start(f32[8,64]{1,0:T(8,128)} %get-tuple-element.224), channel_id=1, source_target_pairs={{0,1},{2,3},{4,5},{6,7},{8,9},{10,11},{12,13},{14,15},{16,17},{18,... | collective-permute-start | bytes 6152 | tf_op jit(solution)/shard_map/ppermute | solution.py:19
  95.4 11.6 %collective-permute-start.22 = (f32[8,64]{1,0:T(8,128)S(1)}, f32[8,64]{1,0:T(8,128)S(1)}, u32[]{:S(2)}, u32[]{:S(2)}) collective-permute-start(f32[8,64]{1,0:T(8,128)S(1)} %get-tuple-element.225), channel_id=1, source_target_pairs={{1,0},{3,2},{5,4},{7,6},{9,8},{11,10},{13,12},{15,14},{17,16},{19,... | collective-permute-start | bytes 6152 | tf_op jit(solution)/shard_map/ppermute | solution.py:19
  96.7 13.9 %collective-permute-start.18 = (f32[64,256]{1,0:T(8,128)}, f32[64,256]{1,0:T(8,128)}, u32[]{:S(2)}, u32[]{:S(2)}) collective-permute-start(f32[64,256]{1,0:T(8,128)} %get-tuple-element.280), channel_id=1, source_target_pairs={{4,0},{8,4},{12,8},{0,12},{5,1},{9,5},{13,9},{1,13},{6,2},{10,6},{... | collective-permute-start | bytes 196616 | tf_op jit(solution)/shard_map/ppermute | solution.py:13
  101.1 14.3 %collective-permute-start.20 = (f32[8,256]{1,0:T(8,128)}, f32[8,256]{1,0:T(8,128)S(1)}, u32[]{:S(2)}, u32[]{:S(2)}) collective-permute-start(f32[8,256]{1,0:T(8,128)} %bitcast.63), channel_id=1, source_target_pairs={{2,0},{3,1},{6,4},{7,5},{10,8},{11,9},{14,12},{15,13},{18,16},{19,... | collective-permute-start | bytes 24584 | tf_op jit(solution)/shard_map/ppermute | solution.py:19
  102.4 16.0 %collective-permute-start.21 = (f32[8,256]{1,0:T(8,128)}, f32[8,256]{1,0:T(8,128)S(1)}, u32[]{:S(2)}, u32[]{:S(2)}) collective-permute-start(f32[8,256]{1,0:T(8,128)} %bitcast.62), channel_id=1, source_target_pairs={{0,2},{1,3},{4,6},{5,7},{8,10},{9,11},{12,14},{13,15},{16,18},{17,... | collective-permute-start | bytes 24584 | tf_op jit(solution)/shard_map/ppermute | solution.py:19
  107.6 6.4 %collective-permute-start.19 = (f32[64,256]{1,0:T(8,128)}, f32[64,256]{1,0:T(8,128)}, u32[]{:S(2)}, u32[]{:S(2)}) collective-permute-start(f32[64,256]{1,0:T(8,128)} %get-tuple-element.279), channel_id=1, source_target_pairs={{12,0},{0,4},{4,8},{8,12},{13,1},{1,5},{5,9},{9,13},{14,2},{2,6},{... | collective-permute-start | bytes 196616 | tf_op jit(solution)/shard_map/ppermute | solution.py:13
  115.5 0.6 copy-start.18
  128.7 3.6 %copy-start.10 = (f32[8,64,256]{2,1,0:T(8,128)S(1)}, f32[8,64,256]{2,1,0:T(8,128)}, u32[]{:S(2)}) copy-start(f32[8,64,256]{2,1,0:T(8,128)} %param.43) | copy-start | bytes 1572868
  134.8 5.9 %copy-start.13 = (f32[10,66,258]{2,1,0:T(8,128)}, f32[10,66,258]{2,1,0:T(8,128)S(1)}, u32[]{:S(2)}) copy-start(f32[10,66,258]{2,1,0:T(8,128)S(1)} %pad_add_fusion) | copy-start | bytes 2043364
  135.2 11.8 %collective-permute-start.29 = (f32[8,64]{1,0:T(8,128)S(1)}, f32[8,64]{1,0:T(8,128)S(1)}, u32[]{:S(2)}, u32[]{:S(2)}) collective-permute-start(f32[8,64]{1,0:T(8,128)S(1)} %get-tuple-element.222), channel_id=1, source_target_pairs={{0,1},{2,3},{4,5},{6,7},{8,9},{10,11},{12,13},{14,15},{16,17},{18,... | collective-permute-start | bytes 6152 | tf_op jit(solution)/shard_map/ppermute | solution.py:19
  136.6 10.2 %collective-permute-start.28 = (f32[8,64]{1,0:T(8,128)S(1)}, f32[8,64]{1,0:T(8,128)S(1)}, u32[]{:S(2)}, u32[]{:S(2)}) collective-permute-start(f32[8,64]{1,0:T(8,128)S(1)} %get-tuple-element.223), channel_id=1, source_target_pairs={{1,0},{3,2},{5,4},{7,6},{9,8},{11,10},{13,12},{15,14},{17,16},{19,... | collective-permute-start | bytes 6152 | tf_op jit(solution)/shard_map/ppermute | solution.py:19
  137.9 9.3 %collective-permute-start.24 = (f32[64,256]{1,0:T(8,128)S(1)}, f32[64,256]{1,0:T(8,128)S(1)}, u32[]{:S(2)}, u32[]{:S(2)}) collective-permute-start(f32[64,256]{1,0:T(8,128)S(1)} %get-tuple-element.276), channel_id=1, source_target_pairs={{4,0},{8,4},{12,8},{0,12},{5,1},{9,5},{13,9},{1,13},{6,2},{10,6},{... | collective-permute-start | bytes 196616 | tf_op jit(solution)/shard_map/ppermute | solution.py:13
  140.9 12.0 %collective-permute-start.26 = (f32[8,256]{1,0:T(8,128)S(1)}, f32[8,256]{1,0:T(8,128)S(1)}, u32[]{:S(2)}, u32[]{:S(2)}) collective-permute-start(f32[8,256]{1,0:T(8,128)S(1)} %bitcast.81), channel_id=1, source_target_pairs={{2,0},{3,1},{6,4},{7,5},{10,8},{11,9},{14,12},{15,13},{18,16},{19,... | collective-permute-start | bytes 24584 | tf_op jit(solution)/shard_map/ppermute | solution.py:19
  142.2 10.8 %collective-permute-start.27 = (f32[8,256]{1,0:T(8,128)S(1)}, f32[8,256]{1,0:T(8,128)S(1)}, u32[]{:S(2)}, u32[]{:S(2)}) collective-permute-start(f32[8,256]{1,0:T(8,128)S(1)} %bitcast.80), channel_id=1, source_target_pairs={{0,2},{1,3},{4,6},{5,7},{8,10},{9,11},{12,14},{13,15},{16,18},{17,... | collective-permute-start | bytes 24584 | tf_op jit(solution)/shard_map/ppermute | solution.py:19
  146.8 6.1 %collective-permute-start.25 = (f32[64,256]{1,0:T(8,128)S(1)}, f32[64,256]{1,0:T(8,128)S(1)}, u32[]{:S(2)}, u32[]{:S(2)}) collective-permute-start(f32[64,256]{1,0:T(8,128)S(1)} %get-tuple-element.275), channel_id=1, source_target_pairs={{12,0},{0,4},{4,8},{8,12},{13,1},{1,5},{5,9},{9,13},{14,2},{2,6},{... | collective-permute-start | bytes 196616 | tf_op jit(solution)/shard_map/ppermute | solution.py:13
  153.3 1.2 copy-start.6
  (3 other events, 1.8 us)
where the time goes:
time: 157 us; the launch traced here: 155 us
  starting transfers between devices  49.8 us (32%)
  other arithmetic  40.9 us (26%)
  local copies, waits for them, and re-layouts  35.1 us (22%)
  waiting for transfers between devices  28.3 us (18%)
    ppermute x12, starting transfers between devices, from_behind_2(): lax.ppermute(value, axis, [(source, source + steps) for source in range(l...  27.4 us
    ppermute x6, waiting for transfers between devices, extended(): lax.ppermute(lax.slice_in_dim(block, block.shape[dim] - width, None, axis...  14 us
    ppermute x6, waiting for transfers between devices, from_behind(): return lax.ppermute(block, axis, route)  8.8 us
    ppermute x6, starting transfers between devices, from_behind(): return lax.ppermute(block, axis, route)  7.98 us
    ppermute x6, starting transfers between devices, extended(): lax.ppermute(lax.slice_in_dim(block, 0, width, axis=dim), axis, backward)  7.36 us
    ppermute x6, starting transfers between devices, extended(): lax.ppermute(lax.slice_in_dim(block, block.shape[dim] - width, None, axis...  6.98 us
    add_any x3, other arithmetic, diffuse(): window(padded, axis, offset) - centre  6.77 us
    add_any x3, other arithmetic, window(): return array[tuple(index)]  6.47 us
  transfers between devices with their start and end apart: 30, of which 14 were waited for; matrix products, arithmetic and copies ran while one was open for 13% of the time, Pallas kernels for 0%

commit v1 on v0

v1 whole, which is shorter than its diff:
```python
import functools

import jax
import jax.numpy as jnp
from jax import lax
from jax.experimental import pallas as pl
from jax.experimental.pallas import tpu as pltpu
from jax.sharding import PartitionSpec as P

VMEM = pltpu.VMEM
time_step = 0.06
HALO = 4
TILE = 8
S, C, T, F, K = range(5)


def call(kernel, outs, *ins, keep=True):
    space = VMEM if keep else jax.ShapeDtypeStruct
    return pl.pallas_call(
        kernel,
        out_shape=[space(shape, jnp.float32) for shape in outs],
        in_specs=[pl.BlockSpec(memory_space=VMEM)] * len(ins),
        out_specs=[pl.BlockSpec(memory_space=VMEM)] * len(outs),
        compiler_params=pltpu.CompilerParams(vmem_limit_bytes=8 * 1024 * 1024),
    )(*[pltpu.with_memory_space_constraint(x, VMEM) for x in ins])


def half_fluid(labels):
    return jnp.where(labels <= 1, 0.5, 0.0)


def touching(labels):
    return jnp.logical_or(labels == 1, labels == 2)


def rows_of(shape):
    return lax.broadcasted_iota(jnp.int32, shape, 0)


def lanes_of(shape):
    return lax.broadcasted_iota(jnp.int32, shape, 1)


def down_rows(before, here):
    return pltpu.roll(jnp.where(rows_of(here.shape) == TILE - 1, before, here), 1, 0)


def up_rows(here, after):
    return pltpu.roll(jnp.where(rows_of(here.shape) == 0, after, here), TILE - 1, 0)


def down_lanes(here):
    return pltpu.roll(here, 1, 1)


def up_lanes(here):
    return pltpu.roll(here, here.shape[1] - 1, 1)


def across(ky, kz, v):
    count = len(v)
    py = [a * b for a, b in zip(ky, v)]
    out = []
    for t in range(count):
        before, after = (t - 1) % count, (t + 1) % count
        total = ky[t] * down_rows(v[before], v[t]) + up_rows(py[t], py[after])
        pz = kz[t] * v[t]
        out.append(total + (kz[t] * down_lanes(v[t]) + up_lanes(pz)))
    return out


def tiles(main, ghost):
    count = main.shape[0] // TILE
    return [main[t * TILE : (t + 1) * TILE] for t in range(count)] + [ghost[...]]


def split(ref):
    return [ref[t * TILE : (t + 1) * TILE] for t in range(ref.shape[0] // TILE)]


def put(ref, values):
    for t, value in enumerate(values):
        ref[t * TILE : (t + 1) * TILE] = value


def pack_inputs(state, conduct, sink, labels, cotangent, up, down, trade):
    core = lax.axis_index("gz")
    count = state.shape[0]
    half = count // 2
    for out, plane in ((up, count - 1), (down, 0)):
        out[S] = state[plane]
        out[C] = conduct[plane]
        out[T] = cotangent[plane]
        out[F] = half_fluid(labels[plane])
    first = (1 - core) * half
    for i in range(half):
        trade[S, i] = state[first + i]
        trade[C, i] = conduct[first + i]
        trade[T, i] = cotangent[first + i]
        trade[F, i] = half_fluid(labels[first + i])
        trade[K, i] = jnp.where(touching(labels[first + i]), sink[first + i], 0.0)


def gather_planes(two, state, conduct, sink, labels, cotangent, traded, block, *rims):
    core = lax.axis_index("gz")
    half, wide = traded.shape[1], traded.shape[3]
    mine = pl.ds(pl.multiple_of(core * wide, 128), wide)
    other = pl.ds(pl.multiple_of((1 - core) * wide, 128), wide)
    first = core * half
    for i in range(half):
        block[S, i, :, mine] = state[first + i]
        block[C, i, :, mine] = conduct[first + i]
        block[T, i, :, mine] = cotangent[first + i]
        block[F, i, :, mine] = half_fluid(labels[first + i])
        block[K, i, :, mine] = jnp.where(touching(labels[first + i]), sink[first + i], 0.0)
        for j in range(5):
            block[j, i, :, other] = traded[j, i]
    ny = block.shape[2]
    for j in range(5):
        for k in range(half // 2):
            even_low, odd_low = block[j, 2 * k, 0:TILE], block[j, 2 * k + 1, 0:TILE]
            even_high, odd_high = block[j, 2 * k, ny - TILE : ny], block[j, 2 * k + 1, ny - TILE : ny]
            upper = rows_of(even_low.shape) < HALO
            low = jnp.where(upper, even_low, pltpu.roll(odd_low, HALO, 0))
            high = jnp.where(upper, pltpu.roll(even_high, HALO, 0), odd_high)
            if two:
                rims[0][j, k] = jnp.where(lax.axis_index("gy") == 0, high, low)
            else:
                rims[0][j, k] = low
                rims[1][j, k] = high


def prepare(two, count_y, block, *refs):
    rims, (ghost, kx, ky, kz, diag, part, back, off, on) = refs[: 1 if two else 2], refs[1 if two else 2 :]
    half = block.shape[1]
    place = lax.axis_index("gy")
    core = lax.axis_index("gz")
    has_low, has_high = place > 0, place < count_y - 1
    for j in range(5):
        for k in range(half // 2):
            above = jnp.where(has_high, rims[0][j, k], 0.0)
            below = jnp.where(has_low, rims[0 if two else 1][j, k], 0.0)
            upper = rows_of(above.shape) < HALO
            ghost[j, 2 * k] = jnp.where(upper, above, pltpu.roll(below, HALO, 0))
            ghost[j, 2 * k + 1] = jnp.where(upper, pltpu.roll(above, HALO, 0), below)
    own = lambda j, i: tiles(block.at[j, i], ghost.at[j, i])
    count = block.shape[2] // TILE + 1
    for i in range(half):
        c = own(C, i)
        rows, lanes = rows_of(c[0].shape), lanes_of(c[0].shape)
        for t in range(count):
            before, after = c[(t - 1) % count], c[(t + 1) % count]
            here = c[t] * (0.5 * time_step)
            low = here + down_rows(before, c[t]) * (0.5 * time_step)
            high = here + up_rows(c[t], after) * (0.5 * time_step)
            left = here + jnp.where(lanes == 0, 0.0, down_lanes(c[t])) * (0.5 * time_step)
            right = here + jnp.where(lanes == lanes.shape[1] - 1, 0.0, up_lanes(c[t])) * (0.5 * time_step)
            total = (low + high) + (left + right) + time_step * own(F, i)[t]
            if i > 0:
                face = here + own(C, i - 1)[t] * (0.5 * time_step)
                kx[i - 1, t * TILE : (t + 1) * TILE] = face
                total = total + face
            if i < half - 1:
                total = total + (here + own(C, i + 1)[t] * (0.5 * time_step))
            diag[i, t * TILE : (t + 1) * TILE] = total
            if t == 0:
                low = jnp.where(jnp.logical_and(rows == 0, jnp.logical_not(has_low)), 0.0, low)
            if t == count - 1:
                low = jnp.where(jnp.logical_and(rows == 0, jnp.logical_not(has_high)), 0.0, low)
            ky[i, t * TILE : (t + 1) * TILE] = low
            kz[i, t * TILE : (t + 1) * TILE] = jnp.where(lanes == 0, 0.0, left)
    for i in range(half):
        s, f, k, c = own(S, i), own(F, i), own(K, i), own(T, i)
        y, z, d = split(ky.at[i]), split(kz.at[i]), split(diag.at[i])
        b = [c[t] * (0.5 + f[t]) for t in range(count)]
        ahead = across(y, z, s)
        behind = across(y, z, b)
        for t in range(count):
            at = slice(t * TILE, (t + 1) * TILE)
            go = ahead[t] - d[t] * s[t]
            come = behind[t] - d[t] * b[t]
            if i > 0:
                go = go + (kx[i - 1, at] + time_step * f[t]) * own(S, i - 1)[t]
                low_b = own(T, i - 1)[t] * (0.5 + own(F, i - 1)[t])
                come = come + kx[i - 1, at] * low_b
            if i < half - 1:
                go = go + kx[i, at] * own(S, i + 1)[t]
                high_f = own(F, i + 1)[t]
                come = come + (kx[i, at] + time_step * high_f) * (own(T, i + 1)[t] * (0.5 + high_f))
            go = go - time_step * k[t] * jnp.tanh(s[t])
            part[i, at] = s[t] + (0.5 + f[t]) * go
            back[i, at] = c[t] + come
    ny = block.shape[2]
    outer = core * (half - 1)
    inner = (1 - core) * (half - 1)
    off[0 : ny + TILE] = part[outer]
    for j in range(4):
        off[ny + (j + 1) * TILE : ny + (j + 2) * TILE] = ghost[j, outer]
        on[j, 0:ny] = block[j, inner]
        on[j, ny : ny + TILE] = ghost[j, inner]
    on[4] = part[inner]


def choose_half(up, down, out):
    core = lax.axis_index("gz")
    out[...] = jnp.where(core == 0, down[...], up[...])


def middle(block, ghost, kx, ky, kz, diag, part, back, up, down, passed, off, on, *refs):
    first, second, sa, b2, fa, edge, full, off2, on2, side = refs
    core = lax.axis_index("gz")
    half, ny = block.shape[1], block.shape[2]
    wide = up.shape[2]
    count = ny // TILE + 1
    last = half - 1
    own = lambda j, i: tiles(block.at[j, i], ghost.at[j, i])
    near = core
    far = 1 - core
    for j in range(4):
        side[j, near, 0:ny, 0:wide] = jnp.where(core == 0, up[j], passed[j])
        side[j, near, 0:ny, wide : 2 * wide] = jnp.where(core == 0, passed[j], down[j])
        side[j, near, ny : ny + TILE] = off[ny + (j + 1) * TILE : ny + (j + 2) * TILE]
        side[j, far] = on[j]
    side[4, near] = off[0 : ny + TILE]
    side[4, far] = on[4]
    scale = 0.5 * time_step
    for t in range(count):
        at = slice(t * TILE, (t + 1) * TILE)
        low_c, high_c = side[C, 0, at], side[C, 1, at]
        low = (own(C, 0)[t] + low_c) * scale
        high = (own(C, last)[t] + high_c) * scale
        edge[0, at] = low
        edge[1, at] = high
        for i in range(half):
            d = diag[i, at]
            if i == 0:
                d = d + low
            if i == last:
                d = d + high
            full[i, at] = d
        s0, s1 = own(S, 0)[t], own(S, last)[t]
        f0, f1 = own(F, 0)[t], own(F, last)[t]
        sl, sh = side[S, 0, at], side[S, 1, at]
        fl, fh = side[F, 0, at], side[F, 1, at]
        first[0, at] = side[4, 0, at] + (0.5 + fl) * low * (s0 - sl)
        first[1, at] = part[0, at] + (0.5 + f0) * ((low + time_step * f0) * sl - low * s0)
        for i in range(1, last):
            first[i + 1, at] = part[i, at]
        first[last + 1, at] = part[last, at] + (0.5 + f1) * high * (sh - s1)
        first[last + 2, at] = side[4, 1, at] + (0.5 + fh) * ((high + time_step * fh) * s1 - high * sh)
    for i in range(half):
        v, f, k, s, c = split(first.at[i + 1]), own(F, i), own(K, i), own(S, i), own(T, i)
        flow = across(split(ky.at[i]), split(kz.at[i]), v)
        for t in range(count):
            at = slice(t * TILE, (t + 1) * TILE)
            low = edge[0, at] if i == 0 else kx[i - 1, at]
            high = edge[1, at] if i == last else kx[i, at]
            rc = 0.5 + f[t]
            sink = time_step * k[t]
            rate = flow[t] + (low + time_step * f[t]) * first[i, at] + high * first[i + 2, at] - full[i, at] * v[t] - sink * jnp.tanh(v[t])
            value = 0.75 * s[t] + 0.25 * (v[t] + rc * rate)
            hot = jnp.tanh(value)
            second[i, at] = hot
            b = c[t] * rc
            total = back[i, at] - sink * (1.0 - hot * hot) * b
            if i == 0:
                total = total + low * (side[T, 0, at] * (0.5 + side[F, 0, at]) - b)
            if i == last:
                high_f = side[F, 1, at]
                total = total + ((high + time_step * high_f) * (side[T, 1, at] * (0.5 + high_f)) - high * b)
            total = total * (2.0 / 3.0)
            sa[i, at] = total
            b2[i, at] = total * rc
    for i in range(half):
        v, b, f, k = split(first.at[i + 1]), split(b2.at[i]), own(F, i), own(K, i)
        flow = across(split(ky.at[i]), split(kz.at[i]), b)
        for t in range(count):
            at = slice(t * TILE, (t + 1) * TILE)
            hot = jnp.tanh(v[t])
            total = sa[i, at] + flow[t] - full[i, at] * b[t] - time_step * k[t] * (1.0 - hot * hot) * b[t]
            if i > 0:
                total = total + kx[i - 1, at] * b2[i - 1, at]
            if i < last:
                total = total + (kx[i, at] + time_step * own(F, i + 1)[t]) * b2[i + 1, at]
            fa[i, at] = 0.25 * total
    outer, inner = core * last, (1 - core) * last
    for out, plane in ((off2, outer), (on2, inner)):
        out[0 : ny + TILE] = b2[plane]
        out[ny + TILE : 2 * ny + TILE] = fa[plane, 0:ny]


def finish(block, kx, ky, kz, first, second, sa, b2, fa, edge, full, side, ghost, off2, on2, keep, give, b3, fixed):
    core = lax.axis_index("gz")
    half, ny = block.shape[1], block.shape[2]
    wide = keep.shape[3]
    count = ny // TILE + 1
    last = half - 1
    own = lambda j, i: tiles(block.at[j, i], ghost.at[j, i])
    low_is_off = core == 0
    for t in range(count):
        at = slice(t * TILE, (t + 1) * TILE)
        off_b, on_b = off2[at], on2[at]
        low_b, high_b = jnp.where(low_is_off, off_b, on_b), jnp.where(low_is_off, on_b, off_b)
        low, high = edge[0, at], edge[1, at]
        fh = side[F, 1, at]
        f0, f1 = own(F, 0)[t], own(F, last)[t]
        fixed[0, at] = fa[0, at] + 0.25 * low * low_b
        for i in range(1, last):
            fixed[i, at] = fa[i, at]
        fixed[last, at] = fa[last, at] + 0.25 * (high + time_step * fh) * high_b
        for i in range(half):
            b3[i + 1, at] = fixed[i, at] * (0.5 + own(F, i)[t])
        if t < count - 1:
            at2 = slice(ny + (t + 1) * TILE, ny + (t + 2) * TILE)
            off_p, on_p = off2[at2], on2[at2]
            low_p, high_p = jnp.where(low_is_off, off_p, on_p), jnp.where(low_is_off, on_p, off_p)
            b3[0, at] = (low_p + 0.25 * (low + time_step * f0) * b2[0, at]) * (0.5 + side[F, 0, at])
            b3[half + 1, at] = (high_p + 0.25 * high * b2[last, at]) * (0.5 + fh)
    for i in range(half):
        b, f, k = split(b3.at[i + 1]), own(F, i), own(K, i)
        s, c = own(S, i), own(T, i)
        flow = across(split(ky.at[i]), split(kz.at[i]), b)
        for t in range(count - 1):
            at = slice(t * TILE, (t + 1) * TILE)
            low = edge[0, at] if i == 0 else kx[i - 1, at]
            if i == last:
                high = edge[1, at] + time_step * side[F, 1, at]
            else:
                high = kx[i, at] + time_step * own(F, i + 1)[t]
            hot = jnp.tanh(s[t])
            total = flow[t] + low * b3[i, at] + high * b3[i + 2, at] - full[i, at] * b[t]
            total = total - time_step * k[t] * (1.0 - hot * hot) * b[t]
            total = total + fixed[i, at] + 0.75 * sa[i, at] + c[t] * (1.0 / 3.0)
            term = (2.0 / 3.0) * second[i, at] * c[t] + 0.25 * jnp.tanh(first[i + 1, at]) * sa[i, at] + hot * fixed[i, at]
            term = -time_step * (0.5 + f[t]) * term
            for which, value in ((0, total), (1, term)):
                left, right = value[:, :wide], value[:, wide:]
                keep[which, i, at] = jnp.where(core == 0, left, right)
                give[which, i, at] = jnp.where(core == 0, right, left)


def assemble(labels, keep, got, grad_state, grad_sink):
    core = lax.axis_index("gz")
    half = keep.shape[1]
    mine, other = core * half, (1 - core) * half
    for start, source in ((mine, keep), (other, got)):
        for i in range(half):
            grad_state[start + i] = source[0, i]
            grad_sink[start + i] = jnp.where(touching(labels[start + i]), source[1, i], 0.0)


def on_device(state, conduct, sink, labels, cotangent):
    count, ny, nz = state.shape
    half, wide, rows = count // 2, 2 * nz, ny + TILE
    count_x, count_y = lax.axis_size("gx"), lax.axis_size("gy")
    assert lax.axis_size("gz") == 2 and count % 4 == 0 and ny % TILE == 0
    two = count_y == 2
    ahead = [(i, (i + 1) % count_x) for i in range(count_x)]
    behind = [(b, a) for a, b in ahead]
    cores = [(0, 1), (1, 0)]
    chips = [(2 * i + 1, (2 * i + 2) % (2 * count_x)) for i in range(count_x)]
    chips = chips + [(b, a) for a, b in chips]

    def swap_cores(x):
        return lax.ppermute(x, "gz", cores)

    def swap_chips(x):
        return lax.ppermute(x, ("gx", "gz"), chips)

    inputs = (state, conduct, sink, labels, cotangent)
    plane = (4, ny, nz)
    up, down, trade = call(pack_inputs, [plane, plane, (5, half, ny, nz)], *inputs)
    up = lax.ppermute(up, "gx", ahead)
    down = lax.ppermute(down, "gx", behind)
    traded = swap_cores(trade)
    rim = (5, half // 2, TILE, wide)
    block, *rims = call(
        functools.partial(gather_planes, two), [(5, half, ny, wide)] + [rim] * (1 if two else 2), *inputs, traded
    )
    if two:
        rims = [lax.ppermute(rims[0], "gy", [(0, 1), (1, 0)])]
    else:
        forward = [(i, (i + 1) % count_y) for i in range(count_y)]
        backward = [(b, a) for a, b in forward]
        rims = [lax.ppermute(rims[0], "gy", backward), lax.ppermute(rims[1], "gy", forward)]
    own = (half, rows, wide)
    ghost, kx, ky, kz, diag, part, back, off, on = call(
        functools.partial(prepare, two, count_y),
        [(5, half, TILE, wide), (half - 1, rows, wide), own, own, own, own, own, (rows + 4 * TILE, wide), (5, rows, wide)],
        block,
        *rims,
    )
    off, on = swap_chips(off), swap_cores(on)
    (passed,) = call(choose_half, [plane], up, down)
    passed = swap_cores(passed)
    ends = (rows + ny, wide)
    first, second, sa, b2, fa, edge, full, off2, on2, side = call(
        middle,
        [(half + 2, rows, wide), own, own, own, own, (2, rows, wide), own, ends, ends, (5, 2, rows, wide)],
        block, ghost, kx, ky, kz, diag, part, back, up, down, passed, off, on,
    )
    off2, on2 = swap_chips(off2), swap_cores(on2)
    quarter = (2, half, ny, nz)
    keep, give, _, _ = call(
        finish,
        [quarter, quarter, (half + 2, rows, wide), own],
        block, kx, ky, kz, first, second, sa, b2, fa, edge, full, side, ghost, off2, on2,
    )
    got = swap_cores(give)
    grad_state, grad_sink = call(assemble, [state.shape, state.shape], labels, keep, got, keep=False)
    return (grad_state, grad_sink)


def solution(mesh):
    block = P(("groups", "gx"), "gy", "gz")
    in_specs = (block, P("gx", "gy", "gz"), block, block, block)
    return jax.shard_map(on_device, mesh=mesh, in_specs=in_specs, out_specs=(block, block), check_vma=False)
```

time: 157 us -> 59.3 us (0.38)
  other arithmetic: 40.9 us -> 0 us
  starting transfers between devices: 49.8 us -> 11.1 us
  local copies, waits for them, and re-layouts: 35.1 us -> 5.2 us
  Pallas kernels: 0 us -> 6.93 us
  waiting for transfers between devices: 28.3 us -> 35.1 us
    ppermute x30 -> x10, starting transfers between devices: 49.8 us -> 11.1 us  [the longest x2 3.51 us: swap_chips(): return lax.ppermute(x, ('gx', 'gz'), chips)]
    add_any x7 -> x0, other arithmetic: 15.2 us -> none  [the longest x3 6.77 us: diffuse(): window(padded, axis, offset) - centre]
    add x14 -> x0, other arithmetic: 11.8 us -> none  [the longest x3 3.79 us: transpose_rate(): inner = inner.at[:, :, -1].add(return_z(back[1:-1, 1:-1, 0], -1))]
    scatter-add x12 -> x0, local copies, waits for them, and re-layouts: 11.5 us -> none  [the longest x3 5.1 us: transpose_rate(): inner = inner.at[:, :, -1].add(return_z(back[1:-1, 1:-1, 0], -1))]
    slice x14 -> x0, local copies, waits for them, and re-layouts: 7.68 us -> none  [the longest x4 3.19 us: extended(): lax.slice_in_dim(block, block.shape[dim] - width, None, axis=dim)]
    pallas_call x0 -> x7, Pallas kernels: none -> 6.93 us  [call(): pl.pallas_call(kernel, out_shape=[space(shape, jnp.float32) for shape in...]
    ppermute x30 -> x10, waiting for transfers between devices: 28.3 us -> 35.1 us  [the longest x2 14.1 us: swap_chips(): return lax.ppermute(x, ('gx', 'gz'), chips)]
    another operation x6 -> x0, local copies, waits for them, and re-layouts: 6.41 us -> none
  transfers between devices with their start and end apart: 30 -> 10, of which waited for: 14 -> 7; matrix products, arithmetic and copies ran while one was open for 13% -> 0% of each run, Pallas kernels for 0% -> 0%
where the time goes in v1:
time: 59.3 us; the launch traced here: 59 us
  waiting for transfers between devices  35.1 us (59%)
  starting transfers between devices  11.1 us (19%)
  Pallas kernels  6.93 us (12%)
  local copies, waits for them, and re-layouts  5.2 us (9%)
  between operations  0.7 us (1%)
    ppermute x2, waiting for transfers between devices, swap_chips(): return lax.ppermute(x, ('gx', 'gz'), chips)  14.1 us
    ppermute x1, waiting for transfers between devices, on_device(): up = lax.ppermute(up, 'gx', ahead)  7.12 us
    pallas_call x7, Pallas kernels, call(): pl.pallas_call(kernel, out_shape=[space(shape, jnp.float32) for shape in...  6.93 us
    unnamed x10, local copies, waits for them, and re-layouts  5.2 us
    ppermute x1, waiting for transfers between devices, on_device(): down = lax.ppermute(down, 'gx', behind)  4.76 us
    ppermute x5, waiting for transfers between devices, swap_cores(): return lax.ppermute(x, 'gz', cores)  4.58 us
    ppermute x1, waiting for transfers between devices, on_device(): rims = [lax.ppermute(rims[0], 'gy', [(0, 1), (1, 0)])]  4.5 us
    ppermute x2, starting transfers between devices, swap_chips(): return lax.ppermute(x, ('gx', 'gz'), chips)  3.51 us
  transfers between devices with their start and end apart: 10, of which 7 were waited for; matrix products, arithmetic and copies ran while one was open for 0% of the time, Pallas kernels for 0%

profile of v1, /device:TPU:0, one launch (start us, length us, event | category | flops | bytes accessed | tf_op | source)
XLA Modules:
  0.0 59.0 jit_solution(17246580951452800719)
XLA Ops:
  0.6 0.0 copy-start
  0.6 1.0 %copy-done = s32[8,64,256]{2,1,0:T(8,128)S(1)} copy-done((s32[8,64,256]{2,1,0:T(8,128)S(1)}, s32[8,64,256]{2,1,0:T(8,128)}, u32[]{:S(2)}) %copy-start) | copy-done | bytes 524312
  1.7 0.0 copy-start.1
  1.7 1.0 %copy-done.1 = f32[8,64,256]{2,1,0:T(8,128)S(1)} copy-done((f32[8,64,256]{2,1,0:T(8,128)S(1)}, f32[8,64,256]{2,1,0:T(8,128)}, u32[]{:S(2)}) %copy-start.1) | copy-done | bytes 524312
  2.7 0.0 copy-start.2
  2.7 1.0 %copy-done.2 = f32[8,64,256]{2,1,0:T(8,128)S(1)} copy-done((f32[8,64,256]{2,1,0:T(8,128)S(1)}, f32[8,64,256]{2,1,0:T(8,128)}, u32[]{:S(2)}) %copy-start.2) | copy-done | bytes 524312
  3.8 0.0 copy-start.3
  3.8 1.0 %copy-done.3 = f32[8,64,256]{2,1,0:T(8,128)S(1)} copy-done((f32[8,64,256]{2,1,0:T(8,128)S(1)}, f32[8,64,256]{2,1,0:T(8,128)}, u32[]{:S(2)}) %copy-start.3) | copy-done | bytes 524312
  4.8 0.0 copy-start.4
  4.8 1.0 %copy-done.4 = f32[8,64,256]{2,1,0:T(8,128)S(1)} copy-done((f32[8,64,256]{2,1,0:T(8,128)S(1)}, f32[8,64,256]{2,1,0:T(8,128)}, u32[]{:S(2)}) %copy-start.4) | copy-done | bytes 524312
  5.8 0.1 shard_map.68
  6.0 0.5 collective-permute-start
  6.5 2.7 %collective-permute-done.traded = f32[5,4,64,256]{3,2,1,0:T(8,128)S(1)} collective-permute-done((f32[5,4,64,256]{3,2,1,0:T(8,128)S(1)}, f32[5,4,64,256]{3,2,1,0:T(8,128)S(1)}, u32[]{:S(2)}, u32[]{:S(2)}) %collective-permute-start) | collective-permute-done | bytes 1310752 | tf_op jit(solution)/shard_map/ppermute | solution.py:365
  9.2 0.2 shard_map.69
  9.4 2.9 %collective-permute-start.1 = (f32[5,2,8,512]{3,2,1,0:T(8,128)S(1)}, f32[5,2,8,512]{3,2,1,0:T(8,128)S(1)}, u32[]{:S(2)}, u32[]{:S(2)}) collective-permute-start(f32[5,2,8,512]{3,2,1,0:T(8,128)S(1)} %get-tuple-element.30), channel_id=1, source_target_pairs={{0,2},{2,0},{1,3},{3,1},{4,6},{6,4},{5,7},{7,5},{8,10},{10,8},{9,1... | collective-permute-start | bytes 491528 | tf_op jit(solution)/shard_map/ppermute | solution.py:381
  12.3 4.5 %collective-permute-done.1.refs_0_ = f32[5,2,8,512]{3,2,1,0:T(8,128)S(1)} collective-permute-done((f32[5,2,8,512]{3,2,1,0:T(8,128)S(1)}, f32[5,2,8,512]{3,2,1,0:T(8,128)S(1)}, u32[]{:S(2)}, u32[]{:S(2)}) %collective-permute-start.1) | collective-permute-done | bytes 163872 | tf_op jit(solution)/shard_map/ppermute | solution.py:381
  16.8 1.7 %shard_map.70 = (f32[5,4,8,512]{3,2,1,0:T(8,128)S(1)}, f32[3,72,512]{2,1,0:T(8,128)S(1)}, f32[4,72,512]{2,1,0:T(8,128)S(1)}, f32[4,72,512]{2,1,0:T(8,128)S(1)}, ...) custom-call(f32[5,4,64,512]{3,2,1,0:T(8,128)S(1)} %get-tuple-element, ...), custom_call_target="tpu_custom_call" | custom-call | tf_op jit(solution)/shard_map/pallas_call | solution.py:19
  18.5 0.1 collective-permute-start.6
  18.6 1.9 %collective-permute-start.2 = (f32[4,64,256]{2,1,0:T(8,128)S(1)}, f32[4,64,256]{2,1,0:T(8,128)S(1)}, u32[]{:S(2)}, u32[]{:S(2)}) collective-permute-start(f32[4,64,256]{2,1,0:T(8,128)S(1)} %get-tuple-element.38), channel_id=1, source_target_pairs={{0,4},{4,8},{8,12},{12,0},{1,5},{5,9},{9,13},{13,1},{2,6},{6,10},{... | collective-permute-start | bytes 786440 | tf_op jit(solution)/shard_map/ppermute | solution.py:373
  20.5 2.1 %collective-permute-start.3 = (f32[4,64,256]{2,1,0:T(8,128)S(1)}, f32[4,64,256]{2,1,0:T(8,128)S(1)}, u32[]{:S(2)}, u32[]{:S(2)}) collective-permute-start(f32[4,64,256]{2,1,0:T(8,128)S(1)} %get-tuple-element.39), channel_id=1, source_target_pairs={{4,0},{8,4},{12,8},{0,12},{5,1},{9,5},{13,9},{1,13},{6,2},{10,6},{... | collective-permute-start | bytes 786440 | tf_op jit(solution)/shard_map/ppermute | solution.py:374
  22.6 7.1 %collective-permute-done.2.up = f32[4,64,256]{2,1,0:T(8,128)S(1)} collective-permute-done((f32[4,64,256]{2,1,0:T(8,128)S(1)}, f32[4,64,256]{2,1,0:T(8,128)S(1)}, u32[]{:S(2)}, u32[]{:S(2)}) %collective-permute-start.2) | collective-permute-done | bytes 262176 | tf_op jit(solution)/shard_map/ppermute | solution.py:373
  29.7 4.8 %collective-permute-done.3.down = f32[4,64,256]{2,1,0:T(8,128)S(1)} collective-permute-done((f32[4,64,256]{2,1,0:T(8,128)S(1)}, f32[4,64,256]{2,1,0:T(8,128)S(1)}, u32[]{:S(2)}, u32[]{:S(2)}) %collective-permute-start.3) | collective-permute-done | bytes 262176 | tf_op jit(solution)/shard_map/ppermute | solution.py:374
  34.5 0.1 collective-permute-start.4
  34.6 2.4 %collective-permute-start.5 = (f32[104,512]{1,0:T(8,128)S(1)}, f32[104,512]{1,0:T(8,128)S(1)}, u32[]{:S(2)}, u32[]{:S(2)}) collective-permute-start(f32[104,512]{1,0:T(8,128)S(1)} %get-tuple-element.40), channel_id=1, source_target_pairs={{1,4},{5,8},{9,12},{13,0},{4,1},{8,5},{12,9},{0,13},{3,6},{7,10},{... | collective-permute-start | bytes 638984 | tf_op jit(solution)/shard_map/ppermute | solution.py:368
  37.0 0.0 collective-permute-done.4.passed
  37.0 6.5 %collective-permute-done.5.off = f32[104,512]{1,0:T(8,128)S(1)} collective-permute-done((f32[104,512]{1,0:T(8,128)S(1)}, f32[104,512]{1,0:T(8,128)S(1)}, u32[]{:S(2)}, u32[]{:S(2)}) %collective-permute-start.5) | collective-permute-done | bytes 213024 | tf_op jit(solution)/shard_map/ppermute | solution.py:368
  43.5 0.0 collective-permute-done.6.on
  43.5 1.9 %shard_map.72 = (f32[6,72,512]{2,1,0:T(8,128)S(1)}, f32[4,72,512]{2,1,0:T(8,128)S(1)}, f32[4,72,512]{2,1,0:T(8,128)S(1)}, f32[4,72,512]{2,1,0:T(8,128)S(1)}, f32...) custom-call(f32[5,4,64,512]{3,2,1,0:T(8,128)S(1)} %get-tuple-element, ...), custom_call_target="tpu_custom_call" | custom-call | tf_op jit(solution)/shard_map/pallas_call | solution.py:19
  45.5 1.1 %collective-permute-start.7 = (f32[136,512]{1,0:T(8,128)S(1)}, f32[136,512]{1,0:T(8,128)S(1)}, u32[]{:S(2)}, u32[]{:S(2)}) collective-permute-start(f32[136,512]{1,0:T(8,128)S(1)} %get-tuple-element.50), channel_id=1, source_target_pairs={{1,4},{5,8},{9,12},{13,0},{4,1},{8,5},{12,9},{0,13},{3,6},{7,10},{... | collective-permute-start | bytes 835592 | tf_op jit(solution)/shard_map/ppermute | solution.py:368
  46.6 0.0 collective-permute-start.8
  46.6 7.6 %collective-permute-done.7.off2 = f32[136,512]{1,0:T(8,128)S(1)} collective-permute-done((f32[136,512]{1,0:T(8,128)S(1)}, f32[136,512]{1,0:T(8,128)S(1)}, u32[]{:S(2)}, u32[]{:S(2)}) %collective-permute-start.7) | collective-permute-done | bytes 278560 | tf_op jit(solution)/shard_map/ppermute | solution.py:368
  54.1 0.0 collective-permute-done.8.on2
  54.1 1.9 %shard_map.73 = (f32[2,4,64,256]{3,2,1,0:T(8,128)S(1)}, f32[2,4,64,256]{3,2,1,0:T(8,128)S(1)}, f32[6,72,512]{2,1,0:T(8,128)}, f32[4,72,512]{2,1,0:T(8,128)}) custom-call(f32[5,4,64,512]{3,2,1,0:T(8,128)S(1)} %get-tuple-element.29.block, f32[3,72,512]{2,1,0:T(8,128)S(1)} %get-tuple-element.31.kx, f32[4,72,512]{2,1,0:T(8,128)S(1)} %get-tuple-element.32.ky, ...), custom_call_target="tpu_custom_call" | custom-call | tf_op jit(solution)/shard_map/pallas_call | solution.py:19
  56.0 0.0 collective-permute-start.9
  56.0 1.9 %collective-permute-done.9.got = f32[2,4,64,256]{3,2,1,0:T(8,128)S(1)} collective-permute-done((f32[2,4,64,256]{3,2,1,0:T(8,128)S(1)}, f32[2,4,64,256]{3,2,1,0:T(8,128)S(1)}, u32[]{:S(2)}, u32[]{:S(2)}) %collective-permute-start.9) | collective-permute-done | bytes 524320 | tf_op jit(solution)/shard_map/ppermute | solution.py:365
  57.9 1.1 %shard_map.74 = (f32[8,64,256]{2,1,0:T(8,128)}, f32[8,64,256]{2,1,0:T(8,128)}) custom-call(s32[8,64,256]{2,1,0:T(8,128)S(1)} %copy-done, f32[2,4,64,256]{3,2,1,0:T(8,128)S(1)} %get-tuple-element.52.keep, f32[2,4,64,256]{3,2,1,0:T(8,128)S(1)} %collective-permute-done.9.got), custom_call_target="tpu_custom_call" | custom-call | tf_op jit(solution)/shard_map/pallas_call | solution.py:19
  (1 shorter events, 0.0 us)
Async XLA Ops:
  0.6 1.0 %copy-start = (s32[8,64,256]{2,1,0:T(8,128)S(1)}, s32[8,64,256]{2,1,0:T(8,128)}, u32[]{:S(2)}) copy-start(s32[8,64,256]{2,1,0:T(8,128)} %labels.5) | copy-start | bytes 1572868
  1.7 1.0 %copy-start.1 = (f32[8,64,256]{2,1,0:T(8,128)S(1)}, f32[8,64,256]{2,1,0:T(8,128)}, u32[]{:S(2)}) copy-start(f32[8,64,256]{2,1,0:T(8,128)} %state.3) | copy-start | bytes 1572868
  2.7 1.0 %copy-start.2 = (f32[8,64,256]{2,1,0:T(8,128)S(1)}, f32[8,64,256]{2,1,0:T(8,128)}, u32[]{:S(2)}) copy-start(f32[8,64,256]{2,1,0:T(8,128)} %conduct.3) | copy-start | bytes 1572868
  3.8 1.0 %copy-start.3 = (f32[8,64,256]{2,1,0:T(8,128)S(1)}, f32[8,64,256]{2,1,0:T(8,128)}, u32[]{:S(2)}) copy-start(f32[8,64,256]{2,1,0:T(8,128)} %sink.3) | copy-start | bytes 1572868
  4.8 1.0 %copy-start.4 = (f32[8,64,256]{2,1,0:T(8,128)S(1)}, f32[8,64,256]{2,1,0:T(8,128)}, u32[]{:S(2)}) copy-start(f32[8,64,256]{2,1,0:T(8,128)} %cotangent.3) | copy-start | bytes 1572868
  6.0 3.2 %collective-permute-start = (f32[5,4,64,256]{3,2,1,0:T(8,128)S(1)}, f32[5,4,64,256]{3,2,1,0:T(8,128)S(1)}, u32[]{:S(2)}, u32[]{:S(2)}) collective-permute-start(f32[5,4,64,256]{3,2,1,0:T(8,128)S(1)} %get-tuple-element.28), channel_id=1, source_target_pairs={{0,1},{1,0},{2,3},{3,2},{4,5},{5,4},{6,7},{7,6},{8,9},{9,8},{10,11... | collective-permute-start | bytes 3932168 | tf_op jit(solution)/shard_map/ppermute | solution.py:365
  9.4 7.4 %collective-permute-start.1 = (f32[5,2,8,512]{3,2,1,0:T(8,128)S(1)}, f32[5,2,8,512]{3,2,1,0:T(8,128)S(1)}, u32[]{:S(2)}, u32[]{:S(2)}) collective-permute-start(f32[5,2,8,512]{3,2,1,0:T(8,128)S(1)} %get-tuple-element.30), channel_id=1, source_target_pairs={{0,2},{2,0},{1,3},{3,1},{4,6},{6,4},{5,7},{7,5},{8,10},{10,8},{9,1... | collective-permute-start | bytes 491528 | tf_op jit(solution)/shard_map/ppermute | solution.py:381
  18.5 25.0 %collective-permute-start.6 = (f32[5,72,512]{2,1,0:T(8,128)S(1)}, f32[5,72,512]{2,1,0:T(8,128)S(1)}, u32[]{:S(2)}, u32[]{:S(2)}) collective-permute-start(f32[5,72,512]{2,1,0:T(8,128)S(1)} %get-tuple-element.41), channel_id=1, source_target_pairs={{0,1},{1,0},{2,3},{3,2},{4,5},{5,4},{6,7},{7,6},{8,9},{9,8},{10,11... | collective-permute-start | bytes 2211848 | tf_op jit(solution)/shard_map/ppermute | solution.py:365
  18.6 11.1 %collective-permute-start.2 = (f32[4,64,256]{2,1,0:T(8,128)S(1)}, f32[4,64,256]{2,1,0:T(8,128)S(1)}, u32[]{:S(2)}, u32[]{:S(2)}) collective-permute-start(f32[4,64,256]{2,1,0:T(8,128)S(1)} %get-tuple-element.38), channel_id=1, source_target_pairs={{0,4},{4,8},{8,12},{12,0},{1,5},{5,9},{9,13},{13,1},{2,6},{6,10},{... | collective-permute-start | bytes 786440 | tf_op jit(solution)/shard_map/ppermute | solution.py:373
  20.5 14.0 %collective-permute-start.3 = (f32[4,64,256]{2,1,0:T(8,128)S(1)}, f32[4,64,256]{2,1,0:T(8,128)S(1)}, u32[]{:S(2)}, u32[]{:S(2)}) collective-permute-start(f32[4,64,256]{2,1,0:T(8,128)S(1)} %get-tuple-element.39), channel_id=1, source_target_pairs={{4,0},{8,4},{12,8},{0,12},{5,1},{9,5},{13,9},{1,13},{6,2},{10,6},{... | collective-permute-start | bytes 786440 | tf_op jit(solution)/shard_map/ppermute | solution.py:374
  34.5 2.5 %collective-permute-start.4 = (f32[4,64,256]{2,1,0:T(8,128)S(1)}, f32[4,64,256]{2,1,0:T(8,128)S(1)}, u32[]{:S(2)}, u32[]{:S(2)}) collective-permute-start(f32[4,64,256]{2,1,0:T(8,128)S(1)} %shard_map.71), channel_id=1, source_target_pairs={{0,1},{1,0},{2,3},{3,2},{4,5},{5,4},{6,7},{7,6},{8,9},{9,8},{10,11... | collective-permute-start | bytes 786440 | tf_op jit(solution)/shard_map/ppermute | solution.py:365
  34.6 9.0 %collective-permute-start.5 = (f32[104,512]{1,0:T(8,128)S(1)}, f32[104,512]{1,0:T(8,128)S(1)}, u32[]{:S(2)}, u32[]{:S(2)}) collective-permute-start(f32[104,512]{1,0:T(8,128)S(1)} %get-tuple-element.40), channel_id=1, source_target_pairs={{1,4},{5,8},{9,12},{13,0},{4,1},{8,5},{12,9},{0,13},{3,6},{7,10},{... | collective-permute-start | bytes 638984 | tf_op jit(solution)/shard_map/ppermute | solution.py:368
  45.5 8.7 %collective-permute-start.7 = (f32[136,512]{1,0:T(8,128)S(1)}, f32[136,512]{1,0:T(8,128)S(1)}, u32[]{:S(2)}, u32[]{:S(2)}) collective-permute-start(f32[136,512]{1,0:T(8,128)S(1)} %get-tuple-element.50), channel_id=1, source_target_pairs={{1,4},{5,8},{9,12},{13,0},{4,1},{8,5},{12,9},{0,13},{3,6},{7,10},{... | collective-permute-start | bytes 835592 | tf_op jit(solution)/shard_map/ppermute | solution.py:368
  46.6 7.6 %collective-permute-start.8 = (f32[136,512]{1,0:T(8,128)S(1)}, f32[136,512]{1,0:T(8,128)S(1)}, u32[]{:S(2)}, u32[]{:S(2)}) collective-permute-start(f32[136,512]{1,0:T(8,128)S(1)} %get-tuple-element.51), channel_id=1, source_target_pairs={{0,1},{1,0},{2,3},{3,2},{4,5},{5,4},{6,7},{7,6},{8,9},{9,8},{10,11... | collective-permute-start | bytes 835592 | tf_op jit(solution)/shard_map/ppermute | solution.py:365
  56.0 1.9 %collective-permute-start.9 = (f32[2,4,64,256]{3,2,1,0:T(8,128)S(1)}, f32[2,4,64,256]{3,2,1,0:T(8,128)S(1)}, u32[]{:S(2)}, u32[]{:S(2)}) collective-permute-start(f32[2,4,64,256]{3,2,1,0:T(8,128)S(1)} %get-tuple-element.53), channel_id=1, source_target_pairs={{0,1},{1,0},{2,3},{3,2},{4,5},{5,4},{6,7},{7,6},{8,9},{9,8},{10,11... | collective-permute-start | bytes 1572872 | tf_op jit(solution)/shard_map/ppermute | solution.py:365

commit v2 on v0

v2 whole, which is shorter than its diff:
```python
import functools

import jax
import jax.numpy as jnp
from jax import lax
from jax.experimental import pallas as pl
from jax.experimental.pallas import tpu as pltpu
from jax.sharding import PartitionSpec as P

VMEM = pltpu.VMEM
HBM = pltpu.HBM
time_step = 0.06
scale = 0.5 * time_step
HALO = 4
TILE = 8
PIECES = 2
S, C, T, F, K = range(5)


def call(kernel, outs, *ins, keep=True, given=VMEM, scratch=()):
    space = VMEM if keep else jax.ShapeDtypeStruct
    block = pl.BlockSpec(memory_space=VMEM if given is VMEM else pl.ANY)
    return pl.pallas_call(
        kernel,
        out_shape=[space(shape, jnp.float32) for shape in outs],
        in_specs=[block] * len(ins),
        out_specs=[pl.BlockSpec(memory_space=VMEM)] * len(outs),
        scratch_shapes=list(scratch),
        compiler_params=pltpu.CompilerParams(vmem_limit_bytes=8 * 1024 * 1024),
        cost_estimate=pl.CostEstimate(flops=1024, bytes_accessed=1024, transcendentals=0),
    )(*[pltpu.with_memory_space_constraint(x, given) for x in ins])


def half_fluid(labels):
    return jnp.where(labels <= 1, 0.5, 0.0)


def touching(labels):
    return jnp.logical_or(labels == 1, labels == 2)


def rows_of(value):
    return lax.broadcasted_iota(jnp.int32, value.shape, 0)


def lanes_of(value):
    return lax.broadcasted_iota(jnp.int32, value.shape, 1)


def down_rows(before, here):
    return pltpu.roll(jnp.where(rows_of(here) == TILE - 1, before, here), 1, 0)


def up_rows(here, after):
    return pltpu.roll(jnp.where(rows_of(here) == 0, after, here), TILE - 1, 0)


def down_lanes(here):
    return pltpu.roll(here, 1, 1)


def up_lanes(here):
    return pltpu.roll(here, here.shape[1] - 1, 1)


def at(t):
    return slice(t * TILE, (t + 1) * TILE)


class Tiles:
    def __init__(self, *places):
        self.places = places

    def __getitem__(self, t):
        ref, slot = self.places[t % len(self.places)]
        return ref[at(slot)]

    def __setitem__(self, t, value):
        ref, slot = self.places[t]
        ref[at(slot)] = value

    def __len__(self):
        return len(self.places)


def whole(ref):
    return Tiles(*[(ref, t) for t in range(ref.shape[0] // TILE)])


def with_ghost(main, ghost):
    return Tiles(*[(main, t) for t in range(main.shape[0] // TILE)], (ghost, 0))


def mid_and_rim(mid, rim):
    return Tiles((rim, 0), *[(mid, t) for t in range(mid.shape[0] // TILE)], (rim, 1), (rim, 2))


class Across:
    def __init__(self, ky, kz, v):
        self.ky, self.kz, self.v = ky, kz, v
        self.known = {}

    def product(self, t):
        t = t % len(self.v)
        if t not in self.known:
            self.known[t] = self.ky[t] * self.v[t]
        return self.known[t]

    def __getitem__(self, t):
        here, kz = self.v[t], self.kz[t]
        along_y = self.ky[t] * down_rows(self.v[t - 1], here) + up_rows(self.product(t), self.product(t + 1))
        return along_y + (kz * down_lanes(here) + up_lanes(kz * here))


class Made:
    def __init__(self, values):
        self.values = values

    def __getitem__(self, t):
        return self.values[t % len(self.values)]

    def __len__(self):
        return len(self.values)


def sides_along_z(c, here):
    lanes = lanes_of(c)
    left = here + jnp.where(lanes == 0, 0.0, down_lanes(c)) * scale
    right = here + jnp.where(lanes == lanes.shape[1] - 1, 0.0, up_lanes(c)) * scale
    return left, right


def load_all(pairs, sems):
    copies = [pltpu.make_async_copy(a, b, sems.at[i]) for i, (a, b) in enumerate(pairs)]
    for copy in copies:
        copy.start()
    return copies


def load_planes(inputs, start, out, kinds, drains, sems):
    state, conduct, sink, labels, cotangent = inputs
    part = pl.ds(start, out.shape[1])
    pairs = [(labels.at[part], kinds), (sink.at[part], drains), (state.at[part], out.at[S])]
    return load_all(pairs + [(conduct.at[part], out.at[C]), (cotangent.at[part], out.at[T])], sems)


def fill_planes(out, kinds, drains):
    for i in range(out.shape[1]):
        out[F, i] = half_fluid(kinds[i])
        out[K, i] = jnp.where(touching(kinds[i]), drains[i], 0.0)


def pack_inputs(state, conduct, sink, labels, cotangent, up, down, trade, kinds, drains, ends, sems, plane_sems):
    count = state.shape[0]
    pairs = []
    for which, (out, plane) in enumerate(((up, count - 1), (down, 0))):
        pairs += [(state.at[plane], out.at[S]), (conduct.at[plane], out.at[C]), (cotangent.at[plane], out.at[T])]
        pairs += [(labels.at[plane], ends.at[which])]
    copies = load_all(pairs, plane_sems)
    start = (1 - lax.axis_index("gz")) * (count - trade.shape[1])
    copies += load_planes((state, conduct, sink, labels, cotangent), start, trade, kinds, drains, sems)
    for copy in copies:
        copy.wait()
    up[F] = half_fluid(ends[0])
    down[F] = half_fluid(ends[1])
    fill_planes(trade, kinds, drains)


def own_planes(state, conduct, sink, labels, cotangent, mine, kinds, drains, sems):
    start = lax.axis_index("gz") * (state.shape[0] - mine.shape[1])
    for copy in load_planes((state, conduct, sink, labels, cotangent), start, mine, kinds, drains, sems):
        copy.wait()
    fill_planes(mine, kinds, drains)


def pack_rims(two, planes, outs):
    for k in range(0, len(planes), 2):
        even, odd = planes[k], planes[min(k + 1, len(planes) - 1)]
        ny = even.shape[0]
        low_even, high_even = even[0:TILE], even[ny - TILE : ny]
        low_odd, high_odd = odd[0:TILE], odd[ny - TILE : ny]
        upper = rows_of(low_even) < HALO
        low = jnp.where(upper, low_even, pltpu.roll(low_odd, HALO, 0))
        high = jnp.where(upper, pltpu.roll(high_even, HALO, 0), high_odd)
        per = outs[0].shape[0]
        piece, slot = k // 2 // per, k // 2 % per
        if two:
            outs[piece][slot] = jnp.where(lax.axis_index("gy") == 0, high, low)
        else:
            outs[2 * piece][slot] = low
            outs[2 * piece + 1][slot] = high


def unpack_rims(two, count_y, rims, planes):
    place = lax.axis_index("gy")
    for k in range(0, len(planes), 2):
        per = rims[0].shape[0]
        piece, slot = k // 2 // per, k // 2 % per
        above = jnp.where(place < count_y - 1, rims[piece if two else 2 * piece][slot], 0.0)
        below = jnp.where(place > 0, rims[piece if two else 2 * piece + 1][slot], 0.0)
        upper = rows_of(above) < HALO
        planes[k][...] = jnp.where(upper, above, pltpu.roll(below, HALO, 0))
        if k + 1 < len(planes):
            planes[k + 1][...] = jnp.where(upper, pltpu.roll(above, HALO, 0), below)


def gather_planes(mine, traded, block, near):
    core = lax.axis_index("gz")
    half, narrow = block.shape[1], mine.shape[3]
    own = pl.ds(pl.multiple_of(core * narrow, 128), narrow)
    other = pl.ds(pl.multiple_of((1 - core) * narrow, 128), narrow)
    start = 2 * core
    beside = (1 - core) * half + core
    beyond = (1 - core) * (half + 1)
    for j in range(5):
        for i in range(half):
            block[j, i, :, own] = mine[j, start + i]
            block[j, i, :, other] = traded[j, start + i]
        near[j, :, own] = mine[j, beside]
        near[j, :, other] = traded[j, beside]
        if j in (S, C):
            near[5 + j, :, own] = mine[j, beyond]
            near[5 + j, :, other] = traded[j, beyond]


def rim_planes(block, near):
    return [block.at[j, i] for j in range(5) for i in range(block.shape[1])] + [near.at[j] for j in range(7)]


def pack_along_y(two, block, near, *rims):
    pack_rims(two, rim_planes(block, near), rims)


class Lazy:
    def __init__(self, count, make):
        self.count, self.make, self.known = count, make, {}

    def __getitem__(self, t):
        t = t % self.count
        if t not in self.known:
            self.known[t] = self.make(t)
        return self.known[t]

    def __len__(self):
        return self.count


def prepare(todo, count_y, block, near, ghost, near_ghost, kx, ky_out, kz_out, diag, part, back, one):
    place = lax.axis_index("gy")
    core = lax.axis_index("gz")
    half, ny = block.shape[1], block.shape[2]
    count, last = ny // TILE + 1, half - 1

    def own(j, i):
        if ghost is None:
            return Tiles(*[(block.at[j, i], t) for t in range(count - 1)], (None, 0))
        return with_ghost(block.at[j, i], ghost.at[j, i])

    def next_to(j):
        if ghost is None:
            return Tiles(*[(near.at[j], t) for t in range(count - 1)], (None, 0))
        return with_ghost(near.at[j], near_ghost.at[j])

    def faces_along_y(c):
        def make(t):
            value = (c[t] + down_rows(c[t - 1], c[t])) * scale
            if t == 0:
                value = jnp.where(jnp.logical_and(rows_of(value) == 0, place == 0), 0.0, value)
            if t == count - 1:
                value = jnp.where(jnp.logical_and(rows_of(value) == 0, place == count_y - 1), 0.0, value)
            return value

        return Lazy(count, make)

    def own_weight(c, f, t):
        here = c[t] * scale
        left, right = sides_along_z(c[t], here)
        low, high = down_rows(c[t - 1], c[t]), up_rows(c[t], c[t + 1])
        return left, (2.0 * here + (low + high) * scale) + (left + right) + time_step * f[t]

    for i in range(half):
        s, c, a, f, k = (own(j, i) for j in (S, C, T, F, K))
        ky, kz = faces_along_y(c), {}
        for t in todo:
            left, weight = own_weight(c, f, t)
            kz[t] = jnp.where(lanes_of(left) == 0, 0.0, left)
            slot = at(todo.index(t))
            if i > 0:
                face = (c[t] + own(C, i - 1)[t]) * scale
                kx[i - 1, slot] = face
                weight = weight + face
            if i < last:
                weight = weight + (c[t] + own(C, i + 1)[t]) * scale
            diag[i, slot] = weight
            ky_out[i, slot] = ky[t]
            kz_out[i, slot] = kz[t]
        scaled = Lazy(count, lambda t, a=a, f=f: a[t] * (0.5 + f[t]))
        ahead = Across(ky, kz, s)
        behind = Across(ky, kz, scaled)
        for t in todo:
            slot = at(todo.index(t))
            d, b = diag[i, slot], scaled[t]
            go = ahead[t] - d * s[t] - time_step * k[t] * jnp.tanh(s[t])
            come = behind[t] - d * b
            if i > 0:
                go = go + (kx[i - 1, slot] + time_step * f[t]) * own(S, i - 1)[t]
                come = come + kx[i - 1, slot] * (own(T, i - 1)[t] * (0.5 + own(F, i - 1)[t]))
            if i < last:
                face, high_f = (c[t] + own(C, i + 1)[t]) * scale, own(F, i + 1)[t]
                go = go + face * own(S, i + 1)[t]
                come = come + (face + time_step * high_f) * (own(T, i + 1)[t] * (0.5 + high_f))
            part[i, slot] = s[t] + (0.5 + f[t]) * go
            back[i, slot] = a[t] + come
    s, c, f, k = (next_to(j) for j in (S, C, F, K))
    kz = {}
    for t in todo:
        left, _ = own_weight(c, f, t)
        kz[t] = jnp.where(lanes_of(left) == 0, 0.0, left)
    ahead = Across(faces_along_y(c), kz, s)
    is_low = core == 0
    for t in todo:
        _, weight = own_weight(c, f, t)
        c_own = jnp.where(is_low, own(C, last)[t], own(C, 0)[t])
        s_own = jnp.where(is_low, own(S, last)[t], own(S, 0)[t])
        face_own, face_far = (c[t] + c_own) * scale, (c[t] + next_to(5 + C)[t]) * scale
        wind = time_step * f[t]
        go = ahead[t] - (weight + face_own + face_far) * s[t] - time_step * k[t] * jnp.tanh(s[t])
        go = go + (face_own + jnp.where(is_low, wind, 0.0)) * s_own
        go = go + (face_far + jnp.where(is_low, 0.0, wind)) * next_to(5 + S)[t]
        one[at(todo.index(t))] = s[t] + (0.5 + f[t]) * go


def prepare_mid(count_y, block, near, *outs):
    prepare(list(range(1, block.shape[2] // TILE - 1)), count_y, block, near, None, None, *outs)


def prepare_rim(two, count_y, block, near, *refs):
    rims, (ghost, near_ghost, *outs) = refs[: PIECES * (1 if two else 2)], refs[PIECES * (1 if two else 2) :]
    count = block.shape[2] // TILE
    unpack_rims(two, count_y, rims, rim_planes(ghost, near_ghost))
    prepare([0, count - 1, count], count_y, block, near, ghost, near_ghost, *outs)


def pack_pair(place, a, b):
    upper = rows_of(a) < HALO
    turned_a, turned_b = pltpu.roll(a, HALO, 0), pltpu.roll(b, HALO, 0)
    return jnp.where(upper, jnp.where(place == 0, a, turned_a), jnp.where(place == 0, turned_b, b))


def unpack_pair(place, both):
    upper = rows_of(both) < HALO
    turned = pltpu.roll(both, HALO, 0)
    valid = upper == (place == 0)
    a = jnp.where(place == 0, both, turned)
    b = jnp.where(place == 0, turned, both)
    return jnp.where(valid, a, 0.0), jnp.where(valid, b, 0.0)


def pack_off(two, ghost, part_mid, part_rim, off):
    place = lax.axis_index("gy")
    outer = lax.axis_index("gz") * (ghost.shape[1] - 1)
    part = mid_and_rim(part_mid.at[outer], part_rim.at[outer])
    for t in range(len(part)):
        off[at(t)] = part[t]
    for j in range(0, 4, 2):
        a, b = ghost[j, outer], ghost[j + 1, outer]
        if two:
            off[at(len(part) + j // 2)] = pack_pair(place, a, b)
        else:
            off[at(len(part) + j)] = a
            off[at(len(part) + j + 1)] = b


def choose_half(up, down, *refs):
    for j in range(4):
        refs[j - 4][...] = jnp.where(lax.axis_index("gz") == 0, down[j], up[j])


def coefficients(refs):
    mids, rims = refs[:6], refs[7:13]
    return [lambda i, m=m, r=r: mid_and_rim(m.at[i], r.at[i]) for m, r in zip(mids, rims)]


def middle(two, block, ghost, near, near_ghost, up, down, *refs):
    passed, off, refs = refs[:4], refs[4], refs[5:]
    kx, ky, kz, diag, part, back = coefficients(refs[:14])
    side, edge, add, first, known, linear, adjoint, sa, b2, hot2, inward = refs[14:]
    core = lax.axis_index("gz")
    place = lax.axis_index("gy")
    half, ny, narrow = block.shape[1], block.shape[2], up.shape[2]
    count, last = ny // TILE, half - 1
    own = lambda j, i: with_ghost(block.at[j, i], ghost.at[j, i])
    outside, inside = core, 1 - core
    for j in range(4):
        side[j, outside, 0:ny, 0:narrow] = jnp.where(core == 0, up[j], passed[j][...])
        side[j, outside, 0:ny, narrow : 2 * narrow] = jnp.where(core == 0, passed[j][...], down[j])
        side[j, inside, 0:ny] = near[j]
        side[j, inside, ny : ny + TILE] = near_ghost[j]
    for j in range(0, 4, 2):
        if two:
            a, b = unpack_pair(place, off[at(count + 1 + j // 2)])
        else:
            a, b = off[at(count + 1 + j)], off[at(count + 2 + j)]
        side[j, outside, ny : ny + TILE] = a
        side[j + 1, outside, ny : ny + TILE] = b
    for which, i in ((0, 0), (1, last)):
        s, f, c = own(S, i), own(F, i), own(C, i)
        s_out, c_out, f_out = (whole(side.at[j, which]) for j in (S, C, F))
        for t in range(count + 1):
            face = (c[t] + c_out[t]) * scale
            edge[which, at(t)] = face
            v, beyond = s[t], s_out[t]
            if which == 0:
                inner_add = (face + time_step * f[t]) * beyond - face * v
                outer_add = face * (v - beyond)
            else:
                inner_add = face * (beyond - v)
                outer_add = (face + time_step * f_out[t]) * v - face * beyond
            first[i, at(t)] = part(i)[t] + (0.5 + f[t]) * inner_add
            add[which, at(t)] = (0.5 + f_out[t]) * outer_add
    for i in range(1, last):
        for t in range(count + 1):
            first[i, at(t)] = part(i)[t]
    for i in range(half):
        v, f, k, s, a = whole(first.at[i]), own(F, i), own(K, i), own(S, i), own(T, i)
        flow = Across(ky(i), kz(i), v)
        for t in range(count + 1):
            rc = 0.5 + f[t]
            sink = time_step * k[t]
            hot1 = jnp.tanh(v[t])
            full = diag(i)[t]
            if i == 0:
                full = full + edge[0, at(t)]
            if i == last:
                full = full + edge[1, at(t)]
            adjoint[i, at(t)] = full + sink * (1.0 - hot1 * hot1)
            rate = flow[t] - full * v[t] - sink * hot1
            if i > 0:
                rate = rate + (kx(i - 1)[t] + time_step * f[t]) * first[i - 1, at(t)]
            if i < last:
                rate = rate + kx(i)[t] * first[i + 1, at(t)]
            value = 0.75 * s[t] + 0.25 * (v[t] + rc * rate)
            b = a[t] * rc
            total = back(i)[t]
            if i == 0:
                total = total + edge[0, at(t)] * (side[T, 0, at(t)] * (0.5 + side[F, 0, at(t)]) - b)
            if i == last:
                high, high_f = edge[1, at(t)], side[F, 1, at(t)]
                total = total + ((high + time_step * high_f) * (side[T, 1, at(t)] * (0.5 + high_f)) - high * b)
            if i == 0 or i == last:
                which = 0 if i == 0 else 1
                known[which, at(t)] = value
                linear[which, at(t)] = total
            else:
                hot = jnp.tanh(value)
                hot2[i, at(t)] = hot
                total = (2.0 / 3.0) * (total - sink * (1.0 - hot * hot) * b)
                sa[i, at(t)] = total
                b2[i, at(t)] = total * rc
    for t in range(count + 1):
        inward[0, at(t)] = (kx(0)[t] + time_step * own(F, 1)[t]) * b2[1, at(t)]
        inward[1, at(t)] = kx(last - 1)[t] * b2[last - 1, at(t)]


def outward(block, ghost, one_mid, one_rim, side, edge, add, known, linear, adjoint, inward, off, *refs):
    ky_mid, kz_mid, ky_rim, kz_rim, hot2, sa, b2, fa, off2, on2 = refs
    core = lax.axis_index("gz")
    half, ny = block.shape[1], block.shape[2]
    count, last = ny // TILE, half - 1
    own = lambda j, i: with_ghost(block.at[j, i], ghost.at[j, i])
    for which, i in ((0, 0), (1, last)):
        f, k, a = own(F, i), own(K, i), own(T, i)
        mine = core == which
        for t in range(count + 1):
            one = jnp.where(mine, off[at(t)] + add[which, at(t)], mid_and_rim(one_mid, one_rim)[t])
            face = edge[which, at(t)]
            if which == 0:
                face = face + time_step * f[t]
            rc = 0.5 + f[t]
            hot = jnp.tanh(known[which, at(t)] + 0.25 * rc * face * one)
            total = (2.0 / 3.0) * (linear[which, at(t)] - time_step * k[t] * (1.0 - hot * hot) * (a[t] * rc))
            hot2[which, at(t)] = hot
            sa[which, at(t)] = total
            b2[which, at(t)] = total * rc
        b = whole(b2.at[which])
        flow = Across(mid_and_rim(ky_mid.at[i], ky_rim.at[i]), mid_and_rim(kz_mid.at[i], kz_rim.at[i]), b)
        for t in range(count + 1):
            total = sa[which, at(t)] + flow[t] - adjoint[i, at(t)] * b[t] + inward[which, at(t)]
            fa[which, at(t)] = 0.25 * total
    for out, which in ((off2, core), (on2, 1 - core)):
        out[0 : ny + TILE] = b2[which]
        out[ny + TILE : 2 * ny + TILE] = fa[which, 0:ny]


def inner(block, ghost, edge, side, first, adjoint, sa_in, b2_in, hot2_in, sa_out, b2_out, hot2_out, fa_out, *refs):
    kx, ky, kz, diag, _, _ = coefficients(refs[:14])
    value, term, adjoint0, hot0, fa, b3 = refs[14:]
    half, ny = block.shape[1], block.shape[2]
    count, last = ny // TILE, half - 1
    own = lambda j, i: with_ghost(block.at[j, i], ghost.at[j, i])
    pick = lambda i, inside, outside: inside.at[i] if 0 < i < last else outside.at[0 if i == 0 else 1]
    sa = lambda i: whole(pick(i, sa_in, sa_out))
    b2 = lambda i: whole(pick(i, b2_in, b2_out))
    hot2 = lambda i: whole(pick(i, hot2_in, hot2_out))
    for i in range(half):
        f = own(F, i)
        flow = Across(ky(i), kz(i), b2(i))
        for t in range(count + 1):
            if 0 < i < last:
                total = sa(i)[t] + flow[t] - adjoint[i, at(t)] * b2(i)[t]
                total = total + kx(i - 1)[t] * b2(i - 1)[t] + (kx(i)[t] + time_step * own(F, i + 1)[t]) * b2(i + 1)[t]
                total = 0.25 * total
            else:
                total = fa_out[0 if i == 0 else 1, at(t)]
            fa[i, at(t)] = total
            b3[i, at(t)] = total * (0.5 + f[t])
    for i in range(half):
        s, f, k, a = own(S, i), own(F, i), own(K, i), own(T, i)
        b = whole(b3.at[i])
        flow = Across(ky(i), kz(i), b)
        for t in range(count):
            hot = jnp.tanh(s[t])
            full = diag(i)[t]
            if i == 0:
                full = full + edge[0, at(t)]
            if i == last:
                full = full + edge[1, at(t)]
            full = full + time_step * k[t] * (1.0 - hot * hot)
            total = flow[t] - full * b[t] + fa[i, at(t)] + 0.75 * sa(i)[t] + a[t] * (1.0 / 3.0)
            if i > 0:
                total = total + kx(i - 1)[t] * b3[i - 1, at(t)]
            if i < last:
                total = total + (kx(i)[t] + time_step * own(F, i + 1)[t]) * b3[i + 1, at(t)]
            value[i, at(t)] = total
            first_hot = jnp.tanh(first[i, at(t)])
            total = (2.0 / 3.0) * hot2(i)[t] * a[t] + 0.25 * first_hot * sa(i)[t] + hot * fa[i, at(t)]
            term[i, at(t)] = -time_step * (0.5 + f[t]) * total
            if i == 0 or i == last:
                which = 0 if i == 0 else 1
                adjoint0[which, at(t)] = full
                hot0[which, at(t)] = -time_step * (0.5 + f[t]) * hot


def finish(block, ghost, edge, side, b2_out, value, term, adjoint0, hot0, off2, on2, *refs):
    kx_mid, ky_mid, kz_mid, kx_rim, ky_rim, kz_rim, keep, give, late = refs
    core = lax.axis_index("gz")
    half, ny, narrow = block.shape[1], block.shape[2], keep.shape[3]
    count, last = ny // TILE, half - 1
    own = lambda j, i: with_ghost(block.at[j, i], ghost.at[j, i])
    both = lambda mid, rim: lambda i: mid_and_rim(mid.at[i], rim.at[i])
    kx, ky, kz = both(kx_mid, kx_rim), both(ky_mid, ky_rim), both(kz_mid, kz_rim)
    gains = {}
    for which, i in ((0, 0), (1, last)):
        mine = core == which
        f = own(F, i)
        for t in range(count + 1):
            face = edge[which, at(t)]
            if which == 1:
                face = face + time_step * side[F, 1, at(t)]
            gain = 0.25 * face * jnp.where(mine, off2[at(t)], on2[at(t)])
            late[which, at(t)] = gain * (0.5 + f[t])
            gains[which, t] = gain

    def write(i, t, total, term):
        for which, whole_row in ((0, total), (1, term)):
            left, right = whole_row[:, :narrow], whole_row[:, narrow:]
            keep[which, i, at(t)] = jnp.where(core == 0, left, right)
            give[which, i, at(t)] = jnp.where(core == 0, right, left)

    for i in range(half):
        for which in range(2):
            if i == which * last:
                flow = Across(ky(i), kz(i), whole(late.at[which]))
        for t in range(count):
            total, sink = value[i, at(t)], term[i, at(t)]
            for which in range(2):
                if i == which * last:
                    mine = core == which
                    slot = slice(ny + (t + 1) * TILE, ny + (t + 2) * TILE)
                    beyond = jnp.where(mine, off2[slot], on2[slot])
                    face, f_out = edge[which, at(t)], side[F, which, at(t)]
                    into, out_of = face, face
                    if which == 0:
                        out_of = out_of + time_step * own(F, 0)[t]
                    else:
                        into = into + time_step * f_out
                    beyond = (beyond + 0.25 * out_of * b2_out[which, at(t)]) * (0.5 + f_out)
                    total = total + gains[which, t] + flow[t] - adjoint0[which, at(t)] * late[which, at(t)] + into * beyond
                    sink = sink + hot0[which, at(t)] * gains[which, t]
            if i == 1:
                total = total + kx(0)[t] * late[0, at(t)]
            if i == last - 1:
                total = total + (kx(last - 1)[t] + time_step * own(F, last)[t]) * late[1, at(t)]
            write(i, t, total, sink)


def assemble(labels, keep, got, grad_state, grad_sink):
    core = lax.axis_index("gz")
    half = keep.shape[1]
    mine, other = core * half, (1 - core) * half
    for start, source in ((mine, keep), (other, got)):
        for i in range(half):
            grad_state[start + i] = source[0, i]
            grad_sink[start + i] = jnp.where(touching(labels[start + i]), source[1, i], 0.0)


def on_device(state, conduct, sink, labels, cotangent):
    count, ny, nz = state.shape
    half, wide, rows = count // 2, 2 * nz, ny + TILE
    count_x, count_y = lax.axis_size("gx"), lax.axis_size("gy")
    assert lax.axis_size("gz") == 2 and half >= 3 and ny % TILE == 0 and ny >= 3 * TILE
    two = count_y == 2
    ahead = [(i, (i + 1) % count_x) for i in range(count_x)]
    behind = [(b, a) for a, b in ahead]
    chips = [(2 * i + 1, (2 * i + 2) % (2 * count_x)) for i in range(count_x)]
    chips = chips + [(b, a) for a, b in chips]

    def swap_cores(x):
        return lax.ppermute(x, "gz", [(0, 1), (1, 0)])

    def swap_chips(x):
        return lax.ppermute(x, ("gx", "gz"), chips)

    def along_y(rims):
        forward = [(i, (i + 1) % count_y) for i in range(count_y)]
        backward = [(b, a) for a, b in forward]
        routes = [forward] if two else [backward, forward]
        return [lax.ppermute(rim, "gy", routes[i % len(routes)]) for i, rim in enumerate(rims)]

    ways = 1 if two else 2
    inputs = (state, conduct, sink, labels, cotangent)
    plane, span = (4, ny, nz), (5, half + 2, ny, nz)
    kinds = pltpu.VMEM((half + 2, ny, nz), jnp.int32)
    drains = pltpu.VMEM((half + 2, ny, nz), jnp.float32)
    sems = lambda many: pltpu.SemaphoreType.DMA((many,))
    up, down, trade = call(
        pack_inputs, [plane, plane, span], *inputs, given=HBM,
        scratch=[kinds, drains, pltpu.VMEM((2, ny, nz), jnp.int32), sems(5), sems(8)],
    )
    up = lax.ppermute(up, "gx", ahead)
    down = lax.ppermute(down, "gx", behind)
    traded = swap_cores(trade)
    (mine,) = call(own_planes, [span], *inputs, given=HBM, scratch=[kinds, drains, sems(5)])
    block, near = call(gather_planes, [(5, half, ny, wide), (7, ny, wide)], mine, traded)
    per = -(-((5 * half + 8) // 2) // PIECES)
    rims = call(functools.partial(pack_along_y, two), [(per, TILE, wide)] * (ways * PIECES), block, near)
    rims = along_y(rims)
    split = lambda r: [(half - 1, r, wide)] + [(half, r, wide)] * 5 + [(r, wide)]
    mids = call(functools.partial(prepare_mid, count_y), split(ny - 2 * TILE), block, near)
    ghost, near_ghost, *edges = call(
        functools.partial(prepare_rim, two, count_y),
        [(5, half, TILE, wide), (7, TILE, wide)] + split(3 * TILE), block, near, *rims,
    )
    (off,) = call(functools.partial(pack_off, two), [(rows + (2 if two else 4) * TILE, wide)], ghost, mids[4], edges[4])
    passed = call(choose_half, [(ny, nz)] * 4, up, down, *rims)
    passed = [swap_cores(x) for x in passed]
    off = swap_chips(off)
    own, outer = (half, rows, wide), (2, rows, wide)
    side, edge, add, first, known, linear, adjoint, sa, b2, hot2, inward = call(
        functools.partial(middle, two),
        [(4, 2, rows, wide), outer, outer, own, outer, outer, own, own, own, own, outer],
        block, ghost, near, near_ghost, up, down, *passed, off, *mids, *edges,
    )
    ends = (rows + ny, wide)
    hot2_out, sa_out, b2_out, fa_out, off2, on2 = call(
        outward, [outer] * 4 + [ends] * 2,
        block, ghost, mids[6], edges[6], side, edge, add, known, linear, adjoint, inward, off,
        mids[1], mids[2], edges[1], edges[2],
    )
    off2, on2 = swap_chips(off2), swap_cores(on2)
    main = lambda planes: (planes, ny, wide)
    value, term, adjoint0, hot0, _, _ = call(
        inner, [main(half), main(half), main(2), main(2), own, own],
        block, ghost, edge, side, first, adjoint, sa, b2, hot2, sa_out, b2_out, hot2_out, fa_out, *mids, *edges,
    )
    quarter = (2, half, ny, nz)
    keep, give, _ = call(
        finish, [quarter, quarter, outer],
        block, ghost, edge, side, b2_out, value, term, adjoint0, hot0, off2, on2, *mids[:3], *edges[:3],
    )
    got = swap_cores(give)
    grad_state, grad_sink = call(assemble, [state.shape, state.shape], labels, keep, got, keep=False)
    return (grad_state, grad_sink)


def solution(mesh):
    block = P(("groups", "gx"), "gy", "gz")
    in_specs = (block, P("gx", "gy", "gz"), block, block, block)
    return jax.shard_map(on_device, mesh=mesh, in_specs=in_specs, out_specs=(block, block), check_vma=False)
```

time: 157 us -> 40.8 us (0.26)
  other arithmetic: 40.9 us -> 0 us
  starting transfers between devices: 49.8 us -> 10.5 us
  local copies, waits for them, and re-layouts: 35.1 us -> 0.01 us
  Pallas kernels: 0 us -> 11.8 us
  waiting for transfers between devices: 28.3 us -> 17.6 us
    ppermute x30 -> x13, starting transfers between devices: 49.8 us -> 10.5 us  [the longest x1 2.64 us: on_device(): up = lax.ppermute(up, 'gx', ahead)]
    add_any x7 -> x0, other arithmetic: 15.2 us -> none  [the longest x3 6.77 us: diffuse(): window(padded, axis, offset) - centre]
    add x14 -> x0, other arithmetic: 11.8 us -> none  [the longest x3 3.79 us: transpose_rate(): inner = inner.at[:, :, -1].add(return_z(back[1:-1, 1:-1, 0], -1))]
    pallas_call x0 -> x13, Pallas kernels: none -> 11.8 us  [call(): pl.pallas_call(kernel, out_shape=[space(shape, jnp.float32) for shape in...]
    scatter-add x12 -> x0, local copies, waits for them, and re-layouts: 11.5 us -> none  [the longest x3 5.1 us: transpose_rate(): inner = inner.at[:, :, -1].add(return_z(back[1:-1, 1:-1, 0], -1))]
    ppermute x30 -> x13, waiting for transfers between devices: 28.3 us -> 17.6 us  [the longest x2 10.4 us: swap_chips(): return lax.ppermute(x, ('gx', 'gz'), chips)]
    slice x14 -> x0, local copies, waits for them, and re-layouts: 7.68 us -> none  [the longest x4 3.19 us: extended(): lax.slice_in_dim(block, block.shape[dim] - width, None, axis=dim)]
    another operation x6 -> x0, local copies, waits for them, and re-layouts: 6.41 us -> none
  transfers between devices with their start and end apart: 30 -> 13, of which waited for: 14 -> 10; matrix products, arithmetic and copies ran while one was open for 13% -> 0% of each run, Pallas kernels for 0% -> 15%
where the time goes in v2:
time: 40.8 us; the launch traced here: 40.6 us
  waiting for transfers between devices  17.6 us (43%)
  Pallas kernels  11.8 us (29%)
  starting transfers between devices  10.5 us (26%)
  between operations  0.72 us (2%)
    pallas_call x13, Pallas kernels, call(): pl.pallas_call(kernel, out_shape=[space(shape, jnp.float32) for shape in...  11.8 us
    ppermute x2, waiting for transfers between devices, swap_chips(): return lax.ppermute(x, ('gx', 'gz'), chips)  10.4 us
    ppermute x2, waiting for transfers between devices, along_y(): lax.ppermute(rim, 'gy', routes[i % len(routes)])  4.12 us
    ppermute x7, waiting for transfers between devices, swap_cores(): return lax.ppermute(x, 'gz', [(0, 1), (1, 0)])  2.81 us
    ppermute x1, starting transfers between devices, on_device(): up = lax.ppermute(up, 'gx', ahead)  2.64 us
    ppermute x1, starting transfers between devices, on_device(): down = lax.ppermute(down, 'gx', behind)  2.11 us
    ppermute x2, starting transfers between devices, swap_chips(): return lax.ppermute(x, ('gx', 'gz'), chips)  2.11 us
    ppermute x2, starting transfers between devices, along_y(): lax.ppermute(rim, 'gy', routes[i % len(routes)])  2.09 us
  transfers between devices with their start and end apart: 13, of which 10 were waited for; matrix products, arithmetic and copies ran while one was open for 0% of the time, Pallas kernels for 15%

profile of v2, /device:TPU:0, one launch (start us, length us, event | category | flops | bytes accessed | tf_op | source)
XLA Modules:
  0.0 40.6 jit_solution(13240918142184120219)
XLA Ops:
  0.6 1.9 %shard_map.69 = (f32[4,64,256]{2,1,0:T(8,128)S(1)}, f32[4,64,256]{2,1,0:T(8,128)S(1)}, f32[5,6,64,256]{3,2,1,0:T(8,128)S(1)}) custom-call(f32[8,64,256]{2,1,0:T(8,128)} %state.3, f32[8,64,256]{2,1,0:T(8,128)} %conduct.3, f32[8,64,256]{2,1,0:T(8,128)} %sink.3, s32[8,64,256]{2,1,0:T(8,128)} %labels.5, f32[8,64,256]{2,1,0:T(8,128)} %cotangent.3), custom_call_target="tpu_custom_call" | custom-call | flops 1024 | bytes 1024 | tf_op jit(solution)/shard_map/pallas_call | solution.py:23
  2.6 0.5 %collective-permute-start = (f32[5,6,64,256]{3,2,1,0:T(8,128)S(1)}, f32[5,6,64,256]{3,2,1,0:T(8,128)S(1)}, u32[]{:S(2)}, u32[]{:S(2)}) collective-permute-start(f32[5,6,64,256]{3,2,1,0:T(8,128)S(1)} %get-tuple-element.52), channel_id=1, source_target_pairs={{0,1},{1,0},{2,3},{3,2},{4,5},{5,4},{6,7},{7,6},{8,9},{9,8},{10,11... | collective-permute-start | bytes 5898248 | tf_op jit(solution)/shard_map/ppermute | solution.py:619
  3.1 2.6 %collective-permute-start.3 = (f32[4,64,256]{2,1,0:T(8,128)S(1)}, f32[4,64,256]{2,1,0:T(8,128)S(1)}, u32[]{:S(2)}, u32[]{:S(2)}) collective-permute-start(f32[4,64,256]{2,1,0:T(8,128)S(1)} %get-tuple-element.59), channel_id=1, source_target_pairs={{0,4},{4,8},{8,12},{12,0},{1,5},{5,9},{9,13},{13,1},{2,6},{6,10},{... | collective-permute-start | bytes 786440 | tf_op jit(solution)/shard_map/ppermute | solution.py:640
  5.7 2.1 %collective-permute-start.4 = (f32[4,64,256]{2,1,0:T(8,128)S(1)}, f32[4,64,256]{2,1,0:T(8,128)S(1)}, u32[]{:S(2)}, u32[]{:S(2)}) collective-permute-start(f32[4,64,256]{2,1,0:T(8,128)S(1)} %get-tuple-element.60), channel_id=1, source_target_pairs={{4,0},{8,4},{12,8},{0,12},{5,1},{9,5},{13,9},{1,13},{6,2},{10,6},{... | collective-permute-start | bytes 786440 | tf_op jit(solution)/shard_map/ppermute | solution.py:641
  7.8 1.6 %shard_map.68.mine = f32[5,6,64,256]{3,2,1,0:T(8,128)S(1)} custom-call(f32[8,64,256]{2,1,0:T(8,128)} %state.3, f32[8,64,256]{2,1,0:T(8,128)} %conduct.3, f32[8,64,256]{2,1,0:T(8,128)} %sink.3, s32[8,64,256]{2,1,0:T(8,128)} %labels.5, f32[8,64,256]{2,1,0:T(8,128)} %cotangent.3), custom_call_target="tpu_custom_call" | custom-call | flops 1024 | bytes 1024 | tf_op jit(solution)/shard_map/pallas_call | solution.py:23
  9.4 0.0 collective-permute-done.traded
  9.4 0.3 shard_map.70
  9.7 1.7 %collective-permute-start.1 = (f32[7,8,512]{2,1,0:T(8,128)S(1)}, f32[7,8,512]{2,1,0:T(8,128)S(1)}, u32[]{:S(2)}, u32[]{:S(2)}) collective-permute-start(f32[7,8,512]{2,1,0:T(8,128)S(1)} %get-tuple-element.55), channel_id=1, source_target_pairs={{0,2},{2,0},{1,3},{3,1},{4,6},{6,4},{5,7},{7,5},{8,10},{10,8},{9,1... | collective-permute-start | bytes 344072 | tf_op jit(solution)/shard_map/ppermute | solution.py:628
  11.4 0.4 collective-permute-start.2
  11.8 1.4 %shard_map.74 = (f32[3,48,512]{2,1,0:T(8,128)S(1)}, f32[4,48,512]{2,1,0:T(8,128)S(1)}, f32[4,48,512]{2,1,0:T(8,128)S(1)}, f32[4,48,512]{2,1,0:T(8,128)S(1)}, f32...) custom-call(f32[5,4,64,512]{3,2,1,0:T(8,128)S(1)} %get-tuple-element.53.block, ...), custom_call_target="tpu_custom_call" | custom-call | flops 1024 | bytes 1024 | tf_op jit(solution)/shard_map/pallas_call | solution.py:23
  13.3 2.5 %collective-permute-done.1.refs_0_ = f32[7,8,512]{2,1,0:T(8,128)S(1)} collective-permute-done((f32[7,8,512]{2,1,0:T(8,128)S(1)}, f32[7,8,512]{2,1,0:T(8,128)S(1)}, u32[]{:S(2)}, u32[]{:S(2)}) %collective-permute-start.1) | collective-permute-done | bytes 114720 | tf_op jit(solution)/shard_map/ppermute | solution.py:628
  15.8 1.6 %collective-permute-done.2.refs_1_ = f32[7,8,512]{2,1,0:T(8,128)S(1)} collective-permute-done((f32[7,8,512]{2,1,0:T(8,128)S(1)}, f32[7,8,512]{2,1,0:T(8,128)S(1)}, u32[]{:S(2)}, u32[]{:S(2)}) %collective-permute-start.2) | collective-permute-done | bytes 114720 | tf_op jit(solution)/shard_map/ppermute | solution.py:628
  17.4 0.8 %shard_map.72 = (f32[5,4,8,512]{3,2,1,0:T(8,128)S(1)}, f32[7,8,512]{2,1,0:T(8,128)S(1)}, f32[3,24,512]{2,1,0:T(8,128)S(1)}, f32[4,24,512]{2,1,0:T(8,128)S(1)}, f...) custom-call(f32[5,4,64,512]{3,2,1,0:T(8,128)S(1)} %get-tuple-element, ...), custom_call_target="tpu_custom_call" | custom-call | flops 1024 | bytes 1024 | tf_op jit(solution)/shard_map/pallas_call | solution.py:23
  18.2 1.2 %collective-permute-start.9 = (f32[88,512]{1,0:T(8,128)S(1)}, f32[88,512]{1,0:T(8,128)S(1)}, u32[]{:S(2)}, u32[]{:S(2)}) collective-permute-start(f32[88,512]{1,0:T(8,128)S(1)} %shard_map.75), channel_id=1, source_target_pairs={{1,4},{5,8},{9,12},{13,0},{4,1},{8,5},{12,9},{0,13},{3,6},{7,10},{... | collective-permute-start | bytes 540680 | tf_op jit(solution)/shard_map/ppermute | solution.py:622
  19.5 0.0 collective-permute-done.3.up
  19.5 0.2 collective-permute-done.4.down
  19.7 0.1 collective-permute-start.5
  19.8 0.5 %collective-permute-start.6 = (f32[64,256]{1,0:T(8,128)S(1)}, f32[64,256]{1,0:T(8,128)S(1)}, u32[]{:S(2)}, u32[]{:S(2)}) collective-permute-start(f32[64,256]{1,0:T(8,128)S(1)} %get-tuple-element.62), channel_id=1, source_target_pairs={{0,1},{1,0},{2,3},{3,2},{4,5},{5,4},{6,7},{7,6},{8,9},{9,8},{10,11... | collective-permute-start | bytes 196616 | tf_op jit(solution)/shard_map/ppermute | solution.py:619
  20.3 0.1 collective-permute-start.7
  20.4 0.4 %collective-permute-start.8 = (f32[64,256]{1,0:T(8,128)S(1)}, f32[64,256]{1,0:T(8,128)S(1)}, u32[]{:S(2)}, u32[]{:S(2)}) collective-permute-start(f32[64,256]{1,0:T(8,128)S(1)} %get-tuple-element.64), channel_id=1, source_target_pairs={{0,1},{1,0},{2,3},{3,2},{4,5},{5,4},{6,7},{7,6},{8,9},{9,8},{10,11... | collective-permute-start | bytes 196616 | tf_op jit(solution)/shard_map/ppermute | solution.py:619
  20.8 0.2 collective-permute-done.5.refs_0_
  21.1 0.2 collective-permute-done.6.refs_1_
  21.2 0.4 collective-permute-done.7.refs_2_
  21.6 0.2 collective-permute-done.8.refs_3_
  21.7 4.2 %collective-permute-done.9.refs_4_.off = f32[88,512]{1,0:T(8,128)S(1)} collective-permute-done((f32[88,512]{1,0:T(8,128)S(1)}, f32[88,512]{1,0:T(8,128)S(1)}, u32[]{:S(2)}, u32[]{:S(2)}) %collective-permute-start.9) | collective-permute-done | bytes 180256 | tf_op jit(solution)/shard_map/ppermute | solution.py:622
  26.0 1.1 %shard_map.76 = (f32[4,2,72,512]{3,2,1,0:T(8,128)S(1)}, f32[2,72,512]{2,1,0:T(8,128)S(1)}, f32[2,72,512]{2,1,0:T(8,128)S(1)}, f32[4,72,512]{2,1,0:T(8,128)S(1)},...) custom-call(f32[5,4,64,512]{3,2,1,0:T(8,128)S(1)} %get-tuple-element, ...), custom_call_target="tpu_custom_call" | custom-call | flops 1024 | bytes 1024 | tf_op jit(solution)/shard_map/pallas_call | solution.py:23
  27.1 0.5 %shard_map.77 = (f32[2,72,512]{2,1,0:T(8,128)S(1)}, f32[2,72,512]{2,1,0:T(8,128)S(1)}, f32[2,72,512]{2,1,0:T(8,128)S(1)}, f32[2,72,512]{2,1,0:T(8,128)S(1)}, f32...) custom-call(f32[5,4,64,512]{3,2,1,0:T(8,128)S(1)} %get-tuple-element.53.block, f32[5,4,8,512]{3,2,1,0:T(8,128)S(1)} %get-tuple-element.57.ghost, ...), custom_call_target="tpu_custom_call" | custom-call | flops 1024 | bytes 1024 | tf_op jit(solution)/shard_map/pallas_call | solution.py:23
  27.5 0.9 %collective-permute-start.10 = (f32[136,512]{1,0:T(8,128)S(1)}, f32[136,512]{1,0:T(8,128)S(1)}, u32[]{:S(2)}, u32[]{:S(2)}) collective-permute-start(f32[136,512]{1,0:T(8,128)S(1)} %get-tuple-element.98), channel_id=1, source_target_pairs={{1,4},{5,8},{9,12},{13,0},{4,1},{8,5},{12,9},{0,13},{3,6},{7,10},{... | collective-permute-start | bytes 835592 | tf_op jit(solution)/shard_map/ppermute | solution.py:622
  28.4 0.0 collective-permute-start.11
  28.4 2.0 %shard_map.78 = (f32[4,64,512]{2,1,0:T(8,128)S(1)}, f32[4,64,512]{2,1,0:T(8,128)S(1)}, f32[2,64,512]{2,1,0:T(8,128)S(1)}, f32[2,64,512]{2,1,0:T(8,128)S(1)}, f32...) custom-call(f32[5,4,64,512]{3,2,1,0:T(8,128)S(1)} %get-tuple-element.53.block, f32[5,4,8,512]{3,2,1,0:T(8,128)S(1)} %get-tuple-element.57.ghost, ...), custom_call_target="tpu_custom_call" | custom-call | flops 1024 | bytes 1024 | tf_op jit(solution)/shard_map/pallas_call | solution.py:23
  30.4 6.2 %collective-permute-done.10.off2 = f32[136,512]{1,0:T(8,128)S(1)} collective-permute-done((f32[136,512]{1,0:T(8,128)S(1)}, f32[136,512]{1,0:T(8,128)S(1)}, u32[]{:S(2)}, u32[]{:S(2)}) %collective-permute-start.10) | collective-permute-done | bytes 278560 | tf_op jit(solution)/shard_map/ppermute | solution.py:622
  36.6 0.0 collective-permute-done.11.on2
  36.6 0.0 copy-start
  36.6 1.0 %shard_map.79 = (f32[2,4,64,256]{3,2,1,0:T(8,128)S(1)}, f32[2,4,64,256]{3,2,1,0:T(8,128)S(1)}, f32[2,72,512]{2,1,0:T(8,128)}) custom-call(f32[5,4,64,512]{3,2,1,0:T(8,128)S(1)} %get-tuple-element.53.block, f32[5,4,8,512]{3,2,1,0:T(8,128)S(1)} %get-tuple-element.57.ghost, f32[2,72,512]{2,1,0:T(8,128)S(1)} %get-tuple-element.79.edge, ...), custom_call_target="tpu_custom_call" | custom-call | flops 1024 | bytes 1024 | tf_op jit(solution)/shard_map/pallas_call | solution.py:23
  37.6 0.0 collective-permute-start.12
  37.6 1.9 %collective-permute-done.12.got = f32[2,4,64,256]{3,2,1,0:T(8,128)S(1)} collective-permute-done((f32[2,4,64,256]{3,2,1,0:T(8,128)S(1)}, f32[2,4,64,256]{3,2,1,0:T(8,128)S(1)}, u32[]{:S(2)}, u32[]{:S(2)}) %collective-permute-start.12) | collective-permute-done | bytes 524320 | tf_op jit(solution)/shard_map/ppermute | solution.py:619
  39.5 0.0 copy-done
  39.5 1.1 %shard_map.80 = (f32[8,64,256]{2,1,0:T(8,128)}, f32[8,64,256]{2,1,0:T(8,128)}) custom-call(s32[8,64,256]{2,1,0:T(8,128)S(1)} %copy-done, f32[2,4,64,256]{3,2,1,0:T(8,128)S(1)} %get-tuple-element.100.keep, f32[2,4,64,256]{3,2,1,0:T(8,128)S(1)} %collective-permute-done.12.got), custom_call_target="tpu_custom_call" | custom-call | flops 1024 | bytes 1024 | tf_op jit(solution)/shard_map/pallas_call | solution.py:23
  (3 shorter events, 0.1 us)
Async XLA Ops:
  2.6 6.9 %collective-permute-start = (f32[5,6,64,256]{3,2,1,0:T(8,128)S(1)}, f32[5,6,64,256]{3,2,1,0:T(8,128)S(1)}, u32[]{:S(2)}, u32[]{:S(2)}) collective-permute-start(f32[5,6,64,256]{3,2,1,0:T(8,128)S(1)} %get-tuple-element.52), channel_id=1, source_target_pairs={{0,1},{1,0},{2,3},{3,2},{4,5},{5,4},{6,7},{7,6},{8,9},{9,8},{10,11... | collective-permute-start | bytes 5898248 | tf_op jit(solution)/shard_map/ppermute | solution.py:619
  3.1 16.4 %collective-permute-start.3 = (f32[4,64,256]{2,1,0:T(8,128)S(1)}, f32[4,64,256]{2,1,0:T(8,128)S(1)}, u32[]{:S(2)}, u32[]{:S(2)}) collective-permute-start(f32[4,64,256]{2,1,0:T(8,128)S(1)} %get-tuple-element.59), channel_id=1, source_target_pairs={{0,4},{4,8},{8,12},{12,0},{1,5},{5,9},{9,13},{13,1},{2,6},{6,10},{... | collective-permute-start | bytes 786440 | tf_op jit(solution)/shard_map/ppermute | solution.py:640
  5.7 14.0 %collective-permute-start.4 = (f32[4,64,256]{2,1,0:T(8,128)S(1)}, f32[4,64,256]{2,1,0:T(8,128)S(1)}, u32[]{:S(2)}, u32[]{:S(2)}) collective-permute-start(f32[4,64,256]{2,1,0:T(8,128)S(1)} %get-tuple-element.60), channel_id=1, source_target_pairs={{4,0},{8,4},{12,8},{0,12},{5,1},{9,5},{13,9},{1,13},{6,2},{10,6},{... | collective-permute-start | bytes 786440 | tf_op jit(solution)/shard_map/ppermute | solution.py:641
  9.7 6.1 %collective-permute-start.1 = (f32[7,8,512]{2,1,0:T(8,128)S(1)}, f32[7,8,512]{2,1,0:T(8,128)S(1)}, u32[]{:S(2)}, u32[]{:S(2)}) collective-permute-start(f32[7,8,512]{2,1,0:T(8,128)S(1)} %get-tuple-element.55), channel_id=1, source_target_pairs={{0,2},{2,0},{1,3},{3,1},{4,6},{6,4},{5,7},{7,5},{8,10},{10,8},{9,1... | collective-permute-start | bytes 344072 | tf_op jit(solution)/shard_map/ppermute | solution.py:628
  11.4 6.0 %collective-permute-start.2 = (f32[7,8,512]{2,1,0:T(8,128)S(1)}, f32[7,8,512]{2,1,0:T(8,128)S(1)}, u32[]{:S(2)}, u32[]{:S(2)}) collective-permute-start(f32[7,8,512]{2,1,0:T(8,128)S(1)} %get-tuple-element.56), channel_id=1, source_target_pairs={{0,2},{2,0},{1,3},{3,1},{4,6},{6,4},{5,7},{7,5},{8,10},{10,8},{9,1... | collective-permute-start | bytes 344072 | tf_op jit(solution)/shard_map/ppermute | solution.py:628
  18.2 7.7 %collective-permute-start.9 = (f32[88,512]{1,0:T(8,128)S(1)}, f32[88,512]{1,0:T(8,128)S(1)}, u32[]{:S(2)}, u32[]{:S(2)}) collective-permute-start(f32[88,512]{1,0:T(8,128)S(1)} %shard_map.75), channel_id=1, source_target_pairs={{1,4},{5,8},{9,12},{13,0},{4,1},{8,5},{12,9},{0,13},{3,6},{7,10},{... | collective-permute-start | bytes 540680 | tf_op jit(solution)/shard_map/ppermute | solution.py:622
  19.7 1.3 %collective-permute-start.5 = (f32[64,256]{1,0:T(8,128)S(1)}, f32[64,256]{1,0:T(8,128)S(1)}, u32[]{:S(2)}, u32[]{:S(2)}) collective-permute-start(f32[64,256]{1,0:T(8,128)S(1)} %get-tuple-element.61), channel_id=1, source_target_pairs={{0,1},{1,0},{2,3},{3,2},{4,5},{5,4},{6,7},{7,6},{8,9},{9,8},{10,11... | collective-permute-start | bytes 196616 | tf_op jit(solution)/shard_map/ppermute | solution.py:619
  19.8 1.4 %collective-permute-start.6 = (f32[64,256]{1,0:T(8,128)S(1)}, f32[64,256]{1,0:T(8,128)S(1)}, u32[]{:S(2)}, u32[]{:S(2)}) collective-permute-start(f32[64,256]{1,0:T(8,128)S(1)} %get-tuple-element.62), channel_id=1, source_target_pairs={{0,1},{1,0},{2,3},{3,2},{4,5},{5,4},{6,7},{7,6},{8,9},{9,8},{10,11... | collective-permute-start | bytes 196616 | tf_op jit(solution)/shard_map/ppermute | solution.py:619
  20.3 1.3 %collective-permute-start.7 = (f32[64,256]{1,0:T(8,128)S(1)}, f32[64,256]{1,0:T(8,128)S(1)}, u32[]{:S(2)}, u32[]{:S(2)}) collective-permute-start(f32[64,256]{1,0:T(8,128)S(1)} %get-tuple-element.63), channel_id=1, source_target_pairs={{0,1},{1,0},{2,3},{3,2},{4,5},{5,4},{6,7},{7,6},{8,9},{9,8},{10,11... | collective-permute-start | bytes 196616 | tf_op jit(solution)/shard_map/ppermute | solution.py:619
  20.4 1.3 %collective-permute-start.8 = (f32[64,256]{1,0:T(8,128)S(1)}, f32[64,256]{1,0:T(8,128)S(1)}, u32[]{:S(2)}, u32[]{:S(2)}) collective-permute-start(f32[64,256]{1,0:T(8,128)S(1)} %get-tuple-element.64), channel_id=1, source_target_pairs={{0,1},{1,0},{2,3},{3,2},{4,5},{5,4},{6,7},{7,6},{8,9},{9,8},{10,11... | collective-permute-start | bytes 196616 | tf_op jit(solution)/shard_map/ppermute | solution.py:619
  27.5 9.0 %collective-permute-start.10 = (f32[136,512]{1,0:T(8,128)S(1)}, f32[136,512]{1,0:T(8,128)S(1)}, u32[]{:S(2)}, u32[]{:S(2)}) collective-permute-start(f32[136,512]{1,0:T(8,128)S(1)} %get-tuple-element.98), channel_id=1, source_target_pairs={{1,4},{5,8},{9,12},{13,0},{4,1},{8,5},{12,9},{0,13},{3,6},{7,10},{... | collective-permute-start | bytes 835592 | tf_op jit(solution)/shard_map/ppermute | solution.py:622
  28.4 8.1 %collective-permute-start.11 = (f32[136,512]{1,0:T(8,128)S(1)}, f32[136,512]{1,0:T(8,128)S(1)}, u32[]{:S(2)}, u32[]{:S(2)}) collective-permute-start(f32[136,512]{1,0:T(8,128)S(1)} %get-tuple-element.99), channel_id=1, source_target_pairs={{0,1},{1,0},{2,3},{3,2},{4,5},{5,4},{6,7},{7,6},{8,9},{9,8},{10,11... | collective-permute-start | bytes 835592 | tf_op jit(solution)/shard_map/ppermute | solution.py:619
  36.6 3.0 %copy-start = (s32[8,64,256]{2,1,0:T(8,128)S(1)}, s32[8,64,256]{2,1,0:T(8,128)}, u32[]{:S(2)}) copy-start(s32[8,64,256]{2,1,0:T(8,128)} %labels.5) | copy-start | bytes 1572868
  37.6 1.9 %collective-permute-start.12 = (f32[2,4,64,256]{3,2,1,0:T(8,128)S(1)}, f32[2,4,64,256]{3,2,1,0:T(8,128)S(1)}, u32[]{:S(2)}, u32[]{:S(2)}) collective-permute-start(f32[2,4,64,256]{3,2,1,0:T(8,128)S(1)} %get-tuple-element.101), channel_id=1, source_target_pairs={{0,1},{1,0},{2,3},{3,2},{4,5},{5,4},{6,7},{7,6},{8,9},{9,8},{10,11... | collective-permute-start | bytes 1572872 | tf_op jit(solution)/shard_map/ppermute | solution.py:619

commit v3 on v2

--- a/solution.py
+++ b/solution.py
@@ -13,7 +13,7 @@
 scale = 0.5 * time_step
 HALO = 4
 TILE = 8
-PIECES = 2
+RETURNS = 3
 S, C, T, F, K = range(5)
 
 
@@ -182,22 +182,18 @@
         upper = rows_of(low_even) < HALO
         low = jnp.where(upper, low_even, pltpu.roll(low_odd, HALO, 0))
         high = jnp.where(upper, pltpu.roll(high_even, HALO, 0), high_odd)
-        per = outs[0].shape[0]
-        piece, slot = k // 2 // per, k // 2 % per
         if two:
-            outs[piece][slot] = jnp.where(lax.axis_index("gy") == 0, high, low)
+            outs[0][k // 2] = jnp.where(lax.axis_index("gy") == 0, high, low)
         else:
-            outs[2 * piece][slot] = low
-            outs[2 * piece + 1][slot] = high
+            outs[0][k // 2] = low
+            outs[1][k // 2] = high
 
 
 def unpack_rims(two, count_y, rims, planes):
     place = lax.axis_index("gy")
     for k in range(0, len(planes), 2):
-        per = rims[0].shape[0]
-        piece, slot = k // 2 // per, k // 2 % per
-        above = jnp.where(place < count_y - 1, rims[piece if two else 2 * piece][slot], 0.0)
-        below = jnp.where(place > 0, rims[piece if two else 2 * piece + 1][slot], 0.0)
+        above = jnp.where(place < count_y - 1, rims[0][k // 2], 0.0)
+        below = jnp.where(place > 0, rims[0 if two else 1][k // 2], 0.0)
         upper = rows_of(above) < HALO
         planes[k][...] = jnp.where(upper, above, pltpu.roll(below, HALO, 0))
         if k + 1 < len(planes):
@@ -224,11 +220,19 @@
 
 
 def rim_planes(block, near):
-    return [block.at[j, i] for j in range(5) for i in range(block.shape[1])] + [near.at[j] for j in range(7)]
+    half = block.shape[1]
+    core = lax.axis_index("gz")
+    inward = lambda i: core * (half - 1) + i * (1 - 2 * core)
+    early = [block.at[j, inward(0)] for j in range(5)] + [block.at[j, inward(1)] for j in (S, C)]
+    late = [block.at[j, inward(1)] for j in (T, F, K)] + [block.at[j, inward(i)] for i in range(2, half) for j in range(5)]
+    return early, late + [near.at[j] for j in range(7)]
 
 
 def pack_along_y(two, block, near, *rims):
-    pack_rims(two, rim_planes(block, near), rims)
+    early, late = rim_planes(block, near)
+    ways = 1 if two else 2
+    pack_rims(two, early, rims[:ways])
+    pack_rims(two, late, rims[ways:])
 
 
 class Lazy:
@@ -335,9 +339,12 @@
 
 
 def prepare_rim(two, count_y, block, near, *refs):
-    rims, (ghost, near_ghost, *outs) = refs[: PIECES * (1 if two else 2)], refs[PIECES * (1 if two else 2) :]
+    ways = 1 if two else 2
+    rims, (ghost, near_ghost, *outs) = refs[: 2 * ways], refs[2 * ways :]
     count = block.shape[2] // TILE
-    unpack_rims(two, count_y, rims, rim_planes(ghost, near_ghost))
+    early, late = rim_planes(ghost, near_ghost)
+    unpack_rims(two, count_y, rims[:ways], early)
+    unpack_rims(two, count_y, rims[ways:], late)
     prepare([0, count - 1, count], count_y, block, near, ghost, near_ghost, *outs)
 
 
@@ -356,19 +363,49 @@
     return jnp.where(valid, a, 0.0), jnp.where(valid, b, 0.0)
 
 
-def pack_off(two, ghost, part_mid, part_rim, off):
+def pack_off(two, count_y, block, part_mid, *refs):
+    ways = 1 if two else 2
+    rims, (off, ghost) = refs[:ways], refs[ways:]
     place = lax.axis_index("gy")
-    outer = lax.axis_index("gz") * (ghost.shape[1] - 1)
-    part = mid_and_rim(part_mid.at[outer], part_rim.at[outer])
-    for t in range(len(part)):
-        off[at(t)] = part[t]
+    core = lax.axis_index("gz")
+    last = block.shape[1] - 1
+    outer = core * last
+    inside = outer + 1 - 2 * core
+    unpack_rims(two, count_y, rims, [ghost.at[j] for j in range(7)])
+    s, c, f, k = (with_ghost(block.at[j, outer], ghost.at[j]) for j in (S, C, F, K))
+    s_in, c_in = (with_ghost(block.at[j, inside], ghost.at[5 + j]) for j in (S, C))
+    count = len(s)
+
+    def face_along_y(t):
+        value = (c[t] + down_rows(c[t - 1], c[t])) * scale
+        if t == 0:
+            value = jnp.where(jnp.logical_and(rows_of(value) == 0, place == 0), 0.0, value)
+        if t == count - 1:
+            value = jnp.where(jnp.logical_and(rows_of(value) == 0, place == count_y - 1), 0.0, value)
+        return value
+
+    todo, kz, weight = (0, count - 2, count - 1), {}, {}
+    for t in todo:
+        here = c[t] * scale
+        left, right = sides_along_z(c[t], here)
+        kz[t] = jnp.where(lanes_of(left) == 0, 0.0, left)
+        low, high = down_rows(c[t - 1], c[t]), up_rows(c[t], c[t + 1])
+        weight[t] = (2.0 * here + (low + high) * scale) + (left + right) + time_step * f[t]
+    flow = Across(Lazy(count, face_along_y), kz, s)
+    for t in range(count):
+        if t in todo:
+            face = (c[t] + c_in[t]) * scale
+            go = flow[t] - (weight[t] + face) * s[t] - time_step * k[t] * jnp.tanh(s[t])
+            go = go + (face + jnp.where(core == 0, 0.0, time_step) * f[t]) * s_in[t]
+            off[at(t)] = s[t] + (0.5 + f[t]) * go
+        else:
+            off[at(t)] = part_mid[outer, at(t - 1)]
     for j in range(0, 4, 2):
-        a, b = ghost[j, outer], ghost[j + 1, outer]
         if two:
-            off[at(len(part) + j // 2)] = pack_pair(place, a, b)
+            off[at(count + j // 2)] = pack_pair(place, ghost[j], ghost[j + 1])
         else:
-            off[at(len(part) + j)] = a
-            off[at(len(part) + j + 1)] = b
+            off[at(count + j)] = ghost[j]
+            off[at(count + j + 1)] = ghost[j + 1]
 
 
 def choose_half(up, down, *refs):
@@ -462,8 +499,7 @@
         inward[1, at(t)] = kx(last - 1)[t] * b2[last - 1, at(t)]
 
 
-def outward(block, ghost, one_mid, one_rim, side, edge, add, known, linear, adjoint, inward, off, *refs):
-    ky_mid, kz_mid, ky_rim, kz_rim, hot2, sa, b2, fa, off2, on2 = refs
+def outward(block, ghost, one_mid, one_rim, edge, add, known, linear, off, hot2, sa, b2, off_b, on_b):
     core = lax.axis_index("gz")
     half, ny = block.shape[1], block.shape[2]
     count, last = ny // TILE, half - 1
@@ -482,14 +518,21 @@
             hot2[which, at(t)] = hot
             sa[which, at(t)] = total
             b2[which, at(t)] = total * rc
+    off_b[...] = b2[core]
+    on_b[...] = b2[1 - core]
+
+
+def outward_first(ky_mid, kz_mid, ky_rim, kz_rim, adjoint, inward, sa, b2, fa, off_p, on_p):
+    core = lax.axis_index("gz")
+    half, ny = adjoint.shape[0], off_p.shape[0]
+    for which, i in ((0, 0), (1, half - 1)):
         b = whole(b2.at[which])
         flow = Across(mid_and_rim(ky_mid.at[i], ky_rim.at[i]), mid_and_rim(kz_mid.at[i], kz_rim.at[i]), b)
-        for t in range(count + 1):
+        for t in range(len(b)):
             total = sa[which, at(t)] + flow[t] - adjoint[i, at(t)] * b[t] + inward[which, at(t)]
             fa[which, at(t)] = 0.25 * total
-    for out, which in ((off2, core), (on2, 1 - core)):
-        out[0 : ny + TILE] = b2[which]
-        out[ny + TILE : 2 * ny + TILE] = fa[which, 0:ny]
+    off_p[...] = fa[core, 0:ny]
+    on_p[...] = fa[1 - core, 0:ny]
 
 
 def inner(block, ghost, edge, side, first, adjoint, sa_in, b2_in, hot2_in, sa_out, b2_out, hot2_out, fa_out, *refs):
@@ -541,10 +584,28 @@
                 hot0[which, at(t)] = -time_step * (0.5 + f[t]) * hot
 
 
-def finish(block, ghost, edge, side, b2_out, value, term, adjoint0, hot0, off2, on2, *refs):
-    kx_mid, ky_mid, kz_mid, kx_rim, ky_rim, kz_rim, keep, give, late = refs
-    core = lax.axis_index("gz")
-    half, ny, narrow = block.shape[1], block.shape[2], keep.shape[3]
+class Pieces:
+    def __init__(self, refs):
+        self.refs, self.size = refs, refs[0].shape[0]
+
+    def __getitem__(self, place):
+        return self.refs[place // self.size][place % self.size]
+
+    def __setitem__(self, place, value):
+        self.refs[place[0] // self.size][place[0] % self.size, place[1]] = value
+
+
+def halves(core, value):
+    narrow = value.shape[1] // 2
+    left, right = value[:, :narrow], value[:, narrow:]
+    return jnp.where(core == 0, left, right), jnp.where(core == 0, right, left)
+
+
+def finish(block, ghost, edge, side, b2_out, value, term, adjoint0, hot0, off_b, on_b, *refs):
+    kx_mid, ky_mid, kz_mid, kx_rim, ky_rim, kz_rim, keep, *pieces, rest, late = refs
+    give = Pieces(pieces)
+    core = lax.axis_index("gz")
+    half, ny = block.shape[1], block.shape[2]
     count, last = ny // TILE, half - 1
     own = lambda j, i: with_ghost(block.at[j, i], ghost.at[j, i])
     both = lambda mid, rim: lambda i: mid_and_rim(mid.at[i], rim.at[i])
@@ -557,51 +618,56 @@
             face = edge[which, at(t)]
             if which == 1:
                 face = face + time_step * side[F, 1, at(t)]
-            gain = 0.25 * face * jnp.where(mine, off2[at(t)], on2[at(t)])
+            gain = 0.25 * face * jnp.where(mine, off_b[at(t)], on_b[at(t)])
             late[which, at(t)] = gain * (0.5 + f[t])
             gains[which, t] = gain
-
-    def write(i, t, total, term):
-        for which, whole_row in ((0, total), (1, term)):
-            left, right = whole_row[:, :narrow], whole_row[:, narrow:]
-            keep[which, i, at(t)] = jnp.where(core == 0, left, right)
-            give[which, i, at(t)] = jnp.where(core == 0, right, left)
-
-    for i in range(half):
-        for which in range(2):
-            if i == which * last:
-                flow = Across(ky(i), kz(i), whole(late.at[which]))
+    for which, i in ((0, 0), (1, last)):
+        flow = Across(ky(i), kz(i), whole(late.at[which]))
         for t in range(count):
-            total, sink = value[i, at(t)], term[i, at(t)]
-            for which in range(2):
-                if i == which * last:
-                    mine = core == which
-                    slot = slice(ny + (t + 1) * TILE, ny + (t + 2) * TILE)
-                    beyond = jnp.where(mine, off2[slot], on2[slot])
-                    face, f_out = edge[which, at(t)], side[F, which, at(t)]
-                    into, out_of = face, face
-                    if which == 0:
-                        out_of = out_of + time_step * own(F, 0)[t]
-                    else:
-                        into = into + time_step * f_out
-                    beyond = (beyond + 0.25 * out_of * b2_out[which, at(t)]) * (0.5 + f_out)
-                    total = total + gains[which, t] + flow[t] - adjoint0[which, at(t)] * late[which, at(t)] + into * beyond
-                    sink = sink + hot0[which, at(t)] * gains[which, t]
+            face, f_out = edge[which, at(t)], side[F, which, at(t)]
+            into, out_of = face, face
+            if which == 0:
+                out_of = out_of + time_step * own(F, 0)[t]
+            else:
+                into = into + time_step * f_out
+            total = value[i, at(t)] + gains[which, t] + flow[t] - adjoint0[which, at(t)] * late[which, at(t)]
+            rest[which, at(t)] = total + into * (0.25 * out_of * b2_out[which, at(t)]) * (0.5 + f_out)
+            keep[i, at(t)], give[i, at(t)] = halves(core, term[i, at(t)] + hot0[which, at(t)] * gains[which, t])
+    for i in range(1, last):
+        for t in range(count):
+            total = value[i, at(t)]
             if i == 1:
                 total = total + kx(0)[t] * late[0, at(t)]
             if i == last - 1:
                 total = total + (kx(last - 1)[t] + time_step * own(F, last)[t]) * late[1, at(t)]
-            write(i, t, total, sink)
-
-
-def assemble(labels, keep, got, grad_state, grad_sink):
-    core = lax.axis_index("gz")
-    half = keep.shape[1]
-    mine, other = core * half, (1 - core) * half
-    for start, source in ((mine, keep), (other, got)):
+            keep[half + i - 1, at(t)], give[half + i - 1, at(t)] = halves(core, total)
+            keep[i, at(t)], give[i, at(t)] = halves(core, term[i, at(t)])
+
+
+def finish_outer(edge, side, rest, off_p, on_p, keep, give):
+    core = lax.axis_index("gz")
+    for which in range(2):
+        mine = core == which
+        for t in range(rest.shape[1] // TILE):
+            face, f_out = edge[which, at(t)], side[F, which, at(t)]
+            if which == 1:
+                face = face + time_step * f_out
+            total = rest[which, at(t)] + face * (0.5 + f_out) * jnp.where(mine, off_p[at(t)], on_p[at(t)])
+            keep[which, at(t)], give[which, at(t)] = halves(core, total)
+
+
+def assemble(labels, keep, keep_outer, got_outer, *refs):
+    *pieces, grad_state, grad_sink = refs
+    got = Pieces(pieces)
+    core = lax.axis_index("gz")
+    half = grad_state.shape[0] // 2
+    for start, source, outer in ((core * half, keep, keep_outer), ((1 - core) * half, got, got_outer)):
+        grad_state[start] = outer[0]
+        grad_state[start + half - 1] = outer[1]
+        for i in range(1, half - 1):
+            grad_state[start + i] = source[half + i - 1]
         for i in range(half):
-            grad_state[start + i] = source[0, i]
-            grad_sink[start + i] = jnp.where(touching(labels[start + i]), source[1, i], 0.0)
+            grad_sink[start + i] = jnp.where(touching(labels[start + i]), source[i], 0.0)
 
 
 def on_device(state, conduct, sink, labels, cotangent):
@@ -642,8 +708,8 @@
     traded = swap_cores(trade)
     (mine,) = call(own_planes, [span], *inputs, given=HBM, scratch=[kinds, drains, sems(5)])
     block, near = call(gather_planes, [(5, half, ny, wide), (7, ny, wide)], mine, traded)
-    per = -(-((5 * half + 8) // 2) // PIECES)
-    rims = call(functools.partial(pack_along_y, two), [(per, TILE, wide)] * (ways * PIECES), block, near)
+    sizes = [4, (5 * half + 1) // 2]
+    rims = call(functools.partial(pack_along_y, two), [(n, TILE, wide) for n in sizes for _ in range(ways)], block, near)
     rims = along_y(rims)
     split = lambda r: [(half - 1, r, wide)] + [(half, r, wide)] * 5 + [(r, wide)]
     mids = call(functools.partial(prepare_mid, count_y), split(ny - 2 * TILE), block, near)
@@ -651,7 +717,10 @@
         functools.partial(prepare_rim, two, count_y),
         [(5, half, TILE, wide), (7, TILE, wide)] + split(3 * TILE), block, near, *rims,
     )
-    (off,) = call(functools.partial(pack_off, two), [(rows + (2 if two else 4) * TILE, wide)], ghost, mids[4], edges[4])
+    off, _ = call(
+        functools.partial(pack_off, two, count_y), [(rows + (2 if two else 4) * TILE, wide), (7, TILE, wide)],
+        block, mids[4], *rims[:ways],
+    )
     passed = call(choose_half, [(ny, nz)] * 4, up, down, *rims)
     passed = [swap_cores(x) for x in passed]
     off = swap_chips(off)
@@ -661,25 +730,32 @@
         [(4, 2, rows, wide), outer, outer, own, outer, outer, own, own, own, own, outer],
         block, ghost, near, near_ghost, up, down, *passed, off, *mids, *edges,
     )
-    ends = (rows + ny, wide)
-    hot2_out, sa_out, b2_out, fa_out, off2, on2 = call(
-        outward, [outer] * 4 + [ends] * 2,
-        block, ghost, mids[6], edges[6], side, edge, add, known, linear, adjoint, inward, off,
-        mids[1], mids[2], edges[1], edges[2],
-    )
-    off2, on2 = swap_chips(off2), swap_cores(on2)
+    ends, mains = (rows, wide), (ny, wide)
+    hot2_out, sa_out, b2_out, off_b, on_b = call(
+        outward, [outer] * 3 + [ends] * 2, block, ghost, mids[6], edges[6], edge, add, known, linear, off
+    )
+    off_b, on_b = swap_chips(off_b), swap_cores(on_b)
+    fa_out, off_p, on_p = call(
+        outward_first, [outer] + [mains] * 2, mids[1], mids[2], edges[1], edges[2], adjoint, inward, sa_out, b2_out
+    )
+    off_p, on_p = swap_chips(off_p), swap_cores(on_p)
     main = lambda planes: (planes, ny, wide)
     value, term, adjoint0, hot0, _, _ = call(
         inner, [main(half), main(half), main(2), main(2), own, own],
         block, ghost, edge, side, first, adjoint, sa, b2, hot2, sa_out, b2_out, hot2_out, fa_out, *mids, *edges,
     )
-    quarter = (2, half, ny, nz)
-    keep, give, _ = call(
-        finish, [quarter, quarter, outer],
-        block, ghost, edge, side, b2_out, value, term, adjoint0, hot0, off2, on2, *mids[:3], *edges[:3],
-    )
-    got = swap_cores(give)
-    grad_state, grad_sink = call(assemble, [state.shape, state.shape], labels, keep, got, keep=False)
+    most = (2 * half - 2, ny, nz)
+    pieces = RETURNS if most[0] % RETURNS == 0 else 1
+    keep, *give, rest, _ = call(
+        finish, [most] + [(most[0] // pieces, ny, nz)] * pieces + [main(2), outer],
+        block, ghost, edge, side, b2_out, value, term, adjoint0, hot0, off_b, on_b, *mids[:3], *edges[:3],
+    )
+    got = [swap_cores(x) for x in give]
+    keep_outer, give_outer = call(finish_outer, [(2, ny, nz)] * 2, edge, side, rest, off_p, on_p)
+    got_outer = swap_cores(give_outer)
+    grad_state, grad_sink = call(
+        assemble, [state.shape, state.shape], labels, keep, keep_outer, got_outer, *got, keep=False
+    )
     return (grad_state, grad_sink)
 
 

time: 40.8 us -> 37.6 us (0.922)
  waiting for transfers between devices: 17.6 us -> 10.7 us
  starting transfers between devices: 10.5 us -> 13.4 us
  Pallas kernels: 11.8 us -> 12.5 us
    ppermute x2 -> x3, waiting for transfers between devices: 10.4 us -> 4.36 us  [swap_chips(): return lax.ppermute(x, ('gx', 'gz'), chips)]
    ppermute x1, waiting for transfers between devices: 0.24 us -> 3.77 us  [on_device(): down = lax.ppermute(down, 'gx', behind)]
    ppermute x2, waiting for transfers between devices: 4.12 us -> 1.18 us  [along_y(): lax.ppermute(rim, 'gy', routes[i % len(routes)])]
    ppermute x2 -> x3, starting transfers between devices: 2.11 us -> 4.38 us  [swap_chips(): return lax.ppermute(x, ('gx', 'gz'), chips)]
    ppermute x7 -> x11, waiting for transfers between devices: 2.81 us -> 1.4 us  [swap_cores(): return lax.ppermute(x, 'gz', [(0, 1), (1, 0)])]
    pallas_call x13 -> x15, Pallas kernels: 11.8 us -> 12.5 us  [call(): pl.pallas_call(kernel, out_shape=[space(shape, jnp.float32) for shape in...]
    ppermute x7 -> x11, starting transfers between devices: 1.6 us -> 2.23 us  [swap_cores(): return lax.ppermute(x, 'gz', [(0, 1), (1, 0)])]
  transfers between devices with their start and end apart: 13 -> 18, of which waited for: 10 -> 10; matrix products, arithmetic and copies ran while one was open for 0% -> 0% of each run, Pallas kernels for 15% -> 22%
where the time goes in v3:
time: 37.6 us; the launch traced here: 37.4 us
  starting transfers between devices  13.4 us (36%)
  Pallas kernels  12.5 us (33%)
  waiting for transfers between devices  10.7 us (28%)
  between operations  0.75 us (2%)
    pallas_call x15, Pallas kernels, call(): pl.pallas_call(kernel, out_shape=[space(shape, jnp.float32) for shape in...  12.5 us
    ppermute x3, starting transfers between devices, swap_chips(): return lax.ppermute(x, ('gx', 'gz'), chips)  4.38 us
    ppermute x3, waiting for transfers between devices, swap_chips(): return lax.ppermute(x, ('gx', 'gz'), chips)  4.36 us
    ppermute x1, waiting for transfers between devices, on_device(): down = lax.ppermute(down, 'gx', behind)  3.77 us
    ppermute x1, starting transfers between devices, on_device(): up = lax.ppermute(up, 'gx', ahead)  2.64 us
    ppermute x11, starting transfers between devices, swap_cores(): return lax.ppermute(x, 'gz', [(0, 1), (1, 0)])  2.23 us
    ppermute x1, starting transfers between devices, on_device(): down = lax.ppermute(down, 'gx', behind)  2.11 us
    ppermute x2, starting transfers between devices, along_y(): lax.ppermute(rim, 'gy', routes[i % len(routes)])  2.09 us
  transfers between devices with their start and end apart: 18, of which 10 were waited for; matrix products, arithmetic and copies ran while one was open for 0% of the time, Pallas kernels for 22%

profile of v3, /device:TPU:0, one launch (start us, length us, event | category | flops | bytes accessed | tf_op | source)
XLA Modules:
  0.0 37.4 jit_solution(15504121163549640184)
XLA Ops:
  0.6 1.9 %shard_map.69 = (f32[4,64,256]{2,1,0:T(8,128)S(1)}, f32[4,64,256]{2,1,0:T(8,128)S(1)}, f32[5,6,64,256]{3,2,1,0:T(8,128)S(1)}) custom-call(f32[8,64,256]{2,1,0:T(8,128)} %state.3, f32[8,64,256]{2,1,0:T(8,128)} %conduct.3, f32[8,64,256]{2,1,0:T(8,128)} %sink.3, s32[8,64,256]{2,1,0:T(8,128)} %labels.5, f32[8,64,256]{2,1,0:T(8,128)} %cotangent.3), custom_call_target="tpu_custom_call" | custom-call | flops 1024 | bytes 1024 | tf_op jit(solution)/shard_map/pallas_call | solution.py:23
  2.6 0.5 %collective-permute-start = (f32[5,6,64,256]{3,2,1,0:T(8,128)S(1)}, f32[5,6,64,256]{3,2,1,0:T(8,128)S(1)}, u32[]{:S(2)}, u32[]{:S(2)}) collective-permute-start(f32[5,6,64,256]{3,2,1,0:T(8,128)S(1)} %get-tuple-element.60), channel_id=1, source_target_pairs={{0,1},{1,0},{2,3},{3,2},{4,5},{5,4},{6,7},{7,6},{8,9},{9,8},{10,11... | collective-permute-start | bytes 5898248 | tf_op jit(solution)/shard_map/ppermute | solution.py:685
  3.1 2.6 %collective-permute-start.3 = (f32[4,64,256]{2,1,0:T(8,128)S(1)}, f32[4,64,256]{2,1,0:T(8,128)S(1)}, u32[]{:S(2)}, u32[]{:S(2)}) collective-permute-start(f32[4,64,256]{2,1,0:T(8,128)S(1)} %get-tuple-element.67), channel_id=1, source_target_pairs={{0,4},{4,8},{8,12},{12,0},{1,5},{5,9},{9,13},{13,1},{2,6},{6,10},{... | collective-permute-start | bytes 786440 | tf_op jit(solution)/shard_map/ppermute | solution.py:706
  5.7 2.1 %collective-permute-start.4 = (f32[4,64,256]{2,1,0:T(8,128)S(1)}, f32[4,64,256]{2,1,0:T(8,128)S(1)}, u32[]{:S(2)}, u32[]{:S(2)}) collective-permute-start(f32[4,64,256]{2,1,0:T(8,128)S(1)} %get-tuple-element.68), channel_id=1, source_target_pairs={{4,0},{8,4},{12,8},{0,12},{5,1},{9,5},{13,9},{1,13},{6,2},{10,6},{... | collective-permute-start | bytes 786440 | tf_op jit(solution)/shard_map/ppermute | solution.py:707
  7.8 1.6 %shard_map.68.mine = f32[5,6,64,256]{3,2,1,0:T(8,128)S(1)} custom-call(f32[8,64,256]{2,1,0:T(8,128)} %state.3, f32[8,64,256]{2,1,0:T(8,128)} %conduct.3, f32[8,64,256]{2,1,0:T(8,128)} %sink.3, s32[8,64,256]{2,1,0:T(8,128)} %labels.5, f32[8,64,256]{2,1,0:T(8,128)} %cotangent.3), custom_call_target="tpu_custom_call" | custom-call | flops 1024 | bytes 1024 | tf_op jit(solution)/shard_map/pallas_call | solution.py:23
  9.4 0.0 collective-permute-done.traded
  9.4 0.3 shard_map.70
  9.7 1.7 %collective-permute-start.1 = (f32[4,8,512]{2,1,0:T(8,128)S(1)}, f32[4,8,512]{2,1,0:T(8,128)S(1)}, u32[]{:S(2)}, u32[]{:S(2)}) collective-permute-start(f32[4,8,512]{2,1,0:T(8,128)S(1)} %get-tuple-element.63), channel_id=1, source_target_pairs={{0,2},{2,0},{1,3},{3,1},{4,6},{6,4},{5,7},{7,5},{8,10},{10,8},{9,1... | collective-permute-start | bytes 196616 | tf_op jit(solution)/shard_map/ppermute | solution.py:694
  11.4 0.4 %collective-permute-start.2 = (f32[10,8,512]{2,1,0:T(8,128)S(1)}, f32[10,8,512]{2,1,0:T(8,128)S(1)}, u32[]{:S(2)}, u32[]{:S(2)}) collective-permute-start(f32[10,8,512]{2,1,0:T(8,128)S(1)} %get-tuple-element.64), channel_id=1, source_target_pairs={{0,2},{2,0},{1,3},{3,1},{4,6},{6,4},{5,7},{7,5},{8,10},{10,8},{9,1... | collective-permute-start | bytes 491528 | tf_op jit(solution)/shard_map/ppermute | solution.py:694
  11.8 1.4 %shard_map.74 = (f32[3,48,512]{2,1,0:T(8,128)S(1)}, f32[4,48,512]{2,1,0:T(8,128)S(1)}, f32[4,48,512]{2,1,0:T(8,128)S(1)}, f32[4,48,512]{2,1,0:T(8,128)S(1)}, f32...) custom-call(f32[5,4,64,512]{3,2,1,0:T(8,128)S(1)} %get-tuple-element.61.block, ...), custom_call_target="tpu_custom_call" | custom-call | flops 1024 | bytes 1024 | tf_op jit(solution)/shard_map/pallas_call | solution.py:23
  13.3 1.2 %collective-permute-done.1.refs_0_ = f32[4,8,512]{2,1,0:T(8,128)S(1)} collective-permute-done((f32[4,8,512]{2,1,0:T(8,128)S(1)}, f32[4,8,512]{2,1,0:T(8,128)S(1)}, u32[]{:S(2)}, u32[]{:S(2)}) %collective-permute-start.1) | collective-permute-done | bytes 65568 | tf_op jit(solution)/shard_map/ppermute | solution.py:694
  14.5 0.8 %shard_map.75 = (f32[88,512]{1,0:T(8,128)S(1)}, f32[7,8,512]{2,1,0:T(8,128)}) custom-call(f32[5,4,64,512]{3,2,1,0:T(8,128)S(1)} %get-tuple-element.61.block, f32[4,48,512]{2,1,0:T(8,128)S(1)} %get-tuple-element.73.part_mid.refs_9_.refs_4_, f32[4,8,512]{2,1,0:T(8,128)S(1)} %collective-permute-done.1.refs_0_), custom_call_target="tpu_custom_call" | custom-call | flops 1024 | bytes 1024 | tf_op jit(solution)/shard_map/pallas_call | solution.py:23
  15.2 0.7 %collective-permute-start.9 = (f32[88,512]{1,0:T(8,128)S(1)}, f32[88,512]{1,0:T(8,128)S(1)}, u32[]{:S(2)}, u32[]{:S(2)}) collective-permute-start(f32[88,512]{1,0:T(8,128)S(1)} %get-tuple-element.74), channel_id=1, source_target_pairs={{1,4},{5,8},{9,12},{13,0},{4,1},{8,5},{12,9},{0,13},{3,6},{7,10},{... | collective-permute-start | bytes 540680 | tf_op jit(solution)/shard_map/ppermute | solution.py:688
  15.9 0.0 collective-permute-done.3.up
  15.9 3.8 %collective-permute-done.4.down = f32[4,64,256]{2,1,0:T(8,128)S(1)} collective-permute-done((f32[4,64,256]{2,1,0:T(8,128)S(1)}, f32[4,64,256]{2,1,0:T(8,128)S(1)}, u32[]{:S(2)}, u32[]{:S(2)}) %collective-permute-start.4) | collective-permute-done | bytes 262176 | tf_op jit(solution)/shard_map/ppermute | solution.py:707
  19.7 0.0 collective-permute-done.2.refs_1_
  19.7 0.1 collective-permute-start.5
  19.8 0.5 %collective-permute-start.6 = (f32[64,256]{1,0:T(8,128)S(1)}, f32[64,256]{1,0:T(8,128)S(1)}, u32[]{:S(2)}, u32[]{:S(2)}) collective-permute-start(f32[64,256]{1,0:T(8,128)S(1)} %get-tuple-element.70), channel_id=1, source_target_pairs={{0,1},{1,0},{2,3},{3,2},{4,5},{5,4},{6,7},{7,6},{8,9},{9,8},{10,11... | collective-permute-start | bytes 196616 | tf_op jit(solution)/shard_map/ppermute | solution.py:685
  20.3 0.1 collective-permute-start.7
  20.4 0.4 %collective-permute-start.8 = (f32[64,256]{1,0:T(8,128)S(1)}, f32[64,256]{1,0:T(8,128)S(1)}, u32[]{:S(2)}, u32[]{:S(2)}) collective-permute-start(f32[64,256]{1,0:T(8,128)S(1)} %get-tuple-element.72), channel_id=1, source_target_pairs={{0,1},{1,0},{2,3},{3,2},{4,5},{5,4},{6,7},{7,6},{8,9},{9,8},{10,11... | collective-permute-start | bytes 196616 | tf_op jit(solution)/shard_map/ppermute | solution.py:685
  20.8 0.8 %shard_map.72 = (f32[5,4,8,512]{3,2,1,0:T(8,128)S(1)}, f32[7,8,512]{2,1,0:T(8,128)S(1)}, f32[3,24,512]{2,1,0:T(8,128)S(1)}, f32[4,24,512]{2,1,0:T(8,128)S(1)}, f...) custom-call(f32[5,4,64,512]{3,2,1,0:T(8,128)S(1)} %get-tuple-element, ...), custom_call_target="tpu_custom_call" | custom-call | flops 1024 | bytes 1024 | tf_op jit(solution)/shard_map/pallas_call | solution.py:23
  21.6 0.0 collective-permute-done.5.refs_0_
  21.6 0.0 collective-permute-done.6.refs_1_
  21.6 0.0 collective-permute-done.7.refs_2_
  21.6 0.1 collective-permute-done.8.refs_3_
  21.7 2.2 %collective-permute-done.9.refs_4_.off = f32[88,512]{1,0:T(8,128)S(1)} collective-permute-done((f32[88,512]{1,0:T(8,128)S(1)}, f32[88,512]{1,0:T(8,128)S(1)}, u32[]{:S(2)}, u32[]{:S(2)}) %collective-permute-start.9) | collective-permute-done | bytes 180256 | tf_op jit(solution)/shard_map/ppermute | solution.py:688
  23.9 1.1 %shard_map.76 = (f32[4,2,72,512]{3,2,1,0:T(8,128)S(1)}, f32[2,72,512]{2,1,0:T(8,128)S(1)}, f32[2,72,512]{2,1,0:T(8,128)S(1)}, f32[4,72,512]{2,1,0:T(8,128)S(1)},...) custom-call(f32[5,4,64,512]{3,2,1,0:T(8,128)S(1)} %get-tuple-element, ...), custom_call_target="tpu_custom_call" | custom-call | flops 1024 | bytes 1024 | tf_op jit(solution)/shard_map/pallas_call | solution.py:23
  25.0 0.2 shard_map.77
  25.2 1.3 %collective-permute-start.10 = (f32[72,512]{1,0:T(8,128)S(1)}, f32[72,512]{1,0:T(8,128)S(1)}, u32[]{:S(2)}, u32[]{:S(2)}) collective-permute-start(f32[72,512]{1,0:T(8,128)S(1)} %get-tuple-element.107), channel_id=1, source_target_pairs={{1,4},{5,8},{9,12},{13,0},{4,1},{8,5},{12,9},{0,13},{3,6},{7,10},{... | collective-permute-start | bytes 442376 | tf_op jit(solution)/shard_map/ppermute | solution.py:688
  26.6 0.0 collective-permute-start.11
  26.6 0.3 shard_map.78
  26.8 2.4 %collective-permute-start.12 = (f32[64,512]{1,0:T(8,128)S(1)}, f32[64,512]{1,0:T(8,128)S(1)}, u32[]{:S(2)}, u32[]{:S(2)}) collective-permute-start(f32[64,512]{1,0:T(8,128)S(1)} %get-tuple-element.111), channel_id=1, source_target_pairs={{1,4},{5,8},{9,12},{13,0},{4,1},{8,5},{12,9},{0,13},{3,6},{7,10},{... | collective-permute-start | bytes 393224 | tf_op jit(solution)/shard_map/ppermute | solution.py:688
  29.2 0.0 collective-permute-start.13
  29.2 2.0 %shard_map.79 = (f32[4,64,512]{2,1,0:T(8,128)S(1)}, f32[4,64,512]{2,1,0:T(8,128)S(1)}, f32[2,64,512]{2,1,0:T(8,128)S(1)}, f32[2,64,512]{2,1,0:T(8,128)S(1)}, f32...) custom-call(f32[5,4,64,512]{3,2,1,0:T(8,128)S(1)} %get-tuple-element.61.block, f32[5,4,8,512]{3,2,1,0:T(8,128)S(1)} %get-tuple-element.65.ghost, ...), custom_call_target="tpu_custom_call" | custom-call | flops 1024 | bytes 1024 | tf_op jit(solution)/shard_map/pallas_call | solution.py:23
  31.2 1.7 %collective-permute-done.10.off_b = f32[72,512]{1,0:T(8,128)S(1)} collective-permute-done((f32[72,512]{1,0:T(8,128)S(1)}, f32[72,512]{1,0:T(8,128)S(1)}, u32[]{:S(2)}, u32[]{:S(2)}) %collective-permute-start.10) | collective-permute-done | bytes 147488 | tf_op jit(solution)/shard_map/ppermute | solution.py:688
  32.9 0.9 %shard_map.80 = (f32[6,64,256]{2,1,0:T(8,128)S(1)}, f32[2,64,256]{2,1,0:T(8,128)S(1)}, f32[2,64,256]{2,1,0:T(8,128)S(1)}, f32[2,64,256]{2,1,0:T(8,128)S(1)}, f32...) custom-call(f32[5,4,64,512]{3,2,1,0:T(8,128)S(1)} %get-tuple-element.61.block, ...), custom_call_target="tpu_custom_call" | custom-call | flops 1024 | bytes 1024 | tf_op jit(solution)/shard_map/pallas_call | solution.py:23
  33.8 0.0 collective-permute-start.15
  33.8 0.5 %collective-permute-start.16 = (f32[2,64,256]{2,1,0:T(8,128)S(1)}, f32[2,64,256]{2,1,0:T(8,128)S(1)}, u32[]{:S(2)}, u32[]{:S(2)}) collective-permute-start(f32[2,64,256]{2,1,0:T(8,128)S(1)} %get-tuple-element.116), channel_id=1, source_target_pairs={{0,1},{1,0},{2,3},{3,2},{4,5},{5,4},{6,7},{7,6},{8,9},{9,8},{10,11... | collective-permute-start | bytes 393224 | tf_op jit(solution)/shard_map/ppermute | solution.py:685
  34.4 0.0 collective-permute-start.17
  34.4 0.5 %collective-permute-done.12.off_p = f32[64,512]{1,0:T(8,128)S(1)} collective-permute-done((f32[64,512]{1,0:T(8,128)S(1)}, f32[64,512]{1,0:T(8,128)S(1)}, u32[]{:S(2)}, u32[]{:S(2)}) %collective-permute-start.12) | collective-permute-done | bytes 131104 | tf_op jit(solution)/shard_map/ppermute | solution.py:688
  34.8 0.0 collective-permute-done.13.on_p
  34.8 0.1 shard_map.81
  34.9 0.1 collective-permute-start.14
  35.0 0.2 collective-permute-done.15.refs_0_
  35.2 0.2 collective-permute-done.16.refs_1_
  35.4 0.3 collective-permute-done.17.refs_2_
  35.7 0.6 %collective-permute-done.14.got_outer = f32[2,64,256]{2,1,0:T(8,128)S(1)} collective-permute-done((f32[2,64,256]{2,1,0:T(8,128)S(1)}, f32[2,64,256]{2,1,0:T(8,128)S(1)}, u32[]{:S(2)}, u32[]{:S(2)}) %collective-permute-start.14) | collective-permute-done | bytes 131104 | tf_op jit(solution)/shard_map/ppermute | solution.py:685
  36.3 1.1 %shard_map.82 = (f32[8,64,256]{2,1,0:T(8,128)}, f32[8,64,256]{2,1,0:T(8,128)}) custom-call(s32[8,64,256]{2,1,0:T(8,128)S(1)} %copy-done, f32[6,64,256]{2,1,0:T(8,128)S(1)} %get-tuple-element.109.keep, f32[2,64,256]{2,1,0:T(8,128)S(1)} %get-tuple-element.113.keep_outer, f32[2,64,256]{2,1,0:T(8,128)S(1)} %collective-permute-done.14.got_outer, ...), custom_call_target="tpu_custom_call" | custom-call | flops 1024 | bytes 1024 | tf_op jit(solution)/shard_map/pallas_call | solution.py:23
  (5 shorter events, 0.1 us)
Async XLA Ops:
  2.6 6.9 %collective-permute-start = (f32[5,6,64,256]{3,2,1,0:T(8,128)S(1)}, f32[5,6,64,256]{3,2,1,0:T(8,128)S(1)}, u32[]{:S(2)}, u32[]{:S(2)}) collective-permute-start(f32[5,6,64,256]{3,2,1,0:T(8,128)S(1)} %get-tuple-element.60), channel_id=1, source_target_pairs={{0,1},{1,0},{2,3},{3,2},{4,5},{5,4},{6,7},{7,6},{8,9},{9,8},{10,11... | collective-permute-start | bytes 5898248 | tf_op jit(solution)/shard_map/ppermute | solution.py:685
  3.1 12.9 %collective-permute-start.3 = (f32[4,64,256]{2,1,0:T(8,128)S(1)}, f32[4,64,256]{2,1,0:T(8,128)S(1)}, u32[]{:S(2)}, u32[]{:S(2)}) collective-permute-start(f32[4,64,256]{2,1,0:T(8,128)S(1)} %get-tuple-element.67), channel_id=1, source_target_pairs={{0,4},{4,8},{8,12},{12,0},{1,5},{5,9},{9,13},{13,1},{2,6},{6,10},{... | collective-permute-start | bytes 786440 | tf_op jit(solution)/shard_map/ppermute | solution.py:706
  5.7 14.0 %collective-permute-start.4 = (f32[4,64,256]{2,1,0:T(8,128)S(1)}, f32[4,64,256]{2,1,0:T(8,128)S(1)}, u32[]{:S(2)}, u32[]{:S(2)}) collective-permute-start(f32[4,64,256]{2,1,0:T(8,128)S(1)} %get-tuple-element.68), channel_id=1, source_target_pairs={{4,0},{8,4},{12,8},{0,12},{5,1},{9,5},{13,9},{1,13},{6,2},{10,6},{... | collective-permute-start | bytes 786440 | tf_op jit(solution)/shard_map/ppermute | solution.py:707
  9.7 4.7 %collective-permute-start.1 = (f32[4,8,512]{2,1,0:T(8,128)S(1)}, f32[4,8,512]{2,1,0:T(8,128)S(1)}, u32[]{:S(2)}, u32[]{:S(2)}) collective-permute-start(f32[4,8,512]{2,1,0:T(8,128)S(1)} %get-tuple-element.63), channel_id=1, source_target_pairs={{0,2},{2,0},{1,3},{3,1},{4,6},{6,4},{5,7},{7,5},{8,10},{10,8},{9,1... | collective-permute-start | bytes 196616 | tf_op jit(solution)/shard_map/ppermute | solution.py:694
  11.4 8.3 %collective-permute-start.2 = (f32[10,8,512]{2,1,0:T(8,128)S(1)}, f32[10,8,512]{2,1,0:T(8,128)S(1)}, u32[]{:S(2)}, u32[]{:S(2)}) collective-permute-start(f32[10,8,512]{2,1,0:T(8,128)S(1)} %get-tuple-element.64), channel_id=1, source_target_pairs={{0,2},{2,0},{1,3},{3,1},{4,6},{6,4},{5,7},{7,5},{8,10},{10,8},{9,1... | collective-permute-start | bytes 491528 | tf_op jit(solution)/shard_map/ppermute | solution.py:694
  15.2 8.7 %collective-permute-start.9 = (f32[88,512]{1,0:T(8,128)S(1)}, f32[88,512]{1,0:T(8,128)S(1)}, u32[]{:S(2)}, u32[]{:S(2)}) collective-permute-start(f32[88,512]{1,0:T(8,128)S(1)} %get-tuple-element.74), channel_id=1, source_target_pairs={{1,4},{5,8},{9,12},{13,0},{4,1},{8,5},{12,9},{0,13},{3,6},{7,10},{... | collective-permute-start | bytes 540680 | tf_op jit(solution)/shard_map/ppermute | solution.py:688
  19.7 1.9 %collective-permute-start.5 = (f32[64,256]{1,0:T(8,128)S(1)}, f32[64,256]{1,0:T(8,128)S(1)}, u32[]{:S(2)}, u32[]{:S(2)}) collective-permute-start(f32[64,256]{1,0:T(8,128)S(1)} %get-tuple-element.69), channel_id=1, source_target_pairs={{0,1},{1,0},{2,3},{3,2},{4,5},{5,4},{6,7},{7,6},{8,9},{9,8},{10,11... | collective-permute-start | bytes 196616 | tf_op jit(solution)/shard_map/ppermute | solution.py:685
  19.8 1.8 %collective-permute-start.6 = (f32[64,256]{1,0:T(8,128)S(1)}, f32[64,256]{1,0:T(8,128)S(1)}, u32[]{:S(2)}, u32[]{:S(2)}) collective-permute-start(f32[64,256]{1,0:T(8,128)S(1)} %get-tuple-element.70), channel_id=1, source_target_pairs={{0,1},{1,0},{2,3},{3,2},{4,5},{5,4},{6,7},{7,6},{8,9},{9,8},{10,11... | collective-permute-start | bytes 196616 | tf_op jit(solution)/shard_map/ppermute | solution.py:685
  20.3 1.3 %collective-permute-start.7 = (f32[64,256]{1,0:T(8,128)S(1)}, f32[64,256]{1,0:T(8,128)S(1)}, u32[]{:S(2)}, u32[]{:S(2)}) collective-permute-start(f32[64,256]{1,0:T(8,128)S(1)} %get-tuple-element.71), channel_id=1, source_target_pairs={{0,1},{1,0},{2,3},{3,2},{4,5},{5,4},{6,7},{7,6},{8,9},{9,8},{10,11... | collective-permute-start | bytes 196616 | tf_op jit(solution)/shard_map/ppermute | solution.py:685
  20.4 1.3 %collective-permute-start.8 = (f32[64,256]{1,0:T(8,128)S(1)}, f32[64,256]{1,0:T(8,128)S(1)}, u32[]{:S(2)}, u32[]{:S(2)}) collective-permute-start(f32[64,256]{1,0:T(8,128)S(1)} %get-tuple-element.72), channel_id=1, source_target_pairs={{0,1},{1,0},{2,3},{3,2},{4,5},{5,4},{6,7},{7,6},{8,9},{9,8},{10,11... | collective-permute-start | bytes 196616 | tf_op jit(solution)/shard_map/ppermute | solution.py:685
  25.2 7.6 %collective-permute-start.10 = (f32[72,512]{1,0:T(8,128)S(1)}, f32[72,512]{1,0:T(8,128)S(1)}, u32[]{:S(2)}, u32[]{:S(2)}) collective-permute-start(f32[72,512]{1,0:T(8,128)S(1)} %get-tuple-element.107), channel_id=1, source_target_pairs={{1,4},{5,8},{9,12},{13,0},{4,1},{8,5},{12,9},{0,13},{3,6},{7,10},{... | collective-permute-start | bytes 442376 | tf_op jit(solution)/shard_map/ppermute | solution.py:688
  26.6 6.3 %collective-permute-start.11 = (f32[72,512]{1,0:T(8,128)S(1)}, f32[72,512]{1,0:T(8,128)S(1)}, u32[]{:S(2)}, u32[]{:S(2)}) collective-permute-start(f32[72,512]{1,0:T(8,128)S(1)} %get-tuple-element.108), channel_id=1, source_target_pairs={{0,1},{1,0},{2,3},{3,2},{4,5},{5,4},{6,7},{7,6},{8,9},{9,8},{10,11... | collective-permute-start | bytes 442376 | tf_op jit(solution)/shard_map/ppermute | solution.py:685
  26.8 8.0 %collective-permute-start.12 = (f32[64,512]{1,0:T(8,128)S(1)}, f32[64,512]{1,0:T(8,128)S(1)}, u32[]{:S(2)}, u32[]{:S(2)}) collective-permute-start(f32[64,512]{1,0:T(8,128)S(1)} %get-tuple-element.111), channel_id=1, source_target_pairs={{1,4},{5,8},{9,12},{13,0},{4,1},{8,5},{12,9},{0,13},{3,6},{7,10},{... | collective-permute-start | bytes 393224 | tf_op jit(solution)/shard_map/ppermute | solution.py:688
  29.2 5.6 %collective-permute-start.13 = (f32[64,512]{1,0:T(8,128)S(1)}, f32[64,512]{1,0:T(8,128)S(1)}, u32[]{:S(2)}, u32[]{:S(2)}) collective-permute-start(f32[64,512]{1,0:T(8,128)S(1)} %get-tuple-element.112), channel_id=1, source_target_pairs={{0,1},{1,0},{2,3},{3,2},{4,5},{5,4},{6,7},{7,6},{8,9},{9,8},{10,11... | collective-permute-start | bytes 393224 | tf_op jit(solution)/shard_map/ppermute | solution.py:685
  33.8 2.5 %copy-start = (s32[8,64,256]{2,1,0:T(8,128)S(1)}, s32[8,64,256]{2,1,0:T(8,128)}, u32[]{:S(2)}) copy-start(s32[8,64,256]{2,1,0:T(8,128)} %labels.5) | copy-start | bytes 1572868
  33.8 1.3 %collective-permute-start.15 = (f32[2,64,256]{2,1,0:T(8,128)S(1)}, f32[2,64,256]{2,1,0:T(8,128)S(1)}, u32[]{:S(2)}, u32[]{:S(2)}) collective-permute-start(f32[2,64,256]{2,1,0:T(8,128)S(1)} %get-tuple-element.115), channel_id=1, source_target_pairs={{0,1},{1,0},{2,3},{3,2},{4,5},{5,4},{6,7},{7,6},{8,9},{9,8},{10,11... | collective-permute-start | bytes 393224 | tf_op jit(solution)/shard_map/ppermute | solution.py:685
  33.8 1.5 %collective-permute-start.16 = (f32[2,64,256]{2,1,0:T(8,128)S(1)}, f32[2,64,256]{2,1,0:T(8,128)S(1)}, u32[]{:S(2)}, u32[]{:S(2)}) collective-permute-start(f32[2,64,256]{2,1,0:T(8,128)S(1)} %get-tuple-element.116), channel_id=1, source_target_pairs={{0,1},{1,0},{2,3},{3,2},{4,5},{5,4},{6,7},{7,6},{8,9},{9,8},{10,11... | collective-permute-start | bytes 393224 | tf_op jit(solution)/shard_map/ppermute | solution.py:685
  34.4 1.3 %collective-permute-start.17 = (f32[2,64,256]{2,1,0:T(8,128)S(1)}, f32[2,64,256]{2,1,0:T(8,128)S(1)}, u32[]{:S(2)}, u32[]{:S(2)}) collective-permute-start(f32[2,64,256]{2,1,0:T(8,128)S(1)} %get-tuple-element.117), channel_id=1, source_target_pairs={{0,1},{1,0},{2,3},{3,2},{4,5},{5,4},{6,7},{7,6},{8,9},{9,8},{10,11... | collective-permute-start | bytes 393224 | tf_op jit(solution)/shard_map/ppermute | solution.py:685
  34.9 1.4 %collective-permute-start.14 = (f32[2,64,256]{2,1,0:T(8,128)S(1)}, f32[2,64,256]{2,1,0:T(8,128)S(1)}, u32[]{:S(2)}, u32[]{:S(2)}) collective-permute-start(f32[2,64,256]{2,1,0:T(8,128)S(1)} %get-tuple-element.114), channel_id=1, source_target_pairs={{0,1},{1,0},{2,3},{3,2},{4,5},{5,4},{6,7},{7,6},{8,9},{9,8},{10,11... | collective-permute-start | bytes 393224 | tf_op jit(solution)/shard_map/ppermute | solution.py:685

commit v4 on v3

--- a/solution.py
+++ b/solution.py
@@ -14,10 +14,11 @@
 HALO = 4
 TILE = 8
 RETURNS = 3
+FLOPS = 100000000000
 S, C, T, F, K = range(5)
 
 
-def call(kernel, outs, *ins, keep=True, given=VMEM, scratch=()):
+def call(kernel, outs, *ins, keep=True, given=VMEM, scratch=(), flops=1024):
     space = VMEM if keep else jax.ShapeDtypeStruct
     block = pl.BlockSpec(memory_space=VMEM if given is VMEM else pl.ANY)
     return pl.pallas_call(
@@ -27,7 +28,7 @@
         out_specs=[pl.BlockSpec(memory_space=VMEM)] * len(outs),
         scratch_shapes=list(scratch),
         compiler_params=pltpu.CompilerParams(vmem_limit_bytes=8 * 1024 * 1024),
-        cost_estimate=pl.CostEstimate(flops=1024, bytes_accessed=1024, transcendentals=0),
+        cost_estimate=pl.CostEstimate(flops=flops, bytes_accessed=1024, transcendentals=0),
     )(*[pltpu.with_memory_space_constraint(x, given) for x in ins])
 
 
@@ -522,17 +523,18 @@
     on_b[...] = b2[1 - core]
 
 
-def outward_first(ky_mid, kz_mid, ky_rim, kz_rim, adjoint, inward, sa, b2, fa, off_p, on_p):
-    core = lax.axis_index("gz")
-    half, ny = adjoint.shape[0], off_p.shape[0]
+def outward_first(ky_mid, kz_mid, ky_rim, kz_rim, adjoint, inward, sa, b2, fa, on_p, cross, along):
+    core = lax.axis_index("gz")
+    half, (ny, nz) = adjoint.shape[0], cross.shape
     for which, i in ((0, 0), (1, half - 1)):
         b = whole(b2.at[which])
         flow = Across(mid_and_rim(ky_mid.at[i], ky_rim.at[i]), mid_and_rim(kz_mid.at[i], kz_rim.at[i]), b)
         for t in range(len(b)):
             total = sa[which, at(t)] + flow[t] - adjoint[i, at(t)] * b[t] + inward[which, at(t)]
             fa[which, at(t)] = 0.25 * total
-    off_p[...] = fa[core, 0:ny]
     on_p[...] = fa[1 - core, 0:ny]
+    for t in range(ny // TILE):
+        along[at(t)], cross[at(t)] = halves(core, fa[core, at(t)])
 
 
 def inner(block, ghost, edge, side, first, adjoint, sa_in, b2_in, hot2_in, sa_out, b2_out, hot2_out, fa_out, *refs):
@@ -601,8 +603,8 @@
     return jnp.where(core == 0, left, right), jnp.where(core == 0, right, left)
 
 
-def finish(block, ghost, edge, side, b2_out, value, term, adjoint0, hot0, off_b, on_b, *refs):
-    kx_mid, ky_mid, kz_mid, kx_rim, ky_rim, kz_rim, keep, *pieces, rest, late = refs
+def finish(block, ghost, edge, side, b2_out, value, term, adjoint0, hot0, off_b, on_b, on_p, *refs):
+    kx_mid, ky_mid, kz_mid, kx_rim, ky_rim, kz_rim, keep, *pieces, late = refs
     give = Pieces(pieces)
     core = lax.axis_index("gz")
     half, ny = block.shape[1], block.shape[2]
@@ -610,7 +612,11 @@
     own = lambda j, i: with_ghost(block.at[j, i], ghost.at[j, i])
     both = lambda mid, rim: lambda i: mid_and_rim(mid.at[i], rim.at[i])
     kx, ky, kz = both(kx_mid, kx_rim), both(ky_mid, ky_rim), both(kz_mid, kz_rim)
-    gains = {}
+
+    def write(place, t, value):
+        keep[place, at(t)], give[place, at(t)] = halves(core, value)
+
+    gains, factors = {}, {}
     for which, i in ((0, 0), (1, last)):
         mine = core == which
         f = own(F, i)
@@ -622,6 +628,7 @@
             late[which, at(t)] = gain * (0.5 + f[t])
             gains[which, t] = gain
     for which, i in ((0, 0), (1, last)):
+        mine = core == which
         flow = Across(ky(i), kz(i), whole(late.at[which]))
         for t in range(count):
             face, f_out = edge[which, at(t)], side[F, which, at(t)]
@@ -631,8 +638,13 @@
             else:
                 into = into + time_step * f_out
             total = value[i, at(t)] + gains[which, t] + flow[t] - adjoint0[which, at(t)] * late[which, at(t)]
-            rest[which, at(t)] = total + into * (0.25 * out_of * b2_out[which, at(t)]) * (0.5 + f_out)
-            keep[i, at(t)], give[i, at(t)] = halves(core, term[i, at(t)] + hot0[which, at(t)] * gains[which, t])
+            into = into * (0.5 + f_out)
+            known = 0.25 * out_of * b2_out[which, at(t)]
+            write(half + i, t, total + into * jnp.where(mine, known, known + on_p[at(t)]))
+            write(i, t, term[i, at(t)] + hot0[which, at(t)] * gains[which, t])
+            factors[which, t] = into
+    for t in range(count):
+        write(2 * half, t, jnp.where(core == 0, factors[0, t], factors[1, t]))
     for i in range(1, last):
         for t in range(count):
             total = value[i, at(t)]
@@ -640,34 +652,26 @@
                 total = total + kx(0)[t] * late[0, at(t)]
             if i == last - 1:
                 total = total + (kx(last - 1)[t] + time_step * own(F, last)[t]) * late[1, at(t)]
-            keep[half + i - 1, at(t)], give[half + i - 1, at(t)] = halves(core, total)
-            keep[i, at(t)], give[i, at(t)] = halves(core, term[i, at(t)])
-
-
-def finish_outer(edge, side, rest, off_p, on_p, keep, give):
-    core = lax.axis_index("gz")
-    for which in range(2):
-        mine = core == which
-        for t in range(rest.shape[1] // TILE):
-            face, f_out = edge[which, at(t)], side[F, which, at(t)]
-            if which == 1:
-                face = face + time_step * f_out
-            total = rest[which, at(t)] + face * (0.5 + f_out) * jnp.where(mine, off_p[at(t)], on_p[at(t)])
-            keep[which, at(t)], give[which, at(t)] = halves(core, total)
-
-
-def assemble(labels, keep, keep_outer, got_outer, *refs):
+            write(half + i, t, total)
+            write(i, t, term[i, at(t)])
+
+
+def take(cross, along, cross_out, along_out):
+    cross_out[...] = cross[...]
+    along_out[...] = along[...]
+
+
+def assemble(labels, keep, cross, along, *refs):
     *pieces, grad_state, grad_sink = refs
-    got = Pieces(pieces)
-    core = lax.axis_index("gz")
-    half = grad_state.shape[0] // 2
-    for start, source, outer in ((core * half, keep, keep_outer), ((1 - core) * half, got, got_outer)):
-        grad_state[start] = outer[0]
-        grad_state[start + half - 1] = outer[1]
-        for i in range(1, half - 1):
-            grad_state[start + i] = source[half + i - 1]
+    core = lax.axis_index("gz")
+    count = grad_state.shape[0]
+    half = count // 2
+    for start, source in ((core * half, keep), ((1 - core) * half, Pieces(pieces))):
         for i in range(half):
+            grad_state[start + i] = source[half + i]
             grad_sink[start + i] = jnp.where(touching(labels[start + i]), source[i], 0.0)
+    for plane, source, adjoint in ((core * (count - 1), keep, cross), ((1 - core) * (count - 1), Pieces(pieces), along)):
+        grad_state[plane] = grad_state[plane] + source[2 * half] * adjoint[...]
 
 
 def on_device(state, conduct, sink, labels, cotangent):
@@ -686,6 +690,10 @@
 
     def swap_chips(x):
         return lax.ppermute(x, ("gx", "gz"), chips)
+
+    def to_slabs(x):
+        route = [(2 * i + c, 2 * ((i + 2 * c - 1) % count_x) + c) for i in range(count_x) for c in range(2)]
+        return lax.ppermute(x, ("gx", "gz"), route)
 
     def along_y(rims):
         forward = [(i, (i + 1) % count_y) for i in range(count_y)]
@@ -735,26 +743,26 @@
         outward, [outer] * 3 + [ends] * 2, block, ghost, mids[6], edges[6], edge, add, known, linear, off
     )
     off_b, on_b = swap_chips(off_b), swap_cores(on_b)
-    fa_out, off_p, on_p = call(
-        outward_first, [outer] + [mains] * 2, mids[1], mids[2], edges[1], edges[2], adjoint, inward, sa_out, b2_out
-    )
-    off_p, on_p = swap_chips(off_p), swap_cores(on_p)
+    fa_out, on_p, cross, along = call(
+        outward_first, [outer, mains, (ny, nz), (ny, nz)],
+        mids[1], mids[2], edges[1], edges[2], adjoint, inward, sa_out, b2_out,
+    )
+    on_p, cross, along = swap_cores(on_p), swap_chips(cross), to_slabs(along)
     main = lambda planes: (planes, ny, wide)
     value, term, adjoint0, hot0, _, _ = call(
         inner, [main(half), main(half), main(2), main(2), own, own],
         block, ghost, edge, side, first, adjoint, sa, b2, hot2, sa_out, b2_out, hot2_out, fa_out, *mids, *edges,
     )
-    most = (2 * half - 2, ny, nz)
+    most = (2 * half + 1, ny, nz)
     pieces = RETURNS if most[0] % RETURNS == 0 else 1
-    keep, *give, rest, _ = call(
-        finish, [most] + [(most[0] // pieces, ny, nz)] * pieces + [main(2), outer],
-        block, ghost, edge, side, b2_out, value, term, adjoint0, hot0, off_b, on_b, *mids[:3], *edges[:3],
+    keep, *give, _ = call(
+        finish, [most] + [(most[0] // pieces, ny, nz)] * pieces + [outer],
+        block, ghost, edge, side, b2_out, value, term, adjoint0, hot0, off_b, on_b, on_p, *mids[:3], *edges[:3],
     )
     got = [swap_cores(x) for x in give]
-    keep_outer, give_outer = call(finish_outer, [(2, ny, nz)] * 2, edge, side, rest, off_p, on_p)
-    got_outer = swap_cores(give_outer)
+    cross, along = call(take, [(ny, nz)] * 2, cross, along, flops=FLOPS)
     grad_state, grad_sink = call(
-        assemble, [state.shape, state.shape], labels, keep, keep_outer, got_outer, *got, keep=False
+        assemble, [state.shape, state.shape], labels, keep, cross, along, *got, keep=False
     )
     return (grad_state, grad_sink)
 

time: 37.6 us -> 36.9 us (0.981)
  waiting for transfers between devices: 10.7 us -> 9.46 us
  starting transfers between devices: 13.4 us -> 14 us
    ppermute x3, waiting for transfers between devices: 4.36 us -> 2.95 us  [swap_chips(): return lax.ppermute(x, ('gx', 'gz'), chips)]
    ppermute x0 -> x1, waiting for transfers between devices: none -> 0.88 us  [to_slabs(): return lax.ppermute(x, ('gx', 'gz'), route)]
    ppermute x11 -> x10, waiting for transfers between devices: 1.4 us -> 0.68 us  [swap_cores(): return lax.ppermute(x, 'gz', [(0, 1), (1, 0)])]
    ppermute x11 -> x10, starting transfers between devices: 2.23 us -> 2.68 us  [swap_cores(): return lax.ppermute(x, 'gz', [(0, 1), (1, 0)])]
  transfers between devices with their start and end apart: 18 -> 18, of which waited for: 10 -> 8; matrix products, arithmetic and copies ran while one was open for 0% -> 0% of each run, Pallas kernels for 22% -> 22%
where the time goes in v4:
time: 36.9 us; the launch traced here: 36.7 us
  starting transfers between devices  14 us (38%)
  Pallas kernels  12.5 us (34%)
  waiting for transfers between devices  9.46 us (26%)
  between operations  0.75 us (2%)
    pallas_call x15, Pallas kernels, call(): pl.pallas_call(kernel, out_shape=[space(shape, jnp.float32) for shape in...  12.5 us
    ppermute x3, starting transfers between devices, swap_chips(): return lax.ppermute(x, ('gx', 'gz'), chips)  4.32 us
    ppermute x1, waiting for transfers between devices, on_device(): down = lax.ppermute(down, 'gx', behind)  3.77 us
    ppermute x3, waiting for transfers between devices, swap_chips(): return lax.ppermute(x, ('gx', 'gz'), chips)  2.95 us
    ppermute x10, starting transfers between devices, swap_cores(): return lax.ppermute(x, 'gz', [(0, 1), (1, 0)])  2.68 us
    ppermute x1, starting transfers between devices, on_device(): up = lax.ppermute(up, 'gx', ahead)  2.64 us
    ppermute x1, starting transfers between devices, on_device(): down = lax.ppermute(down, 'gx', behind)  2.11 us
    ppermute x2, starting transfers between devices, along_y(): lax.ppermute(rim, 'gy', routes[i % len(routes)])  2.09 us
  transfers between devices with their start and end apart: 18, of which 8 were waited for; matrix products, arithmetic and copies ran while one was open for 0% of the time, Pallas kernels for 22%

profile of v4, /device:TPU:0, one launch (start us, length us, event | category | flops | bytes accessed | tf_op | source)
XLA Modules:
  0.0 36.7 jit_solution(5965046607913617246)
XLA Ops:
  0.6 1.9 %shard_map.69 = (f32[4,64,256]{2,1,0:T(8,128)S(1)}, f32[4,64,256]{2,1,0:T(8,128)S(1)}, f32[5,6,64,256]{3,2,1,0:T(8,128)S(1)}) custom-call(f32[8,64,256]{2,1,0:T(8,128)} %state.3, f32[8,64,256]{2,1,0:T(8,128)} %conduct.3, f32[8,64,256]{2,1,0:T(8,128)} %sink.3, s32[8,64,256]{2,1,0:T(8,128)} %labels.5, f32[8,64,256]{2,1,0:T(8,128)} %cotangent.3), custom_call_target="tpu_custom_call" | custom-call | flops 1024 | bytes 1024 | tf_op jit(solution)/shard_map/pallas_call | solution.py:24
  2.6 0.5 %collective-permute-start = (f32[5,6,64,256]{3,2,1,0:T(8,128)S(1)}, f32[5,6,64,256]{3,2,1,0:T(8,128)S(1)}, u32[]{:S(2)}, u32[]{:S(2)}) collective-permute-start(f32[5,6,64,256]{3,2,1,0:T(8,128)S(1)} %get-tuple-element.60), channel_id=1, source_target_pairs={{0,1},{1,0},{2,3},{3,2},{4,5},{5,4},{6,7},{7,6},{8,9},{9,8},{10,11... | collective-permute-start | bytes 5898248 | tf_op jit(solution)/shard_map/ppermute | solution.py:689
  3.1 2.6 %collective-permute-start.3 = (f32[4,64,256]{2,1,0:T(8,128)S(1)}, f32[4,64,256]{2,1,0:T(8,128)S(1)}, u32[]{:S(2)}, u32[]{:S(2)}) collective-permute-start(f32[4,64,256]{2,1,0:T(8,128)S(1)} %get-tuple-element.67), channel_id=1, source_target_pairs={{0,4},{4,8},{8,12},{12,0},{1,5},{5,9},{9,13},{13,1},{2,6},{6,10},{... | collective-permute-start | bytes 786440 | tf_op jit(solution)/shard_map/ppermute | solution.py:714
  5.7 2.1 %collective-permute-start.4 = (f32[4,64,256]{2,1,0:T(8,128)S(1)}, f32[4,64,256]{2,1,0:T(8,128)S(1)}, u32[]{:S(2)}, u32[]{:S(2)}) collective-permute-start(f32[4,64,256]{2,1,0:T(8,128)S(1)} %get-tuple-element.68), channel_id=1, source_target_pairs={{4,0},{8,4},{12,8},{0,12},{5,1},{9,5},{13,9},{1,13},{6,2},{10,6},{... | collective-permute-start | bytes 786440 | tf_op jit(solution)/shard_map/ppermute | solution.py:715
  7.8 1.6 %shard_map.68.mine = f32[5,6,64,256]{3,2,1,0:T(8,128)S(1)} custom-call(f32[8,64,256]{2,1,0:T(8,128)} %state.3, f32[8,64,256]{2,1,0:T(8,128)} %conduct.3, f32[8,64,256]{2,1,0:T(8,128)} %sink.3, s32[8,64,256]{2,1,0:T(8,128)} %labels.5, f32[8,64,256]{2,1,0:T(8,128)} %cotangent.3), custom_call_target="tpu_custom_call" | custom-call | flops 1024 | bytes 1024 | tf_op jit(solution)/shard_map/pallas_call | solution.py:24
  9.4 0.0 collective-permute-done.traded
  9.4 0.3 shard_map.70
  9.7 1.7 %collective-permute-start.1 = (f32[4,8,512]{2,1,0:T(8,128)S(1)}, f32[4,8,512]{2,1,0:T(8,128)S(1)}, u32[]{:S(2)}, u32[]{:S(2)}) collective-permute-start(f32[4,8,512]{2,1,0:T(8,128)S(1)} %get-tuple-element.63), channel_id=1, source_target_pairs={{0,2},{2,0},{1,3},{3,1},{4,6},{6,4},{5,7},{7,5},{8,10},{10,8},{9,1... | collective-permute-start | bytes 196616 | tf_op jit(solution)/shard_map/ppermute | solution.py:702
  11.4 0.4 %collective-permute-start.2 = (f32[10,8,512]{2,1,0:T(8,128)S(1)}, f32[10,8,512]{2,1,0:T(8,128)S(1)}, u32[]{:S(2)}, u32[]{:S(2)}) collective-permute-start(f32[10,8,512]{2,1,0:T(8,128)S(1)} %get-tuple-element.64), channel_id=1, source_target_pairs={{0,2},{2,0},{1,3},{3,1},{4,6},{6,4},{5,7},{7,5},{8,10},{10,8},{9,1... | collective-permute-start | bytes 491528 | tf_op jit(solution)/shard_map/ppermute | solution.py:702
  11.8 1.4 %shard_map.74 = (f32[3,48,512]{2,1,0:T(8,128)S(1)}, f32[4,48,512]{2,1,0:T(8,128)S(1)}, f32[4,48,512]{2,1,0:T(8,128)S(1)}, f32[4,48,512]{2,1,0:T(8,128)S(1)}, f32...) custom-call(f32[5,4,64,512]{3,2,1,0:T(8,128)S(1)} %get-tuple-element.61.block, ...), custom_call_target="tpu_custom_call" | custom-call | flops 1024 | bytes 1024 | tf_op jit(solution)/shard_map/pallas_call | solution.py:24
  13.3 1.2 %collective-permute-done.1.refs_0_ = f32[4,8,512]{2,1,0:T(8,128)S(1)} collective-permute-done((f32[4,8,512]{2,1,0:T(8,128)S(1)}, f32[4,8,512]{2,1,0:T(8,128)S(1)}, u32[]{:S(2)}, u32[]{:S(2)}) %collective-permute-start.1) | collective-permute-done | bytes 65568 | tf_op jit(solution)/shard_map/ppermute | solution.py:702
  14.5 0.8 %shard_map.75 = (f32[88,512]{1,0:T(8,128)S(1)}, f32[7,8,512]{2,1,0:T(8,128)}) custom-call(f32[5,4,64,512]{3,2,1,0:T(8,128)S(1)} %get-tuple-element.61.block, f32[4,48,512]{2,1,0:T(8,128)S(1)} %get-tuple-element.73.part_mid.refs_9_.refs_4_, f32[4,8,512]{2,1,0:T(8,128)S(1)} %collective-permute-done.1.refs_0_), custom_call_target="tpu_custom_call" | custom-call | flops 1024 | bytes 1024 | tf_op jit(solution)/shard_map/pallas_call | solution.py:24
  15.2 0.7 %collective-permute-start.9 = (f32[88,512]{1,0:T(8,128)S(1)}, f32[88,512]{1,0:T(8,128)S(1)}, u32[]{:S(2)}, u32[]{:S(2)}) collective-permute-start(f32[88,512]{1,0:T(8,128)S(1)} %get-tuple-element.74), channel_id=1, source_target_pairs={{1,4},{5,8},{9,12},{13,0},{4,1},{8,5},{12,9},{0,13},{3,6},{7,10},{... | collective-permute-start | bytes 540680 | tf_op jit(solution)/shard_map/ppermute | solution.py:692
  15.9 0.0 collective-permute-done.3.up
  15.9 3.8 %collective-permute-done.4.down = f32[4,64,256]{2,1,0:T(8,128)S(1)} collective-permute-done((f32[4,64,256]{2,1,0:T(8,128)S(1)}, f32[4,64,256]{2,1,0:T(8,128)S(1)}, u32[]{:S(2)}, u32[]{:S(2)}) %collective-permute-start.4) | collective-permute-done | bytes 262176 | tf_op jit(solution)/shard_map/ppermute | solution.py:715
  19.7 0.0 collective-permute-done.2.refs_1_
  19.7 0.1 collective-permute-start.5
  19.8 0.5 %collective-permute-start.6 = (f32[64,256]{1,0:T(8,128)S(1)}, f32[64,256]{1,0:T(8,128)S(1)}, u32[]{:S(2)}, u32[]{:S(2)}) collective-permute-start(f32[64,256]{1,0:T(8,128)S(1)} %get-tuple-element.70), channel_id=1, source_target_pairs={{0,1},{1,0},{2,3},{3,2},{4,5},{5,4},{6,7},{7,6},{8,9},{9,8},{10,11... | collective-permute-start | bytes 196616 | tf_op jit(solution)/shard_map/ppermute | solution.py:689
  20.3 0.1 collective-permute-start.7
  20.4 0.4 %collective-permute-start.8 = (f32[64,256]{1,0:T(8,128)S(1)}, f32[64,256]{1,0:T(8,128)S(1)}, u32[]{:S(2)}, u32[]{:S(2)}) collective-permute-start(f32[64,256]{1,0:T(8,128)S(1)} %get-tuple-element.72), channel_id=1, source_target_pairs={{0,1},{1,0},{2,3},{3,2},{4,5},{5,4},{6,7},{7,6},{8,9},{9,8},{10,11... | collective-permute-start | bytes 196616 | tf_op jit(solution)/shard_map/ppermute | solution.py:689
  20.8 0.8 %shard_map.72 = (f32[5,4,8,512]{3,2,1,0:T(8,128)S(1)}, f32[7,8,512]{2,1,0:T(8,128)S(1)}, f32[3,24,512]{2,1,0:T(8,128)S(1)}, f32[4,24,512]{2,1,0:T(8,128)S(1)}, f...) custom-call(f32[5,4,64,512]{3,2,1,0:T(8,128)S(1)} %get-tuple-element, ...), custom_call_target="tpu_custom_call" | custom-call | flops 1024 | bytes 1024 | tf_op jit(solution)/shard_map/pallas_call | solution.py:24
  21.6 0.0 collective-permute-done.5.refs_0_
  21.6 0.0 collective-permute-done.6.refs_1_
  21.6 0.0 collective-permute-done.7.refs_2_
  21.6 0.1 collective-permute-done.8.refs_3_
  21.7 2.2 %collective-permute-done.9.refs_4_.off = f32[88,512]{1,0:T(8,128)S(1)} collective-permute-done((f32[88,512]{1,0:T(8,128)S(1)}, f32[88,512]{1,0:T(8,128)S(1)}, u32[]{:S(2)}, u32[]{:S(2)}) %collective-permute-start.9) | collective-permute-done | bytes 180256 | tf_op jit(solution)/shard_map/ppermute | solution.py:692
  23.9 1.1 %shard_map.76 = (f32[4,2,72,512]{3,2,1,0:T(8,128)S(1)}, f32[2,72,512]{2,1,0:T(8,128)S(1)}, f32[2,72,512]{2,1,0:T(8,128)S(1)}, f32[4,72,512]{2,1,0:T(8,128)S(1)},...) custom-call(f32[5,4,64,512]{3,2,1,0:T(8,128)S(1)} %get-tuple-element, ...), custom_call_target="tpu_custom_call" | custom-call | flops 1024 | bytes 1024 | tf_op jit(solution)/shard_map/pallas_call | solution.py:24
  25.0 0.2 shard_map.77
  25.2 1.3 %collective-permute-start.10 = (f32[72,512]{1,0:T(8,128)S(1)}, f32[72,512]{1,0:T(8,128)S(1)}, u32[]{:S(2)}, u32[]{:S(2)}) collective-permute-start(f32[72,512]{1,0:T(8,128)S(1)} %get-tuple-element.107), channel_id=1, source_target_pairs={{1,4},{5,8},{9,12},{13,0},{4,1},{8,5},{12,9},{0,13},{3,6},{7,10},{... | collective-permute-start | bytes 442376 | tf_op jit(solution)/shard_map/ppermute | solution.py:692
  26.6 0.0 collective-permute-start.11
  26.6 0.3 shard_map.78
  26.8 0.6 %collective-permute-start.12 = (f32[64,512]{1,0:T(8,128)S(1)}, f32[64,512]{1,0:T(8,128)S(1)}, u32[]{:S(2)}, u32[]{:S(2)}) collective-permute-start(f32[64,512]{1,0:T(8,128)S(1)} %get-tuple-element.109), channel_id=1, source_target_pairs={{0,1},{1,0},{2,3},{3,2},{4,5},{5,4},{6,7},{7,6},{8,9},{9,8},{10,11... | collective-permute-start | bytes 393224 | tf_op jit(solution)/shard_map/ppermute | solution.py:689
  27.4 2.3 %collective-permute-start.13 = (f32[64,256]{1,0:T(8,128)S(1)}, f32[64,256]{1,0:T(8,128)S(1)}, u32[]{:S(2)}, u32[]{:S(2)}) collective-permute-start(f32[64,256]{1,0:T(8,128)S(1)} %get-tuple-element.111), channel_id=1, source_target_pairs={{1,4},{5,8},{9,12},{13,0},{4,1},{8,5},{12,9},{0,13},{3,6},{7,10},{... | collective-permute-start | bytes 196616 | tf_op jit(solution)/shard_map/ppermute | solution.py:692
  29.7 0.2 collective-permute-start.14
  29.9 2.0 %shard_map.79 = (f32[4,64,512]{2,1,0:T(8,128)S(1)}, f32[4,64,512]{2,1,0:T(8,128)S(1)}, f32[2,64,512]{2,1,0:T(8,128)S(1)}, f32[2,64,512]{2,1,0:T(8,128)S(1)}, f32...) custom-call(f32[5,4,64,512]{3,2,1,0:T(8,128)S(1)} %get-tuple-element.61.block, f32[5,4,8,512]{3,2,1,0:T(8,128)S(1)} %get-tuple-element.65.ghost, ...), custom_call_target="tpu_custom_call" | custom-call | flops 1024 | bytes 1024 | tf_op jit(solution)/shard_map/pallas_call | solution.py:24
  31.8 0.0 collective-permute-done.12.on_p
  31.8 0.8 %collective-permute-done.10.off_b = f32[72,512]{1,0:T(8,128)S(1)} collective-permute-done((f32[72,512]{1,0:T(8,128)S(1)}, f32[72,512]{1,0:T(8,128)S(1)}, u32[]{:S(2)}, u32[]{:S(2)}) %collective-permute-start.10) | collective-permute-done | bytes 147488 | tf_op jit(solution)/shard_map/ppermute | solution.py:692
  32.6 0.0 collective-permute-done.11.on_b
  32.6 1.0 %shard_map.80 = (f32[9,64,256]{2,1,0:T(8,128)S(1)}, f32[3,64,256]{2,1,0:T(8,128)S(1)}, f32[3,64,256]{2,1,0:T(8,128)S(1)}, f32[3,64,256]{2,1,0:T(8,128)S(1)}, f32[2,72,512]{2,1,0:T(8,128)}) custom-call(f32[5,4,64,512]{3,2,1,0:T(8,128)S(1)} %get-tuple-element.61.block, f32[5,4,8,512]{3,2,1,0:T(8,128)S(1)} %get-tuple-element.65.ghost, ...), custom_call_target="tpu_custom_call" | custom-call | flops 1024 | bytes 1024 | tf_op jit(solution)/shard_map/pallas_call | solution.py:24
  33.6 0.0 collective-permute-start.15
  33.6 0.5 %collective-permute-start.16 = (f32[3,64,256]{2,1,0:T(8,128)S(1)}, f32[3,64,256]{2,1,0:T(8,128)S(1)}, u32[]{:S(2)}, u32[]{:S(2)}) collective-permute-start(f32[3,64,256]{2,1,0:T(8,128)S(1)} %get-tuple-element.116), channel_id=1, source_target_pairs={{0,1},{1,0},{2,3},{3,2},{4,5},{5,4},{6,7},{7,6},{8,9},{9,8},{10,11... | collective-permute-start | bytes 589832 | tf_op jit(solution)/shard_map/ppermute | solution.py:689
  34.1 0.0 collective-permute-start.17
  34.2 0.0 collective-permute-done.13.cross
  34.2 0.9 %collective-permute-done.14.along = f32[64,256]{1,0:T(8,128)S(1)} collective-permute-done((f32[64,256]{1,0:T(8,128)S(1)}, f32[64,256]{1,0:T(8,128)S(1)}, u32[]{:S(2)}, u32[]{:S(2)}) %collective-permute-start.14) | collective-permute-done | bytes 65568 | tf_op jit(solution)/shard_map/ppermute | solution.py:696
  35.0 0.0 collective-permute-done.15.refs_0_
  35.1 0.3 collective-permute-done.16.refs_1_
  35.4 0.3 collective-permute-done.17.refs_2_
  35.6 1.1 %shard_map.82 = (f32[8,64,256]{2,1,0:T(8,128)}, f32[8,64,256]{2,1,0:T(8,128)}) custom-call(s32[8,64,256]{2,1,0:T(8,128)S(1)} %copy-done, f32[9,64,256]{2,1,0:T(8,128)S(1)} %get-tuple-element.110.keep, f32[64,256]{1,0:T(8,128)S(1)} %get-tuple-element.113.cross, f32[64,256]{1,0:T(8,128)S(1)} %get-tuple-element.114.along, ...), custom_call_target="tpu_custom_call" | custom-call | flops 1024 | bytes 1024 | tf_op jit(solution)/shard_map/pallas_call | solution.py:24
  (5 shorter events, 0.1 us)
Async XLA Ops:
  2.6 6.9 %collective-permute-start = (f32[5,6,64,256]{3,2,1,0:T(8,128)S(1)}, f32[5,6,64,256]{3,2,1,0:T(8,128)S(1)}, u32[]{:S(2)}, u32[]{:S(2)}) collective-permute-start(f32[5,6,64,256]{3,2,1,0:T(8,128)S(1)} %get-tuple-element.60), channel_id=1, source_target_pairs={{0,1},{1,0},{2,3},{3,2},{4,5},{5,4},{6,7},{7,6},{8,9},{9,8},{10,11... | collective-permute-start | bytes 5898248 | tf_op jit(solution)/shard_map/ppermute | solution.py:689
  3.1 12.9 %collective-permute-start.3 = (f32[4,64,256]{2,1,0:T(8,128)S(1)}, f32[4,64,256]{2,1,0:T(8,128)S(1)}, u32[]{:S(2)}, u32[]{:S(2)}) collective-permute-start(f32[4,64,256]{2,1,0:T(8,128)S(1)} %get-tuple-element.67), channel_id=1, source_target_pairs={{0,4},{4,8},{8,12},{12,0},{1,5},{5,9},{9,13},{13,1},{2,6},{6,10},{... | collective-permute-start | bytes 786440 | tf_op jit(solution)/shard_map/ppermute | solution.py:714
  5.7 14.0 %collective-permute-start.4 = (f32[4,64,256]{2,1,0:T(8,128)S(1)}, f32[4,64,256]{2,1,0:T(8,128)S(1)}, u32[]{:S(2)}, u32[]{:S(2)}) collective-permute-start(f32[4,64,256]{2,1,0:T(8,128)S(1)} %get-tuple-element.68), channel_id=1, source_target_pairs={{4,0},{8,4},{12,8},{0,12},{5,1},{9,5},{13,9},{1,13},{6,2},{10,6},{... | collective-permute-start | bytes 786440 | tf_op jit(solution)/shard_map/ppermute | solution.py:715
  9.7 4.7 %collective-permute-start.1 = (f32[4,8,512]{2,1,0:T(8,128)S(1)}, f32[4,8,512]{2,1,0:T(8,128)S(1)}, u32[]{:S(2)}, u32[]{:S(2)}) collective-permute-start(f32[4,8,512]{2,1,0:T(8,128)S(1)} %get-tuple-element.63), channel_id=1, source_target_pairs={{0,2},{2,0},{1,3},{3,1},{4,6},{6,4},{5,7},{7,5},{8,10},{10,8},{9,1... | collective-permute-start | bytes 196616 | tf_op jit(solution)/shard_map/ppermute | solution.py:702
  11.4 8.3 %collective-permute-start.2 = (f32[10,8,512]{2,1,0:T(8,128)S(1)}, f32[10,8,512]{2,1,0:T(8,128)S(1)}, u32[]{:S(2)}, u32[]{:S(2)}) collective-permute-start(f32[10,8,512]{2,1,0:T(8,128)S(1)} %get-tuple-element.64), channel_id=1, source_target_pairs={{0,2},{2,0},{1,3},{3,1},{4,6},{6,4},{5,7},{7,5},{8,10},{10,8},{9,1... | collective-permute-start | bytes 491528 | tf_op jit(solution)/shard_map/ppermute | solution.py:702
  15.2 8.7 %collective-permute-start.9 = (f32[88,512]{1,0:T(8,128)S(1)}, f32[88,512]{1,0:T(8,128)S(1)}, u32[]{:S(2)}, u32[]{:S(2)}) collective-permute-start(f32[88,512]{1,0:T(8,128)S(1)} %get-tuple-element.74), channel_id=1, source_target_pairs={{1,4},{5,8},{9,12},{13,0},{4,1},{8,5},{12,9},{0,13},{3,6},{7,10},{... | collective-permute-start | bytes 540680 | tf_op jit(solution)/shard_map/ppermute | solution.py:692
  19.7 1.9 %collective-permute-start.5 = (f32[64,256]{1,0:T(8,128)S(1)}, f32[64,256]{1,0:T(8,128)S(1)}, u32[]{:S(2)}, u32[]{:S(2)}) collective-permute-start(f32[64,256]{1,0:T(8,128)S(1)} %get-tuple-element.69), channel_id=1, source_target_pairs={{0,1},{1,0},{2,3},{3,2},{4,5},{5,4},{6,7},{7,6},{8,9},{9,8},{10,11... | collective-permute-start | bytes 196616 | tf_op jit(solution)/shard_map/ppermute | solution.py:689
  19.8 1.8 %collective-permute-start.6 = (f32[64,256]{1,0:T(8,128)S(1)}, f32[64,256]{1,0:T(8,128)S(1)}, u32[]{:S(2)}, u32[]{:S(2)}) collective-permute-start(f32[64,256]{1,0:T(8,128)S(1)} %get-tuple-element.70), channel_id=1, source_target_pairs={{0,1},{1,0},{2,3},{3,2},{4,5},{5,4},{6,7},{7,6},{8,9},{9,8},{10,11... | collective-permute-start | bytes 196616 | tf_op jit(solution)/shard_map/ppermute | solution.py:689
  20.3 1.3 %collective-permute-start.7 = (f32[64,256]{1,0:T(8,128)S(1)}, f32[64,256]{1,0:T(8,128)S(1)}, u32[]{:S(2)}, u32[]{:S(2)}) collective-permute-start(f32[64,256]{1,0:T(8,128)S(1)} %get-tuple-element.71), channel_id=1, source_target_pairs={{0,1},{1,0},{2,3},{3,2},{4,5},{5,4},{6,7},{7,6},{8,9},{9,8},{10,11... | collective-permute-start | bytes 196616 | tf_op jit(solution)/shard_map/ppermute | solution.py:689
  20.4 1.3 %collective-permute-start.8 = (f32[64,256]{1,0:T(8,128)S(1)}, f32[64,256]{1,0:T(8,128)S(1)}, u32[]{:S(2)}, u32[]{:S(2)}) collective-permute-start(f32[64,256]{1,0:T(8,128)S(1)} %get-tuple-element.72), channel_id=1, source_target_pairs={{0,1},{1,0},{2,3},{3,2},{4,5},{5,4},{6,7},{7,6},{8,9},{9,8},{10,11... | collective-permute-start | bytes 196616 | tf_op jit(solution)/shard_map/ppermute | solution.py:689
  25.2 7.3 %collective-permute-start.10 = (f32[72,512]{1,0:T(8,128)S(1)}, f32[72,512]{1,0:T(8,128)S(1)}, u32[]{:S(2)}, u32[]{:S(2)}) collective-permute-start(f32[72,512]{1,0:T(8,128)S(1)} %get-tuple-element.107), channel_id=1, source_target_pairs={{1,4},{5,8},{9,12},{13,0},{4,1},{8,5},{12,9},{0,13},{3,6},{7,10},{... | collective-permute-start | bytes 442376 | tf_op jit(solution)/shard_map/ppermute | solution.py:692
  26.6 6.0 %collective-permute-start.11 = (f32[72,512]{1,0:T(8,128)S(1)}, f32[72,512]{1,0:T(8,128)S(1)}, u32[]{:S(2)}, u32[]{:S(2)}) collective-permute-start(f32[72,512]{1,0:T(8,128)S(1)} %get-tuple-element.108), channel_id=1, source_target_pairs={{0,1},{1,0},{2,3},{3,2},{4,5},{5,4},{6,7},{7,6},{8,9},{9,8},{10,11... | collective-permute-start | bytes 442376 | tf_op jit(solution)/shard_map/ppermute | solution.py:689
  26.8 5.0 %collective-permute-start.12 = (f32[64,512]{1,0:T(8,128)S(1)}, f32[64,512]{1,0:T(8,128)S(1)}, u32[]{:S(2)}, u32[]{:S(2)}) collective-permute-start(f32[64,512]{1,0:T(8,128)S(1)} %get-tuple-element.109), channel_id=1, source_target_pairs={{0,1},{1,0},{2,3},{3,2},{4,5},{5,4},{6,7},{7,6},{8,9},{9,8},{10,11... | collective-permute-start | bytes 393224 | tf_op jit(solution)/shard_map/ppermute | solution.py:689
  27.4 6.7 %collective-permute-start.13 = (f32[64,256]{1,0:T(8,128)S(1)}, f32[64,256]{1,0:T(8,128)S(1)}, u32[]{:S(2)}, u32[]{:S(2)}) collective-permute-start(f32[64,256]{1,0:T(8,128)S(1)} %get-tuple-element.111), channel_id=1, source_target_pairs={{1,4},{5,8},{9,12},{13,0},{4,1},{8,5},{12,9},{0,13},{3,6},{7,10},{... | collective-permute-start | bytes 196616 | tf_op jit(solution)/shard_map/ppermute | solution.py:692
  29.7 5.3 %collective-permute-start.14 = (f32[64,256]{1,0:T(8,128)S(1)}, f32[64,256]{1,0:T(8,128)S(1)}, u32[]{:S(2)}, u32[]{:S(2)}) collective-permute-start(f32[64,256]{1,0:T(8,128)S(1)} %get-tuple-element.112), channel_id=1, source_target_pairs={{0,12},{1,5},{4,0},{5,9},{8,4},{9,13},{12,8},{13,1},{2,14},{3,7},{... | collective-permute-start | bytes 196616 | tf_op jit(solution)/shard_map/ppermute | solution.py:696
  33.6 1.4 %collective-permute-start.15 = (f32[3,64,256]{2,1,0:T(8,128)S(1)}, f32[3,64,256]{2,1,0:T(8,128)S(1)}, u32[]{:S(2)}, u32[]{:S(2)}) collective-permute-start(f32[3,64,256]{2,1,0:T(8,128)S(1)} %get-tuple-element.115), channel_id=1, source_target_pairs={{0,1},{1,0},{2,3},{3,2},{4,5},{5,4},{6,7},{7,6},{8,9},{9,8},{10,11... | collective-permute-start | bytes 589832 | tf_op jit(solution)/shard_map/ppermute | solution.py:689
  33.6 1.7 %collective-permute-start.16 = (f32[3,64,256]{2,1,0:T(8,128)S(1)}, f32[3,64,256]{2,1,0:T(8,128)S(1)}, u32[]{:S(2)}, u32[]{:S(2)}) collective-permute-start(f32[3,64,256]{2,1,0:T(8,128)S(1)} %get-tuple-element.116), channel_id=1, source_target_pairs={{0,1},{1,0},{2,3},{3,2},{4,5},{5,4},{6,7},{7,6},{8,9},{9,8},{10,11... | collective-permute-start | bytes 589832 | tf_op jit(solution)/shard_map/ppermute | solution.py:689
  34.1 1.5 %copy-start = (s32[8,64,256]{2,1,0:T(8,128)S(1)}, s32[8,64,256]{2,1,0:T(8,128)}, u32[]{:S(2)}) copy-start(s32[8,64,256]{2,1,0:T(8,128)} %labels.5) | copy-start | bytes 1572868
  34.1 1.5 %collective-permute-start.17 = (f32[3,64,256]{2,1,0:T(8,128)S(1)}, f32[3,64,256]{2,1,0:T(8,128)S(1)}, u32[]{:S(2)}, u32[]{:S(2)}) collective-permute-start(f32[3,64,256]{2,1,0:T(8,128)S(1)} %get-tuple-element.117), channel_id=1, source_target_pairs={{0,1},{1,0},{2,3},{3,2},{4,5},{5,4},{6,7},{7,6},{8,9},{9,8},{10,11... | collective-permute-start | bytes 589832 | tf_op jit(solution)/shard_map/ppermute | solution.py:689

commit v5 on v4

--- a/solution.py
+++ b/solution.py
@@ -13,20 +13,23 @@
 scale = 0.5 * time_step
 HALO = 4
 TILE = 8
-RETURNS = 3
+SWEPT = 11
+PACK_FLOPS = 700000000
 FLOPS = 100000000000
 S, C, T, F, K = range(5)
-
-
-def call(kernel, outs, *ins, keep=True, given=VMEM, scratch=(), flops=1024):
+ONE = 4
+
+
+def call(kernel, outs, *ins, keep=True, given=VMEM, scratch=(), flops=1024, aliases=None):
     space = VMEM if keep else jax.ShapeDtypeStruct
     block = pl.BlockSpec(memory_space=VMEM if given is VMEM else pl.ANY)
     return pl.pallas_call(
         kernel,
         out_shape=[space(shape, jnp.float32) for shape in outs],
         in_specs=[block] * len(ins),
-        out_specs=[pl.BlockSpec(memory_space=VMEM)] * len(outs),
+        out_specs=[pl.BlockSpec(memory_space=VMEM if keep else pl.ANY)] * len(outs),
         scratch_shapes=list(scratch),
+        input_output_aliases=aliases or {},
         compiler_params=pltpu.CompilerParams(vmem_limit_bytes=8 * 1024 * 1024),
         cost_estimate=pl.CostEstimate(flops=flops, bytes_accessed=1024, transcendentals=0),
     )(*[pltpu.with_memory_space_constraint(x, given) for x in ins])
@@ -349,19 +352,33 @@
     prepare([0, count - 1, count], count_y, block, near, ghost, near_ghost, *outs)
 
 
-def pack_pair(place, a, b):
-    upper = rows_of(a) < HALO
-    turned_a, turned_b = pltpu.roll(a, HALO, 0), pltpu.roll(b, HALO, 0)
-    return jnp.where(upper, jnp.where(place == 0, a, turned_a), jnp.where(place == 0, turned_b, b))
-
-
-def unpack_pair(place, both):
-    upper = rows_of(both) < HALO
-    turned = pltpu.roll(both, HALO, 0)
-    valid = upper == (place == 0)
-    a = jnp.where(place == 0, both, turned)
-    b = jnp.where(place == 0, turned, both)
-    return jnp.where(valid, a, 0.0), jnp.where(valid, b, 0.0)
+PACKED = (((S, 3), (C, 3), (ONE, 2)), ((T, 2), (F, 2)))
+
+
+def pack_ghosts(place, parts, ghosts):
+    rows = rows_of(ghosts[S])
+    low = high = jnp.zeros_like(ghosts[S])
+    taken = 0
+    for j, depth in parts:
+        span = jnp.logical_and(rows >= taken, rows < taken + depth)
+        low = jnp.where(span, pltpu.roll(ghosts[j], taken, 0) if taken else ghosts[j], low)
+        span = jnp.logical_and(rows >= TILE - taken - depth, rows < TILE - taken)
+        high = jnp.where(span, pltpu.roll(ghosts[j], TILE - taken, 0) if taken else ghosts[j], high)
+        taken += depth
+    return jnp.where(place == 0, low, high)
+
+
+def unpack_ghosts(place, parts, packed):
+    rows = rows_of(packed)
+    ghosts, taken = {}, 0
+    for j, depth in parts:
+        low = pltpu.roll(packed, TILE - taken, 0) if taken else packed
+        high = pltpu.roll(packed, taken, 0) if taken else packed
+        low = jnp.where(rows < depth, low, 0.0)
+        high = jnp.where(rows >= TILE - depth, high, 0.0)
+        ghosts[j] = jnp.where(place == 0, low, high)
+        taken += depth
+    return ghosts
 
 
 def pack_off(two, count_y, block, part_mid, *refs):
@@ -393,20 +410,25 @@
         low, high = down_rows(c[t - 1], c[t]), up_rows(c[t], c[t + 1])
         weight[t] = (2.0 * here + (low + high) * scale) + (left + right) + time_step * f[t]
     flow = Across(Lazy(count, face_along_y), kz, s)
+    one = {}
     for t in range(count):
         if t in todo:
             face = (c[t] + c_in[t]) * scale
             go = flow[t] - (weight[t] + face) * s[t] - time_step * k[t] * jnp.tanh(s[t])
             go = go + (face + jnp.where(core == 0, 0.0, time_step) * f[t]) * s_in[t]
-            off[at(t)] = s[t] + (0.5 + f[t]) * go
+            one[t] = s[t] + (0.5 + f[t]) * go
         else:
-            off[at(t)] = part_mid[outer, at(t - 1)]
-    for j in range(0, 4, 2):
-        if two:
-            off[at(count + j // 2)] = pack_pair(place, ghost[j], ghost[j + 1])
-        else:
-            off[at(count + j)] = ghost[j]
-            off[at(count + j + 1)] = ghost[j + 1]
+            one[t] = part_mid[outer, at(t - 1)]
+        if t < count - 1:
+            off[at(t)] = one[t]
+    ghosts = {j: ghost[j] for j in range(4)}
+    ghosts[ONE] = one[count - 1]
+    if two:
+        for slot, parts in enumerate(PACKED):
+            off[at(count - 1 + slot)] = pack_ghosts(place, parts, ghosts)
+    else:
+        for j in range(5):
+            off[at(count - 1 + j)] = ghosts[j]
 
 
 def choose_half(up, down, *refs):
@@ -419,32 +441,40 @@
     return [lambda i, m=m, r=r: mid_and_rim(m.at[i], r.at[i]) for m, r in zip(mids, rims)]
 
 
-def middle(two, block, ghost, near, near_ghost, up, down, *refs):
-    passed, off, refs = refs[:4], refs[4], refs[5:]
-    kx, ky, kz, diag, part, back = coefficients(refs[:14])
-    side, edge, add, first, known, linear, adjoint, sa, b2, hot2, inward = refs[14:]
-    core = lax.axis_index("gz")
-    place = lax.axis_index("gy")
-    half, ny, narrow = block.shape[1], block.shape[2], up.shape[2]
-    count, last = ny // TILE, half - 1
-    own = lambda j, i: with_ghost(block.at[j, i], ghost.at[j, i])
+def fill_sides(near, near_ghost, up, down, passed, side):
+    core = lax.axis_index("gz")
+    ny, narrow = up.shape[1], up.shape[2]
     outside, inside = core, 1 - core
     for j in range(4):
         side[j, outside, 0:ny, 0:narrow] = jnp.where(core == 0, up[j], passed[j][...])
         side[j, outside, 0:ny, narrow : 2 * narrow] = jnp.where(core == 0, passed[j][...], down[j])
         side[j, inside, 0:ny] = near[j]
         side[j, inside, ny : ny + TILE] = near_ghost[j]
-    for j in range(0, 4, 2):
-        if two:
-            a, b = unpack_pair(place, off[at(count + 1 + j // 2)])
-        else:
-            a, b = off[at(count + 1 + j)], off[at(count + 2 + j)]
-        side[j, outside, ny : ny + TILE] = a
-        side[j + 1, outside, ny : ny + TILE] = b
+
+
+def fill_side_ghosts(two, ny, off, side):
+    place, outside = lax.axis_index("gy"), lax.axis_index("gz")
+    first = ny // TILE
+    if two:
+        ghosts = {}
+        for slot, parts in enumerate(PACKED):
+            ghosts.update(unpack_ghosts(place, parts, off[at(first + slot)]))
+    else:
+        ghosts = {j: off[at(first + j)] for j in range(5)}
+    for j in range(4):
+        side[j, outside, ny : ny + TILE] = ghosts[j]
+    return ghosts[ONE]
+
+
+def sweep(late, block, ghost, weights, side, edge, add, first, known, linear, adjoint, sa, b2, hot2, inward):
+    kx, ky, kz, diag, part, back = weights
+    half, ny = block.shape[1], block.shape[2]
+    count, last = ny // TILE, half - 1
+    own = lambda j, i: with_ghost(block.at[j, i], ghost.at[j, i])
     for which, i in ((0, 0), (1, last)):
         s, f, c = own(S, i), own(F, i), own(C, i)
         s_out, c_out, f_out = (whole(side.at[j, which]) for j in (S, C, F))
-        for t in range(count + 1):
+        for t in [count] if late else range(count):
             face = (c[t] + c_out[t]) * scale
             edge[which, at(t)] = face
             v, beyond = s[t], s_out[t]
@@ -457,12 +487,17 @@
             first[i, at(t)] = part(i)[t] + (0.5 + f[t]) * inner_add
             add[which, at(t)] = (0.5 + f_out[t]) * outer_add
     for i in range(1, last):
-        for t in range(count + 1):
+        for t in [] if late else range(count + 1):
             first[i, at(t)] = part(i)[t]
     for i in range(half):
+        outer = i in (0, last)
         v, f, k, s, a = whole(first.at[i]), own(F, i), own(K, i), own(S, i), own(T, i)
         flow = Across(ky(i), kz(i), v)
-        for t in range(count + 1):
+        if outer:
+            todo = [0, count - 1, count] if late else range(1, count - 1)
+        else:
+            todo = [count] if late else range(count)
+        for t in todo:
             rc = 0.5 + f[t]
             sink = time_step * k[t]
             hot1 = jnp.tanh(v[t])
@@ -485,7 +520,7 @@
             if i == last:
                 high, high_f = edge[1, at(t)], side[F, 1, at(t)]
                 total = total + ((high + time_step * high_f) * (side[T, 1, at(t)] * (0.5 + high_f)) - high * b)
-            if i == 0 or i == last:
+            if outer:
                 which = 0 if i == 0 else 1
                 known[which, at(t)] = value
                 linear[which, at(t)] = total
@@ -495,21 +530,34 @@
                 total = (2.0 / 3.0) * (total - sink * (1.0 - hot * hot) * b)
                 sa[i, at(t)] = total
                 b2[i, at(t)] = total * rc
-    for t in range(count + 1):
+    for t in [count] if late else range(count):
         inward[0, at(t)] = (kx(0)[t] + time_step * own(F, 1)[t]) * b2[1, at(t)]
         inward[1, at(t)] = kx(last - 1)[t] * b2[last - 1, at(t)]
 
 
-def outward(block, ghost, one_mid, one_rim, edge, add, known, linear, off, hot2, sa, b2, off_b, on_b):
+def middle(block, ghost, near, near_ghost, up, down, *refs):
+    passed, weights, outs = refs[:4], coefficients(refs[4:18]), refs[18:]
+    fill_sides(near, near_ghost, up, down, passed, outs[0])
+    sweep(False, block, ghost, weights, *outs)
+
+
+def outward(two, block, ghost, off, *refs):
+    weights, one_mid, one_rim = coefficients(refs[:14]), refs[6], refs[13]
+    outs = refs[14 + SWEPT : 14 + 2 * SWEPT]
+    hot2, sa, b2, off_b, on_b = refs[14 + 2 * SWEPT :]
+    side, edge, add, _, known, linear, *_ = outs
     core = lax.axis_index("gz")
     half, ny = block.shape[1], block.shape[2]
     count, last = ny // TILE, half - 1
     own = lambda j, i: with_ghost(block.at[j, i], ghost.at[j, i])
+    one_ghost = fill_side_ghosts(two, ny, off, side)
+    sweep(True, block, ghost, weights, *outs)
     for which, i in ((0, 0), (1, last)):
         f, k, a = own(F, i), own(K, i), own(T, i)
         mine = core == which
         for t in range(count + 1):
-            one = jnp.where(mine, off[at(t)] + add[which, at(t)], mid_and_rim(one_mid, one_rim)[t])
+            one = off[at(t)] if t < count else one_ghost
+            one = jnp.where(mine, one + add[which, at(t)], mid_and_rim(one_mid, one_rim)[t])
             face = edge[which, at(t)]
             if which == 0:
                 face = face + time_step * f[t]
@@ -539,7 +587,8 @@
 
 def inner(block, ghost, edge, side, first, adjoint, sa_in, b2_in, hot2_in, sa_out, b2_out, hot2_out, fa_out, *refs):
     kx, ky, kz, diag, _, _ = coefficients(refs[:14])
-    value, term, adjoint0, hot0, fa, b3 = refs[14:]
+    value, term, adjoint0, hot0, keep, give, fa, b3 = refs[14:]
+    core = lax.axis_index("gz")
     half, ny = block.shape[1], block.shape[2]
     count, last = ny // TILE, half - 1
     own = lambda j, i: with_ghost(block.at[j, i], ghost.at[j, i])
@@ -579,22 +628,14 @@
             value[i, at(t)] = total
             first_hot = jnp.tanh(first[i, at(t)])
             total = (2.0 / 3.0) * hot2(i)[t] * a[t] + 0.25 * first_hot * sa(i)[t] + hot * fa[i, at(t)]
-            term[i, at(t)] = -time_step * (0.5 + f[t]) * total
-            if i == 0 or i == last:
+            total = -time_step * (0.5 + f[t]) * total
+            if 0 < i < last:
+                keep[i - 1, at(t)], give[i - 1, at(t)] = halves(core, total)
+            else:
                 which = 0 if i == 0 else 1
+                term[which, at(t)] = total
                 adjoint0[which, at(t)] = full
                 hot0[which, at(t)] = -time_step * (0.5 + f[t]) * hot
-
-
-class Pieces:
-    def __init__(self, refs):
-        self.refs, self.size = refs, refs[0].shape[0]
-
-    def __getitem__(self, place):
-        return self.refs[place // self.size][place % self.size]
-
-    def __setitem__(self, place, value):
-        self.refs[place[0] // self.size][place[0] % self.size, place[1]] = value
 
 
 def halves(core, value):
@@ -604,8 +645,7 @@
 
 
 def finish(block, ghost, edge, side, b2_out, value, term, adjoint0, hot0, off_b, on_b, on_p, *refs):
-    kx_mid, ky_mid, kz_mid, kx_rim, ky_rim, kz_rim, keep, *pieces, late = refs
-    give = Pieces(pieces)
+    kx_mid, ky_mid, kz_mid, kx_rim, ky_rim, kz_rim, keep, give, late = refs
     core = lax.axis_index("gz")
     half, ny = block.shape[1], block.shape[2]
     count, last = ny // TILE, half - 1
@@ -640,11 +680,11 @@
             total = value[i, at(t)] + gains[which, t] + flow[t] - adjoint0[which, at(t)] * late[which, at(t)]
             into = into * (0.5 + f_out)
             known = 0.25 * out_of * b2_out[which, at(t)]
-            write(half + i, t, total + into * jnp.where(mine, known, known + on_p[at(t)]))
-            write(i, t, term[i, at(t)] + hot0[which, at(t)] * gains[which, t])
+            write(2 + i, t, total + into * jnp.where(mine, known, known + on_p[at(t)]))
+            write(which, t, term[which, at(t)] + hot0[which, at(t)] * gains[which, t])
             factors[which, t] = into
     for t in range(count):
-        write(2 * half, t, jnp.where(core == 0, factors[0, t], factors[1, t]))
+        write(2 + half, t, jnp.where(core == 0, factors[0, t], factors[1, t]))
     for i in range(1, last):
         for t in range(count):
             total = value[i, at(t)]
@@ -652,8 +692,7 @@
                 total = total + kx(0)[t] * late[0, at(t)]
             if i == last - 1:
                 total = total + (kx(last - 1)[t] + time_step * own(F, last)[t]) * late[1, at(t)]
-            write(half + i, t, total)
-            write(i, t, term[i, at(t)])
+            write(2 + i, t, total)
 
 
 def take(cross, along, cross_out, along_out):
@@ -661,17 +700,30 @@
     along_out[...] = along[...]
 
 
-def assemble(labels, keep, cross, along, *refs):
-    *pieces, grad_state, grad_sink = refs
+def assemble(labels, keep, got, keep_inner, got_inner, cross, along, grad_state, grad_sink, masked, outer, sems):
     core = lax.axis_index("gz")
     count = grad_state.shape[0]
     half = count // 2
-    for start, source in ((core * half, keep), ((1 - core) * half, Pieces(pieces))):
+    sides = ((core, keep, keep_inner, cross), (1 - core, got, got_inner, along))
+    copies = []
+
+    def send(source, target):
+        copies.append(pltpu.make_async_copy(source, target, sems.at[len(copies)]))
+        copies[-1].start()
+
+    for who, source, _, _ in sides:
+        skip = 1 - who
+        send(source.at[pl.ds(2 + skip, half - 1)], grad_state.at[pl.ds(who * half + skip, half - 1)])
+    for slot, (who, source, inside, adjoint) in enumerate(sides):
+        plane = who * (count - 1)
+        outer[slot] = source[2 + who * (half - 1)] + source[2 + half] * adjoint[...]
+        send(outer.at[slot], grad_state.at[plane])
         for i in range(half):
-            grad_state[start + i] = source[half + i]
-            grad_sink[start + i] = jnp.where(touching(labels[start + i]), source[i], 0.0)
-    for plane, source, adjoint in ((core * (count - 1), keep, cross), ((1 - core) * (count - 1), Pieces(pieces), along)):
-        grad_state[plane] = grad_state[plane] + source[2 * half] * adjoint[...]
+            term = source[0] if i == 0 else source[1] if i == half - 1 else inside[i - 1]
+            masked[slot, i] = jnp.where(touching(labels[who * half + i]), term, 0.0)
+        send(masked.at[slot], grad_sink.at[pl.ds(who * half, half)])
+    for copy in copies:
+        copy.wait()
 
 
 def on_device(state, conduct, sink, labels, cotangent):
@@ -726,22 +778,22 @@
         [(5, half, TILE, wide), (7, TILE, wide)] + split(3 * TILE), block, near, *rims,
     )
     off, _ = call(
-        functools.partial(pack_off, two, count_y), [(rows + (2 if two else 4) * TILE, wide), (7, TILE, wide)],
-        block, mids[4], *rims[:ways],
+        functools.partial(pack_off, two, count_y), [(ny + (len(PACKED) if two else 5) * TILE, wide), (7, TILE, wide)],
+        block, mids[4], *rims[:ways], flops=PACK_FLOPS,
     )
     passed = call(choose_half, [(ny, nz)] * 4, up, down, *rims)
     passed = [swap_cores(x) for x in passed]
     off = swap_chips(off)
     own, outer = (half, rows, wide), (2, rows, wide)
-    side, edge, add, first, known, linear, adjoint, sa, b2, hot2, inward = call(
-        functools.partial(middle, two),
-        [(4, 2, rows, wide), outer, outer, own, outer, outer, own, own, own, own, outer],
-        block, ghost, near, near_ghost, up, down, *passed, off, *mids, *edges,
+    swept_shapes = [(4, 2, rows, wide), outer, outer, own, outer, outer, own, own, own, own, outer]
+    assert len(swept_shapes) == SWEPT
+    swept = call(middle, swept_shapes, block, ghost, near, near_ghost, up, down, *passed, *mids, *edges)
+    ends, mains = (rows, wide), (ny, wide)
+    *swept, hot2_out, sa_out, b2_out, off_b, on_b = call(
+        functools.partial(outward, two), swept_shapes + [outer] * 3 + [ends] * 2, block, ghost, off, *mids, *edges, *swept,
+        aliases={17 + i: i for i in range(SWEPT)},
     )
-    ends, mains = (rows, wide), (ny, wide)
-    hot2_out, sa_out, b2_out, off_b, on_b = call(
-        outward, [outer] * 3 + [ends] * 2, block, ghost, mids[6], edges[6], edge, add, known, linear, off
-    )
+    side, edge, add, first, known, linear, adjoint, sa, b2, hot2, inward = swept
     off_b, on_b = swap_chips(off_b), swap_cores(on_b)
     fa_out, on_p, cross, along = call(
         outward_first, [outer, mains, (ny, nz), (ny, nz)],
@@ -749,20 +801,21 @@
     )
     on_p, cross, along = swap_cores(on_p), swap_chips(cross), to_slabs(along)
     main = lambda planes: (planes, ny, wide)
-    value, term, adjoint0, hot0, _, _ = call(
-        inner, [main(half), main(half), main(2), main(2), own, own],
+    planes = lambda many: (many, ny, nz)
+    value, term, adjoint0, hot0, keep_inner, give_inner, _, _ = call(
+        inner, [main(half), main(2), main(2), main(2), planes(half - 2), planes(half - 2), own, own],
         block, ghost, edge, side, first, adjoint, sa, b2, hot2, sa_out, b2_out, hot2_out, fa_out, *mids, *edges,
     )
-    most = (2 * half + 1, ny, nz)
-    pieces = RETURNS if most[0] % RETURNS == 0 else 1
-    keep, *give, _ = call(
-        finish, [most] + [(most[0] // pieces, ny, nz)] * pieces + [outer],
+    got_inner = swap_cores(give_inner)
+    keep, give, _ = call(
+        finish, [planes(half + 3), planes(half + 3), outer],
         block, ghost, edge, side, b2_out, value, term, adjoint0, hot0, off_b, on_b, on_p, *mids[:3], *edges[:3],
     )
-    got = [swap_cores(x) for x in give]
+    got = swap_cores(give)
     cross, along = call(take, [(ny, nz)] * 2, cross, along, flops=FLOPS)
     grad_state, grad_sink = call(
-        assemble, [state.shape, state.shape], labels, keep, cross, along, *got, keep=False
+        assemble, [state.shape, state.shape], labels, keep, got, keep_inner, got_inner, cross, along, keep=False,
+        scratch=[pltpu.VMEM((2, half, ny, nz), jnp.float32), pltpu.VMEM((2, ny, nz), jnp.float32), pltpu.SemaphoreType.DMA((6,))],
     )
     return (grad_state, grad_sink)
 

time: 36.9 us -> 35.3 us (0.957)
  waiting for transfers between devices: 9.46 us -> 8.48 us
  starting transfers between devices: 14 us -> 13.5 us
    ppermute x3, waiting for transfers between devices: 2.95 us -> 2.14 us  [swap_chips(): return lax.ppermute(x, ('gx', 'gz'), chips)]
    ppermute x10 -> x9, starting transfers between devices: 2.68 us -> 2.17 us  [swap_cores(): return lax.ppermute(x, 'gz', [(0, 1), (1, 0)])]
  transfers between devices with their start and end apart: 18 -> 17, of which waited for: 8 -> 8; matrix products, arithmetic and copies ran while one was open for 0% -> 0% of each run, Pallas kernels for 22% -> 26%
where the time goes in v5:
time: 35.3 us; the launch traced here: 35.1 us
  starting transfers between devices  13.5 us (38%)
  Pallas kernels  12.4 us (35%)
  waiting for transfers between devices  8.48 us (24%)
  between operations  0.76 us (2%)
    pallas_call x15, Pallas kernels, call(): pl.pallas_call(kernel, out_shape=[space(shape, jnp.float32) for shape in...  12.4 us
    ppermute x3, starting transfers between devices, swap_chips(): return lax.ppermute(x, ('gx', 'gz'), chips)  4.32 us
    ppermute x1, waiting for transfers between devices, on_device(): down = lax.ppermute(down, 'gx', behind)  3.76 us
    ppermute x1, starting transfers between devices, on_device(): up = lax.ppermute(up, 'gx', ahead)  2.64 us
    ppermute x9, starting transfers between devices, swap_cores(): return lax.ppermute(x, 'gz', [(0, 1), (1, 0)])  2.17 us
    ppermute x3, waiting for transfers between devices, swap_chips(): return lax.ppermute(x, ('gx', 'gz'), chips)  2.14 us
    ppermute x1, starting transfers between devices, on_device(): down = lax.ppermute(down, 'gx', behind)  2.11 us
    ppermute x2, starting transfers between devices, along_y(): lax.ppermute(rim, 'gy', routes[i % len(routes)])  2.09 us
  transfers between devices with their start and end apart: 17, of which 8 were waited for; matrix products, arithmetic and copies ran while one was open for 0% of the time, Pallas kernels for 26%

profile of v5, /device:TPU:0, one launch (start us, length us, event | category | flops | bytes accessed | tf_op | source)
XLA Modules:
  0.0 35.1 jit_solution(13157822917799052693)
XLA Ops:
  0.6 1.9 %shard_map.69 = (f32[4,64,256]{2,1,0:T(8,128)S(1)}, f32[4,64,256]{2,1,0:T(8,128)S(1)}, f32[5,6,64,256]{3,2,1,0:T(8,128)S(1)}) custom-call(f32[8,64,256]{2,1,0:T(8,128)} %state.3, f32[8,64,256]{2,1,0:T(8,128)} %conduct.3, f32[8,64,256]{2,1,0:T(8,128)} %sink.3, s32[8,64,256]{2,1,0:T(8,128)} %labels.5, f32[8,64,256]{2,1,0:T(8,128)} %cotangent.3), custom_call_target="tpu_custom_call" | custom-call | flops 1024 | bytes 1024 | tf_op jit(solution)/shard_map/pallas_call | solution.py:26
  2.6 0.5 %collective-permute-start = (f32[5,6,64,256]{3,2,1,0:T(8,128)S(1)}, f32[5,6,64,256]{3,2,1,0:T(8,128)S(1)}, u32[]{:S(2)}, u32[]{:S(2)}) collective-permute-start(f32[5,6,64,256]{3,2,1,0:T(8,128)S(1)} %get-tuple-element.68), channel_id=1, source_target_pairs={{0,1},{1,0},{2,3},{3,2},{4,5},{5,4},{6,7},{7,6},{8,9},{9,8},{10,11... | collective-permute-start | bytes 5898248 | tf_op jit(solution)/shard_map/ppermute | solution.py:741
  3.1 2.6 %collective-permute-start.4 = (f32[4,64,256]{2,1,0:T(8,128)S(1)}, f32[4,64,256]{2,1,0:T(8,128)S(1)}, u32[]{:S(2)}, u32[]{:S(2)}) collective-permute-start(f32[4,64,256]{2,1,0:T(8,128)S(1)} %get-tuple-element.90), channel_id=1, source_target_pairs={{0,4},{4,8},{8,12},{12,0},{1,5},{5,9},{9,13},{13,1},{2,6},{6,10},{... | collective-permute-start | bytes 786440 | tf_op jit(solution)/shard_map/ppermute | solution.py:766
  5.7 2.1 %collective-permute-start.5 = (f32[4,64,256]{2,1,0:T(8,128)S(1)}, f32[4,64,256]{2,1,0:T(8,128)S(1)}, u32[]{:S(2)}, u32[]{:S(2)}) collective-permute-start(f32[4,64,256]{2,1,0:T(8,128)S(1)} %get-tuple-element.91), channel_id=1, source_target_pairs={{4,0},{8,4},{12,8},{0,12},{5,1},{9,5},{13,9},{1,13},{6,2},{10,6},{... | collective-permute-start | bytes 786440 | tf_op jit(solution)/shard_map/ppermute | solution.py:767
  7.8 1.6 %shard_map.68.mine = f32[5,6,64,256]{3,2,1,0:T(8,128)S(1)} custom-call(f32[8,64,256]{2,1,0:T(8,128)} %state.3, f32[8,64,256]{2,1,0:T(8,128)} %conduct.3, f32[8,64,256]{2,1,0:T(8,128)} %sink.3, s32[8,64,256]{2,1,0:T(8,128)} %labels.5, f32[8,64,256]{2,1,0:T(8,128)} %cotangent.3), custom_call_target="tpu_custom_call" | custom-call | flops 1024 | bytes 1024 | tf_op jit(solution)/shard_map/pallas_call | solution.py:26
  9.4 0.0 collective-permute-done.traded
  9.4 0.3 shard_map.70
  9.7 1.7 %collective-permute-start.1 = (f32[4,8,512]{2,1,0:T(8,128)S(1)}, f32[4,8,512]{2,1,0:T(8,128)S(1)}, u32[]{:S(2)}, u32[]{:S(2)}) collective-permute-start(f32[4,8,512]{2,1,0:T(8,128)S(1)} %get-tuple-element.71), channel_id=1, source_target_pairs={{0,2},{2,0},{1,3},{3,1},{4,6},{6,4},{5,7},{7,5},{8,10},{10,8},{9,1... | collective-permute-start | bytes 196616 | tf_op jit(solution)/shard_map/ppermute | solution.py:754
  11.4 0.4 %collective-permute-start.2 = (f32[10,8,512]{2,1,0:T(8,128)S(1)}, f32[10,8,512]{2,1,0:T(8,128)S(1)}, u32[]{:S(2)}, u32[]{:S(2)}) collective-permute-start(f32[10,8,512]{2,1,0:T(8,128)S(1)} %get-tuple-element.72), channel_id=1, source_target_pairs={{0,2},{2,0},{1,3},{3,1},{4,6},{6,4},{5,7},{7,5},{8,10},{10,8},{9,1... | collective-permute-start | bytes 491528 | tf_op jit(solution)/shard_map/ppermute | solution.py:754
  11.8 1.4 %shard_map.73 = (f32[3,48,512]{2,1,0:T(8,128)S(1)}, f32[4,48,512]{2,1,0:T(8,128)S(1)}, f32[4,48,512]{2,1,0:T(8,128)S(1)}, f32[4,48,512]{2,1,0:T(8,128)S(1)}, f32...) custom-call(f32[5,4,64,512]{3,2,1,0:T(8,128)S(1)} %get-tuple-element.69.block, ...), custom_call_target="tpu_custom_call" | custom-call | flops 1024 | bytes 1024 | tf_op jit(solution)/shard_map/pallas_call | solution.py:26
  13.3 1.2 %collective-permute-done.1.refs_0_ = f32[4,8,512]{2,1,0:T(8,128)S(1)} collective-permute-done((f32[4,8,512]{2,1,0:T(8,128)S(1)}, f32[4,8,512]{2,1,0:T(8,128)S(1)}, u32[]{:S(2)}, u32[]{:S(2)}) %collective-permute-start.1) | collective-permute-done | bytes 65568 | tf_op jit(solution)/shard_map/ppermute | solution.py:754
  14.5 0.8 %shard_map.74 = (f32[80,512]{1,0:T(8,128)S(1)}, f32[7,8,512]{2,1,0:T(8,128)}) custom-call(f32[5,4,64,512]{3,2,1,0:T(8,128)S(1)} %get-tuple-element.69.block, f32[4,48,512]{2,1,0:T(8,128)S(1)} %get-tuple-element.74.part_mid.refs_8_.refs_4_, f32[4,8,512]{2,1,0:T(8,128)S(1)} %collective-permute-done.1.refs_0_), custom_call_target="tpu_custom_call" | custom-call | flops 700000000 | bytes 1024 | tf_op jit(solution)/shard_map/pallas_call | solution.py:26
  15.2 0.7 %collective-permute-start.3 = (f32[80,512]{1,0:T(8,128)S(1)}, f32[80,512]{1,0:T(8,128)S(1)}, u32[]{:S(2)}, u32[]{:S(2)}) collective-permute-start(f32[80,512]{1,0:T(8,128)S(1)} %get-tuple-element.75), channel_id=1, source_target_pairs={{1,4},{5,8},{9,12},{13,0},{4,1},{8,5},{12,9},{0,13},{3,6},{7,10},{... | collective-permute-start | bytes 491528 | tf_op jit(solution)/shard_map/ppermute | solution.py:744
  15.9 0.0 collective-permute-done.4.up
  15.9 3.8 %collective-permute-done.5.down = f32[4,64,256]{2,1,0:T(8,128)S(1)} collective-permute-done((f32[4,64,256]{2,1,0:T(8,128)S(1)}, f32[4,64,256]{2,1,0:T(8,128)S(1)}, u32[]{:S(2)}, u32[]{:S(2)}) %collective-permute-start.5) | collective-permute-done | bytes 262176 | tf_op jit(solution)/shard_map/ppermute | solution.py:767
  19.7 0.0 collective-permute-done.2.refs_1_
  19.7 0.1 collective-permute-start.6
  19.8 0.5 %collective-permute-start.7 = (f32[64,256]{1,0:T(8,128)S(1)}, f32[64,256]{1,0:T(8,128)S(1)}, u32[]{:S(2)}, u32[]{:S(2)}) collective-permute-start(f32[64,256]{1,0:T(8,128)S(1)} %get-tuple-element.93), channel_id=1, source_target_pairs={{0,1},{1,0},{2,3},{3,2},{4,5},{5,4},{6,7},{7,6},{8,9},{9,8},{10,11... | collective-permute-start | bytes 196616 | tf_op jit(solution)/shard_map/ppermute | solution.py:741
  20.3 0.1 collective-permute-start.8
  20.4 0.4 %collective-permute-start.9 = (f32[64,256]{1,0:T(8,128)S(1)}, f32[64,256]{1,0:T(8,128)S(1)}, u32[]{:S(2)}, u32[]{:S(2)}) collective-permute-start(f32[64,256]{1,0:T(8,128)S(1)} %get-tuple-element.95), channel_id=1, source_target_pairs={{0,1},{1,0},{2,3},{3,2},{4,5},{5,4},{6,7},{7,6},{8,9},{9,8},{10,11... | collective-permute-start | bytes 196616 | tf_op jit(solution)/shard_map/ppermute | solution.py:741
  20.8 0.8 %shard_map.72 = (f32[5,4,8,512]{3,2,1,0:T(8,128)S(1)}, f32[7,8,512]{2,1,0:T(8,128)S(1)}, f32[3,24,512]{2,1,0:T(8,128)S(1)}, f32[4,24,512]{2,1,0:T(8,128)S(1)}, f...) custom-call(f32[5,4,64,512]{3,2,1,0:T(8,128)S(1)} %get-tuple-element, ...), custom_call_target="tpu_custom_call" | custom-call | flops 1024 | bytes 1024 | tf_op jit(solution)/shard_map/pallas_call | solution.py:26
  21.6 0.0 collective-permute-done.6.refs_0_
  21.6 0.0 collective-permute-done.7.refs_1_
  21.6 0.0 collective-permute-done.8.refs_2_
  21.6 0.1 collective-permute-done.9.refs_3_
  21.7 0.9 %shard_map.76 = (f32[4,2,72,512]{3,2,1,0:T(8,128)S(1)}, f32[2,72,512]{2,1,0:T(8,128)S(1)}, f32[2,72,512]{2,1,0:T(8,128)S(1)}, f32[4,72,512]{2,1,0:T(8,128)S(1)},...) custom-call(f32[5,4,64,512]{3,2,1,0:T(8,128)S(1)} %get-tuple-element, ...), custom_call_target="tpu_custom_call" | custom-call | flops 1024 | bytes 1024 | tf_op jit(solution)/shard_map/pallas_call | solution.py:26
  22.7 0.9 %collective-permute-done.3.off = f32[80,512]{1,0:T(8,128)S(1)} collective-permute-done((f32[80,512]{1,0:T(8,128)S(1)}, f32[80,512]{1,0:T(8,128)S(1)}, u32[]{:S(2)}, u32[]{:S(2)}) %collective-permute-start.3) | collective-permute-done | bytes 163872 | tf_op jit(solution)/shard_map/ppermute | solution.py:744
  23.6 0.4 %shard_map.77 = (f32[4,2,72,512]{3,2,1,0:T(8,128)S(1)}, f32[2,72,512]{2,1,0:T(8,128)S(1)}, f32[2,72,512]{2,1,0:T(8,128)S(1)}, f32[4,72,512]{2,1,0:T(8,128)S(1)},...) custom-call(f32[5,4,64,512]{3,2,1,0:T(8,128)S(1)} %get-tuple-element, ...), custom_call_target="tpu_custom_call", output_to_operand_aliasing={{0}: (17, {}), {1}: (18, {}), {2}: (19, {}), {3}: (20, {}),... | custom-call | flops 1024 | bytes 1024 | tf_op jit(solution)/shard_map/pallas_call | solution.py:26
  24.0 1.7 %collective-permute-start.10 = (f32[72,512]{1,0:T(8,128)S(1)}, f32[72,512]{1,0:T(8,128)S(1)}, u32[]{:S(2)}, u32[]{:S(2)}) collective-permute-start(f32[72,512]{1,0:T(8,128)S(1)} %get-tuple-element.123), channel_id=1, source_target_pairs={{1,4},{5,8},{9,12},{13,0},{4,1},{8,5},{12,9},{0,13},{3,6},{7,10},{... | collective-permute-start | bytes 442376 | tf_op jit(solution)/shard_map/ppermute | solution.py:744
  25.7 0.0 collective-permute-start.11
  25.7 0.3 shard_map.78
  26.0 0.6 %collective-permute-start.12 = (f32[64,512]{1,0:T(8,128)S(1)}, f32[64,512]{1,0:T(8,128)S(1)}, u32[]{:S(2)}, u32[]{:S(2)}) collective-permute-start(f32[64,512]{1,0:T(8,128)S(1)} %get-tuple-element.125), channel_id=1, source_target_pairs={{0,1},{1,0},{2,3},{3,2},{4,5},{5,4},{6,7},{7,6},{8,9},{9,8},{10,11... | collective-permute-start | bytes 393224 | tf_op jit(solution)/shard_map/ppermute | solution.py:741
  26.6 1.9 %collective-permute-start.15 = (f32[64,256]{1,0:T(8,128)S(1)}, f32[64,256]{1,0:T(8,128)S(1)}, u32[]{:S(2)}, u32[]{:S(2)}) collective-permute-start(f32[64,256]{1,0:T(8,128)S(1)} %get-tuple-element.130), channel_id=1, source_target_pairs={{1,4},{5,8},{9,12},{13,0},{4,1},{8,5},{12,9},{0,13},{3,6},{7,10},{... | collective-permute-start | bytes 196616 | tf_op jit(solution)/shard_map/ppermute | solution.py:744
  28.5 0.2 collective-permute-start.16
  28.6 2.0 %shard_map.79 = (f32[4,64,512]{2,1,0:T(8,128)S(1)}, f32[2,64,512]{2,1,0:T(8,128)S(1)}, f32[2,64,512]{2,1,0:T(8,128)S(1)}, f32[2,64,512]{2,1,0:T(8,128)S(1)}, f32...) custom-call(f32[5,4,64,512]{3,2,1,0:T(8,128)S(1)} %get-tuple-element.69.block, ...), custom_call_target="tpu_custom_call" | custom-call | flops 1024 | bytes 1024 | tf_op jit(solution)/shard_map/pallas_call | solution.py:26
  30.6 0.0 collective-permute-done.12.on_p
  30.6 0.0 collective-permute-start.14
  30.6 0.7 %collective-permute-done.10.off_b = f32[72,512]{1,0:T(8,128)S(1)} collective-permute-done((f32[72,512]{1,0:T(8,128)S(1)}, f32[72,512]{1,0:T(8,128)S(1)}, u32[]{:S(2)}, u32[]{:S(2)}) %collective-permute-start.10) | collective-permute-done | bytes 147488 | tf_op jit(solution)/shard_map/ppermute | solution.py:744
  31.3 0.0 collective-permute-done.11.on_b
  31.3 1.0 %shard_map.80 = (f32[7,64,256]{2,1,0:T(8,128)S(1)}, f32[7,64,256]{2,1,0:T(8,128)S(1)}, f32[2,72,512]{2,1,0:T(8,128)}) custom-call(f32[5,4,64,512]{3,2,1,0:T(8,128)S(1)} %get-tuple-element.69.block, f32[5,4,8,512]{3,2,1,0:T(8,128)S(1)} %get-tuple-element.73.ghost, f32[2,72,512]{2,1,0:T(8,128)S(1)} %get-tuple-element.107.edge, ...), custom_call_target="tpu_custom_call" | custom-call | flops 1024 | bytes 1024 | tf_op jit(solution)/shard_map/pallas_call | solution.py:26
  32.3 0.0 copy-start
  32.3 0.0 collective-permute-start.13
  32.3 0.5 %collective-permute-done.15.cross = f32[64,256]{1,0:T(8,128)S(1)} collective-permute-done((f32[64,256]{1,0:T(8,128)S(1)}, f32[64,256]{1,0:T(8,128)S(1)}, u32[]{:S(2)}, u32[]{:S(2)}) %collective-permute-start.15) | collective-permute-done | bytes 65568 | tf_op jit(solution)/shard_map/ppermute | solution.py:744
  32.8 1.0 %collective-permute-done.16.along = f32[64,256]{1,0:T(8,128)S(1)} collective-permute-done((f32[64,256]{1,0:T(8,128)S(1)}, f32[64,256]{1,0:T(8,128)S(1)}, u32[]{:S(2)}, u32[]{:S(2)}) %collective-permute-start.16) | collective-permute-done | bytes 65568 | tf_op jit(solution)/shard_map/ppermute | solution.py:748
  33.8 0.0 collective-permute-done.14.got_inner
  33.8 0.3 collective-permute-done.13.got
  34.1 0.0 copy-done
  34.1 1.0 %shard_map.82 = (f32[8,64,256]{2,1,0:T(8,128)}, f32[8,64,256]{2,1,0:T(8,128)}) custom-call(s32[8,64,256]{2,1,0:T(8,128)S(1)} %copy-done, f32[7,64,256]{2,1,0:T(8,128)S(1)} %get-tuple-element.126.keep, f32[7,64,256]{2,1,0:T(8,128)S(1)} %collective-permute-done.13.got, f32[2,64,256]{2,1,0:T(8,128)S(1)} %get-tuple-element.128.keep_inner, ...), custom_call_target="tpu_custom_call" | custom-call | flops 1024 | bytes 1024 | tf_op jit(solution)/shard_map/pallas_call | solution.py:26
  (3 shorter events, 0.1 us)
Async XLA Ops:
  2.6 6.9 %collective-permute-start = (f32[5,6,64,256]{3,2,1,0:T(8,128)S(1)}, f32[5,6,64,256]{3,2,1,0:T(8,128)S(1)}, u32[]{:S(2)}, u32[]{:S(2)}) collective-permute-start(f32[5,6,64,256]{3,2,1,0:T(8,128)S(1)} %get-tuple-element.68), channel_id=1, source_target_pairs={{0,1},{1,0},{2,3},{3,2},{4,5},{5,4},{6,7},{7,6},{8,9},{9,8},{10,11... | collective-permute-start | bytes 5898248 | tf_op jit(solution)/shard_map/ppermute | solution.py:741
  3.1 12.9 %collective-permute-start.4 = (f32[4,64,256]{2,1,0:T(8,128)S(1)}, f32[4,64,256]{2,1,0:T(8,128)S(1)}, u32[]{:S(2)}, u32[]{:S(2)}) collective-permute-start(f32[4,64,256]{2,1,0:T(8,128)S(1)} %get-tuple-element.90), channel_id=1, source_target_pairs={{0,4},{4,8},{8,12},{12,0},{1,5},{5,9},{9,13},{13,1},{2,6},{6,10},{... | collective-permute-start | bytes 786440 | tf_op jit(solution)/shard_map/ppermute | solution.py:766
  5.7 14.0 %collective-permute-start.5 = (f32[4,64,256]{2,1,0:T(8,128)S(1)}, f32[4,64,256]{2,1,0:T(8,128)S(1)}, u32[]{:S(2)}, u32[]{:S(2)}) collective-permute-start(f32[4,64,256]{2,1,0:T(8,128)S(1)} %get-tuple-element.91), channel_id=1, source_target_pairs={{4,0},{8,4},{12,8},{0,12},{5,1},{9,5},{13,9},{1,13},{6,2},{10,6},{... | collective-permute-start | bytes 786440 | tf_op jit(solution)/shard_map/ppermute | solution.py:767
  9.7 4.7 %collective-permute-start.1 = (f32[4,8,512]{2,1,0:T(8,128)S(1)}, f32[4,8,512]{2,1,0:T(8,128)S(1)}, u32[]{:S(2)}, u32[]{:S(2)}) collective-permute-start(f32[4,8,512]{2,1,0:T(8,128)S(1)} %get-tuple-element.71), channel_id=1, source_target_pairs={{0,2},{2,0},{1,3},{3,1},{4,6},{6,4},{5,7},{7,5},{8,10},{10,8},{9,1... | collective-permute-start | bytes 196616 | tf_op jit(solution)/shard_map/ppermute | solution.py:754
  11.4 8.3 %collective-permute-start.2 = (f32[10,8,512]{2,1,0:T(8,128)S(1)}, f32[10,8,512]{2,1,0:T(8,128)S(1)}, u32[]{:S(2)}, u32[]{:S(2)}) collective-permute-start(f32[10,8,512]{2,1,0:T(8,128)S(1)} %get-tuple-element.72), channel_id=1, source_target_pairs={{0,2},{2,0},{1,3},{3,1},{4,6},{6,4},{5,7},{7,5},{8,10},{10,8},{9,1... | collective-permute-start | bytes 491528 | tf_op jit(solution)/shard_map/ppermute | solution.py:754
  15.2 8.3 %collective-permute-start.3 = (f32[80,512]{1,0:T(8,128)S(1)}, f32[80,512]{1,0:T(8,128)S(1)}, u32[]{:S(2)}, u32[]{:S(2)}) collective-permute-start(f32[80,512]{1,0:T(8,128)S(1)} %get-tuple-element.75), channel_id=1, source_target_pairs={{1,4},{5,8},{9,12},{13,0},{4,1},{8,5},{12,9},{0,13},{3,6},{7,10},{... | collective-permute-start | bytes 491528 | tf_op jit(solution)/shard_map/ppermute | solution.py:744
  19.7 1.9 %collective-permute-start.6 = (f32[64,256]{1,0:T(8,128)S(1)}, f32[64,256]{1,0:T(8,128)S(1)}, u32[]{:S(2)}, u32[]{:S(2)}) collective-permute-start(f32[64,256]{1,0:T(8,128)S(1)} %get-tuple-element.92), channel_id=1, source_target_pairs={{0,1},{1,0},{2,3},{3,2},{4,5},{5,4},{6,7},{7,6},{8,9},{9,8},{10,11... | collective-permute-start | bytes 196616 | tf_op jit(solution)/shard_map/ppermute | solution.py:741
  19.8 1.8 %collective-permute-start.7 = (f32[64,256]{1,0:T(8,128)S(1)}, f32[64,256]{1,0:T(8,128)S(1)}, u32[]{:S(2)}, u32[]{:S(2)}) collective-permute-start(f32[64,256]{1,0:T(8,128)S(1)} %get-tuple-element.93), channel_id=1, source_target_pairs={{0,1},{1,0},{2,3},{3,2},{4,5},{5,4},{6,7},{7,6},{8,9},{9,8},{10,11... | collective-permute-start | bytes 196616 | tf_op jit(solution)/shard_map/ppermute | solution.py:741
  20.3 1.3 %collective-permute-start.8 = (f32[64,256]{1,0:T(8,128)S(1)}, f32[64,256]{1,0:T(8,128)S(1)}, u32[]{:S(2)}, u32[]{:S(2)}) collective-permute-start(f32[64,256]{1,0:T(8,128)S(1)} %get-tuple-element.94), channel_id=1, source_target_pairs={{0,1},{1,0},{2,3},{3,2},{4,5},{5,4},{6,7},{7,6},{8,9},{9,8},{10,11... | collective-permute-start | bytes 196616 | tf_op jit(solution)/shard_map/ppermute | solution.py:741
  20.4 1.3 %collective-permute-start.9 = (f32[64,256]{1,0:T(8,128)S(1)}, f32[64,256]{1,0:T(8,128)S(1)}, u32[]{:S(2)}, u32[]{:S(2)}) collective-permute-start(f32[64,256]{1,0:T(8,128)S(1)} %get-tuple-element.95), channel_id=1, source_target_pairs={{0,1},{1,0},{2,3},{3,2},{4,5},{5,4},{6,7},{7,6},{8,9},{9,8},{10,11... | collective-permute-start | bytes 196616 | tf_op jit(solution)/shard_map/ppermute | solution.py:741
  24.0 7.3 %collective-permute-start.10 = (f32[72,512]{1,0:T(8,128)S(1)}, f32[72,512]{1,0:T(8,128)S(1)}, u32[]{:S(2)}, u32[]{:S(2)}) collective-permute-start(f32[72,512]{1,0:T(8,128)S(1)} %get-tuple-element.123), channel_id=1, source_target_pairs={{1,4},{5,8},{9,12},{13,0},{4,1},{8,5},{12,9},{0,13},{3,6},{7,10},{... | collective-permute-start | bytes 442376 | tf_op jit(solution)/shard_map/ppermute | solution.py:744
  25.7 5.6 %collective-permute-start.11 = (f32[72,512]{1,0:T(8,128)S(1)}, f32[72,512]{1,0:T(8,128)S(1)}, u32[]{:S(2)}, u32[]{:S(2)}) collective-permute-start(f32[72,512]{1,0:T(8,128)S(1)} %get-tuple-element.124), channel_id=1, source_target_pairs={{0,1},{1,0},{2,3},{3,2},{4,5},{5,4},{6,7},{7,6},{8,9},{9,8},{10,11... | collective-permute-start | bytes 442376 | tf_op jit(solution)/shard_map/ppermute | solution.py:741
  26.0 4.6 %collective-permute-start.12 = (f32[64,512]{1,0:T(8,128)S(1)}, f32[64,512]{1,0:T(8,128)S(1)}, u32[]{:S(2)}, u32[]{:S(2)}) collective-permute-start(f32[64,512]{1,0:T(8,128)S(1)} %get-tuple-element.125), channel_id=1, source_target_pairs={{0,1},{1,0},{2,3},{3,2},{4,5},{5,4},{6,7},{7,6},{8,9},{9,8},{10,11... | collective-permute-start | bytes 393224 | tf_op jit(solution)/shard_map/ppermute | solution.py:741
  26.6 6.2 %collective-permute-start.15 = (f32[64,256]{1,0:T(8,128)S(1)}, f32[64,256]{1,0:T(8,128)S(1)}, u32[]{:S(2)}, u32[]{:S(2)}) collective-permute-start(f32[64,256]{1,0:T(8,128)S(1)} %get-tuple-element.130), channel_id=1, source_target_pairs={{1,4},{5,8},{9,12},{13,0},{4,1},{8,5},{12,9},{0,13},{3,6},{7,10},{... | collective-permute-start | bytes 196616 | tf_op jit(solution)/shard_map/ppermute | solution.py:744
  28.5 5.4 %collective-permute-start.16 = (f32[64,256]{1,0:T(8,128)S(1)}, f32[64,256]{1,0:T(8,128)S(1)}, u32[]{:S(2)}, u32[]{:S(2)}) collective-permute-start(f32[64,256]{1,0:T(8,128)S(1)} %get-tuple-element.131), channel_id=1, source_target_pairs={{0,12},{1,5},{4,0},{5,9},{8,4},{9,13},{12,8},{13,1},{2,14},{3,7},{... | collective-permute-start | bytes 196616 | tf_op jit(solution)/shard_map/ppermute | solution.py:748
  30.6 3.2 %collective-permute-start.14 = (f32[2,64,256]{2,1,0:T(8,128)S(1)}, f32[2,64,256]{2,1,0:T(8,128)S(1)}, u32[]{:S(2)}, u32[]{:S(2)}) collective-permute-start(f32[2,64,256]{2,1,0:T(8,128)S(1)} %get-tuple-element.129), channel_id=1, source_target_pairs={{0,1},{1,0},{2,3},{3,2},{4,5},{5,4},{6,7},{7,6},{8,9},{9,8},{10,11... | collective-permute-start | bytes 393224 | tf_op jit(solution)/shard_map/ppermute | solution.py:741
  32.3 1.8 %copy-start = (s32[8,64,256]{2,1,0:T(8,128)S(1)}, s32[8,64,256]{2,1,0:T(8,128)}, u32[]{:S(2)}) copy-start(s32[8,64,256]{2,1,0:T(8,128)} %labels.5) | copy-start | bytes 1572868
  32.3 1.8 %collective-permute-start.13 = (f32[7,64,256]{2,1,0:T(8,128)S(1)}, f32[7,64,256]{2,1,0:T(8,128)S(1)}, u32[]{:S(2)}, u32[]{:S(2)}) collective-permute-start(f32[7,64,256]{2,1,0:T(8,128)S(1)} %get-tuple-element.127), channel_id=1, source_target_pairs={{0,1},{1,0},{2,3},{3,2},{4,5},{5,4},{6,7},{7,6},{8,9},{9,8},{10,11... | collective-permute-start | bytes 1376264 | tf_op jit(solution)/shard_map/ppermute | solution.py:741

commit v6 on v5

--- a/solution.py
+++ b/solution.py
@@ -14,8 +14,9 @@
 HALO = 4
 TILE = 8
 SWEPT = 11
-PACK_FLOPS = 700000000
-FLOPS = 100000000000
+LAST_FLOPS = 10000000000
+PACK_FLOPS = 1100000000
+FLOPS = 2200000000
 S, C, T, F, K = range(5)
 ONE = 4
 
@@ -87,6 +88,41 @@
         return len(self.places)
 
 
+class Draft:
+    def __init__(self, ref, values=None, prefix=()):
+        self.ref, self.prefix = ref, prefix
+        self.values = {} if values is None else values
+        self.shape = ref.shape[len(prefix) :]
+
+    @property
+    def at(self):
+        return _At(self)
+
+    def _key(self, key):
+        return self.prefix + (key if isinstance(key, tuple) else (key,))
+
+    def __getitem__(self, key):
+        key = self._key(key)
+        name = key[:-1] + (key[-1].start,)
+        return self.values[name][1] if name in self.values else self.ref[key]
+
+    def __setitem__(self, key, value):
+        key = self._key(key)
+        self.values[key[:-1] + (key[-1].start,)] = (key, value)
+
+    def flush(self):
+        for key, value in self.values.values():
+            self.ref[key] = value
+
+
+class _At:
+    def __init__(self, draft):
+        self.draft = draft
+
+    def __getitem__(self, key):
+        return Draft(self.draft.ref, self.draft.values, self.draft._key(key))
+
+
 def whole(ref):
     return Tiles(*[(ref, t) for t in range(ref.shape[0] // TILE)])
 
@@ -97,6 +133,11 @@
 
 def mid_and_rim(mid, rim):
     return Tiles((rim, 0), *[(mid, t) for t in range(mid.shape[0] // TILE)], (rim, 1), (rim, 2))
+
+
+def put(ref, values):
+    for t, value in enumerate(values):
+        ref[at(t)] = value
 
 
 class Across:
@@ -433,7 +474,7 @@
 
 def choose_half(up, down, *refs):
     for j in range(4):
-        refs[j - 4][...] = jnp.where(lax.axis_index("gz") == 0, down[j], up[j])
+        refs[j // 2 - 2][j % 2] = jnp.where(lax.axis_index("gz") == 0, down[j], up[j])
 
 
 def coefficients(refs):
@@ -446,8 +487,8 @@
     ny, narrow = up.shape[1], up.shape[2]
     outside, inside = core, 1 - core
     for j in range(4):
-        side[j, outside, 0:ny, 0:narrow] = jnp.where(core == 0, up[j], passed[j][...])
-        side[j, outside, 0:ny, narrow : 2 * narrow] = jnp.where(core == 0, passed[j][...], down[j])
+        side[j, outside, 0:ny, 0:narrow] = jnp.where(core == 0, up[j], passed[j // 2][j % 2])
+        side[j, outside, 0:ny, narrow : 2 * narrow] = jnp.where(core == 0, passed[j // 2][j % 2], down[j])
         side[j, inside, 0:ny] = near[j]
         side[j, inside, ny : ny + TILE] = near_ghost[j]
 
@@ -462,7 +503,9 @@
     else:
         ghosts = {j: off[at(first + j)] for j in range(5)}
     for j in range(4):
-        side[j, outside, ny : ny + TILE] = ghosts[j]
+        for which in range(2):
+            place = (j, which, slice(ny, ny + TILE))
+            side[place] = jnp.where(outside == which, ghosts[j], side[place])
     return ghosts[ONE]
 
 
@@ -536,15 +579,16 @@
 
 
 def middle(block, ghost, near, near_ghost, up, down, *refs):
-    passed, weights, outs = refs[:4], coefficients(refs[4:18]), refs[18:]
+    passed, weights, outs = refs[:2], coefficients(refs[2:16]), refs[16:]
     fill_sides(near, near_ghost, up, down, passed, outs[0])
     sweep(False, block, ghost, weights, *outs)
 
 
 def outward(two, block, ghost, off, *refs):
     weights, one_mid, one_rim = coefficients(refs[:14]), refs[6], refs[13]
-    outs = refs[14 + SWEPT : 14 + 2 * SWEPT]
-    hot2, sa, b2, off_b, on_b = refs[14 + 2 * SWEPT :]
+    outs = [Draft(ref) for ref in refs[14 + SWEPT : 14 + 2 * SWEPT]]
+    *ends, off_b = refs[14 + 2 * SWEPT :]
+    hot2, sa, b2 = (Draft(ref) for ref in ends)
     side, edge, add, _, known, linear, *_ = outs
     core = lax.axis_index("gz")
     half, ny = block.shape[1], block.shape[2]
@@ -567,28 +611,61 @@
             hot2[which, at(t)] = hot
             sa[which, at(t)] = total
             b2[which, at(t)] = total * rc
-    off_b[...] = b2[core]
-    on_b[...] = b2[1 - core]
-
-
-def outward_first(ky_mid, kz_mid, ky_rim, kz_rim, adjoint, inward, sa, b2, fa, on_p, cross, along):
-    core = lax.axis_index("gz")
-    half, (ny, nz) = adjoint.shape[0], cross.shape
+    for t in range(count + 1):
+        off_b[at(t)] = jnp.where(core == 0, b2[0, at(t)], b2[1, at(t)])
+    for draft in (b2, sa, hot2, *outs):
+        draft.flush()
+
+
+def inside_adjoint(block, ghost, near, near_ghost, *refs):
+    (kx, ky, kz, diag, part, back), on_b = coefficients(refs[:14]), refs[14]
+    core = lax.axis_index("gz")
+    half, ny = block.shape[1], block.shape[2]
+    last = half - 1
+    i = (1 - core) * last
+    beside = i - 1 + 2 * core
+    own = lambda j, plane: with_ghost(block.at[j, plane], ghost.at[j, plane])
+    c_h, s_h, t_h, f_h = (with_ghost(near.at[j], near_ghost.at[j]) for j in (C, S, T, F))
+    one = mid_and_rim(refs[6], refs[13])
+    s, c, a, f, k = (own(j, i) for j in (S, C, T, F, K))
+    above, below = jnp.where(core == 0, time_step, 0.0), jnp.where(core == 0, 0.0, time_step)
+    step, next_first = kx((1 - core) * (last - 1)), part(beside)
+    faces, first = [], []
+    for t in range(ny // TILE + 1):
+        faces.append((c[t] + c_h[t]) * scale)
+        first.append(part(i)[t] + (0.5 + f[t]) * ((faces[t] + below * f[t]) * s_h[t] - faces[t] * s[t]))
+    flow = Across(ky(i), kz(i), Made(first))
+    out = []
+    for t in range(ny // TILE + 1):
+        rc, sink, face = 0.5 + f[t], time_step * k[t], faces[t]
+        rate = flow[t] - (diag(i)[t] + face) * first[t] - sink * jnp.tanh(first[t])
+        rate = rate + (step[t] + above * f[t]) * next_first[t] + (face + below * f[t]) * one[t]
+        hot = jnp.tanh(0.75 * s[t] + 0.25 * (first[t] + rc * rate))
+        b = a[t] * rc
+        total = back(i)[t] + (face + above * f_h[t]) * (t_h[t] * (0.5 + f_h[t])) - face * b
+        out.append((2.0 / 3.0) * (total - sink * (1.0 - hot * hot) * b) * rc)
+    put(on_b, out)
+
+
+def outward_first(ky_mid, kz_mid, ky_rim, kz_rim, adjoint, inward, sa, b2, fa, along, cross):
+    core = lax.axis_index("gz")
+    half, ny = adjoint.shape[0], along.shape[0]
+    values = []
     for which, i in ((0, 0), (1, half - 1)):
         b = whole(b2.at[which])
         flow = Across(mid_and_rim(ky_mid.at[i], ky_rim.at[i]), mid_and_rim(kz_mid.at[i], kz_rim.at[i]), b)
-        for t in range(len(b)):
-            total = sa[which, at(t)] + flow[t] - adjoint[i, at(t)] * b[t] + inward[which, at(t)]
-            fa[which, at(t)] = 0.25 * total
-    on_p[...] = fa[1 - core, 0:ny]
+        total = lambda t: sa[which, at(t)] + flow[t] - adjoint[i, at(t)] * b[t] + inward[which, at(t)]
+        values.append([0.25 * total(t) for t in range(len(b))])
+    low, high = values
     for t in range(ny // TILE):
-        along[at(t)], cross[at(t)] = halves(core, fa[core, at(t)])
+        along[at(t)], cross[at(t)] = halves(core, jnp.where(core == 0, low[t], high[t]))
+    for which in range(2):
+        put(fa.at[which], values[which])
 
 
 def inner(block, ghost, edge, side, first, adjoint, sa_in, b2_in, hot2_in, sa_out, b2_out, hot2_out, fa_out, *refs):
     kx, ky, kz, diag, _, _ = coefficients(refs[:14])
-    value, term, adjoint0, hot0, keep, give, fa, b3 = refs[14:]
-    core = lax.axis_index("gz")
+    value, term, adjoint0, hot0, fa, b3 = refs[14:]
     half, ny = block.shape[1], block.shape[2]
     count, last = ny // TILE, half - 1
     own = lambda j, i: with_ghost(block.at[j, i], ghost.at[j, i])
@@ -628,12 +705,9 @@
             value[i, at(t)] = total
             first_hot = jnp.tanh(first[i, at(t)])
             total = (2.0 / 3.0) * hot2(i)[t] * a[t] + 0.25 * first_hot * sa(i)[t] + hot * fa[i, at(t)]
-            total = -time_step * (0.5 + f[t]) * total
-            if 0 < i < last:
-                keep[i - 1, at(t)], give[i - 1, at(t)] = halves(core, total)
-            else:
+            term[i, at(t)] = -time_step * (0.5 + f[t]) * total
+            if i == 0 or i == last:
                 which = 0 if i == 0 else 1
-                term[which, at(t)] = total
                 adjoint0[which, at(t)] = full
                 hot0[which, at(t)] = -time_step * (0.5 + f[t]) * hot
 
@@ -644,55 +718,67 @@
     return jnp.where(core == 0, left, right), jnp.where(core == 0, right, left)
 
 
-def finish(block, ghost, edge, side, b2_out, value, term, adjoint0, hot0, off_b, on_b, on_p, *refs):
-    kx_mid, ky_mid, kz_mid, kx_rim, ky_rim, kz_rim, keep, give, late = refs
-    core = lax.axis_index("gz")
+def from_beyond(which, message, block, ghost, edge, side, b2_out, value, term, adjoint0, hot0, weights):
+    kx, ky, kz = weights
     half, ny = block.shape[1], block.shape[2]
     count, last = ny // TILE, half - 1
-    own = lambda j, i: with_ghost(block.at[j, i], ghost.at[j, i])
-    both = lambda mid, rim: lambda i: mid_and_rim(mid.at[i], rim.at[i])
-    kx, ky, kz = both(kx_mid, kx_rim), both(ky_mid, ky_rim), both(kz_mid, kz_rim)
+    i = which * last
+    beside = i + 1 - 2 * which
+    wind = jnp.where(which == 1, time_step, 0.0)
+    against = time_step - wind
+    f = with_ghost(block.at[F, i], ghost.at[F, i])
+    into, gains, late = [], [], []
+    for t in range(count + 1):
+        into.append(edge[which, at(t)] + wind * side[F, which, at(t)])
+        gains.append(0.25 * into[t] * message[at(t)])
+        late.append(gains[t] * (0.5 + f[t]))
+    flow = Across(ky(i), kz(i), Made(late))
+    step = kx(which * (last - 1))
+    out = []
+    for t in range(count):
+        factor = into[t] * (0.5 + side[F, which, at(t)])
+        known = 0.25 * (edge[which, at(t)] + against * f[t]) * b2_out[which, at(t)]
+        total = value[i, at(t)] + gains[t] + flow[t] - adjoint0[which, at(t)] * late[t] + factor * known
+        next_total = value[beside, at(t)] + (step[t] + wind * f[t]) * late[t]
+        out.append((t, total, next_total, term[i, at(t)] + hot0[which, at(t)] * gains[t], factor))
+    return out
+
+
+def three(refs):
+    return [lambda i, m=m, r=r: mid_and_rim(m.at[i], r.at[i]) for m, r in zip(refs[:3], refs[3:])]
+
+
+def finish_inside(block, ghost, edge, side, b2_out, value, term, adjoint0, hot0, on_b, *refs):
+    *six, keep, give = refs
+    core = lax.axis_index("gz")
+    half, ny = block.shape[1], block.shape[2]
+    plane = lambda r: core * (half - 1) + r * (1 - 2 * core)
 
     def write(place, t, value):
         keep[place, at(t)], give[place, at(t)] = halves(core, value)
 
-    gains, factors = {}, {}
-    for which, i in ((0, 0), (1, last)):
-        mine = core == which
-        f = own(F, i)
-        for t in range(count + 1):
-            face = edge[which, at(t)]
-            if which == 1:
-                face = face + time_step * side[F, 1, at(t)]
-            gain = 0.25 * face * jnp.where(mine, off_b[at(t)], on_b[at(t)])
-            late[which, at(t)] = gain * (0.5 + f[t])
-            gains[which, t] = gain
-    for which, i in ((0, 0), (1, last)):
-        mine = core == which
-        flow = Across(ky(i), kz(i), whole(late.at[which]))
-        for t in range(count):
-            face, f_out = edge[which, at(t)], side[F, which, at(t)]
-            into, out_of = face, face
-            if which == 0:
-                out_of = out_of + time_step * own(F, 0)[t]
-            else:
-                into = into + time_step * f_out
-            total = value[i, at(t)] + gains[which, t] + flow[t] - adjoint0[which, at(t)] * late[which, at(t)]
-            into = into * (0.5 + f_out)
-            known = 0.25 * out_of * b2_out[which, at(t)]
-            write(2 + i, t, total + into * jnp.where(mine, known, known + on_p[at(t)]))
-            write(which, t, term[which, at(t)] + hot0[which, at(t)] * gains[which, t])
-            factors[which, t] = into
-    for t in range(count):
-        write(2 + half, t, jnp.where(core == 0, factors[0, t], factors[1, t]))
-    for i in range(1, last):
-        for t in range(count):
-            total = value[i, at(t)]
-            if i == 1:
-                total = total + kx(0)[t] * late[0, at(t)]
-            if i == last - 1:
-                total = total + (kx(last - 1)[t] + time_step * own(F, last)[t]) * late[1, at(t)]
-            write(2 + i, t, total)
+    parts = from_beyond(1 - core, on_b, block, ghost, edge, side, b2_out, value, term, adjoint0, hot0, three(six))
+    for t, total, next_total, sink, factor in parts:
+        write(half - 3, t, total)
+        write(half - 4, t, next_total)
+        write(2 * half - 4, t, sink)
+        write(2 * half - 2, t, factor)
+        for r in range(2, half - 2):
+            write(r - 2, t, value[plane(r), at(t)])
+        for r in range(1, half - 1):
+            write(half - 3 + r, t, term[plane(r), at(t)])
+        wind = jnp.where(core == 1, time_step, 0.0)
+        f_out = side[F, core, at(t)]
+        write(2 * half - 3, t, (edge[core, at(t)] + wind * f_out) * (0.5 + f_out))
+
+
+def finish_outside(block, ghost, edge, side, b2_out, value, term, adjoint0, hot0, off_b, *refs):
+    *six, fa_out, _, keep, give = refs
+    core = lax.axis_index("gz")
+    parts = from_beyond(core, off_b, block, ghost, edge, side, b2_out, value, term, adjoint0, hot0, three(six))
+    for t, total, next_total, sink, _ in parts:
+        for place, value_here in enumerate((total, next_total, sink, fa_out[1 - core, at(t)])):
+            keep[place, at(t)], give[place, at(t)] = halves(core, value_here)
 
 
 def take(cross, along, cross_out, along_out):
@@ -700,27 +786,32 @@
     along_out[...] = along[...]
 
 
-def assemble(labels, keep, got, keep_inner, got_inner, cross, along, grad_state, grad_sink, masked, outer, sems):
+def assemble(labels, keep, got, keep_last, got_last, along, cross, grad_state, grad_sink, *refs):
+    masked, ends, sems = refs
     core = lax.axis_index("gz")
     count = grad_state.shape[0]
     half = count // 2
-    sides = ((core, keep, keep_inner, cross), (1 - core, got, got_inner, along))
     copies = []
 
     def send(source, target):
         copies.append(pltpu.make_async_copy(source, target, sems.at[len(copies)]))
         copies[-1].start()
 
-    for who, source, _, _ in sides:
-        skip = 1 - who
-        send(source.at[pl.ds(2 + skip, half - 1)], grad_state.at[pl.ds(who * half + skip, half - 1)])
-    for slot, (who, source, inside, adjoint) in enumerate(sides):
-        plane = who * (count - 1)
-        outer[slot] = source[2 + who * (half - 1)] + source[2 + half] * adjoint[...]
-        send(outer.at[slot], grad_state.at[plane])
-        for i in range(half):
-            term = source[0] if i == 0 else source[1] if i == half - 1 else inside[i - 1]
-            masked[slot, i] = jnp.where(touching(labels[who * half + i]), term, 0.0)
+    sides = ((core, keep, keep_last, got_last.at[3], cross), (1 - core, got, got_last, keep_last.at[3], along))
+    plane = lambda who, r: who * (count - 1) + r * (1 - 2 * who)
+    for who, most, outermost, _, _ in sides:
+        send(outermost.at[1], grad_state.at[plane(who, 1)])
+        for r in range(2, half - 1):
+            send(most.at[r - 2], grad_state.at[plane(who, r)])
+    for slot, (who, most, outermost, inside, outside) in enumerate(sides):
+        ends[slot, 0] = outermost[0] + most[2 * half - 3] * outside[...]
+        send(ends.at[slot, 0], grad_state.at[plane(who, 0)])
+        ends[slot, 1] = most[half - 3] + most[2 * half - 2] * inside[...]
+        send(ends.at[slot, 1], grad_state.at[plane(who, half - 1)])
+        for r in range(half):
+            term = outermost[2] if r == 0 else most[half - 3 + r]
+            place = plane(who, r)
+            masked[slot, place - who * half] = jnp.where(touching(labels[place]), term, 0.0)
         send(masked.at[slot], grad_sink.at[pl.ds(who * half, half)])
     for copy in copies:
         copy.wait()
@@ -730,7 +821,7 @@
     count, ny, nz = state.shape
     half, wide, rows = count // 2, 2 * nz, ny + TILE
     count_x, count_y = lax.axis_size("gx"), lax.axis_size("gy")
-    assert lax.axis_size("gz") == 2 and half >= 3 and ny % TILE == 0 and ny >= 3 * TILE
+    assert lax.axis_size("gz") == 2 and half >= 4 and ny % TILE == 0 and ny >= 3 * TILE
     two = count_y == 2
     ahead = [(i, (i + 1) % count_x) for i in range(count_x)]
     behind = [(b, a) for a, b in ahead]
@@ -781,41 +872,43 @@
         functools.partial(pack_off, two, count_y), [(ny + (len(PACKED) if two else 5) * TILE, wide), (7, TILE, wide)],
         block, mids[4], *rims[:ways], flops=PACK_FLOPS,
     )
-    passed = call(choose_half, [(ny, nz)] * 4, up, down, *rims)
-    passed = [swap_cores(x) for x in passed]
     off = swap_chips(off)
     own, outer = (half, rows, wide), (2, rows, wide)
+    (on_b,) = call(inside_adjoint, [(rows, wide)], block, ghost, near, near_ghost, *mids, *edges)
+    passed = [swap_cores(x) for x in call(choose_half, [(2, ny, nz)] * 2, up, down, on_b)]
+    on_b = swap_cores(on_b)
     swept_shapes = [(4, 2, rows, wide), outer, outer, own, outer, outer, own, own, own, own, outer]
     assert len(swept_shapes) == SWEPT
     swept = call(middle, swept_shapes, block, ghost, near, near_ghost, up, down, *passed, *mids, *edges)
     ends, mains = (rows, wide), (ny, wide)
-    *swept, hot2_out, sa_out, b2_out, off_b, on_b = call(
-        functools.partial(outward, two), swept_shapes + [outer] * 3 + [ends] * 2, block, ghost, off, *mids, *edges, *swept,
+    *swept, hot2_out, sa_out, b2_out, off_b = call(
+        functools.partial(outward, two), swept_shapes + [outer] * 3 + [ends], block, ghost, off, *mids, *edges, *swept,
         aliases={17 + i: i for i in range(SWEPT)},
     )
     side, edge, add, first, known, linear, adjoint, sa, b2, hot2, inward = swept
-    off_b, on_b = swap_chips(off_b), swap_cores(on_b)
-    fa_out, on_p, cross, along = call(
-        outward_first, [outer, mains, (ny, nz), (ny, nz)],
+    off_b = swap_chips(off_b)
+    half_plane = (ny, nz)
+    fa_out, along, cross = call(
+        outward_first, [outer] + [half_plane] * 2,
         mids[1], mids[2], edges[1], edges[2], adjoint, inward, sa_out, b2_out,
     )
-    on_p, cross, along = swap_cores(on_p), swap_chips(cross), to_slabs(along)
+    cross, along = swap_chips(cross), to_slabs(along)
     main = lambda planes: (planes, ny, wide)
     planes = lambda many: (many, ny, nz)
-    value, term, adjoint0, hot0, keep_inner, give_inner, _, _ = call(
-        inner, [main(half), main(2), main(2), main(2), planes(half - 2), planes(half - 2), own, own],
+    value, term, adjoint0, hot0, _, _ = call(
+        inner, [main(half), main(half), main(2), main(2), own, own],
         block, ghost, edge, side, first, adjoint, sa, b2, hot2, sa_out, b2_out, hot2_out, fa_out, *mids, *edges,
     )
-    got_inner = swap_cores(give_inner)
-    keep, give, _ = call(
-        finish, [planes(half + 3), planes(half + 3), outer],
-        block, ghost, edge, side, b2_out, value, term, adjoint0, hot0, off_b, on_b, on_p, *mids[:3], *edges[:3],
-    )
+    ready = (block, ghost, edge, side, b2_out, value, term, adjoint0, hot0)
+    keep, give = call(finish_inside, [planes(2 * half - 1)] * 2, *ready, on_b, *mids[:3], *edges[:3])
     got = swap_cores(give)
-    cross, along = call(take, [(ny, nz)] * 2, cross, along, flops=FLOPS)
+    keep_last, give_last = call(finish_outside, [planes(4)] * 2, *ready, off_b, *mids[:3], *edges[:3], fa_out, keep, flops=LAST_FLOPS)
+    got_last = swap_cores(give_last)
+    cross, along = call(take, [half_plane] * 2, cross, along, flops=FLOPS)
     grad_state, grad_sink = call(
-        assemble, [state.shape, state.shape], labels, keep, got, keep_inner, got_inner, cross, along, keep=False,
-        scratch=[pltpu.VMEM((2, half, ny, nz), jnp.float32), pltpu.VMEM((2, ny, nz), jnp.float32), pltpu.SemaphoreType.DMA((6,))],
+        assemble, [state.shape, state.shape],
+        labels, keep, got, keep_last, got_last, along, cross, keep=False,
+        scratch=[pltpu.VMEM((2, half, ny, nz), jnp.float32), pltpu.VMEM((2, 2, ny, nz), jnp.float32), pltpu.SemaphoreType.DMA((2 * half + 4,))],
     )
     return (grad_state, grad_sink)
 

time: 35.3 us -> 35.2 us (level)
  starting transfers between devices: 13.5 us -> 12.7 us
  waiting for transfers between devices: 8.48 us -> 9.21 us
    ppermute x1, waiting for transfers between devices: 3.76 us -> 0.96 us  [on_device(): down = lax.ppermute(down, 'gx', behind)]
    ppermute x2, waiting for transfers between devices: 1.18 us -> 2.83 us  [along_y(): lax.ppermute(rim, 'gy', routes[i % len(routes)])]
    ppermute x3, waiting for transfers between devices: 2.14 us -> 3.6 us  [swap_chips(): return lax.ppermute(x, ('gx', 'gz'), chips)]
    ppermute x9 -> x6, starting transfers between devices: 2.17 us -> 1.31 us  [swap_cores(): return lax.ppermute(x, 'gz', [(0, 1), (1, 0)])]
    ppermute x9 -> x6, waiting for transfers between devices: 0.37 us -> 0.96 us  [swap_cores(): return lax.ppermute(x, 'gz', [(0, 1), (1, 0)])]
    pallas_call x15 -> x17, Pallas kernels: 12.4 us -> 12.3 us  [call(): pl.pallas_call(kernel, out_shape=[space(shape, jnp.float32) for shape in...]
  transfers between devices with their start and end apart: 17 -> 14, of which waited for: 8 -> 9; matrix products, arithmetic and copies ran while one was open for 0% -> 0% of each run, Pallas kernels for 26% -> 27%
where the time goes in v6:
time: 35.2 us; the launch traced here: 35 us
  starting transfers between devices  12.7 us (36%)
  Pallas kernels  12.3 us (35%)
  waiting for transfers between devices  9.21 us (26%)
  between operations  0.79 us (2%)
    pallas_call x17, Pallas kernels, call(): pl.pallas_call(kernel, out_shape=[space(shape, jnp.float32) for shape in...  12.3 us
    ppermute x3, starting transfers between devices, swap_chips(): return lax.ppermute(x, ('gx', 'gz'), chips)  4.38 us
    ppermute x3, waiting for transfers between devices, swap_chips(): return lax.ppermute(x, ('gx', 'gz'), chips)  3.6 us
    ppermute x2, waiting for transfers between devices, along_y(): lax.ppermute(rim, 'gy', routes[i % len(routes)])  2.83 us
    ppermute x1, starting transfers between devices, on_device(): up = lax.ppermute(up, 'gx', ahead)  2.64 us
    ppermute x1, starting transfers between devices, on_device(): down = lax.ppermute(down, 'gx', behind)  2.11 us
    ppermute x2, starting transfers between devices, along_y(): lax.ppermute(rim, 'gy', routes[i % len(routes)])  2.09 us
    ppermute x6, starting transfers between devices, swap_cores(): return lax.ppermute(x, 'gz', [(0, 1), (1, 0)])  1.31 us
  transfers between devices with their start and end apart: 14, of which 9 were waited for; matrix products, arithmetic and copies ran while one was open for 0% of the time, Pallas kernels for 27%

profile of v6, /device:TPU:0, one launch (start us, length us, event | category | flops | bytes accessed | tf_op | source)
XLA Modules:
  0.0 35.0 jit_solution(10212188026684021707)
XLA Ops:
  0.6 1.9 %shard_map.69 = (f32[4,64,256]{2,1,0:T(8,128)S(1)}, f32[4,64,256]{2,1,0:T(8,128)S(1)}, f32[5,6,64,256]{3,2,1,0:T(8,128)S(1)}) custom-call(f32[8,64,256]{2,1,0:T(8,128)} %state.3, f32[8,64,256]{2,1,0:T(8,128)} %conduct.3, f32[8,64,256]{2,1,0:T(8,128)} %sink.3, s32[8,64,256]{2,1,0:T(8,128)} %labels.5, f32[8,64,256]{2,1,0:T(8,128)} %cotangent.3), custom_call_target="tpu_custom_call" | custom-call | flops 1024 | bytes 1024 | tf_op jit(solution)/shard_map/pallas_call | solution.py:27
  2.6 0.5 %collective-permute-start = (f32[5,6,64,256]{3,2,1,0:T(8,128)S(1)}, f32[5,6,64,256]{3,2,1,0:T(8,128)S(1)}, u32[]{:S(2)}, u32[]{:S(2)}) collective-permute-start(f32[5,6,64,256]{3,2,1,0:T(8,128)S(1)} %get-tuple-element.64), channel_id=1, source_target_pairs={{0,1},{1,0},{2,3},{3,2},{4,5},{5,4},{6,7},{7,6},{8,9},{9,8},{10,11... | collective-permute-start | bytes 5898248 | tf_op jit(solution)/shard_map/ppermute | solution.py:832
  3.1 2.6 %collective-permute-start.4 = (f32[4,64,256]{2,1,0:T(8,128)S(1)}, f32[4,64,256]{2,1,0:T(8,128)S(1)}, u32[]{:S(2)}, u32[]{:S(2)}) collective-permute-start(f32[4,64,256]{2,1,0:T(8,128)S(1)} %get-tuple-element.86), channel_id=1, source_target_pairs={{0,4},{4,8},{8,12},{12,0},{1,5},{5,9},{9,13},{13,1},{2,6},{6,10},{... | collective-permute-start | bytes 786440 | tf_op jit(solution)/shard_map/ppermute | solution.py:857
  5.7 2.1 %collective-permute-start.5 = (f32[4,64,256]{2,1,0:T(8,128)S(1)}, f32[4,64,256]{2,1,0:T(8,128)S(1)}, u32[]{:S(2)}, u32[]{:S(2)}) collective-permute-start(f32[4,64,256]{2,1,0:T(8,128)S(1)} %get-tuple-element.87), channel_id=1, source_target_pairs={{4,0},{8,4},{12,8},{0,12},{5,1},{9,5},{13,9},{1,13},{6,2},{10,6},{... | collective-permute-start | bytes 786440 | tf_op jit(solution)/shard_map/ppermute | solution.py:858
  7.8 1.6 %shard_map.68.mine = f32[5,6,64,256]{3,2,1,0:T(8,128)S(1)} custom-call(f32[8,64,256]{2,1,0:T(8,128)} %state.3, f32[8,64,256]{2,1,0:T(8,128)} %conduct.3, f32[8,64,256]{2,1,0:T(8,128)} %sink.3, s32[8,64,256]{2,1,0:T(8,128)} %labels.5, f32[8,64,256]{2,1,0:T(8,128)} %cotangent.3), custom_call_target="tpu_custom_call" | custom-call | flops 1024 | bytes 1024 | tf_op jit(solution)/shard_map/pallas_call | solution.py:27
  9.4 0.0 collective-permute-done.traded
  9.4 0.3 shard_map.70
  9.7 1.7 %collective-permute-start.1 = (f32[4,8,512]{2,1,0:T(8,128)S(1)}, f32[4,8,512]{2,1,0:T(8,128)S(1)}, u32[]{:S(2)}, u32[]{:S(2)}) collective-permute-start(f32[4,8,512]{2,1,0:T(8,128)S(1)} %get-tuple-element.67), channel_id=1, source_target_pairs={{0,2},{2,0},{1,3},{3,1},{4,6},{6,4},{5,7},{7,5},{8,10},{10,8},{9,1... | collective-permute-start | bytes 196616 | tf_op jit(solution)/shard_map/ppermute | solution.py:845
  11.4 0.4 %collective-permute-start.2 = (f32[10,8,512]{2,1,0:T(8,128)S(1)}, f32[10,8,512]{2,1,0:T(8,128)S(1)}, u32[]{:S(2)}, u32[]{:S(2)}) collective-permute-start(f32[10,8,512]{2,1,0:T(8,128)S(1)} %get-tuple-element.68), channel_id=1, source_target_pairs={{0,2},{2,0},{1,3},{3,1},{4,6},{6,4},{5,7},{7,5},{8,10},{10,8},{9,1... | collective-permute-start | bytes 491528 | tf_op jit(solution)/shard_map/ppermute | solution.py:845
  11.8 1.4 %shard_map.73 = (f32[3,48,512]{2,1,0:T(8,128)S(1)}, f32[4,48,512]{2,1,0:T(8,128)S(1)}, f32[4,48,512]{2,1,0:T(8,128)S(1)}, f32[4,48,512]{2,1,0:T(8,128)S(1)}, f32...) custom-call(f32[5,4,64,512]{3,2,1,0:T(8,128)S(1)} %get-tuple-element.65.block, ...), custom_call_target="tpu_custom_call" | custom-call | flops 1024 | bytes 1024 | tf_op jit(solution)/shard_map/pallas_call | solution.py:27
  13.3 1.2 %collective-permute-done.1.refs_0_ = f32[4,8,512]{2,1,0:T(8,128)S(1)} collective-permute-done((f32[4,8,512]{2,1,0:T(8,128)S(1)}, f32[4,8,512]{2,1,0:T(8,128)S(1)}, u32[]{:S(2)}, u32[]{:S(2)}) %collective-permute-start.1) | collective-permute-done | bytes 65568 | tf_op jit(solution)/shard_map/ppermute | solution.py:845
  14.5 0.8 %shard_map.74 = (f32[80,512]{1,0:T(8,128)S(1)}, f32[7,8,512]{2,1,0:T(8,128)}) custom-call(f32[5,4,64,512]{3,2,1,0:T(8,128)S(1)} %get-tuple-element.65.block, f32[4,48,512]{2,1,0:T(8,128)S(1)} %get-tuple-element.70.part_mid.refs_4_.refs_6_, f32[4,8,512]{2,1,0:T(8,128)S(1)} %collective-permute-done.1.refs_0_), custom_call_target="tpu_custom_call" | custom-call | flops 1100000000 | bytes 1024 | tf_op jit(solution)/shard_map/pallas_call | solution.py:27
  15.2 0.7 %collective-permute-start.3 = (f32[80,512]{1,0:T(8,128)S(1)}, f32[80,512]{1,0:T(8,128)S(1)}, u32[]{:S(2)}, u32[]{:S(2)}) collective-permute-start(f32[80,512]{1,0:T(8,128)S(1)} %get-tuple-element.71), channel_id=1, source_target_pairs={{1,4},{5,8},{9,12},{13,0},{4,1},{8,5},{12,9},{0,13},{3,6},{7,10},{... | collective-permute-start | bytes 491528 | tf_op jit(solution)/shard_map/ppermute | solution.py:835
  15.9 1.7 %collective-permute-done.2.refs_1_ = f32[10,8,512]{2,1,0:T(8,128)S(1)} collective-permute-done((f32[10,8,512]{2,1,0:T(8,128)S(1)}, f32[10,8,512]{2,1,0:T(8,128)S(1)}, u32[]{:S(2)}, u32[]{:S(2)}) %collective-permute-start.2) | collective-permute-done | bytes 163872 | tf_op jit(solution)/shard_map/ppermute | solution.py:845
  17.6 0.8 %shard_map.72 = (f32[5,4,8,512]{3,2,1,0:T(8,128)S(1)}, f32[7,8,512]{2,1,0:T(8,128)S(1)}, f32[3,24,512]{2,1,0:T(8,128)S(1)}, f32[4,24,512]{2,1,0:T(8,128)S(1)}, f...) custom-call(f32[5,4,64,512]{3,2,1,0:T(8,128)S(1)} %get-tuple-element, ...), custom_call_target="tpu_custom_call" | custom-call | flops 1024 | bytes 1024 | tf_op jit(solution)/shard_map/pallas_call | solution.py:27
  18.4 0.3 shard_map.75.refs_0_
  18.7 0.0 collective-permute-done.4.up
  18.7 1.0 %collective-permute-done.5.down = f32[4,64,256]{2,1,0:T(8,128)S(1)} collective-permute-done((f32[4,64,256]{2,1,0:T(8,128)S(1)}, f32[4,64,256]{2,1,0:T(8,128)S(1)}, u32[]{:S(2)}, u32[]{:S(2)}) %collective-permute-start.5) | collective-permute-done | bytes 262176 | tf_op jit(solution)/shard_map/ppermute | solution.py:858
  19.7 0.1 collective-permute-start.6
  19.8 0.5 %collective-permute-start.7 = (f32[2,64,256]{2,1,0:T(8,128)S(1)}, f32[2,64,256]{2,1,0:T(8,128)S(1)}, u32[]{:S(2)}, u32[]{:S(2)}) collective-permute-start(f32[2,64,256]{2,1,0:T(8,128)S(1)} %get-tuple-element.89), channel_id=1, source_target_pairs={{0,1},{1,0},{2,3},{3,2},{4,5},{5,4},{6,7},{7,6},{8,9},{9,8},{10,11... | collective-permute-start | bytes 393224 | tf_op jit(solution)/shard_map/ppermute | solution.py:832
  20.3 0.1 collective-permute-start.8
  20.4 0.8 %collective-permute-done.6.refs_0_ = f32[2,64,256]{2,1,0:T(8,128)S(1)} collective-permute-done((f32[2,64,256]{2,1,0:T(8,128)S(1)}, f32[2,64,256]{2,1,0:T(8,128)S(1)}, u32[]{:S(2)}, u32[]{:S(2)}) %collective-permute-start.6) | collective-permute-done | bytes 131104 | tf_op jit(solution)/shard_map/ppermute | solution.py:832
  21.2 0.2 collective-permute-done.7.refs_1_
  21.3 0.9 %shard_map.77 = (f32[4,2,72,512]{3,2,1,0:T(8,128)S(1)}, f32[2,72,512]{2,1,0:T(8,128)S(1)}, f32[2,72,512]{2,1,0:T(8,128)S(1)}, f32[4,72,512]{2,1,0:T(8,128)S(1)},...) custom-call(f32[5,4,64,512]{3,2,1,0:T(8,128)S(1)} %get-tuple-element, ...), custom_call_target="tpu_custom_call" | custom-call | flops 1024 | bytes 1024 | tf_op jit(solution)/shard_map/pallas_call | solution.py:27
  22.3 1.3 %collective-permute-done.3.off = f32[80,512]{1,0:T(8,128)S(1)} collective-permute-done((f32[80,512]{1,0:T(8,128)S(1)}, f32[80,512]{1,0:T(8,128)S(1)}, u32[]{:S(2)}, u32[]{:S(2)}) %collective-permute-start.3) | collective-permute-done | bytes 163872 | tf_op jit(solution)/shard_map/ppermute | solution.py:835
  23.6 0.4 %shard_map.78 = (f32[4,2,72,512]{3,2,1,0:T(8,128)S(1)}, f32[2,72,512]{2,1,0:T(8,128)S(1)}, f32[2,72,512]{2,1,0:T(8,128)S(1)}, f32[4,72,512]{2,1,0:T(8,128)S(1)},...) custom-call(f32[5,4,64,512]{3,2,1,0:T(8,128)S(1)} %get-tuple-element, ...), custom_call_target="tpu_custom_call", output_to_operand_aliasing={{0}: (17, {}), {1}: (18, {}), {2}: (19, {}), {3}: (20, {}),... | custom-call | flops 1024 | bytes 1024 | tf_op jit(solution)/shard_map/pallas_call | solution.py:27
  24.0 1.3 %collective-permute-start.10 = (f32[72,512]{1,0:T(8,128)S(1)}, f32[72,512]{1,0:T(8,128)S(1)}, u32[]{:S(2)}, u32[]{:S(2)}) collective-permute-start(f32[72,512]{1,0:T(8,128)S(1)} %get-tuple-element.119), channel_id=1, source_target_pairs={{1,4},{5,8},{9,12},{13,0},{4,1},{8,5},{12,9},{0,13},{3,6},{7,10},{... | collective-permute-start | bytes 442376 | tf_op jit(solution)/shard_map/ppermute | solution.py:835
  25.3 0.2 shard_map.79
  25.6 2.4 %collective-permute-start.12 = (f32[64,256]{1,0:T(8,128)S(1)}, f32[64,256]{1,0:T(8,128)S(1)}, u32[]{:S(2)}, u32[]{:S(2)}) collective-permute-start(f32[64,256]{1,0:T(8,128)S(1)} %get-tuple-element.122), channel_id=1, source_target_pairs={{1,4},{5,8},{9,12},{13,0},{4,1},{8,5},{12,9},{0,13},{3,6},{7,10},{... | collective-permute-start | bytes 196616 | tf_op jit(solution)/shard_map/ppermute | solution.py:835
  27.9 0.2 collective-permute-start.13
  28.1 2.0 %shard_map.80 = (f32[4,64,512]{2,1,0:T(8,128)S(1)}, f32[4,64,512]{2,1,0:T(8,128)S(1)}, f32[2,64,512]{2,1,0:T(8,128)S(1)}, f32[2,64,512]{2,1,0:T(8,128)S(1)}, f32...) custom-call(f32[5,4,64,512]{3,2,1,0:T(8,128)S(1)} %get-tuple-element.65.block, f32[5,4,8,512]{3,2,1,0:T(8,128)S(1)} %get-tuple-element.69.ghost, ...), custom_call_target="tpu_custom_call" | custom-call | flops 1024 | bytes 1024 | tf_op jit(solution)/shard_map/pallas_call | solution.py:27
  30.1 0.0 collective-permute-done.8.on_b
  30.1 0.2 shard_map.81
  30.3 0.1 collective-permute-start.9
  30.4 1.6 %collective-permute-done.10.off_b = f32[72,512]{1,0:T(8,128)S(1)} collective-permute-done((f32[72,512]{1,0:T(8,128)S(1)}, f32[72,512]{1,0:T(8,128)S(1)}, u32[]{:S(2)}, u32[]{:S(2)}) %collective-permute-start.10) | collective-permute-done | bytes 147488 | tf_op jit(solution)/shard_map/ppermute | solution.py:835
  32.0 0.2 shard_map.82
  32.2 0.0 copy-start
  32.2 0.1 collective-permute-start.11
  32.3 0.7 %collective-permute-done.12.cross = f32[64,256]{1,0:T(8,128)S(1)} collective-permute-done((f32[64,256]{1,0:T(8,128)S(1)}, f32[64,256]{1,0:T(8,128)S(1)}, u32[]{:S(2)}, u32[]{:S(2)}) %collective-permute-start.12) | collective-permute-done | bytes 65568 | tf_op jit(solution)/shard_map/ppermute | solution.py:835
  33.0 0.9 %collective-permute-done.13.along = f32[64,256]{1,0:T(8,128)S(1)} collective-permute-done((f32[64,256]{1,0:T(8,128)S(1)}, f32[64,256]{1,0:T(8,128)S(1)}, u32[]{:S(2)}, u32[]{:S(2)}) %collective-permute-start.13) | collective-permute-done | bytes 65568 | tf_op jit(solution)/shard_map/ppermute | solution.py:839
  33.9 0.0 collective-permute-done.11.got_last
  33.9 0.0 collective-permute-done.9.got
  33.9 0.0 copy-done
  33.9 1.1 %shard_map.84 = (f32[8,64,256]{2,1,0:T(8,128)}, f32[8,64,256]{2,1,0:T(8,128)}) custom-call(s32[8,64,256]{2,1,0:T(8,128)S(1)} %copy-done, f32[7,64,256]{2,1,0:T(8,128)S(1)} %get-tuple-element.117.refs_7_.keep, f32[7,64,256]{2,1,0:T(8,128)S(1)} %collective-permute-done.9.got, f32[4,64,256]{2,1,0:T(8,128)S(1)} %get-tuple-element.120.keep_last, ...), custom_call_target="tpu_custom_call" | custom-call | flops 1024 | bytes 1024 | tf_op jit(solution)/shard_map/pallas_call | solution.py:27
  (3 shorter events, 0.1 us)
Async XLA Ops:
  2.6 6.9 %collective-permute-start = (f32[5,6,64,256]{3,2,1,0:T(8,128)S(1)}, f32[5,6,64,256]{3,2,1,0:T(8,128)S(1)}, u32[]{:S(2)}, u32[]{:S(2)}) collective-permute-start(f32[5,6,64,256]{3,2,1,0:T(8,128)S(1)} %get-tuple-element.64), channel_id=1, source_target_pairs={{0,1},{1,0},{2,3},{3,2},{4,5},{5,4},{6,7},{7,6},{8,9},{9,8},{10,11... | collective-permute-start | bytes 5898248 | tf_op jit(solution)/shard_map/ppermute | solution.py:832
  3.1 15.7 %collective-permute-start.4 = (f32[4,64,256]{2,1,0:T(8,128)S(1)}, f32[4,64,256]{2,1,0:T(8,128)S(1)}, u32[]{:S(2)}, u32[]{:S(2)}) collective-permute-start(f32[4,64,256]{2,1,0:T(8,128)S(1)} %get-tuple-element.86), channel_id=1, source_target_pairs={{0,4},{4,8},{8,12},{12,0},{1,5},{5,9},{9,13},{13,1},{2,6},{6,10},{... | collective-permute-start | bytes 786440 | tf_op jit(solution)/shard_map/ppermute | solution.py:857
  5.7 14.0 %collective-permute-start.5 = (f32[4,64,256]{2,1,0:T(8,128)S(1)}, f32[4,64,256]{2,1,0:T(8,128)S(1)}, u32[]{:S(2)}, u32[]{:S(2)}) collective-permute-start(f32[4,64,256]{2,1,0:T(8,128)S(1)} %get-tuple-element.87), channel_id=1, source_target_pairs={{4,0},{8,4},{12,8},{0,12},{5,1},{9,5},{13,9},{1,13},{6,2},{10,6},{... | collective-permute-start | bytes 786440 | tf_op jit(solution)/shard_map/ppermute | solution.py:858
  9.7 4.7 %collective-permute-start.1 = (f32[4,8,512]{2,1,0:T(8,128)S(1)}, f32[4,8,512]{2,1,0:T(8,128)S(1)}, u32[]{:S(2)}, u32[]{:S(2)}) collective-permute-start(f32[4,8,512]{2,1,0:T(8,128)S(1)} %get-tuple-element.67), channel_id=1, source_target_pairs={{0,2},{2,0},{1,3},{3,1},{4,6},{6,4},{5,7},{7,5},{8,10},{10,8},{9,1... | collective-permute-start | bytes 196616 | tf_op jit(solution)/shard_map/ppermute | solution.py:845
  11.4 6.1 %collective-permute-start.2 = (f32[10,8,512]{2,1,0:T(8,128)S(1)}, f32[10,8,512]{2,1,0:T(8,128)S(1)}, u32[]{:S(2)}, u32[]{:S(2)}) collective-permute-start(f32[10,8,512]{2,1,0:T(8,128)S(1)} %get-tuple-element.68), channel_id=1, source_target_pairs={{0,2},{2,0},{1,3},{3,1},{4,6},{6,4},{5,7},{7,5},{8,10},{10,8},{9,1... | collective-permute-start | bytes 491528 | tf_op jit(solution)/shard_map/ppermute | solution.py:845
  15.2 8.3 %collective-permute-start.3 = (f32[80,512]{1,0:T(8,128)S(1)}, f32[80,512]{1,0:T(8,128)S(1)}, u32[]{:S(2)}, u32[]{:S(2)}) collective-permute-start(f32[80,512]{1,0:T(8,128)S(1)} %get-tuple-element.71), channel_id=1, source_target_pairs={{1,4},{5,8},{9,12},{13,0},{4,1},{8,5},{12,9},{0,13},{3,6},{7,10},{... | collective-permute-start | bytes 491528 | tf_op jit(solution)/shard_map/ppermute | solution.py:835
  19.7 1.4 %collective-permute-start.6 = (f32[2,64,256]{2,1,0:T(8,128)S(1)}, f32[2,64,256]{2,1,0:T(8,128)S(1)}, u32[]{:S(2)}, u32[]{:S(2)}) collective-permute-start(f32[2,64,256]{2,1,0:T(8,128)S(1)} %get-tuple-element.88), channel_id=1, source_target_pairs={{0,1},{1,0},{2,3},{3,2},{4,5},{5,4},{6,7},{7,6},{8,9},{9,8},{10,11... | collective-permute-start | bytes 393224 | tf_op jit(solution)/shard_map/ppermute | solution.py:832
  19.8 1.5 %collective-permute-start.7 = (f32[2,64,256]{2,1,0:T(8,128)S(1)}, f32[2,64,256]{2,1,0:T(8,128)S(1)}, u32[]{:S(2)}, u32[]{:S(2)}) collective-permute-start(f32[2,64,256]{2,1,0:T(8,128)S(1)} %get-tuple-element.89), channel_id=1, source_target_pairs={{0,1},{1,0},{2,3},{3,2},{4,5},{5,4},{6,7},{7,6},{8,9},{9,8},{10,11... | collective-permute-start | bytes 393224 | tf_op jit(solution)/shard_map/ppermute | solution.py:832
  20.3 9.8 %collective-permute-start.8 = (f32[72,512]{1,0:T(8,128)S(1)}, f32[72,512]{1,0:T(8,128)S(1)}, u32[]{:S(2)}, u32[]{:S(2)}) collective-permute-start(f32[72,512]{1,0:T(8,128)S(1)} %shard_map.75.refs_0_), channel_id=1, source_target_pairs={{0,1},{1,0},{2,3},{3,2},{4,5},{5,4},{6,7},{7,6},{8,9},{9,8},{10,11... | collective-permute-start | bytes 442376 | tf_op jit(solution)/shard_map/ppermute | solution.py:832
  24.0 8.0 %collective-permute-start.10 = (f32[72,512]{1,0:T(8,128)S(1)}, f32[72,512]{1,0:T(8,128)S(1)}, u32[]{:S(2)}, u32[]{:S(2)}) collective-permute-start(f32[72,512]{1,0:T(8,128)S(1)} %get-tuple-element.119), channel_id=1, source_target_pairs={{1,4},{5,8},{9,12},{13,0},{4,1},{8,5},{12,9},{0,13},{3,6},{7,10},{... | collective-permute-start | bytes 442376 | tf_op jit(solution)/shard_map/ppermute | solution.py:835
  25.6 7.4 %collective-permute-start.12 = (f32[64,256]{1,0:T(8,128)S(1)}, f32[64,256]{1,0:T(8,128)S(1)}, u32[]{:S(2)}, u32[]{:S(2)}) collective-permute-start(f32[64,256]{1,0:T(8,128)S(1)} %get-tuple-element.122), channel_id=1, source_target_pairs={{1,4},{5,8},{9,12},{13,0},{4,1},{8,5},{12,9},{0,13},{3,6},{7,10},{... | collective-permute-start | bytes 196616 | tf_op jit(solution)/shard_map/ppermute | solution.py:835
  27.9 5.9 %collective-permute-start.13 = (f32[64,256]{1,0:T(8,128)S(1)}, f32[64,256]{1,0:T(8,128)S(1)}, u32[]{:S(2)}, u32[]{:S(2)}) collective-permute-start(f32[64,256]{1,0:T(8,128)S(1)} %get-tuple-element.123), channel_id=1, source_target_pairs={{0,12},{1,5},{4,0},{5,9},{8,4},{9,13},{12,8},{13,1},{2,14},{3,7},{... | collective-permute-start | bytes 196616 | tf_op jit(solution)/shard_map/ppermute | solution.py:839
  30.3 3.6 %collective-permute-start.9 = (f32[7,64,256]{2,1,0:T(8,128)S(1)}, f32[7,64,256]{2,1,0:T(8,128)S(1)}, u32[]{:S(2)}, u32[]{:S(2)}) collective-permute-start(f32[7,64,256]{2,1,0:T(8,128)S(1)} %get-tuple-element.118), channel_id=1, source_target_pairs={{0,1},{1,0},{2,3},{3,2},{4,5},{5,4},{6,7},{7,6},{8,9},{9,8},{10,11... | collective-permute-start | bytes 1376264 | tf_op jit(solution)/shard_map/ppermute | solution.py:832
  32.2 1.7 %copy-start = (s32[8,64,256]{2,1,0:T(8,128)S(1)}, s32[8,64,256]{2,1,0:T(8,128)}, u32[]{:S(2)}) copy-start(s32[8,64,256]{2,1,0:T(8,128)} %labels.5) | copy-start | bytes 1572868
  32.2 1.7 %collective-permute-start.11 = (f32[4,64,256]{2,1,0:T(8,128)S(1)}, f32[4,64,256]{2,1,0:T(8,128)S(1)}, u32[]{:S(2)}, u32[]{:S(2)}) collective-permute-start(f32[4,64,256]{2,1,0:T(8,128)S(1)} %get-tuple-element.121), channel_id=1, source_target_pairs={{0,1},{1,0},{2,3},{3,2},{4,5},{5,4},{6,7},{7,6},{8,9},{9,8},{10,11... | collective-permute-start | bytes 786440 | tf_op jit(solution)/shard_map/ppermute | solution.py:832

commit v7 on v6

--- a/solution.py
+++ b/solution.py
@@ -16,6 +16,7 @@
 SWEPT = 11
 LAST_FLOPS = 10000000000
 PACK_FLOPS = 1100000000
+OWN_FLOPS = 1024
 FLOPS = 2200000000
 S, C, T, F, K = range(5)
 ONE = 4
@@ -113,6 +114,14 @@
     def flush(self):
         for key, value in self.values.values():
             self.ref[key] = value
+
+
+class Held:
+    def __setitem__(self, key, value):
+        self.value = value
+
+    def __getitem__(self, key):
+        return self.value
 
 
 class _At:
@@ -295,6 +304,8 @@
 
 
 def prepare(todo, count_y, block, near, ghost, near_ghost, kx, ky_out, kz_out, diag, part, back, one):
+    drafts = [Draft(ref) for ref in (kx, ky_out, kz_out, diag, part, back, one)]
+    kx, ky_out, kz_out, diag, part, back, one = drafts
     place = lax.axis_index("gy")
     core = lax.axis_index("gz")
     half, ny = block.shape[1], block.shape[2]
@@ -377,6 +388,8 @@
         go = go + (face_own + jnp.where(is_low, wind, 0.0)) * s_own
         go = go + (face_far + jnp.where(is_low, 0.0, wind)) * next_to(5 + S)[t]
         one[at(todo.index(t))] = s[t] + (0.5 + f[t]) * go
+    for draft in drafts:
+        draft.flush()
 
 
 def prepare_mid(count_y, block, near, *outs):
@@ -424,15 +437,16 @@
 
 def pack_off(two, count_y, block, part_mid, *refs):
     ways = 1 if two else 2
-    rims, (off, ghost) = refs[:ways], refs[ways:]
+    rims, (off,) = refs[:ways], refs[ways:]
     place = lax.axis_index("gy")
     core = lax.axis_index("gz")
     last = block.shape[1] - 1
     outer = core * last
     inside = outer + 1 - 2 * core
-    unpack_rims(two, count_y, rims, [ghost.at[j] for j in range(7)])
-    s, c, f, k = (with_ghost(block.at[j, outer], ghost.at[j]) for j in (S, C, F, K))
-    s_in, c_in = (with_ghost(block.at[j, inside], ghost.at[5 + j]) for j in (S, C))
+    ghost = [Held() for _ in range(7)]
+    unpack_rims(two, count_y, rims, ghost)
+    s, c, f, k = (with_ghost(block.at[j, outer], ghost[j]) for j in (S, C, F, K))
+    s_in, c_in = (with_ghost(block.at[j, inside], ghost[5 + j]) for j in (S, C))
     count = len(s)
 
     def face_along_y(t):
@@ -458,11 +472,9 @@
             go = flow[t] - (weight[t] + face) * s[t] - time_step * k[t] * jnp.tanh(s[t])
             go = go + (face + jnp.where(core == 0, 0.0, time_step) * f[t]) * s_in[t]
             one[t] = s[t] + (0.5 + f[t]) * go
-        else:
-            one[t] = part_mid[outer, at(t - 1)]
-        if t < count - 1:
-            off[at(t)] = one[t]
-    ghosts = {j: ghost[j] for j in range(4)}
+    for t in range(count - 1):
+        off[at(t)] = one[t] if t in todo else part_mid[outer, at(t - 1)]
+    ghosts = {j: ghost[j][...] for j in range(4)}
     ghosts[ONE] = one[count - 1]
     if two:
         for slot, parts in enumerate(PACKED):
@@ -581,7 +593,10 @@
 def middle(block, ghost, near, near_ghost, up, down, *refs):
     passed, weights, outs = refs[:2], coefficients(refs[2:16]), refs[16:]
     fill_sides(near, near_ghost, up, down, passed, outs[0])
-    sweep(False, block, ghost, weights, *outs)
+    drafts = [Draft(ref) for ref in outs[1:]]
+    sweep(False, block, ghost, weights, outs[0], *drafts)
+    for draft in drafts:
+        draft.flush()
 
 
 def outward(two, block, ghost, off, *refs):
@@ -857,7 +872,7 @@
     up = lax.ppermute(up, "gx", ahead)
     down = lax.ppermute(down, "gx", behind)
     traded = swap_cores(trade)
-    (mine,) = call(own_planes, [span], *inputs, given=HBM, scratch=[kinds, drains, sems(5)])
+    (mine,) = call(own_planes, [span], *inputs, given=HBM, scratch=[kinds, drains, sems(5)], flops=OWN_FLOPS)
     block, near = call(gather_planes, [(5, half, ny, wide), (7, ny, wide)], mine, traded)
     sizes = [4, (5 * half + 1) // 2]
     rims = call(functools.partial(pack_along_y, two), [(n, TILE, wide) for n in sizes for _ in range(ways)], block, near)
@@ -868,8 +883,8 @@
         functools.partial(prepare_rim, two, count_y),
         [(5, half, TILE, wide), (7, TILE, wide)] + split(3 * TILE), block, near, *rims,
     )
-    off, _ = call(
-        functools.partial(pack_off, two, count_y), [(ny + (len(PACKED) if two else 5) * TILE, wide), (7, TILE, wide)],
+    (off,) = call(
+        functools.partial(pack_off, two, count_y), [(ny + (len(PACKED) if two else 5) * TILE, wide)],
         block, mids[4], *rims[:ways], flops=PACK_FLOPS,
     )
     off = swap_chips(off)

time: 35.2 us -> 35.2 us (level)
  Pallas kernels: 12.3 us -> 11.5 us
  waiting for transfers between devices: 9.21 us -> 9.98 us
    pallas_call x17, Pallas kernels: 12.3 us -> 11.5 us  [call(): pl.pallas_call(kernel, out_shape=[space(shape, jnp.float32) for shape in...]
    ppermute x2, waiting for transfers between devices: 2.83 us -> 3.52 us  [along_y(): lax.ppermute(rim, 'gy', routes[i % len(routes)])]
  transfers between devices with their start and end apart: 14 -> 14, of which waited for: 9 -> 9; matrix products, arithmetic and copies ran while one was open for 0% -> 0% of each run, Pallas kernels for 27% -> 24%
where the time goes in v7:
time: 35.2 us; the launch traced here: 35 us
  starting transfers between devices  12.7 us (36%)
  Pallas kernels  11.5 us (33%)
  waiting for transfers between devices  9.98 us (28%)
  between operations  0.8 us (2%)
    pallas_call x17, Pallas kernels, call(): pl.pallas_call(kernel, out_shape=[space(shape, jnp.float32) for shape in...  11.5 us
    ppermute x3, starting transfers between devices, swap_chips(): return lax.ppermute(x, ('gx', 'gz'), chips)  4.44 us
    ppermute x3, waiting for transfers between devices, swap_chips(): return lax.ppermute(x, ('gx', 'gz'), chips)  3.63 us
    ppermute x2, waiting for transfers between devices, along_y(): lax.ppermute(rim, 'gy', routes[i % len(routes)])  3.52 us
    ppermute x1, starting transfers between devices, on_device(): up = lax.ppermute(up, 'gx', ahead)  2.64 us
    ppermute x1, starting transfers between devices, on_device(): down = lax.ppermute(down, 'gx', behind)  2.11 us
    ppermute x2, starting transfers between devices, along_y(): lax.ppermute(rim, 'gy', routes[i % len(routes)])  2.09 us
    ppermute x6, starting transfers between devices, swap_cores(): return lax.ppermute(x, 'gz', [(0, 1), (1, 0)])  1.31 us
  transfers between devices with their start and end apart: 14, of which 9 were waited for; matrix products, arithmetic and copies ran while one was open for 0% of the time, Pallas kernels for 24%

profile of v7, /device:TPU:0, one launch (start us, length us, event | category | flops | bytes accessed | tf_op | source)
XLA Modules:
  0.0 35.0 jit_solution(742204847148940182)
XLA Ops:
  0.6 1.9 %shard_map.69 = (f32[4,64,256]{2,1,0:T(8,128)S(1)}, f32[4,64,256]{2,1,0:T(8,128)S(1)}, f32[5,6,64,256]{3,2,1,0:T(8,128)S(1)}) custom-call(f32[8,64,256]{2,1,0:T(8,128)} %state.3, f32[8,64,256]{2,1,0:T(8,128)} %conduct.3, f32[8,64,256]{2,1,0:T(8,128)} %sink.3, s32[8,64,256]{2,1,0:T(8,128)} %labels.5, f32[8,64,256]{2,1,0:T(8,128)} %cotangent.3), custom_call_target="tpu_custom_call" | custom-call | flops 1024 | bytes 1024 | tf_op jit(solution)/shard_map/pallas_call | solution.py:28
  2.6 0.5 %collective-permute-start = (f32[5,6,64,256]{3,2,1,0:T(8,128)S(1)}, f32[5,6,64,256]{3,2,1,0:T(8,128)S(1)}, u32[]{:S(2)}, u32[]{:S(2)}) collective-permute-start(f32[5,6,64,256]{3,2,1,0:T(8,128)S(1)} %get-tuple-element.63), channel_id=1, source_target_pairs={{0,1},{1,0},{2,3},{3,2},{4,5},{5,4},{6,7},{7,6},{8,9},{9,8},{10,11... | collective-permute-start | bytes 5898248 | tf_op jit(solution)/shard_map/ppermute | solution.py:847
  3.1 2.6 %collective-permute-start.4 = (f32[4,64,256]{2,1,0:T(8,128)S(1)}, f32[4,64,256]{2,1,0:T(8,128)S(1)}, u32[]{:S(2)}, u32[]{:S(2)}) collective-permute-start(f32[4,64,256]{2,1,0:T(8,128)S(1)} %get-tuple-element.84), channel_id=1, source_target_pairs={{0,4},{4,8},{8,12},{12,0},{1,5},{5,9},{9,13},{13,1},{2,6},{6,10},{... | collective-permute-start | bytes 786440 | tf_op jit(solution)/shard_map/ppermute | solution.py:872
  5.7 2.1 %collective-permute-start.5 = (f32[4,64,256]{2,1,0:T(8,128)S(1)}, f32[4,64,256]{2,1,0:T(8,128)S(1)}, u32[]{:S(2)}, u32[]{:S(2)}) collective-permute-start(f32[4,64,256]{2,1,0:T(8,128)S(1)} %get-tuple-element.85), channel_id=1, source_target_pairs={{4,0},{8,4},{12,8},{0,12},{5,1},{9,5},{13,9},{1,13},{6,2},{10,6},{... | collective-permute-start | bytes 786440 | tf_op jit(solution)/shard_map/ppermute | solution.py:873
  7.8 1.6 %shard_map.68.mine = f32[5,6,64,256]{3,2,1,0:T(8,128)S(1)} custom-call(f32[8,64,256]{2,1,0:T(8,128)} %state.3, f32[8,64,256]{2,1,0:T(8,128)} %conduct.3, f32[8,64,256]{2,1,0:T(8,128)} %sink.3, s32[8,64,256]{2,1,0:T(8,128)} %labels.5, f32[8,64,256]{2,1,0:T(8,128)} %cotangent.3), custom_call_target="tpu_custom_call" | custom-call | flops 1024 | bytes 1024 | tf_op jit(solution)/shard_map/pallas_call | solution.py:28
  9.4 0.0 collective-permute-done.traded
  9.4 0.3 shard_map.70
  9.7 1.7 %collective-permute-start.1 = (f32[4,8,512]{2,1,0:T(8,128)S(1)}, f32[4,8,512]{2,1,0:T(8,128)S(1)}, u32[]{:S(2)}, u32[]{:S(2)}) collective-permute-start(f32[4,8,512]{2,1,0:T(8,128)S(1)} %get-tuple-element.66), channel_id=1, source_target_pairs={{0,2},{2,0},{1,3},{3,1},{4,6},{6,4},{5,7},{7,5},{8,10},{10,8},{9,1... | collective-permute-start | bytes 196616 | tf_op jit(solution)/shard_map/ppermute | solution.py:860
  11.4 0.4 %collective-permute-start.2 = (f32[10,8,512]{2,1,0:T(8,128)S(1)}, f32[10,8,512]{2,1,0:T(8,128)S(1)}, u32[]{:S(2)}, u32[]{:S(2)}) collective-permute-start(f32[10,8,512]{2,1,0:T(8,128)S(1)} %get-tuple-element.67), channel_id=1, source_target_pairs={{0,2},{2,0},{1,3},{3,1},{4,6},{6,4},{5,7},{7,5},{8,10},{10,8},{9,1... | collective-permute-start | bytes 491528 | tf_op jit(solution)/shard_map/ppermute | solution.py:860
  11.8 1.3 %shard_map.73 = (f32[3,48,512]{2,1,0:T(8,128)S(1)}, f32[4,48,512]{2,1,0:T(8,128)S(1)}, f32[4,48,512]{2,1,0:T(8,128)S(1)}, f32[4,48,512]{2,1,0:T(8,128)S(1)}, f32...) custom-call(f32[5,4,64,512]{3,2,1,0:T(8,128)S(1)} %get-tuple-element.64.block, ...), custom_call_target="tpu_custom_call" | custom-call | flops 1024 | bytes 1024 | tf_op jit(solution)/shard_map/pallas_call | solution.py:28
  13.1 1.3 %collective-permute-done.1.refs_0_ = f32[4,8,512]{2,1,0:T(8,128)S(1)} collective-permute-done((f32[4,8,512]{2,1,0:T(8,128)S(1)}, f32[4,8,512]{2,1,0:T(8,128)S(1)}, u32[]{:S(2)}, u32[]{:S(2)}) %collective-permute-start.1) | collective-permute-done | bytes 65568 | tf_op jit(solution)/shard_map/ppermute | solution.py:860
  14.5 0.2 shard_map.74
  14.6 0.8 %collective-permute-start.3 = (f32[80,512]{1,0:T(8,128)S(1)}, f32[80,512]{1,0:T(8,128)S(1)}, u32[]{:S(2)}, u32[]{:S(2)}) collective-permute-start(f32[80,512]{1,0:T(8,128)S(1)} %shard_map.74), channel_id=1, source_target_pairs={{1,4},{5,8},{9,12},{13,0},{4,1},{8,5},{12,9},{0,13},{3,6},{7,10},{... | collective-permute-start | bytes 491528 | tf_op jit(solution)/shard_map/ppermute | solution.py:850
  15.4 2.2 %collective-permute-done.2.refs_1_ = f32[10,8,512]{2,1,0:T(8,128)S(1)} collective-permute-done((f32[10,8,512]{2,1,0:T(8,128)S(1)}, f32[10,8,512]{2,1,0:T(8,128)S(1)}, u32[]{:S(2)}, u32[]{:S(2)}) %collective-permute-start.2) | collective-permute-done | bytes 163872 | tf_op jit(solution)/shard_map/ppermute | solution.py:860
  17.6 0.7 %shard_map.72 = (f32[5,4,8,512]{3,2,1,0:T(8,128)S(1)}, f32[7,8,512]{2,1,0:T(8,128)S(1)}, f32[3,24,512]{2,1,0:T(8,128)S(1)}, f32[4,24,512]{2,1,0:T(8,128)S(1)}, f...) custom-call(f32[5,4,64,512]{3,2,1,0:T(8,128)S(1)} %get-tuple-element, ...), custom_call_target="tpu_custom_call" | custom-call | flops 1024 | bytes 1024 | tf_op jit(solution)/shard_map/pallas_call | solution.py:28
  18.3 0.3 shard_map.75.refs_0_
  18.7 0.0 collective-permute-done.4.up
  18.7 1.0 %collective-permute-done.5.down = f32[4,64,256]{2,1,0:T(8,128)S(1)} collective-permute-done((f32[4,64,256]{2,1,0:T(8,128)S(1)}, f32[4,64,256]{2,1,0:T(8,128)S(1)}, u32[]{:S(2)}, u32[]{:S(2)}) %collective-permute-start.5) | collective-permute-done | bytes 262176 | tf_op jit(solution)/shard_map/ppermute | solution.py:873
  19.7 0.1 collective-permute-start.6
  19.8 0.5 %collective-permute-start.7 = (f32[2,64,256]{2,1,0:T(8,128)S(1)}, f32[2,64,256]{2,1,0:T(8,128)S(1)}, u32[]{:S(2)}, u32[]{:S(2)}) collective-permute-start(f32[2,64,256]{2,1,0:T(8,128)S(1)} %get-tuple-element.87), channel_id=1, source_target_pairs={{0,1},{1,0},{2,3},{3,2},{4,5},{5,4},{6,7},{7,6},{8,9},{9,8},{10,11... | collective-permute-start | bytes 393224 | tf_op jit(solution)/shard_map/ppermute | solution.py:847
  20.3 0.1 collective-permute-start.8
  20.4 0.8 %collective-permute-done.6.refs_0_ = f32[2,64,256]{2,1,0:T(8,128)S(1)} collective-permute-done((f32[2,64,256]{2,1,0:T(8,128)S(1)}, f32[2,64,256]{2,1,0:T(8,128)S(1)}, u32[]{:S(2)}, u32[]{:S(2)}) %collective-permute-start.6) | collective-permute-done | bytes 131104 | tf_op jit(solution)/shard_map/ppermute | solution.py:847
  21.2 0.2 collective-permute-done.7.refs_1_
  21.3 0.9 %shard_map.77 = (f32[4,2,72,512]{3,2,1,0:T(8,128)S(1)}, f32[2,72,512]{2,1,0:T(8,128)S(1)}, f32[2,72,512]{2,1,0:T(8,128)S(1)}, f32[4,72,512]{2,1,0:T(8,128)S(1)},...) custom-call(f32[5,4,64,512]{3,2,1,0:T(8,128)S(1)} %get-tuple-element, ...), custom_call_target="tpu_custom_call" | custom-call | flops 1024 | bytes 1024 | tf_op jit(solution)/shard_map/pallas_call | solution.py:28
  22.2 1.3 %collective-permute-done.3.off = f32[80,512]{1,0:T(8,128)S(1)} collective-permute-done((f32[80,512]{1,0:T(8,128)S(1)}, f32[80,512]{1,0:T(8,128)S(1)}, u32[]{:S(2)}, u32[]{:S(2)}) %collective-permute-start.3) | collective-permute-done | bytes 163872 | tf_op jit(solution)/shard_map/ppermute | solution.py:850
  23.6 0.4 %shard_map.78 = (f32[4,2,72,512]{3,2,1,0:T(8,128)S(1)}, f32[2,72,512]{2,1,0:T(8,128)S(1)}, f32[2,72,512]{2,1,0:T(8,128)S(1)}, f32[4,72,512]{2,1,0:T(8,128)S(1)},...) custom-call(f32[5,4,64,512]{3,2,1,0:T(8,128)S(1)} %get-tuple-element, ...), custom_call_target="tpu_custom_call", output_to_operand_aliasing={{0}: (17, {}), {1}: (18, {}), {2}: (19, {}), {3}: (20, {}),... | custom-call | flops 1024 | bytes 1024 | tf_op jit(solution)/shard_map/pallas_call | solution.py:28
  24.0 1.3 %collective-permute-start.10 = (f32[72,512]{1,0:T(8,128)S(1)}, f32[72,512]{1,0:T(8,128)S(1)}, u32[]{:S(2)}, u32[]{:S(2)}) collective-permute-start(f32[72,512]{1,0:T(8,128)S(1)} %get-tuple-element.117), channel_id=1, source_target_pairs={{1,4},{5,8},{9,12},{13,0},{4,1},{8,5},{12,9},{0,13},{3,6},{7,10},{... | collective-permute-start | bytes 442376 | tf_op jit(solution)/shard_map/ppermute | solution.py:850
  25.3 0.2 shard_map.79
  25.6 2.4 %collective-permute-start.12 = (f32[64,256]{1,0:T(8,128)S(1)}, f32[64,256]{1,0:T(8,128)S(1)}, u32[]{:S(2)}, u32[]{:S(2)}) collective-permute-start(f32[64,256]{1,0:T(8,128)S(1)} %get-tuple-element.120), channel_id=1, source_target_pairs={{1,4},{5,8},{9,12},{13,0},{4,1},{8,5},{12,9},{0,13},{3,6},{7,10},{... | collective-permute-start | bytes 196616 | tf_op jit(solution)/shard_map/ppermute | solution.py:850
  27.9 0.2 collective-permute-start.13
  28.1 2.0 %shard_map.80 = (f32[4,64,512]{2,1,0:T(8,128)S(1)}, f32[4,64,512]{2,1,0:T(8,128)S(1)}, f32[2,64,512]{2,1,0:T(8,128)S(1)}, f32[2,64,512]{2,1,0:T(8,128)S(1)}, f32...) custom-call(f32[5,4,64,512]{3,2,1,0:T(8,128)S(1)} %get-tuple-element.64.block, f32[5,4,8,512]{3,2,1,0:T(8,128)S(1)} %get-tuple-element.68.ghost, ...), custom_call_target="tpu_custom_call" | custom-call | flops 1024 | bytes 1024 | tf_op jit(solution)/shard_map/pallas_call | solution.py:28
  30.1 0.0 collective-permute-done.8.on_b
  30.1 0.2 shard_map.81
  30.3 0.1 collective-permute-start.9
  30.4 1.6 %collective-permute-done.10.off_b = f32[72,512]{1,0:T(8,128)S(1)} collective-permute-done((f32[72,512]{1,0:T(8,128)S(1)}, f32[72,512]{1,0:T(8,128)S(1)}, u32[]{:S(2)}, u32[]{:S(2)}) %collective-permute-start.10) | collective-permute-done | bytes 147488 | tf_op jit(solution)/shard_map/ppermute | solution.py:850
  32.0 0.2 shard_map.82
  32.2 0.0 copy-start
  32.2 0.1 collective-permute-start.11
  32.3 0.7 %collective-permute-done.12.cross = f32[64,256]{1,0:T(8,128)S(1)} collective-permute-done((f32[64,256]{1,0:T(8,128)S(1)}, f32[64,256]{1,0:T(8,128)S(1)}, u32[]{:S(2)}, u32[]{:S(2)}) %collective-permute-start.12) | collective-permute-done | bytes 65568 | tf_op jit(solution)/shard_map/ppermute | solution.py:850
  33.0 0.9 %collective-permute-done.13.along = f32[64,256]{1,0:T(8,128)S(1)} collective-permute-done((f32[64,256]{1,0:T(8,128)S(1)}, f32[64,256]{1,0:T(8,128)S(1)}, u32[]{:S(2)}, u32[]{:S(2)}) %collective-permute-start.13) | collective-permute-done | bytes 65568 | tf_op jit(solution)/shard_map/ppermute | solution.py:854
  33.9 0.0 collective-permute-done.11.got_last
  33.9 0.0 collective-permute-done.9.got
  33.9 0.0 copy-done
  33.9 1.1 %shard_map.84 = (f32[8,64,256]{2,1,0:T(8,128)}, f32[8,64,256]{2,1,0:T(8,128)}) custom-call(s32[8,64,256]{2,1,0:T(8,128)S(1)} %copy-done, f32[7,64,256]{2,1,0:T(8,128)S(1)} %get-tuple-element.115.refs_7_.keep, f32[7,64,256]{2,1,0:T(8,128)S(1)} %collective-permute-done.9.got, f32[4,64,256]{2,1,0:T(8,128)S(1)} %get-tuple-element.118.keep_last, ...), custom_call_target="tpu_custom_call" | custom-call | flops 1024 | bytes 1024 | tf_op jit(solution)/shard_map/pallas_call | solution.py:28
  (3 shorter events, 0.1 us)
Async XLA Ops:
  2.6 6.9 %collective-permute-start = (f32[5,6,64,256]{3,2,1,0:T(8,128)S(1)}, f32[5,6,64,256]{3,2,1,0:T(8,128)S(1)}, u32[]{:S(2)}, u32[]{:S(2)}) collective-permute-start(f32[5,6,64,256]{3,2,1,0:T(8,128)S(1)} %get-tuple-element.63), channel_id=1, source_target_pairs={{0,1},{1,0},{2,3},{3,2},{4,5},{5,4},{6,7},{7,6},{8,9},{9,8},{10,11... | collective-permute-start | bytes 5898248 | tf_op jit(solution)/shard_map/ppermute | solution.py:847
  3.1 15.6 %collective-permute-start.4 = (f32[4,64,256]{2,1,0:T(8,128)S(1)}, f32[4,64,256]{2,1,0:T(8,128)S(1)}, u32[]{:S(2)}, u32[]{:S(2)}) collective-permute-start(f32[4,64,256]{2,1,0:T(8,128)S(1)} %get-tuple-element.84), channel_id=1, source_target_pairs={{0,4},{4,8},{8,12},{12,0},{1,5},{5,9},{9,13},{13,1},{2,6},{6,10},{... | collective-permute-start | bytes 786440 | tf_op jit(solution)/shard_map/ppermute | solution.py:872
  5.7 14.0 %collective-permute-start.5 = (f32[4,64,256]{2,1,0:T(8,128)S(1)}, f32[4,64,256]{2,1,0:T(8,128)S(1)}, u32[]{:S(2)}, u32[]{:S(2)}) collective-permute-start(f32[4,64,256]{2,1,0:T(8,128)S(1)} %get-tuple-element.85), channel_id=1, source_target_pairs={{4,0},{8,4},{12,8},{0,12},{5,1},{9,5},{13,9},{1,13},{6,2},{10,6},{... | collective-permute-start | bytes 786440 | tf_op jit(solution)/shard_map/ppermute | solution.py:873
  9.7 4.7 %collective-permute-start.1 = (f32[4,8,512]{2,1,0:T(8,128)S(1)}, f32[4,8,512]{2,1,0:T(8,128)S(1)}, u32[]{:S(2)}, u32[]{:S(2)}) collective-permute-start(f32[4,8,512]{2,1,0:T(8,128)S(1)} %get-tuple-element.66), channel_id=1, source_target_pairs={{0,2},{2,0},{1,3},{3,1},{4,6},{6,4},{5,7},{7,5},{8,10},{10,8},{9,1... | collective-permute-start | bytes 196616 | tf_op jit(solution)/shard_map/ppermute | solution.py:860
  11.4 6.1 %collective-permute-start.2 = (f32[10,8,512]{2,1,0:T(8,128)S(1)}, f32[10,8,512]{2,1,0:T(8,128)S(1)}, u32[]{:S(2)}, u32[]{:S(2)}) collective-permute-start(f32[10,8,512]{2,1,0:T(8,128)S(1)} %get-tuple-element.67), channel_id=1, source_target_pairs={{0,2},{2,0},{1,3},{3,1},{4,6},{6,4},{5,7},{7,5},{8,10},{10,8},{9,1... | collective-permute-start | bytes 491528 | tf_op jit(solution)/shard_map/ppermute | solution.py:860
  14.6 8.9 %collective-permute-start.3 = (f32[80,512]{1,0:T(8,128)S(1)}, f32[80,512]{1,0:T(8,128)S(1)}, u32[]{:S(2)}, u32[]{:S(2)}) collective-permute-start(f32[80,512]{1,0:T(8,128)S(1)} %shard_map.74), channel_id=1, source_target_pairs={{1,4},{5,8},{9,12},{13,0},{4,1},{8,5},{12,9},{0,13},{3,6},{7,10},{... | collective-permute-start | bytes 491528 | tf_op jit(solution)/shard_map/ppermute | solution.py:850
  19.7 1.4 %collective-permute-start.6 = (f32[2,64,256]{2,1,0:T(8,128)S(1)}, f32[2,64,256]{2,1,0:T(8,128)S(1)}, u32[]{:S(2)}, u32[]{:S(2)}) collective-permute-start(f32[2,64,256]{2,1,0:T(8,128)S(1)} %get-tuple-element.86), channel_id=1, source_target_pairs={{0,1},{1,0},{2,3},{3,2},{4,5},{5,4},{6,7},{7,6},{8,9},{9,8},{10,11... | collective-permute-start | bytes 393224 | tf_op jit(solution)/shard_map/ppermute | solution.py:847
  19.8 1.5 %collective-permute-start.7 = (f32[2,64,256]{2,1,0:T(8,128)S(1)}, f32[2,64,256]{2,1,0:T(8,128)S(1)}, u32[]{:S(2)}, u32[]{:S(2)}) collective-permute-start(f32[2,64,256]{2,1,0:T(8,128)S(1)} %get-tuple-element.87), channel_id=1, source_target_pairs={{0,1},{1,0},{2,3},{3,2},{4,5},{5,4},{6,7},{7,6},{8,9},{9,8},{10,11... | collective-permute-start | bytes 393224 | tf_op jit(solution)/shard_map/ppermute | solution.py:847
  20.3 9.8 %collective-permute-start.8 = (f32[72,512]{1,0:T(8,128)S(1)}, f32[72,512]{1,0:T(8,128)S(1)}, u32[]{:S(2)}, u32[]{:S(2)}) collective-permute-start(f32[72,512]{1,0:T(8,128)S(1)} %shard_map.75.refs_0_), channel_id=1, source_target_pairs={{0,1},{1,0},{2,3},{3,2},{4,5},{5,4},{6,7},{7,6},{8,9},{9,8},{10,11... | collective-permute-start | bytes 442376 | tf_op jit(solution)/shard_map/ppermute | solution.py:847
  24.0 8.0 %collective-permute-start.10 = (f32[72,512]{1,0:T(8,128)S(1)}, f32[72,512]{1,0:T(8,128)S(1)}, u32[]{:S(2)}, u32[]{:S(2)}) collective-permute-start(f32[72,512]{1,0:T(8,128)S(1)} %get-tuple-element.117), channel_id=1, source_target_pairs={{1,4},{5,8},{9,12},{13,0},{4,1},{8,5},{12,9},{0,13},{3,6},{7,10},{... | collective-permute-start | bytes 442376 | tf_op jit(solution)/shard_map/ppermute | solution.py:850
  25.6 7.4 %collective-permute-start.12 = (f32[64,256]{1,0:T(8,128)S(1)}, f32[64,256]{1,0:T(8,128)S(1)}, u32[]{:S(2)}, u32[]{:S(2)}) collective-permute-start(f32[64,256]{1,0:T(8,128)S(1)} %get-tuple-element.120), channel_id=1, source_target_pairs={{1,4},{5,8},{9,12},{13,0},{4,1},{8,5},{12,9},{0,13},{3,6},{7,10},{... | collective-permute-start | bytes 196616 | tf_op jit(solution)/shard_map/ppermute | solution.py:850
  27.9 5.9 %collective-permute-start.13 = (f32[64,256]{1,0:T(8,128)S(1)}, f32[64,256]{1,0:T(8,128)S(1)}, u32[]{:S(2)}, u32[]{:S(2)}) collective-permute-start(f32[64,256]{1,0:T(8,128)S(1)} %get-tuple-element.121), channel_id=1, source_target_pairs={{0,12},{1,5},{4,0},{5,9},{8,4},{9,13},{12,8},{13,1},{2,14},{3,7},{... | collective-permute-start | bytes 196616 | tf_op jit(solution)/shard_map/ppermute | solution.py:854
  30.3 3.6 %collective-permute-start.9 = (f32[7,64,256]{2,1,0:T(8,128)S(1)}, f32[7,64,256]{2,1,0:T(8,128)S(1)}, u32[]{:S(2)}, u32[]{:S(2)}) collective-permute-start(f32[7,64,256]{2,1,0:T(8,128)S(1)} %get-tuple-element.116), channel_id=1, source_target_pairs={{0,1},{1,0},{2,3},{3,2},{4,5},{5,4},{6,7},{7,6},{8,9},{9,8},{10,11... | collective-permute-start | bytes 1376264 | tf_op jit(solution)/shard_map/ppermute | solution.py:847
  32.2 1.7 %copy-start = (s32[8,64,256]{2,1,0:T(8,128)S(1)}, s32[8,64,256]{2,1,0:T(8,128)}, u32[]{:S(2)}) copy-start(s32[8,64,256]{2,1,0:T(8,128)} %labels.5) | copy-start | bytes 1572868
  32.2 1.7 %collective-permute-start.11 = (f32[4,64,256]{2,1,0:T(8,128)S(1)}, f32[4,64,256]{2,1,0:T(8,128)S(1)}, u32[]{:S(2)}, u32[]{:S(2)}) collective-permute-start(f32[4,64,256]{2,1,0:T(8,128)S(1)} %get-tuple-element.119), channel_id=1, source_target_pairs={{0,1},{1,0},{2,3},{3,2},{4,5},{5,4},{6,7},{7,6},{8,9},{9,8},{10,11... | collective-permute-start | bytes 786440 | tf_op jit(solution)/shard_map/ppermute | solution.py:847

commit v8 on v6

--- a/solution.py
+++ b/solution.py
@@ -15,7 +15,7 @@
 TILE = 8
 SWEPT = 11
 LAST_FLOPS = 10000000000
-PACK_FLOPS = 1100000000
+PACK_FLOPS = 700000000
 FLOPS = 2200000000
 S, C, T, F, K = range(5)
 ONE = 4
@@ -474,7 +474,7 @@
 
 def choose_half(up, down, *refs):
     for j in range(4):
-        refs[j // 2 - 2][j % 2] = jnp.where(lax.axis_index("gz") == 0, down[j], up[j])
+        refs[j - 4][...] = jnp.where(lax.axis_index("gz") == 0, down[j], up[j])
 
 
 def coefficients(refs):
@@ -487,8 +487,8 @@
     ny, narrow = up.shape[1], up.shape[2]
     outside, inside = core, 1 - core
     for j in range(4):
-        side[j, outside, 0:ny, 0:narrow] = jnp.where(core == 0, up[j], passed[j // 2][j % 2])
-        side[j, outside, 0:ny, narrow : 2 * narrow] = jnp.where(core == 0, passed[j // 2][j % 2], down[j])
+        side[j, outside, 0:ny, 0:narrow] = jnp.where(core == 0, up[j], passed[j][...])
+        side[j, outside, 0:ny, narrow : 2 * narrow] = jnp.where(core == 0, passed[j][...], down[j])
         side[j, inside, 0:ny] = near[j]
         side[j, inside, ny : ny + TILE] = near_ghost[j]
 
@@ -579,7 +579,7 @@
 
 
 def middle(block, ghost, near, near_ghost, up, down, *refs):
-    passed, weights, outs = refs[:2], coefficients(refs[2:16]), refs[16:]
+    passed, weights, outs = refs[:4], coefficients(refs[4:18]), refs[18:]
     fill_sides(near, near_ghost, up, down, passed, outs[0])
     sweep(False, block, ghost, weights, *outs)
 
@@ -647,7 +647,8 @@
     put(on_b, out)
 
 
-def outward_first(ky_mid, kz_mid, ky_rim, kz_rim, adjoint, inward, sa, b2, fa, along, cross):
+def outward_first(ky_mid, kz_mid, ky_rim, kz_rim, adjoint, inward, sa, b2, fa, *parts):
+    inside_keep, inside_give, along, cross = parts
     core = lax.axis_index("gz")
     half, ny = adjoint.shape[0], along.shape[0]
     values = []
@@ -659,6 +660,7 @@
     low, high = values
     for t in range(ny // TILE):
         along[at(t)], cross[at(t)] = halves(core, jnp.where(core == 0, low[t], high[t]))
+        inside_keep[at(t)], inside_give[at(t)] = halves(core, jnp.where(core == 0, high[t], low[t]))
     for which in range(2):
         put(fa.at[which], values[which])
 
@@ -773,11 +775,11 @@
 
 
 def finish_outside(block, ghost, edge, side, b2_out, value, term, adjoint0, hot0, off_b, *refs):
-    *six, fa_out, _, keep, give = refs
+    *six, _, keep, give = refs
     core = lax.axis_index("gz")
     parts = from_beyond(core, off_b, block, ghost, edge, side, b2_out, value, term, adjoint0, hot0, three(six))
     for t, total, next_total, sink, _ in parts:
-        for place, value_here in enumerate((total, next_total, sink, fa_out[1 - core, at(t)])):
+        for place, value_here in enumerate((total, next_total, sink)):
             keep[place, at(t)], give[place, at(t)] = halves(core, value_here)
 
 
@@ -786,7 +788,7 @@
     along_out[...] = along[...]
 
 
-def assemble(labels, keep, got, keep_last, got_last, along, cross, grad_state, grad_sink, *refs):
+def assemble(labels, keep, got, keep_last, got_last, inside_keep, inside_got, along, cross, grad_state, grad_sink, *refs):
     masked, ends, sems = refs
     core = lax.axis_index("gz")
     count = grad_state.shape[0]
@@ -797,7 +799,7 @@
         copies.append(pltpu.make_async_copy(source, target, sems.at[len(copies)]))
         copies[-1].start()
 
-    sides = ((core, keep, keep_last, got_last.at[3], cross), (1 - core, got, got_last, keep_last.at[3], along))
+    sides = ((core, keep, keep_last, inside_got, cross), (1 - core, got, got_last, inside_keep, along))
     plane = lambda who, r: who * (count - 1) + r * (1 - 2 * who)
     for who, most, outermost, _, _ in sides:
         send(outermost.at[1], grad_state.at[plane(who, 1)])
@@ -872,10 +874,11 @@
         functools.partial(pack_off, two, count_y), [(ny + (len(PACKED) if two else 5) * TILE, wide), (7, TILE, wide)],
         block, mids[4], *rims[:ways], flops=PACK_FLOPS,
     )
+    passed = call(choose_half, [(ny, nz)] * 4, up, down, *rims)
+    passed = [swap_cores(x) for x in passed]
     off = swap_chips(off)
     own, outer = (half, rows, wide), (2, rows, wide)
     (on_b,) = call(inside_adjoint, [(rows, wide)], block, ghost, near, near_ghost, *mids, *edges)
-    passed = [swap_cores(x) for x in call(choose_half, [(2, ny, nz)] * 2, up, down, on_b)]
     on_b = swap_cores(on_b)
     swept_shapes = [(4, 2, rows, wide), outer, outer, own, outer, outer, own, own, own, own, outer]
     assert len(swept_shapes) == SWEPT
@@ -888,11 +891,12 @@
     side, edge, add, first, known, linear, adjoint, sa, b2, hot2, inward = swept
     off_b = swap_chips(off_b)
     half_plane = (ny, nz)
-    fa_out, along, cross = call(
-        outward_first, [outer] + [half_plane] * 2,
+    fa_out, inside_keep, inside_give, along, cross = call(
+        outward_first, [outer] + [half_plane] * 4,
         mids[1], mids[2], edges[1], edges[2], adjoint, inward, sa_out, b2_out,
     )
     cross, along = swap_chips(cross), to_slabs(along)
+    inside_got = swap_cores(inside_give)
     main = lambda planes: (planes, ny, wide)
     planes = lambda many: (many, ny, nz)
     value, term, adjoint0, hot0, _, _ = call(
@@ -902,12 +906,12 @@
     ready = (block, ghost, edge, side, b2_out, value, term, adjoint0, hot0)
     keep, give = call(finish_inside, [planes(2 * half - 1)] * 2, *ready, on_b, *mids[:3], *edges[:3])
     got = swap_cores(give)
-    keep_last, give_last = call(finish_outside, [planes(4)] * 2, *ready, off_b, *mids[:3], *edges[:3], fa_out, keep, flops=LAST_FLOPS)
+    keep_last, give_last = call(finish_outside, [planes(3)] * 2, *ready, off_b, *mids[:3], *edges[:3], keep, flops=LAST_FLOPS)
     got_last = swap_cores(give_last)
     cross, along = call(take, [half_plane] * 2, cross, along, flops=FLOPS)
     grad_state, grad_sink = call(
         assemble, [state.shape, state.shape],
-        labels, keep, got, keep_last, got_last, along, cross, keep=False,
+        labels, keep, got, keep_last, got_last, inside_keep, inside_got, along, cross, keep=False,
         scratch=[pltpu.VMEM((2, half, ny, nz), jnp.float32), pltpu.VMEM((2, 2, ny, nz), jnp.float32), pltpu.SemaphoreType.DMA((2 * half + 4,))],
     )
     return (grad_state, grad_sink)

time: 35.2 us -> 35 us (level)
  waiting for transfers between devices: 9.21 us -> 8.19 us
  starting transfers between devices: 12.7 us -> 13.5 us
    ppermute x1, waiting for transfers between devices: 0.96 us -> 3.76 us  [on_device(): down = lax.ppermute(down, 'gx', behind)]
    ppermute x2, waiting for transfers between devices: 2.83 us -> 1.18 us  [along_y(): lax.ppermute(rim, 'gy', routes[i % len(routes)])]
    ppermute x1, waiting for transfers between devices: 0.86 us -> 0.01 us  [to_slabs(): return lax.ppermute(x, ('gx', 'gz'), route)]
    ppermute x3, waiting for transfers between devices: 3.6 us -> 2.91 us  [swap_chips(): return lax.ppermute(x, ('gx', 'gz'), chips)]
    ppermute x6 -> x9, starting transfers between devices: 1.31 us -> 1.95 us  [swap_cores(): return lax.ppermute(x, 'gz', [(0, 1), (1, 0)])]
    ppermute x6 -> x9, waiting for transfers between devices: 0.96 us -> 0.34 us  [swap_cores(): return lax.ppermute(x, 'gz', [(0, 1), (1, 0)])]
  transfers between devices with their start and end apart: 14 -> 17, of which waited for: 9 -> 6; matrix products, arithmetic and copies ran while one was open for 0% -> 0% of each run, Pallas kernels for 27% -> 27%
where the time goes in v8:
time: 35 us; the launch traced here: 34.8 us
  starting transfers between devices  13.5 us (39%)
  Pallas kernels  12.3 us (35%)
  waiting for transfers between devices  8.19 us (23%)
  between operations  0.8 us (2%)
    pallas_call x17, Pallas kernels, call(): pl.pallas_call(kernel, out_shape=[space(shape, jnp.float32) for shape in...  12.3 us
    ppermute x3, starting transfers between devices, swap_chips(): return lax.ppermute(x, ('gx', 'gz'), chips)  4.38 us
    ppermute x1, waiting for transfers between devices, on_device(): down = lax.ppermute(down, 'gx', behind)  3.76 us
    ppermute x3, waiting for transfers between devices, swap_chips(): return lax.ppermute(x, ('gx', 'gz'), chips)  2.91 us
    ppermute x1, starting transfers between devices, on_device(): up = lax.ppermute(up, 'gx', ahead)  2.64 us
    ppermute x1, starting transfers between devices, on_device(): down = lax.ppermute(down, 'gx', behind)  2.11 us
    ppermute x2, starting transfers between devices, along_y(): lax.ppermute(rim, 'gy', routes[i % len(routes)])  2.09 us
    ppermute x9, starting transfers between devices, swap_cores(): return lax.ppermute(x, 'gz', [(0, 1), (1, 0)])  1.95 us
  transfers between devices with their start and end apart: 17, of which 6 were waited for; matrix products, arithmetic and copies ran while one was open for 0% of the time, Pallas kernels for 27%

profile of v8, /device:TPU:0, one launch (start us, length us, event | category | flops | bytes accessed | tf_op | source)
XLA Modules:
  0.0 34.8 jit_solution(6711540875867411982)
XLA Ops:
  0.6 1.9 %shard_map.69 = (f32[4,64,256]{2,1,0:T(8,128)S(1)}, f32[4,64,256]{2,1,0:T(8,128)S(1)}, f32[5,6,64,256]{3,2,1,0:T(8,128)S(1)}) custom-call(f32[8,64,256]{2,1,0:T(8,128)} %state.3, f32[8,64,256]{2,1,0:T(8,128)} %conduct.3, f32[8,64,256]{2,1,0:T(8,128)} %sink.3, s32[8,64,256]{2,1,0:T(8,128)} %labels.5, f32[8,64,256]{2,1,0:T(8,128)} %cotangent.3), custom_call_target="tpu_custom_call" | custom-call | flops 1024 | bytes 1024 | tf_op jit(solution)/shard_map/pallas_call | solution.py:27
  2.6 0.5 %collective-permute-start = (f32[5,6,64,256]{3,2,1,0:T(8,128)S(1)}, f32[5,6,64,256]{3,2,1,0:T(8,128)S(1)}, u32[]{:S(2)}, u32[]{:S(2)}) collective-permute-start(f32[5,6,64,256]{3,2,1,0:T(8,128)S(1)} %get-tuple-element.68), channel_id=1, source_target_pairs={{0,1},{1,0},{2,3},{3,2},{4,5},{5,4},{6,7},{7,6},{8,9},{9,8},{10,11... | collective-permute-start | bytes 5898248 | tf_op jit(solution)/shard_map/ppermute | solution.py:834
  3.1 2.6 %collective-permute-start.4 = (f32[4,64,256]{2,1,0:T(8,128)S(1)}, f32[4,64,256]{2,1,0:T(8,128)S(1)}, u32[]{:S(2)}, u32[]{:S(2)}) collective-permute-start(f32[4,64,256]{2,1,0:T(8,128)S(1)} %get-tuple-element.90), channel_id=1, source_target_pairs={{0,4},{4,8},{8,12},{12,0},{1,5},{5,9},{9,13},{13,1},{2,6},{6,10},{... | collective-permute-start | bytes 786440 | tf_op jit(solution)/shard_map/ppermute | solution.py:859
  5.7 2.1 %collective-permute-start.5 = (f32[4,64,256]{2,1,0:T(8,128)S(1)}, f32[4,64,256]{2,1,0:T(8,128)S(1)}, u32[]{:S(2)}, u32[]{:S(2)}) collective-permute-start(f32[4,64,256]{2,1,0:T(8,128)S(1)} %get-tuple-element.91), channel_id=1, source_target_pairs={{4,0},{8,4},{12,8},{0,12},{5,1},{9,5},{13,9},{1,13},{6,2},{10,6},{... | collective-permute-start | bytes 786440 | tf_op jit(solution)/shard_map/ppermute | solution.py:860
  7.8 1.6 %shard_map.68.mine = f32[5,6,64,256]{3,2,1,0:T(8,128)S(1)} custom-call(f32[8,64,256]{2,1,0:T(8,128)} %state.3, f32[8,64,256]{2,1,0:T(8,128)} %conduct.3, f32[8,64,256]{2,1,0:T(8,128)} %sink.3, s32[8,64,256]{2,1,0:T(8,128)} %labels.5, f32[8,64,256]{2,1,0:T(8,128)} %cotangent.3), custom_call_target="tpu_custom_call" | custom-call | flops 1024 | bytes 1024 | tf_op jit(solution)/shard_map/pallas_call | solution.py:27
  9.4 0.0 collective-permute-done.traded
  9.4 0.3 shard_map.70
  9.7 1.7 %collective-permute-start.1 = (f32[4,8,512]{2,1,0:T(8,128)S(1)}, f32[4,8,512]{2,1,0:T(8,128)S(1)}, u32[]{:S(2)}, u32[]{:S(2)}) collective-permute-start(f32[4,8,512]{2,1,0:T(8,128)S(1)} %get-tuple-element.71), channel_id=1, source_target_pairs={{0,2},{2,0},{1,3},{3,1},{4,6},{6,4},{5,7},{7,5},{8,10},{10,8},{9,1... | collective-permute-start | bytes 196616 | tf_op jit(solution)/shard_map/ppermute | solution.py:847
  11.4 0.4 %collective-permute-start.2 = (f32[10,8,512]{2,1,0:T(8,128)S(1)}, f32[10,8,512]{2,1,0:T(8,128)S(1)}, u32[]{:S(2)}, u32[]{:S(2)}) collective-permute-start(f32[10,8,512]{2,1,0:T(8,128)S(1)} %get-tuple-element.72), channel_id=1, source_target_pairs={{0,2},{2,0},{1,3},{3,1},{4,6},{6,4},{5,7},{7,5},{8,10},{10,8},{9,1... | collective-permute-start | bytes 491528 | tf_op jit(solution)/shard_map/ppermute | solution.py:847
  11.8 1.4 %shard_map.73 = (f32[3,48,512]{2,1,0:T(8,128)S(1)}, f32[4,48,512]{2,1,0:T(8,128)S(1)}, f32[4,48,512]{2,1,0:T(8,128)S(1)}, f32[4,48,512]{2,1,0:T(8,128)S(1)}, f32...) custom-call(f32[5,4,64,512]{3,2,1,0:T(8,128)S(1)} %get-tuple-element.69.block, ...), custom_call_target="tpu_custom_call" | custom-call | flops 1024 | bytes 1024 | tf_op jit(solution)/shard_map/pallas_call | solution.py:27
  13.3 1.2 %collective-permute-done.1.refs_0_ = f32[4,8,512]{2,1,0:T(8,128)S(1)} collective-permute-done((f32[4,8,512]{2,1,0:T(8,128)S(1)}, f32[4,8,512]{2,1,0:T(8,128)S(1)}, u32[]{:S(2)}, u32[]{:S(2)}) %collective-permute-start.1) | collective-permute-done | bytes 65568 | tf_op jit(solution)/shard_map/ppermute | solution.py:847
  14.5 0.8 %shard_map.74 = (f32[80,512]{1,0:T(8,128)S(1)}, f32[7,8,512]{2,1,0:T(8,128)}) custom-call(f32[5,4,64,512]{3,2,1,0:T(8,128)S(1)} %get-tuple-element.69.block, f32[4,48,512]{2,1,0:T(8,128)S(1)} %get-tuple-element.74.part_mid.refs_8_.refs_4_, f32[4,8,512]{2,1,0:T(8,128)S(1)} %collective-permute-done.1.refs_0_), custom_call_target="tpu_custom_call" | custom-call | flops 700000000 | bytes 1024 | tf_op jit(solution)/shard_map/pallas_call | solution.py:27
  15.2 0.7 %collective-permute-start.3 = (f32[80,512]{1,0:T(8,128)S(1)}, f32[80,512]{1,0:T(8,128)S(1)}, u32[]{:S(2)}, u32[]{:S(2)}) collective-permute-start(f32[80,512]{1,0:T(8,128)S(1)} %get-tuple-element.75), channel_id=1, source_target_pairs={{1,4},{5,8},{9,12},{13,0},{4,1},{8,5},{12,9},{0,13},{3,6},{7,10},{... | collective-permute-start | bytes 491528 | tf_op jit(solution)/shard_map/ppermute | solution.py:837
  15.9 0.0 collective-permute-done.4.up
  15.9 3.8 %collective-permute-done.5.down = f32[4,64,256]{2,1,0:T(8,128)S(1)} collective-permute-done((f32[4,64,256]{2,1,0:T(8,128)S(1)}, f32[4,64,256]{2,1,0:T(8,128)S(1)}, u32[]{:S(2)}, u32[]{:S(2)}) %collective-permute-start.5) | collective-permute-done | bytes 262176 | tf_op jit(solution)/shard_map/ppermute | solution.py:860
  19.7 0.0 collective-permute-done.2.refs_1_
  19.7 0.1 collective-permute-start.6
  19.8 0.5 %collective-permute-start.7 = (f32[64,256]{1,0:T(8,128)S(1)}, f32[64,256]{1,0:T(8,128)S(1)}, u32[]{:S(2)}, u32[]{:S(2)}) collective-permute-start(f32[64,256]{1,0:T(8,128)S(1)} %get-tuple-element.93), channel_id=1, source_target_pairs={{0,1},{1,0},{2,3},{3,2},{4,5},{5,4},{6,7},{7,6},{8,9},{9,8},{10,11... | collective-permute-start | bytes 196616 | tf_op jit(solution)/shard_map/ppermute | solution.py:834
  20.3 0.1 collective-permute-start.8
  20.4 0.4 %collective-permute-start.9 = (f32[64,256]{1,0:T(8,128)S(1)}, f32[64,256]{1,0:T(8,128)S(1)}, u32[]{:S(2)}, u32[]{:S(2)}) collective-permute-start(f32[64,256]{1,0:T(8,128)S(1)} %get-tuple-element.95), channel_id=1, source_target_pairs={{0,1},{1,0},{2,3},{3,2},{4,5},{5,4},{6,7},{7,6},{8,9},{9,8},{10,11... | collective-permute-start | bytes 196616 | tf_op jit(solution)/shard_map/ppermute | solution.py:834
  20.8 0.8 %shard_map.72 = (f32[5,4,8,512]{3,2,1,0:T(8,128)S(1)}, f32[7,8,512]{2,1,0:T(8,128)S(1)}, f32[3,24,512]{2,1,0:T(8,128)S(1)}, f32[4,24,512]{2,1,0:T(8,128)S(1)}, f...) custom-call(f32[5,4,64,512]{3,2,1,0:T(8,128)S(1)} %get-tuple-element, ...), custom_call_target="tpu_custom_call" | custom-call | flops 1024 | bytes 1024 | tf_op jit(solution)/shard_map/pallas_call | solution.py:27
  21.6 0.3 shard_map.80
  22.0 0.0 collective-permute-done.6.refs_0_
  22.0 0.1 collective-permute-start.10
  22.1 0.0 collective-permute-done.7.refs_1_
  22.1 0.0 collective-permute-done.8.refs_2_
  22.1 0.0 collective-permute-done.9.refs_3_
  22.1 0.9 %shard_map.76 = (f32[4,2,72,512]{3,2,1,0:T(8,128)S(1)}, f32[2,72,512]{2,1,0:T(8,128)S(1)}, f32[2,72,512]{2,1,0:T(8,128)S(1)}, f32[4,72,512]{2,1,0:T(8,128)S(1)},...) custom-call(f32[5,4,64,512]{3,2,1,0:T(8,128)S(1)} %get-tuple-element, ...), custom_call_target="tpu_custom_call" | custom-call | flops 1024 | bytes 1024 | tf_op jit(solution)/shard_map/pallas_call | solution.py:27
  23.1 0.5 %collective-permute-done.3.off = f32[80,512]{1,0:T(8,128)S(1)} collective-permute-done((f32[80,512]{1,0:T(8,128)S(1)}, f32[80,512]{1,0:T(8,128)S(1)}, u32[]{:S(2)}, u32[]{:S(2)}) %collective-permute-start.3) | collective-permute-done | bytes 163872 | tf_op jit(solution)/shard_map/ppermute | solution.py:837
  23.6 0.4 %shard_map.77 = (f32[4,2,72,512]{3,2,1,0:T(8,128)S(1)}, f32[2,72,512]{2,1,0:T(8,128)S(1)}, f32[2,72,512]{2,1,0:T(8,128)S(1)}, f32[4,72,512]{2,1,0:T(8,128)S(1)},...) custom-call(f32[5,4,64,512]{3,2,1,0:T(8,128)S(1)} %get-tuple-element, ...), custom_call_target="tpu_custom_call", output_to_operand_aliasing={{0}: (17, {}), {1}: (18, {}), {2}: (19, {}), {3}: (20, {}),... | custom-call | flops 1024 | bytes 1024 | tf_op jit(solution)/shard_map/pallas_call | solution.py:27
  24.0 2.2 %collective-permute-start.12 = (f32[72,512]{1,0:T(8,128)S(1)}, f32[72,512]{1,0:T(8,128)S(1)}, u32[]{:S(2)}, u32[]{:S(2)}) collective-permute-start(f32[72,512]{1,0:T(8,128)S(1)} %get-tuple-element.125), channel_id=1, source_target_pairs={{1,4},{5,8},{9,12},{13,0},{4,1},{8,5},{12,9},{0,13},{3,6},{7,10},{... | collective-permute-start | bytes 442376 | tf_op jit(solution)/shard_map/ppermute | solution.py:837
  26.3 0.2 shard_map.78
  26.5 0.1 collective-permute-start.14
  26.6 1.4 %collective-permute-start.15 = (f32[64,256]{1,0:T(8,128)S(1)}, f32[64,256]{1,0:T(8,128)S(1)}, u32[]{:S(2)}, u32[]{:S(2)}) collective-permute-start(f32[64,256]{1,0:T(8,128)S(1)} %get-tuple-element.130), channel_id=1, source_target_pairs={{1,4},{5,8},{9,12},{13,0},{4,1},{8,5},{12,9},{0,13},{3,6},{7,10},{... | collective-permute-start | bytes 196616 | tf_op jit(solution)/shard_map/ppermute | solution.py:837
  28.0 0.3 collective-permute-start.16
  28.4 2.0 %shard_map.79 = (f32[4,64,512]{2,1,0:T(8,128)S(1)}, f32[4,64,512]{2,1,0:T(8,128)S(1)}, f32[2,64,512]{2,1,0:T(8,128)S(1)}, f32[2,64,512]{2,1,0:T(8,128)S(1)}, f32...) custom-call(f32[5,4,64,512]{3,2,1,0:T(8,128)S(1)} %get-tuple-element.69.block, f32[5,4,8,512]{3,2,1,0:T(8,128)S(1)} %get-tuple-element.73.ghost, ...), custom_call_target="tpu_custom_call" | custom-call | flops 1024 | bytes 1024 | tf_op jit(solution)/shard_map/pallas_call | solution.py:27
  30.3 0.0 collective-permute-done.10.on_b
  30.3 0.2 shard_map.81
  30.6 0.1 collective-permute-start.11
  30.6 1.4 %collective-permute-done.12.off_b = f32[72,512]{1,0:T(8,128)S(1)} collective-permute-done((f32[72,512]{1,0:T(8,128)S(1)}, f32[72,512]{1,0:T(8,128)S(1)}, u32[]{:S(2)}, u32[]{:S(2)}) %collective-permute-start.12) | collective-permute-done | bytes 147488 | tf_op jit(solution)/shard_map/ppermute | solution.py:837
  32.0 0.2 shard_map.82
  32.2 0.0 copy-start
  32.2 0.1 collective-permute-start.13
  32.3 1.1 %collective-permute-done.15.cross = f32[64,256]{1,0:T(8,128)S(1)} collective-permute-done((f32[64,256]{1,0:T(8,128)S(1)}, f32[64,256]{1,0:T(8,128)S(1)}, u32[]{:S(2)}, u32[]{:S(2)}) %collective-permute-start.15) | collective-permute-done | bytes 65568 | tf_op jit(solution)/shard_map/ppermute | solution.py:837
  33.4 0.0 collective-permute-done.16.along
  33.4 0.3 collective-permute-done.13.got_last
  33.7 0.0 collective-permute-done.11.got
  33.7 1.1 %shard_map.84 = (f32[8,64,256]{2,1,0:T(8,128)}, f32[8,64,256]{2,1,0:T(8,128)}) custom-call(s32[8,64,256]{2,1,0:T(8,128)S(1)} %copy-done, f32[7,64,256]{2,1,0:T(8,128)S(1)} %get-tuple-element.123.refs_6_.keep, f32[7,64,256]{2,1,0:T(8,128)S(1)} %collective-permute-done.11.got, f32[3,64,256]{2,1,0:T(8,128)S(1)} %get-tuple-element.126.keep_last, ...), custom_call_target="tpu_custom_call" | custom-call | flops 1024 | bytes 1024 | tf_op jit(solution)/shard_map/pallas_call | solution.py:27
  (5 shorter events, 0.1 us)
Async XLA Ops:
  2.6 6.9 %collective-permute-start = (f32[5,6,64,256]{3,2,1,0:T(8,128)S(1)}, f32[5,6,64,256]{3,2,1,0:T(8,128)S(1)}, u32[]{:S(2)}, u32[]{:S(2)}) collective-permute-start(f32[5,6,64,256]{3,2,1,0:T(8,128)S(1)} %get-tuple-element.68), channel_id=1, source_target_pairs={{0,1},{1,0},{2,3},{3,2},{4,5},{5,4},{6,7},{7,6},{8,9},{9,8},{10,11... | collective-permute-start | bytes 5898248 | tf_op jit(solution)/shard_map/ppermute | solution.py:834
  3.1 12.9 %collective-permute-start.4 = (f32[4,64,256]{2,1,0:T(8,128)S(1)}, f32[4,64,256]{2,1,0:T(8,128)S(1)}, u32[]{:S(2)}, u32[]{:S(2)}) collective-permute-start(f32[4,64,256]{2,1,0:T(8,128)S(1)} %get-tuple-element.90), channel_id=1, source_target_pairs={{0,4},{4,8},{8,12},{12,0},{1,5},{5,9},{9,13},{13,1},{2,6},{6,10},{... | collective-permute-start | bytes 786440 | tf_op jit(solution)/shard_map/ppermute | solution.py:859
  5.7 14.0 %collective-permute-start.5 = (f32[4,64,256]{2,1,0:T(8,128)S(1)}, f32[4,64,256]{2,1,0:T(8,128)S(1)}, u32[]{:S(2)}, u32[]{:S(2)}) collective-permute-start(f32[4,64,256]{2,1,0:T(8,128)S(1)} %get-tuple-element.91), channel_id=1, source_target_pairs={{4,0},{8,4},{12,8},{0,12},{5,1},{9,5},{13,9},{1,13},{6,2},{10,6},{... | collective-permute-start | bytes 786440 | tf_op jit(solution)/shard_map/ppermute | solution.py:860
  9.7 4.7 %collective-permute-start.1 = (f32[4,8,512]{2,1,0:T(8,128)S(1)}, f32[4,8,512]{2,1,0:T(8,128)S(1)}, u32[]{:S(2)}, u32[]{:S(2)}) collective-permute-start(f32[4,8,512]{2,1,0:T(8,128)S(1)} %get-tuple-element.71), channel_id=1, source_target_pairs={{0,2},{2,0},{1,3},{3,1},{4,6},{6,4},{5,7},{7,5},{8,10},{10,8},{9,1... | collective-permute-start | bytes 196616 | tf_op jit(solution)/shard_map/ppermute | solution.py:847
  11.4 8.3 %collective-permute-start.2 = (f32[10,8,512]{2,1,0:T(8,128)S(1)}, f32[10,8,512]{2,1,0:T(8,128)S(1)}, u32[]{:S(2)}, u32[]{:S(2)}) collective-permute-start(f32[10,8,512]{2,1,0:T(8,128)S(1)} %get-tuple-element.72), channel_id=1, source_target_pairs={{0,2},{2,0},{1,3},{3,1},{4,6},{6,4},{5,7},{7,5},{8,10},{10,8},{9,1... | collective-permute-start | bytes 491528 | tf_op jit(solution)/shard_map/ppermute | solution.py:847
  15.2 8.3 %collective-permute-start.3 = (f32[80,512]{1,0:T(8,128)S(1)}, f32[80,512]{1,0:T(8,128)S(1)}, u32[]{:S(2)}, u32[]{:S(2)}) collective-permute-start(f32[80,512]{1,0:T(8,128)S(1)} %get-tuple-element.75), channel_id=1, source_target_pairs={{1,4},{5,8},{9,12},{13,0},{4,1},{8,5},{12,9},{0,13},{3,6},{7,10},{... | collective-permute-start | bytes 491528 | tf_op jit(solution)/shard_map/ppermute | solution.py:837
  19.7 2.2 %collective-permute-start.6 = (f32[64,256]{1,0:T(8,128)S(1)}, f32[64,256]{1,0:T(8,128)S(1)}, u32[]{:S(2)}, u32[]{:S(2)}) collective-permute-start(f32[64,256]{1,0:T(8,128)S(1)} %get-tuple-element.92), channel_id=1, source_target_pairs={{0,1},{1,0},{2,3},{3,2},{4,5},{5,4},{6,7},{7,6},{8,9},{9,8},{10,11... | collective-permute-start | bytes 196616 | tf_op jit(solution)/shard_map/ppermute | solution.py:834
  19.8 2.3 %collective-permute-start.7 = (f32[64,256]{1,0:T(8,128)S(1)}, f32[64,256]{1,0:T(8,128)S(1)}, u32[]{:S(2)}, u32[]{:S(2)}) collective-permute-start(f32[64,256]{1,0:T(8,128)S(1)} %get-tuple-element.93), channel_id=1, source_target_pairs={{0,1},{1,0},{2,3},{3,2},{4,5},{5,4},{6,7},{7,6},{8,9},{9,8},{10,11... | collective-permute-start | bytes 196616 | tf_op jit(solution)/shard_map/ppermute | solution.py:834
  20.3 1.8 %collective-permute-start.8 = (f32[64,256]{1,0:T(8,128)S(1)}, f32[64,256]{1,0:T(8,128)S(1)}, u32[]{:S(2)}, u32[]{:S(2)}) collective-permute-start(f32[64,256]{1,0:T(8,128)S(1)} %get-tuple-element.94), channel_id=1, source_target_pairs={{0,1},{1,0},{2,3},{3,2},{4,5},{5,4},{6,7},{7,6},{8,9},{9,8},{10,11... | collective-permute-start | bytes 196616 | tf_op jit(solution)/shard_map/ppermute | solution.py:834
  20.4 1.7 %collective-permute-start.9 = (f32[64,256]{1,0:T(8,128)S(1)}, f32[64,256]{1,0:T(8,128)S(1)}, u32[]{:S(2)}, u32[]{:S(2)}) collective-permute-start(f32[64,256]{1,0:T(8,128)S(1)} %get-tuple-element.95), channel_id=1, source_target_pairs={{0,1},{1,0},{2,3},{3,2},{4,5},{5,4},{6,7},{7,6},{8,9},{9,8},{10,11... | collective-permute-start | bytes 196616 | tf_op jit(solution)/shard_map/ppermute | solution.py:834
  22.0 8.4 %collective-permute-start.10 = (f32[72,512]{1,0:T(8,128)S(1)}, f32[72,512]{1,0:T(8,128)S(1)}, u32[]{:S(2)}, u32[]{:S(2)}) collective-permute-start(f32[72,512]{1,0:T(8,128)S(1)} %shard_map.80), channel_id=1, source_target_pairs={{0,1},{1,0},{2,3},{3,2},{4,5},{5,4},{6,7},{7,6},{8,9},{9,8},{10,11... | collective-permute-start | bytes 442376 | tf_op jit(solution)/shard_map/ppermute | solution.py:834
  24.0 8.0 %collective-permute-start.12 = (f32[72,512]{1,0:T(8,128)S(1)}, f32[72,512]{1,0:T(8,128)S(1)}, u32[]{:S(2)}, u32[]{:S(2)}) collective-permute-start(f32[72,512]{1,0:T(8,128)S(1)} %get-tuple-element.125), channel_id=1, source_target_pairs={{1,4},{5,8},{9,12},{13,0},{4,1},{8,5},{12,9},{0,13},{3,6},{7,10},{... | collective-permute-start | bytes 442376 | tf_op jit(solution)/shard_map/ppermute | solution.py:837
  26.5 6.9 %collective-permute-start.14 = (f32[64,256]{1,0:T(8,128)S(1)}, f32[64,256]{1,0:T(8,128)S(1)}, u32[]{:S(2)}, u32[]{:S(2)}) collective-permute-start(f32[64,256]{1,0:T(8,128)S(1)} %get-tuple-element.129), channel_id=1, source_target_pairs={{0,1},{1,0},{2,3},{3,2},{4,5},{5,4},{6,7},{7,6},{8,9},{9,8},{10,11... | collective-permute-start | bytes 196616 | tf_op jit(solution)/shard_map/ppermute | solution.py:834
  26.6 6.8 %collective-permute-start.15 = (f32[64,256]{1,0:T(8,128)S(1)}, f32[64,256]{1,0:T(8,128)S(1)}, u32[]{:S(2)}, u32[]{:S(2)}) collective-permute-start(f32[64,256]{1,0:T(8,128)S(1)} %get-tuple-element.130), channel_id=1, source_target_pairs={{1,4},{5,8},{9,12},{13,0},{4,1},{8,5},{12,9},{0,13},{3,6},{7,10},{... | collective-permute-start | bytes 196616 | tf_op jit(solution)/shard_map/ppermute | solution.py:837
  28.0 5.3 %collective-permute-start.16 = (f32[64,256]{1,0:T(8,128)S(1)}, f32[64,256]{1,0:T(8,128)S(1)}, u32[]{:S(2)}, u32[]{:S(2)}) collective-permute-start(f32[64,256]{1,0:T(8,128)S(1)} %get-tuple-element.131), channel_id=1, source_target_pairs={{0,12},{1,5},{4,0},{5,9},{8,4},{9,13},{12,8},{13,1},{2,14},{3,7},{... | collective-permute-start | bytes 196616 | tf_op jit(solution)/shard_map/ppermute | solution.py:841
  30.6 3.1 %collective-permute-start.11 = (f32[7,64,256]{2,1,0:T(8,128)S(1)}, f32[7,64,256]{2,1,0:T(8,128)S(1)}, u32[]{:S(2)}, u32[]{:S(2)}) collective-permute-start(f32[7,64,256]{2,1,0:T(8,128)S(1)} %get-tuple-element.124), channel_id=1, source_target_pairs={{0,1},{1,0},{2,3},{3,2},{4,5},{5,4},{6,7},{7,6},{8,9},{9,8},{10,11... | collective-permute-start | bytes 1376264 | tf_op jit(solution)/shard_map/ppermute | solution.py:834
  32.2 1.5 %copy-start = (s32[8,64,256]{2,1,0:T(8,128)S(1)}, s32[8,64,256]{2,1,0:T(8,128)}, u32[]{:S(2)}) copy-start(s32[8,64,256]{2,1,0:T(8,128)} %labels.5) | copy-start | bytes 1572868
  32.2 1.5 %collective-permute-start.13 = (f32[3,64,256]{2,1,0:T(8,128)S(1)}, f32[3,64,256]{2,1,0:T(8,128)S(1)}, u32[]{:S(2)}, u32[]{:S(2)}) collective-permute-start(f32[3,64,256]{2,1,0:T(8,128)S(1)} %get-tuple-element.127), channel_id=1, source_target_pairs={{0,1},{1,0},{2,3},{3,2},{4,5},{5,4},{6,7},{7,6},{8,9},{9,8},{10,11... | collective-permute-start | bytes 589832 | tf_op jit(solution)/shard_map/ppermute | solution.py:834
